TPU v7x, 32 devices: a whole 2x2x4 slice. The times are simulated.
32 devices in a mesh: dp: 4 (over y, x), ctx: 4 (over z), tp: 2 (over core).
Axes of the slice: x: 2, y: 2, z: 4, core: 2. Of those that a mesh axis runs over, the one named last changes fastest.
Arguments:
- query: bfloat16 [2048, 8192], P(('dp', 'ctx'), 'tp'), may hold values from -6 to 6
- key_in: bfloat16 [2048, 8192], P(('dp', 'ctx'), 'tp'), may hold values from -6 to 6
- value_in: bfloat16 [2048, 8192], P(('dp', 'ctx'), 'tp'), may hold values from -6 to 6
- gate: bfloat16 [2048, 8192], P(('dp', 'ctx'), 'tp'), may hold values from -6 to 6
- out_grad: bfloat16 [2048, 8192], P(('dp', 'ctx')), may hold values from -6 to 6
- proj_weight: bfloat16 [8192, 8192], P('tp', ('dp', 'ctx')), may hold values from -0.0625 to 0.0625
- mr_filter: bfloat16 [512, 128], P('tp'), may hold values from -0.5 to 0.5
- lr_rate: float32 [512, 16], P('tp'), may hold values from 3.90625e-05 to 0.05
- lr_residue: float32 [512, 16], P('tp'), may hold values from -0.6 to 0.6
Outputs:
- query_grad: bfloat16 [2048, 8192], P(('dp', 'ctx'), 'tp')
- conv_grad: bfloat16 [2048, 8192], P(('dp', 'ctx'), 'tp')
- gate_grad: bfloat16 [2048, 8192], P(('dp', 'ctx'), 'tp')
- weight_grad_t: bfloat16 [8192, 8192], P(('dp', 'ctx'), 'tp')
All inputs are finite; a program needn't handle non-finite values.
Results may differ from a plain program's by a relative error of at most 0.028.
Values may be sent and summed in bfloat16 or wider, within the bound.
No kernel may reach another device: no remote copies, remote signals or barrier semaphores. Data moves between devices by JAX's collectives and lax.ppermute only.
A program may use at most 256 MiB of HBM per device.

v0:
```python
import functools

import jax
import jax.numpy as jnp
from jax import lax
from jax.experimental import pallas as pl
from jax.experimental.pallas import tpu as pltpu
from jax.sharding import PartitionSpec as P

GROUP = 16
TAPS = 128
ORDER = 16
LANES = 128
PER_SLAB = LANES // GROUP
BF16 = jnp.bfloat16
F32 = jnp.float32
VMEM = 50 * 2**20
ANY = pl.BlockSpec(memory_space=pl.ANY)


def call(body, name, flops, nbytes, **kwargs):
    return pl.pallas_call(
        body,
        name=name,
        cost_estimate=pl.CostEstimate(flops=flops, bytes_accessed=nbytes, transcendentals=0),
        compiler_params=pltpu.CompilerParams(vmem_limit_bytes=VMEM),
        **kwargs,
    )


def circulants(rows_ref, base):
    out = []
    for j in range(PER_SLAB):
        row = rows_ref[base + j : base + j + 1, :]
        out.append(
            pltpu.roll(jnp.broadcast_to(row, (LANES, LANES)), 0, 1, stride=1, stride_axis=0)
        )
    return out


def lower_mask():
    t = lax.broadcasted_iota(jnp.int32, (LANES, LANES), 0)
    u = lax.broadcasted_iota(jnp.int32, (LANES, LANES), 1)
    return u <= t


def pick_groups(stacked, rows):
    lane_group = lax.broadcasted_iota(jnp.int32, (rows, LANES), 1) // GROUP
    out = stacked[:rows]
    for j in range(1, PER_SLAB):
        out = jnp.where(lane_group == j, stacked[j * rows : (j + 1) * rows], out)
    return out


def spread_groups(state):
    tiled = jnp.concatenate([state] * PER_SLAB, axis=0)
    row_group = lax.broadcasted_iota(jnp.int32, (LANES, LANES), 0) // ORDER
    lane_group = lax.broadcasted_iota(jnp.int32, (LANES, LANES), 1) // GROUP
    return jnp.where(row_group == lane_group, tiled, jnp.zeros_like(tiled))


def dot(a, b):
    return jnp.dot(a, b, preferred_element_type=F32)


def conv_body(rim, own_part, query, taps, ends_coef, *refs):
    conv, mixed, ends = refs[-3:]
    lower = lower_mask()
    for s in range(rim.shape[1] // LANES):
        cols = slice(s * LANES, (s + 1) * LANES)
        blocks = [
            jnp.where(lower, jnp.zeros_like(circ), circ).astype(BF16)
            for circ in circulants(taps, s * PER_SLAB)
        ]
        out = own_part[:, cols] + pick_groups(
            dot(jnp.concatenate(blocks, axis=0), rim[:, cols]), LANES
        )
        conv[:, cols] = out.astype(conv.dtype)
        mixed[:, cols] = (query[:, cols].astype(F32) * out).astype(BF16)
    for s in range(rim.shape[1] // LANES):
        cols = slice(s * LANES, (s + 1) * LANES)
        ends[:, cols] = pick_groups(
            dot(ends_coef[s * LANES : (s + 1) * LANES, :], mixed[:, cols]), ORDER
        ).astype(ends.dtype)


def local_body(transposed, rows, x, *refs):
    out = refs[-1]
    lower = lower_mask()
    keep = ~lower | (lax.broadcasted_iota(jnp.int32, (LANES, LANES), 0)
                     == lax.broadcasted_iota(jnp.int32, (LANES, LANES), 1)) if transposed else lower
    for s in range(x.shape[1] // LANES):
        cols = slice(s * LANES, (s + 1) * LANES)
        blocks = [
            jnp.where(keep, circ, jnp.zeros_like(circ)).astype(BF16)
            for circ in circulants(rows, s * PER_SLAB)
        ]
        out[:, cols] = pick_groups(
            dot(jnp.concatenate(blocks, axis=0), x[:, cols]), LANES
        ).astype(out.dtype)


def carried(states, coef, cols):
    wide_states = jnp.concatenate([spread_groups(ref[:, cols]) for ref in states], axis=0)
    count = len(states)
    rows = coef.shape[0] // count
    parts = [coef[k * rows : (k + 1) * rows, cols] for k in range(count)]
    return dot(jnp.concatenate(parts, axis=1), wide_states)


def long_body(count, local, coef, gate, *refs):
    states, (long_out, gated) = refs[:count], refs[-2:]
    for s in range(local.shape[1] // LANES):
        cols = slice(s * LANES, (s + 1) * LANES)
        out = local[:, cols].astype(F32) + carried(states, coef, cols)
        long_out[:, cols] = out.astype(long_out.dtype)
        gated[0, :, cols] = (gate[:, cols].astype(F32) * out).astype(BF16)


def seed_body(delta, gate, long_out, starts_coef, seed, starts, gate_grad):
    for s in range(gate.shape[1] // LANES):
        cols = slice(s * LANES, (s + 1) * LANES)
        out = delta[0, :, cols].astype(F32)
        seed[:, cols] = (out * gate[:, cols].astype(F32)).astype(BF16)
        gate_grad[:, cols] = (out * long_out[:, cols].astype(F32)).astype(BF16)
    for s in range(gate.shape[1] // LANES):
        cols = slice(s * LANES, (s + 1) * LANES)
        starts[:, cols] = pick_groups(
            dot(starts_coef[s * LANES : (s + 1) * LANES, :], seed[:, cols]), ORDER
        ).astype(starts.dtype)


def back_body(count, local, coef, conv, query, *refs):
    states, (query_grad, conv_grad) = refs[:count], refs[-2:]
    for s in range(local.shape[1] // LANES):
        cols = slice(s * LANES, (s + 1) * LANES)
        out = local[:, cols].astype(F32) + carried(states, coef, cols)
        query_grad[:, cols] = (out * conv[:, cols].astype(F32)).astype(BF16)
        conv_grad[:, cols] = (out * query[:, cols].astype(F32)).astype(BF16)


def pack_body(count, place, *refs):
    for source, target in zip(refs[:count], refs[-count:]):
        target[...] = source[...]


def join_body(*refs):
    out = refs[-1]
    for k in range(out.shape[0]):
        out[k] = refs[k][...]


def delta_body(count, place, dest, grad, *refs):
    weights, out = refs[:count], refs[-1]
    depth = weights[0].shape[1]
    total = None
    for k, weight in enumerate(weights):
        start = pl.multiple_of((place[0] ^ k) * depth, depth)
        rows = grad[:, :, :, :, pl.ds(start, depth)].reshape(-1, depth)
        term = lax.dot_general(
            rows, weight[...], (((1,), (1,)), ((), ())), preferred_element_type=F32
        )
        total = term if total is None else total + term
    out[...] = total.astype(out.dtype).reshape(out.shape)


def flip_body(place, grad, after, out):
    out[...] = grad[...].reshape(-1, grad.shape[-1]).T


def lay_body(place, *refs):
    sources, out = refs[:-2], refs[-1]
    for k, source in enumerate(sources):
        lanes = source.shape[1]
        out[:, pl.ds(pl.multiple_of((place[0] ^ k) * lanes, lanes), lanes)] = source[...]


def add_body(dests, partial_right, partial_left, right, left, *refs):
    out_right, out_left = refs[-2:]
    out_right[...] = (partial_right[...].astype(F32) + right[...].astype(F32)).astype(BF16)
    out_left[...] = (partial_left[...].astype(F32) + left[...].astype(F32)).astype(BF16)


def merge_body(own, *refs):
    out = refs[-1]
    count = out.shape[0] - 1
    out[0] = own[...]
    for k in range(count):
        out[k + 1] = refs[k][...] + refs[count + k][...]


def sum_body(dest, partial, right, left, out):
    total = partial[0].astype(F32) + right[0].astype(F32) + left[0].astype(F32)
    out[...] = total.astype(BF16)


def weight_body(place, grad_t, gated, after, out):
    out[...] = dot(grad_t[...], gated[...]).astype(out.dtype)


def wide(rows, lanes):
    return pl.BlockSpec((rows, lanes), lambda i: (0, i))


def tall(rows, cols):
    return pl.BlockSpec((rows, cols), lambda i: (i, 0))


def deep(count, rows, lanes):
    return pl.BlockSpec((count, rows, lanes), lambda i: (0, 0, i))


def shape(*dims, dtype=BF16):
    return jax.ShapeDtypeStruct(dims, dtype)


def on_device(query, key_in, value_in, gate, out_grad, proj_weight, mr_filter, lr_rate, lr_residue):
    rows, width = query.shape
    groups = width // GROUP
    n_dp, n_ctx, n_tp = (lax.axis_size(a) for a in ("dp", "ctx", "tp"))
    feats = proj_weight.shape[1]
    quarter = width // n_dp
    depth = n_dp * feats
    block = quarter
    steps = width // block
    part = rows // n_tp

    place = jnp.stack([lax.axis_index(a) for a in ("dp", "ctx", "tp")]).astype(jnp.int32)

    def swap(value, axis, k):
        return lax.ppermute(value, axis, [(i, i ^ k) for i in range(lax.axis_size(axis))])

    def shift(value, k, senders=None):
        ends = [(i, i + k) for i in senders or range(n_ctx) if 0 <= i + k < n_ctx]
        return lax.ppermute(value, "ctx", ends)

    def piece(k):
        return pl.BlockSpec((part, feats), lambda j, p: (p[2], j * n_ctx + (p[1] ^ k)))

    sent = [
        lax.dynamic_slice_in_dim(proj_weight, (place[0] ^ k) * quarter, quarter)
        for k in range(1, n_dp)
    ]
    weights = [proj_weight] + [swap(value, "dp", k) for k, value in enumerate(sent, 1)]
    mine = call(
        functools.partial(pack_body, n_ctx), "pack", 0, 4 * part * depth * n_ctx,
        grid_spec=pltpu.PrefetchScalarGridSpec(
            num_scalar_prefetch=1, grid=(n_dp,),
            in_specs=[piece(k) for k in range(n_ctx)] + [ANY] * len(sent),
            out_specs=[pl.BlockSpec((part, feats), lambda j, p: (0, j))] * n_ctx,
        ),
        out_shape=[shape(part, depth)] * n_ctx,
    )(place, *[out_grad] * n_ctx, *sent)
    mine = [mine[0]] + [swap(mine[k], "ctx", k) for k in range(1, n_ctx)]
    product = (key_in.astype(F32) * value_in.astype(F32)).astype(BF16)
    rim = shift(product, 1)
    rate = lr_rate.reshape(-1, 1)
    residue = lr_residue.reshape(-1, 1)
    counts = jnp.arange(rows, dtype=F32)[None, :]
    ends_coef = jnp.exp(-rate * (rows - 1 - counts)).astype(BF16)
    starts_coef = jnp.exp(-rate * counts).astype(BF16)
    away = jnp.arange((n_ctx - 1) * rows, dtype=F32)[:, None]
    inside = away % rows
    carry_coef = (residue.T * jnp.exp(-rate.T * (away + 1))).astype(BF16)
    back_coef = (residue.T * jnp.exp(-rate.T * (away + rows - 2 * inside))).astype(BF16)
    kernel = jnp.sum(
        lr_residue[:, :, None] * jnp.exp(-lr_rate[:, :, None] * counts[:, None, :]), axis=1
    )

    def reversed_row(values):
        return jnp.roll(values[:, ::-1], 1, axis=1)

    taps = reversed_row(mr_filter.astype(F32))
    kernel_rev = reversed_row(kernel)
    def local(transposed, table, x, *after):
        return call(
            functools.partial(local_body, transposed),
            "local_t" if transposed else "local",
            2 * rows * 128 * width * 8, rows * width * 6,
            grid=(steps,),
            in_specs=[tall(block // GROUP, rows), wide(rows, block)] + [ANY] * len(after),
            out_specs=wide(rows, block),
            out_shape=shape(rows, width, dtype=F32),
        )(table, x, *after)

    conv_own = local(False, taps, product)
    conv, mixed, ends = call(
        conv_body, "conv", 2 * rows * 128 * width * 8, rows * width * 14,
        grid=(steps,),
        in_specs=[wide(rows, block)] * 3 + [tall(block // GROUP, TAPS), tall(block, rows)],
        out_specs=[wide(rows, block), wide(rows, block), wide(ORDER, block)],
        out_shape=[shape(rows, width), shape(rows, width), shape(ORDER, width)],
    )(rim, conv_own, query, taps, ends_coef)
    ends_far = [shift(ends, k) for k in range(1, n_ctx)]
    mine = call(
        join_body, "join", 0, 4 * part * depth * n_ctx,
        grid=(n_dp,),
        in_specs=[wide(part, feats)] * n_ctx + [ANY] * n_dp,
        out_specs=deep(n_ctx, part, feats),
        out_shape=shape(n_ctx, part, depth),
    )(*mine, *weights[1:], mixed)
    grad = lax.all_gather(mine, ("dp", "tp"), axis=0, tiled=False)
    grad = grad.reshape(n_dp, n_tp, n_ctx, part, depth)


    local_fwd = local(False, kernel_rev, mixed, mine)
    long_out, gated = call(
        functools.partial(long_body, n_ctx - 1), "long", 2 * rows * 128 * width, rows * width * 10,
        grid=(steps,),
        in_specs=[wide(rows, block), wide((n_ctx - 1) * rows, block), wide(rows, block)] + [wide(ORDER, block)] * (n_ctx - 1),
        out_specs=[wide(rows, block), pl.BlockSpec((1, rows, block), lambda i: (i, 0, 0))],
        out_shape=[shape(rows, width), shape(n_dp, rows, quarter)],
    )(local_fwd, carry_coef, gate, *ends_far)
    gated_far = lax.all_to_all(gated, "dp", 0, 0, tiled=True)
    tokens = n_ctx * n_dp * rows
    last = n_ctx - 1
    from_left, from_right = [], []
    right = left = gated_far
    for t in range(last):
        right = shift(right, 1, range(t, last))
        left = shift(left, -1, range(1, n_ctx - t))
        from_left.append(right)
        from_right.append(left)

    first_dest = jnp.where(place[1] < n_ctx // 2, last, 0)
    chunk = (1, n_dp, rows, quarter)

    def project(count, dest, *after):
        return call(
            functools.partial(delta_body, n_dp), "delta", 2 * count * n_dp * rows * depth * quarter,
            2 * tokens * depth + 2 * depth * quarter + 2 * count * n_dp * rows * quarter,
            grid_spec=pltpu.PrefetchScalarGridSpec(
                num_scalar_prefetch=2, grid=(count,),
                in_specs=[
                    pl.BlockSpec(
                        (n_dp, n_tp, 1, part, depth), lambda i, p, q: (0, 0, p[1] ^ q[i], 0, 0)
                    ),
                    pl.BlockSpec((quarter, feats), lambda i, p, q: (p[0], 0)),
                ] + [pl.BlockSpec((quarter, feats), lambda i, p, q: (0, 0))] * (n_dp - 1)
                + [ANY] * len(after),
                out_specs=pl.BlockSpec(chunk, lambda i, p, q: (i, 0, 0, 0)),
            ),
            out_shape=shape(count, n_dp, rows, quarter),
        )(place, dest, grad, *weights, *after)

    first = project(1, first_dest[None], from_left[0], from_right[0])
    partial = project(n_ctx, jnp.arange(n_ctx, dtype=jnp.int32), first)
    right, left = shift(first, 1, [0]), shift(first, -1, [last])

    def pick(ahead):
        return pl.BlockSpec(
            (1, 1, rows, quarter), lambda i, q: (q[ahead], i, 0, 0)
        )

    piece_of = pl.BlockSpec((1, 1, rows, quarter), lambda i, q: (0, i, 0, 0))
    for t in range(1, last):
        dests = jnp.clip(jnp.stack([last - t + place[1], t - last + place[1]]), 0, last)
        right, left = call(
            add_body, "add", 0, 12 * n_dp * rows * quarter,
            grid_spec=pltpu.PrefetchScalarGridSpec(
                num_scalar_prefetch=1, grid=(n_dp,),
                in_specs=[pick(0), pick(1), piece_of, piece_of, ANY, ANY],
                out_specs=[piece_of] * 2,
            ),
            out_shape=[shape(*chunk)] * 2,
        )(dests, partial, partial, right, left, from_left[t], from_right[t])
        token = right
        right = shift(right, 1, range(t + 1))
        left = shift(left, -1, range(last - t, n_ctx))
    delta = call(
        sum_body, "sum", 0, 8 * n_dp * rows * quarter,
        grid_spec=pltpu.PrefetchScalarGridSpec(
            num_scalar_prefetch=1, grid=(n_dp,),
            in_specs=[pick(0), piece_of, piece_of],
            out_specs=pl.BlockSpec((1, rows, quarter), lambda i, q: (i, 0, 0)),
        ),
        out_shape=shape(n_dp, rows, quarter),
    )(place[1:2], partial, right, left)
    delta_far = lax.all_to_all(delta, "dp", 0, 0, tiled=True)

    grad_t = call(
        flip_body, "flip", 0, 4 * tokens * depth,
        grid_spec=pltpu.PrefetchScalarGridSpec(
            num_scalar_prefetch=1, grid=(n_ctx, n_dp),
            in_specs=[
                pl.BlockSpec(
                    (1, n_tp, 1, part, depth),
                    lambda i, j, p: (j, 0, p[1] ^ ((p[1] + n_ctx - i) % n_ctx), 0, 0),
                ),
                ANY,
            ],
            out_specs=pl.BlockSpec((depth, rows), lambda i, j, p: (0, i * n_dp + j)),
        ),
        out_shape=shape(depth, tokens),
    )(place, grad, partial)
    gated_all = call(
        merge_body, "merge", 0, 2 * (2 * n_ctx + last) * n_dp * rows * quarter,
        grid=(n_dp,),
        in_specs=[pl.BlockSpec((1, rows, quarter), lambda i: (i, 0, 0))] * (1 + 2 * last) + [ANY],
        out_specs=pl.BlockSpec((n_ctx, 1, rows, quarter), lambda i: (0, i, 0, 0)),
        out_shape=shape(n_ctx, n_dp, rows, quarter),
    )(gated_far, *from_left, *from_right[::-1], token).reshape(tokens, quarter)
    weight_far = []
    for k in list(range(1, n_dp)) + [0]:
        token = call(
            weight_body, "weight", 2 * tokens * feats * quarter, 2 * tokens * (feats + quarter),
            grid_spec=pltpu.PrefetchScalarGridSpec(
                num_scalar_prefetch=1, grid=(2,),
                in_specs=[
                    pl.BlockSpec((feats, tokens), lambda i, p, k=k: (p[0] ^ k, 0)),
                    pl.BlockSpec((tokens, quarter // 2), lambda i, p: (0, i)),
                    ANY,
                ],
                out_specs=pl.BlockSpec((feats, quarter // 2), lambda i, p: (0, i)),
            ),
            out_shape=shape(feats, quarter),
        )(place, grad_t, gated_all, token)
        weight_far.append(swap(token, "dp", k) if k else token)

    seed, starts, gate_grad = call(
        seed_body, "seed", 2 * rows * 128 * width, rows * width * 10,
        grid=(steps,),
        in_specs=[
            pl.BlockSpec((1, rows, block), lambda i: (i, 0, 0)),
            wide(rows, block), wide(rows, block), tall(block, rows),
        ],
        out_specs=[wide(rows, block), wide(ORDER, block), wide(rows, block)],
        out_shape=[shape(rows, width), shape(ORDER, width), shape(rows, width)],
    )(delta_far, gate, long_out, starts_coef)
    starts_far = [shift(starts, -k) for k in range(1, n_ctx)]
    local_bwd = local(True, kernel, seed)
    query_grad, conv_grad = call(
        functools.partial(back_body, n_ctx - 1), "back", 2 * rows * 128 * width, rows * width * 12,
        grid=(steps,),
        in_specs=[wide(rows, block), wide((n_ctx - 1) * rows, block)] + [wide(rows, block)] * 2
        + [wide(ORDER, block)] * (n_ctx - 1),
        out_specs=[wide(rows, block)] * 2,
        out_shape=[shape(rows, width)] * 2,
    )(local_bwd, back_coef, conv, query, *starts_far)

    cut = feats // n_dp
    weight_grad = call(
        lay_body, "lay", 0, 4 * feats * width,
        grid_spec=pltpu.PrefetchScalarGridSpec(
            num_scalar_prefetch=1, grid=(n_dp,),
            in_specs=[pl.BlockSpec((cut, quarter), lambda i, p: (i, 0))] * n_dp + [ANY],
            out_specs=pl.BlockSpec((cut, width), lambda i, p: (i, 0)),
        ),
        out_shape=shape(feats, width),
    )(place, weight_far[-1], *weight_far[:-1], query_grad)
    return query_grad, conv_grad, gate_grad, weight_grad


def solution(mesh):
    rows = P(("dp", "ctx"), "tp")
    return jax.shard_map(
        on_device,
        mesh=mesh,
        in_specs=(rows, rows, rows, rows, P(("dp", "ctx"), None), P("tp", ("dp", "ctx")),
                  P("tp", None), P("tp", None), P("tp", None)),
        out_specs=(rows, rows, rows, rows),
        check_vma=False,
    )
```

profile of v0, /device:TPU:0, one launch (start us, length us, event | category | flops | bytes accessed | tf_op | source)
XLA Modules:
  0.0 334.4 jit_solution(14535567066545319557)
XLA Ops:
  7.2 3.6 %constant_dynamic-slice_fusion = (bf16[1024,512]{1,0:T(8,128)(2,1)}, bf16[1024,512]{1,0:T(8,128)(2,1)}, bf16[1024,512]{1,0:T(8,128)(2,1)}) fusion(bf16[4096,512]{1,0:T(8,128)(2,1)} %refs_0_.5, s32[]{:T(128)S(6)} %select_n.24, s32[]{:T(128)S(6)} %select_n.23, s32[]{:T(128)S(6)} %select_n.22), kind=kLoop, calls=%fused_computation.17 | loop fusion | bytes 6291468 | tf_op jit(solution)/shard_map/dynamic_slice | solution.py:241
  15.4 3.8 %pack.1 = (bf16[64,2048]{1,0:T(8,128)(2,1)S(1)}, bf16[64,2048]{1,0:T(8,128)(2,1)}, bf16[64,2048]{1,0:T(8,128)(2,1)S(1)}, bf16[64,2048]{1,0:T(8,128)(2,1)S(1)}) custom-call(s32[3]{0:T(128)S(1)} %pad_add_fusion.place, bf16[128,8192]{1,0:T(8,128)(2,1)} %refs_3_.1, bf16[128,8192]{1,0:T(8,128)(2,1)} %refs_3_.1, bf16[128,8192]{1,0:T(8,128)(2,1)} %refs_3_.1, ...), custom_call_target="tpu_custom_call" | custom-call | bytes 2097152 | tf_op jit(solution)/shard_map/pack/pallas_call | solution.py:245
  34.9 17.3 %collective-permute-done.6.rim = bf16[128,4096]{1,0:T(8,128)(2,1)} collective-permute-done((bf16[128,4096]{1,0:T(8,128)(2,1)}, bf16[128,4096]{1,0:T(8,128)(2,1)}, u32[]{:S(2)}, u32[]{:S(2)}) %collective-permute-start.6) | collective-permute-done | bytes 1048608 | tf_op jit(solution)/shard_map/ppermute | solution.py:235
  52.2 4.1 %collective-permute-start.2 = (bf16[64,2048]{1,0:T(8,128)(2,1)}, bf16[64,2048]{1,0:T(8,128)(2,1)S(1)}, u32[]{:S(2)}, u32[]{:S(2)}) collective-permute-start(bf16[64,2048]{1,0:T(8,128)(2,1)} %copy-done.24), channel_id=1, source_target_pairs={{0,6},{2,4},{4,2},{6,0},{1,7},{3,5},{5,3},{7,1},{8,14},{10,12},{12... | collective-permute-start | bytes 786440 | tf_op jit(solution)/shard_map/ppermute | solution.py:231
  57.4 4.5 %local.2.own_part = f32[128,4096]{1,0:T(8,128)S(1)} custom-call(f32[256,128]{1,0:T(8,128)S(1)} %pad_maximum_fusion.rows.taps, bf16[128,4096]{1,0:T(8,128)(2,1)} %multiply_convert_fusion.2.x), custom_call_target="tpu_custom_call" | custom-call | flops 1073741824 | bytes 3145728 | tf_op jit(solution)/shard_map/local/pallas_call | solution.py:276
  63.2 5.7 %conv.1 = (bf16[128,4096]{1,0:T(8,128)(2,1)S(1)}, bf16[128,4096]{1,0:T(8,128)(2,1)S(1)}, bf16[16,4096]{1,0:T(8,128)(2,1)S(1)}) custom-call(bf16[128,4096]{1,0:T(8,128)(2,1)} %collective-permute-done.6.rim, f32[128,4096]{1,0:T(8,128)} %copy-done.20, bf16[128,4096]{1,0:T(8,128)(2,1)} %query.3, f32[256,128]{1,0:T(8,128)S(1)} %pad_maximum_fusion.rows.taps, ...), custom_call_target="tpu_custom_call" | custom-call | flops 1073741824 | bytes 7340032 | tf_op jit(solution)/shard_map/conv/pallas_call | solution.py:287
  79.4 4.5 %multiply_convert_fusion = (bf16[384,4096]{1,0:T(8,128)(2,1)}, bf16[384,4096]{1,0:T(8,128)(2,1)}) fusion(f32[384]{0:T(512)S(1)} %get-tuple-element.47, f32[4096]{0:T(1024)} %copy-done.29, f32[4096]{0:T(1024)S(1)} %mul.120, f32[384]{0:T(512)S(1)} %get-tuple-element.48), kind=kLoop, calls=%fused_computation | loop fusion | flops 9437184 | bytes 6327296 | tf_op jit(solution)/shard_map/convert_element_type | solution.py:265
  83.9 12.3 %collective-permute-start.7 = (bf16[16,4096]{1,0:T(8,128)(2,1)S(1)}, bf16[16,4096]{1,0:T(8,128)(2,1)S(1)}, u32[]{:S(2)}, u32[]{:S(2)}) collective-permute-start(bf16[16,4096]{1,0:T(8,128)(2,1)S(1)} %get-tuple-element.27), channel_id=1, source_target_pairs={{0,2},{2,4},{4,6},{1,3},{3,5},{5,7},{8,10},{10,12},{12,14},{9,11},... | collective-permute-start | bytes 393224 | tf_op jit(solution)/shard_map/ppermute | solution.py:235
  99.0 4.2 %local.3 = f32[128,4096]{1,0:T(8,128)} custom-call(f32[256,128]{1,0:T(8,128)S(1)} %pad_maximum_fusion.1.rows, bf16[128,4096]{1,0:T(8,128)(2,1)S(1)} %copy-done.17, bf16[4,64,2048]{2,1,0:T(8,128)(2,1)} %join.1.refs_0_), custom_call_target="tpu_custom_call" | custom-call | flops 1073741824 | bytes 3145728 | tf_op jit(solution)/shard_map/local/pallas_call | solution.py:276
  103.3 4.0 %long.1 = (bf16[128,4096]{1,0:T(8,128)(2,1)S(1)}, bf16[4,128,1024]{2,1,0:T(8,128)(2,1)S(1)}) custom-call(f32[128,4096]{1,0:T(8,128)} %local.3, bf16[384,4096]{1,0:T(8,128)(2,1)} %get-tuple-element.44.coef, bf16[128,4096]{1,0:T(8,128)(2,1)S(1)} %copy-done.6, bf16[16,4096]{1,0:T(8,128)(2,1)S(1)} %collective-permute-done.7.refs_0_, ...), custom_call_target="tpu_custom_call" | custom-call | flops 134217728 | bytes 5242880 | tf_op jit(solution)/shard_map/long/pallas_call | solution.py:307
  107.3 20.6 %all_to_all.10.own = bf16[4,128,1024]{2,1,0:T(8,128)(2,1)S(1)} all-to-all(bf16[4,128,1024]{2,1,0:T(8,128)(2,1)S(1)} %get-tuple-element.28), channel_id=1, replica_groups=mesh['dp'=4,'ctx'=4,'tp'=2] {'dp'}, dimensions={0} | all-to-all | bytes 2097152 | tf_op jit(solution)/shard_map/all_to_all | solution.py:314
  130.5 10.9 %collective-permute-done.10.refs_4_.refs_0_ = bf16[4,128,1024]{2,1,0:T(8,128)(2,1)S(1)} collective-permute-done((bf16[4,128,1024]{2,1,0:T(8,128)(2,1)S(1)}, bf16[4,128,1024]{2,1,0:T(8,128)(2,1)S(1)}, u32[]{:S(2)}, u32[]{:S(2)}) %collective-permute-start.10) | collective-permute-done | bytes 1048608 | tf_op jit(solution)/shard_map/ppermute | solution.py:235
  142.2 14.8 %collective-permute-done.11.refs_5_ = bf16[4,128,1024]{2,1,0:T(8,128)(2,1)} collective-permute-done((bf16[4,128,1024]{2,1,0:T(8,128)(2,1)S(1)}, bf16[4,128,1024]{2,1,0:T(8,128)(2,1)}, u32[]{:S(2)}, u32[]{:S(2)}) %collective-permute-start.11) | collective-permute-done | bytes 1048608 | tf_op jit(solution)/shard_map/ppermute | solution.py:235
  160.8 6.0 %delta.2.refs_4_ = bf16[1,4,128,1024]{3,2,1,0:T(8,128)(2,1)} custom-call(s32[3]{0:T(128)S(1)} %pad_add_fusion.place, s32[1]{0:T(128)} %bitcast.4.dest, bf16[4,2,4,64,2048]{4,3,2,1,0:T(8,128)(2,1)} %bitcast.16, bf16[4096,512]{1,0:T(8,128)(2,1)} %refs_0_.5, bf16[1024,512]{1,0:T(8,128)(2,1)S(1)} %copy-done.9, bf16[1024,512]{1,0:T(8,128)(2,1)S(1)} %copy-done.12, ...), custom_call_target="tpu_custom_call" | custom-call | flops 2147483648 | bytes 13631488 | tf_op jit(solution)/shard_map/delta/pallas_call | solution.py:329
  166.9 5.5 %collective-permute-start.12 = (bf16[1,4,128,1024]{3,2,1,0:T(8,128)(2,1)}, bf16[1,4,128,1024]{3,2,1,0:T(8,128)(2,1)}, u32[]{:S(2)}, u32[]{:S(2)}) collective-permute-start(bf16[1,4,128,1024]{3,2,1,0:T(8,128)(2,1)} %delta.2.refs_4_), channel_id=1, source_target_pairs={{0,2},{1,3},{8,10},{9,11},{16,18},{17,19},{24,26},{25,27}} | collective-permute-start | bytes 3145736 | tf_op jit(solution)/shard_map/ppermute | solution.py:235
  175.7 8.5 %collective-permute-done.15.refs_1_.refs_4_ = bf16[4,128,1024]{2,1,0:T(8,128)(2,1)} collective-permute-done((bf16[4,128,1024]{2,1,0:T(8,128)(2,1)}, bf16[4,128,1024]{2,1,0:T(8,128)(2,1)}, u32[]{:S(2)}, u32[]{:S(2)}) %collective-permute-start.15) | collective-permute-done | bytes 1048608 | tf_op jit(solution)/shard_map/ppermute | solution.py:235
  189.4 12.9 %delta.3.partial_right.partial_left.partial.after = bf16[4,4,128,1024]{3,2,1,0:T(8,128)(2,1)} custom-call(s32[3]{0:T(128)S(1)} %pad_add_fusion.place, s32[4]{0:T(128)S(1)} %iota.21.dest, bf16[4,2,4,64,2048]{4,3,2,1,0:T(8,128)(2,1)} %bitcast.17, bf16[4096,512]{1,0:T(8,128)(2,1)} %refs_0_.5, bf16[1024,512]{1,0:T(8,128)(2,1)S(1)} %copy-done.10, ...), custom_call_target="tpu_custom_call" | custom-call | flops 8589934592 | bytes 16777216 | tf_op jit(solution)/shard_map/delta/pallas_call | solution.py:329
  202.3 4.7 %add.79 = (bf16[1,4,128,1024]{3,2,1,0:T(8,128)(2,1)}, bf16[1,4,128,1024]{3,2,1,0:T(8,128)(2,1)}) custom-call(s32[2]{0:T(128)S(1)} %add_clamp_fusion.1.dests, bf16[4,4,128,1024]{3,2,1,0:T(8,128)(2,1)} %delta.3.partial_right.partial_left.partial.after, bf16[4,4,128,1024]{3,2,1,0:T(8,128)(2,1)} %delta.3.partial_right.partial_left.partial.after, ...), custom_call_target="tpu_custom_call" | custom-call | bytes 6291456 | tf_op jit(solution)/shard_map/add/pallas_call | solution.py:358
  207.0 5.4 %collective-permute-start.16 = (bf16[1,4,128,1024]{3,2,1,0:T(8,128)(2,1)}, bf16[1,4,128,1024]{3,2,1,0:T(8,128)(2,1)S(1)}, u32[]{:S(2)}, u32[]{:S(2)}) collective-permute-start(bf16[1,4,128,1024]{3,2,1,0:T(8,128)(2,1)} %get-tuple-element.29), channel_id=1, source_target_pairs={{0,2},{2,4},{1,3},{3,5},{8,10},{10,12},{9,11},{11,13},{16,18},{18,... | collective-permute-start | bytes 3145736 | tf_op jit(solution)/shard_map/ppermute | solution.py:235
  214.2 18.0 %collective-permute-done.16.right = bf16[1,4,128,1024]{3,2,1,0:T(8,128)(2,1)S(1)} collective-permute-done((bf16[1,4,128,1024]{3,2,1,0:T(8,128)(2,1)}, bf16[1,4,128,1024]{3,2,1,0:T(8,128)(2,1)S(1)}, u32[]{:S(2)}, u32[]{:S(2)}) %collective-permute-start.16) | collective-permute-done | bytes 1048608 | tf_op jit(solution)/shard_map/ppermute | solution.py:235
  235.6 6.5 %collective-permute-start.20 = (bf16[1,4,128,1024]{3,2,1,0:T(8,128)(2,1)S(1)}, bf16[1,4,128,1024]{3,2,1,0:T(8,128)(2,1)S(1)}, u32[]{:S(2)}, u32[]{:S(2)}) collective-permute-start(bf16[1,4,128,1024]{3,2,1,0:T(8,128)(2,1)S(1)} %get-tuple-element.31.refs_6_.after), channel_id=1, source_target_pairs={{0,2},{2,4},{4,6},{1,3},{3,5},{5,7},{8,10},{10,12},{12,14},{9,11},... | collective-permute-start | bytes 3145736 | tf_op jit(solution)/shard_map/ppermute | solution.py:235
  243.6 13.8 %flip.1.grad_t = bf16[2048,2048]{1,0:T(8,128)(2,1)} custom-call(s32[3]{0:T(128)S(1)} %pad_add_fusion.place, bf16[4,2,4,64,2048]{4,3,2,1,0:T(8,128)(2,1)} %bitcast.18, bf16[4,4,128,1024]{3,2,1,0:T(8,128)(2,1)} %delta.3.partial_right.partial_left.partial.after), custom_call_target="tpu_custom_call" | custom-call | bytes 16777216 | tf_op jit(solution)/shard_map/flip/pallas_call | solution.py:381
  257.4 4.7 %merge.1 = bf16[4,4,128,1024]{3,2,1,0:T(8,128)(2,1)} custom-call(bf16[4,128,1024]{2,1,0:T(8,128)(2,1)S(1)} %all_to_all.10.own, bf16[4,128,1024]{2,1,0:T(8,128)(2,1)S(1)} %copy-done.1, bf16[4,128,1024]{2,1,0:T(8,128)(2,1)S(1)} %copy-done.3, bf16[4,128,1024]{2,1,0:T(8,128)(2,1)} %collective-permute-done.18.refs_0_.refs_2_, ...), custom_call_target="tpu_custom_call" | custom-call | bytes 11534336 | tf_op jit(solution)/shard_map/merge/pallas_call | solution.py:396
  263.4 5.4 %weight.4.after = bf16[512,1024]{1,0:T(8,128)(2,1)S(1)} custom-call(s32[3]{0:T(128)S(1)} %pad_add_fusion.place, bf16[2048,2048]{1,0:T(8,128)(2,1)} %flip.1.grad_t, bf16[2048,1024]{1,0:T(8,128)(2,1)} %bitcast.12, bf16[1,4,128,1024]{3,2,1,0:T(8,128)(2,1)S(1)} %copy-done.5), custom_call_target="tpu_custom_call" | custom-call | flops 2147483648 | bytes 6291456 | tf_op jit(solution)/shard_map/weight/pallas_call | solution.py:405
  270.3 5.4 %weight.5.after = bf16[512,1024]{1,0:T(8,128)(2,1)S(1)} custom-call(s32[3]{0:T(128)S(1)} %pad_add_fusion.place, bf16[2048,2048]{1,0:T(8,128)(2,1)} %flip.1.grad_t, bf16[2048,1024]{1,0:T(8,128)(2,1)} %bitcast.13, bf16[512,1024]{1,0:T(8,128)(2,1)S(1)} %weight.4.after), custom_call_target="tpu_custom_call" | custom-call | flops 2147483648 | bytes 6291456 | tf_op jit(solution)/shard_map/weight/pallas_call | solution.py:405
  279.2 4.3 %all-to-all-start.1 = ((bf16[4,128,1024]{2,1,0:T(8,128)(2,1)}), bf16[4,128,1024]{2,1,0:T(8,128)(2,1)}, u32[]{:S(2)}, u32[]{:S(2)}) async-start(bf16[4,128,1024]{2,1,0:T(8,128)(2,1)} %sum.1), calls=%async_computation.1 | async-start | bytes 2097152 | tf_op jit(solution)/shard_map/all_to_all | solution.py:379
  283.4 5.4 %weight.6.after = bf16[512,1024]{1,0:T(8,128)(2,1)S(1)} custom-call(s32[3]{0:T(128)S(1)} %pad_add_fusion.place, bf16[2048,2048]{1,0:T(8,128)(2,1)} %flip.1.grad_t, bf16[2048,1024]{1,0:T(8,128)(2,1)} %bitcast.14, bf16[512,1024]{1,0:T(8,128)(2,1)S(1)} %weight.5.after), custom_call_target="tpu_custom_call" | custom-call | flops 2147483648 | bytes 6291456 | tf_op jit(solution)/shard_map/weight/pallas_call | solution.py:405
  294.2 4.4 %seed.1 = (bf16[128,4096]{1,0:T(8,128)(2,1)S(1)}, bf16[16,4096]{1,0:T(8,128)(2,1)S(1)}, bf16[128,4096]{1,0:T(8,128)(2,1)}) custom-call(bf16[4,128,1024]{2,1,0:T(8,128)(2,1)} %all-to-all-done.1.delta, bf16[128,4096]{1,0:T(8,128)(2,1)S(1)} %copy-done.7, bf16[128,4096]{1,0:T(8,128)(2,1)} %copy-done.21, bf16[4096,128]{1,0:T(8,128)(2,1)} %get-tuple-element.45.starts_coef), custom_call_target="tpu_custom_call" | custom-call | flops 134217728 | bytes 5242880 | tf_op jit(solution)/shard_map/seed/pallas_call | solution.py:420
  301.1 4.9 %collective-permute-done.22.refs_0_ = bf16[16,4096]{1,0:T(8,128)(2,1)S(1)} collective-permute-done((bf16[16,4096]{1,0:T(8,128)(2,1)S(1)}, bf16[16,4096]{1,0:T(8,128)(2,1)S(1)}, u32[]{:S(2)}, u32[]{:S(2)}) %collective-permute-start.22) | collective-permute-done | bytes 131104 | tf_op jit(solution)/shard_map/ppermute | solution.py:235
  307.3 5.4 %weight.7.refs_0_ = bf16[512,1024]{1,0:T(8,128)(2,1)S(1)} custom-call(s32[3]{0:T(128)S(1)} %pad_add_fusion.place, bf16[2048,2048]{1,0:T(8,128)(2,1)} %flip.1.grad_t, bf16[2048,1024]{1,0:T(8,128)(2,1)} %bitcast.15, bf16[512,1024]{1,0:T(8,128)(2,1)S(1)} %weight.6.after), custom_call_target="tpu_custom_call" | custom-call | flops 2147483648 | bytes 6291456 | tf_op jit(solution)/shard_map/weight/pallas_call | solution.py:405
  317.5 5.1 %back.1 = (bf16[128,4096]{1,0:T(8,128)(2,1)}, bf16[128,4096]{1,0:T(8,128)(2,1)}) custom-call(f32[128,4096]{1,0:T(8,128)} %copy-done.19, bf16[384,4096]{1,0:T(8,128)(2,1)} %get-tuple-element.43.coef, bf16[128,4096]{1,0:T(8,128)(2,1)S(1)} %copy-done.23, bf16[128,4096]{1,0:T(8,128)(2,1)S(1)} %copy-done.18, ...), custom_call_target="tpu_custom_call" | custom-call | flops 134217728 | bytes 6291456 | tf_op jit(solution)/shard_map/back/pallas_call | solution.py:432
  322.6 4.9 %lay.1 = bf16[512,4096]{1,0:T(8,128)(2,1)} custom-call(s32[3]{0:T(128)S(1)} %pad_add_fusion.place, bf16[512,1024]{1,0:T(8,128)(2,1)S(1)} %weight.7.refs_0_, bf16[512,1024]{1,0:T(8,128)(2,1)} %collective-permute-done.25.refs_1_, bf16[512,1024]{1,0:T(8,128)(2,1)} %collective-permute-done.26.refs_2_, bf16[512,1024]{1,0:T(8,128)(2,1)} %collective-permute-done.27.refs_3_, ...), custom_call_target="tpu_custom_call" | custom-call | bytes 8388608 | tf_op jit(solution)/shard_map/lay/pallas_call | solution.py:442
  (136 shorter events, 78.1 us)
Async XLA Ops:
  7.2 151.2 %all-gather.3.cloned.1.call-start = ((), (), s32[]{:S(2)}) async-start(), calls=%async_computation.2 | async-start | bytes 9437184 | tf_op jit(solution)/shard_map/all_gather | solution.py:302
  10.8 60.0 %collective-permute-start.3 = (bf16[1024,512]{1,0:T(8,128)(2,1)}, bf16[1024,512]{1,0:T(8,128)(2,1)S(1)}, u32[]{:S(2)}, u32[]{:S(2)}) collective-permute-start(bf16[1024,512]{1,0:T(8,128)(2,1)} %get-tuple-element.42.refs_4_), channel_id=1, source_target_pairs={{0,8},{8,0},{16,24},{24,16},{1,9},{9,1},{17,25},{25,17},{2,10},{10... | collective-permute-start | bytes 3145736 | tf_op jit(solution)/shard_map/ppermute | solution.py:231
  13.8 57.1 %collective-permute-start.4 = (bf16[1024,512]{1,0:T(8,128)(2,1)}, bf16[1024,512]{1,0:T(8,128)(2,1)S(1)}, u32[]{:S(2)}, u32[]{:S(2)}) collective-permute-start(bf16[1024,512]{1,0:T(8,128)(2,1)} %get-tuple-element.41.refs_5_), channel_id=1, source_target_pairs={{0,16},{8,24},{16,0},{24,8},{1,17},{9,25},{17,1},{25,9},{2,18},{10... | collective-permute-start | bytes 3145736 | tf_op jit(solution)/shard_map/ppermute | solution.py:231
  15.3 55.6 %collective-permute-start.5 = (bf16[1024,512]{1,0:T(8,128)(2,1)}, bf16[1024,512]{1,0:T(8,128)(2,1)S(1)}, u32[]{:S(2)}, u32[]{:S(2)}) collective-permute-start(bf16[1024,512]{1,0:T(8,128)(2,1)} %get-tuple-element.40.refs_6_), channel_id=1, source_target_pairs={{0,24},{8,16},{16,8},{24,0},{1,25},{9,17},{17,9},{25,1},{2,26},{10... | collective-permute-start | bytes 3145736 | tf_op jit(solution)/shard_map/ppermute | solution.py:231
  20.6 12.2 %collective-permute-start = (bf16[64,2048]{1,0:T(8,128)(2,1)}, bf16[64,2048]{1,0:T(8,128)(2,1)}, u32[]{:S(2)}, u32[]{:S(2)}) collective-permute-start(bf16[64,2048]{1,0:T(8,128)(2,1)} %get-tuple-element.23), channel_id=1, source_target_pairs={{0,2},{2,0},{4,6},{6,4},{1,3},{3,1},{5,7},{7,5},{8,10},{10,8},{12,... | collective-permute-start | bytes 786440 | tf_op jit(solution)/shard_map/ppermute | solution.py:231
  23.9 28.3 %collective-permute-start.6 = (bf16[128,4096]{1,0:T(8,128)(2,1)}, bf16[128,4096]{1,0:T(8,128)(2,1)}, u32[]{:S(2)}, u32[]{:S(2)}) collective-permute-start(bf16[128,4096]{1,0:T(8,128)(2,1)} %multiply_convert_fusion.2.x), channel_id=1, source_target_pairs={{0,2},{2,4},{4,6},{1,3},{3,5},{5,7},{8,10},{10,12},{12,14},{9,11},... | collective-permute-start | bytes 3145736 | tf_op jit(solution)/shard_map/ppermute | solution.py:235
  32.8 38.0 %collective-permute-start.1 = (bf16[64,2048]{1,0:T(8,128)(2,1)}, bf16[64,2048]{1,0:T(8,128)(2,1)S(1)}, u32[]{:S(2)}, u32[]{:S(2)}) collective-permute-start(bf16[64,2048]{1,0:T(8,128)(2,1)} %copy-done.25), channel_id=1, source_target_pairs={{0,4},{2,6},{4,0},{6,2},{1,5},{3,7},{5,1},{7,3},{8,12},{10,14},{12... | collective-permute-start | bytes 786440 | tf_op jit(solution)/shard_map/ppermute | solution.py:231
  52.2 18.6 %collective-permute-start.2 = (bf16[64,2048]{1,0:T(8,128)(2,1)}, bf16[64,2048]{1,0:T(8,128)(2,1)S(1)}, u32[]{:S(2)}, u32[]{:S(2)}) collective-permute-start(bf16[64,2048]{1,0:T(8,128)(2,1)} %copy-done.24), channel_id=1, source_target_pairs={{0,6},{2,4},{4,2},{6,0},{1,7},{3,5},{5,3},{7,1},{8,14},{10,12},{12... | collective-permute-start | bytes 786440 | tf_op jit(solution)/shard_map/ppermute | solution.py:231
  83.9 19.3 %collective-permute-start.7 = (bf16[16,4096]{1,0:T(8,128)(2,1)S(1)}, bf16[16,4096]{1,0:T(8,128)(2,1)S(1)}, u32[]{:S(2)}, u32[]{:S(2)}) collective-permute-start(bf16[16,4096]{1,0:T(8,128)(2,1)S(1)} %get-tuple-element.27), channel_id=1, source_target_pairs={{0,2},{2,4},{4,6},{1,3},{3,5},{5,7},{8,10},{10,12},{12,14},{9,11},... | collective-permute-start | bytes 393224 | tf_op jit(solution)/shard_map/ppermute | solution.py:235
  96.3 7.0 %collective-permute-start.8 = (bf16[16,4096]{1,0:T(8,128)(2,1)S(1)}, bf16[16,4096]{1,0:T(8,128)(2,1)S(1)}, u32[]{:S(2)}, u32[]{:S(2)}) collective-permute-start(bf16[16,4096]{1,0:T(8,128)(2,1)S(1)} %get-tuple-element.27), channel_id=1, source_target_pairs={{0,4},{2,6},{1,5},{3,7},{8,12},{10,14},{9,13},{11,15},{16,20},{18,... | collective-permute-start | bytes 393224 | tf_op jit(solution)/shard_map/ppermute | solution.py:235
  97.6 5.7 %collective-permute-start.9 = (bf16[16,4096]{1,0:T(8,128)(2,1)S(1)}, bf16[16,4096]{1,0:T(8,128)(2,1)S(1)}, u32[]{:S(2)}, u32[]{:S(2)}) collective-permute-start(bf16[16,4096]{1,0:T(8,128)(2,1)S(1)} %get-tuple-element.27), channel_id=1, source_target_pairs={{0,6},{1,7},{8,14},{9,15},{16,22},{17,23},{24,30},{25,31}} | collective-permute-start | bytes 393224 | tf_op jit(solution)/shard_map/ppermute | solution.py:235
  107.3 49.8 %copy-start.21 = (bf16[128,4096]{1,0:T(8,128)(2,1)}, bf16[128,4096]{1,0:T(8,128)(2,1)S(1)}, u32[]{:S(2)}) copy-start(bf16[128,4096]{1,0:T(8,128)(2,1)S(1)} %get-tuple-element.33.long_out) | copy-start | bytes 3145732
  127.9 13.6 %collective-permute-start.10 = (bf16[4,128,1024]{2,1,0:T(8,128)(2,1)S(1)}, bf16[4,128,1024]{2,1,0:T(8,128)(2,1)S(1)}, u32[]{:S(2)}, u32[]{:S(2)}) collective-permute-start(bf16[4,128,1024]{2,1,0:T(8,128)(2,1)S(1)} %all_to_all.10.own), channel_id=1, source_target_pairs={{0,2},{2,4},{4,6},{1,3},{3,5},{5,7},{8,10},{10,12},{12,14},{9,11},... | collective-permute-start | bytes 3145736 | tf_op jit(solution)/shard_map/ppermute | solution.py:235
  129.2 27.8 %collective-permute-start.11 = (bf16[4,128,1024]{2,1,0:T(8,128)(2,1)S(1)}, bf16[4,128,1024]{2,1,0:T(8,128)(2,1)}, u32[]{:S(2)}, u32[]{:S(2)}) collective-permute-start(bf16[4,128,1024]{2,1,0:T(8,128)(2,1)S(1)} %all_to_all.10.own), channel_id=1, source_target_pairs={{2,0},{4,2},{6,4},{3,1},{5,3},{7,5},{10,8},{12,10},{14,12},{11,9},... | collective-permute-start | bytes 3145736 | tf_op jit(solution)/shard_map/ppermute | solution.py:235
  141.5 32.6 %collective-permute-start.14 = (bf16[4,128,1024]{2,1,0:T(8,128)(2,1)S(1)}, bf16[4,128,1024]{2,1,0:T(8,128)(2,1)S(1)}, u32[]{:S(2)}, u32[]{:S(2)}) collective-permute-start(bf16[4,128,1024]{2,1,0:T(8,128)(2,1)S(1)} %collective-permute-done.10.refs_4_.refs_0_), channel_id=1, source_target_pairs={{2,4},{4,6},{3,5},{5,7},{10,12},{12,14},{11,13},{13,15},{18,20},{2... | collective-permute-start | bytes 3145736 | tf_op jit(solution)/shard_map/ppermute | solution.py:235
  157.0 27.2 %collective-permute-start.15 = (bf16[4,128,1024]{2,1,0:T(8,128)(2,1)}, bf16[4,128,1024]{2,1,0:T(8,128)(2,1)}, u32[]{:S(2)}, u32[]{:S(2)}) collective-permute-start(bf16[4,128,1024]{2,1,0:T(8,128)(2,1)} %collective-permute-done.11.refs_5_), channel_id=1, source_target_pairs={{2,0},{4,2},{3,1},{5,3},{10,8},{12,10},{11,9},{13,11},{18,16},{20,... | collective-permute-start | bytes 3145736 | tf_op jit(solution)/shard_map/ppermute | solution.py:235
  166.9 35.4 %collective-permute-start.12 = (bf16[1,4,128,1024]{3,2,1,0:T(8,128)(2,1)}, bf16[1,4,128,1024]{3,2,1,0:T(8,128)(2,1)}, u32[]{:S(2)}, u32[]{:S(2)}) collective-permute-start(bf16[1,4,128,1024]{3,2,1,0:T(8,128)(2,1)} %delta.2.refs_4_), channel_id=1, source_target_pairs={{0,2},{1,3},{8,10},{9,11},{16,18},{17,19},{24,26},{25,27}} | collective-permute-start | bytes 3145736 | tf_op jit(solution)/shard_map/ppermute | solution.py:235
  172.4 29.9 %collective-permute-start.13 = (bf16[1,4,128,1024]{3,2,1,0:T(8,128)(2,1)}, bf16[1,4,128,1024]{3,2,1,0:T(8,128)(2,1)}, u32[]{:S(2)}, u32[]{:S(2)}) collective-permute-start(bf16[1,4,128,1024]{3,2,1,0:T(8,128)(2,1)} %delta.2.refs_4_), channel_id=1, source_target_pairs={{6,4},{7,5},{14,12},{15,13},{22,20},{23,21},{30,28},{31,29}} | collective-permute-start | bytes 3145736 | tf_op jit(solution)/shard_map/ppermute | solution.py:235
  174.1 28.2 %copy-start.2 = (bf16[4,128,1024]{2,1,0:T(8,128)(2,1)}, bf16[4,128,1024]{2,1,0:T(8,128)(2,1)S(1)}, u32[]{:S(2)}) copy-start(bf16[4,128,1024]{2,1,0:T(8,128)(2,1)S(1)} %collective-permute-done.14.refs_0_.refs_1_) | copy-start | bytes 3145732
  174.1 40.1 %collective-permute-start.18 = (bf16[4,128,1024]{2,1,0:T(8,128)(2,1)S(1)}, bf16[4,128,1024]{2,1,0:T(8,128)(2,1)}, u32[]{:S(2)}, u32[]{:S(2)}) collective-permute-start(bf16[4,128,1024]{2,1,0:T(8,128)(2,1)S(1)} %collective-permute-done.14.refs_0_.refs_1_), channel_id=1, source_target_pairs={{4,6},{5,7},{12,14},{13,15},{20,22},{21,23},{28,30},{29,31}} | collective-permute-start | bytes 3145736 | tf_op jit(solution)/shard_map/ppermute | solution.py:235
  184.2 30.0 %collective-permute-start.19 = (bf16[4,128,1024]{2,1,0:T(8,128)(2,1)}, bf16[4,128,1024]{2,1,0:T(8,128)(2,1)}, u32[]{:S(2)}, u32[]{:S(2)}) collective-permute-start(bf16[4,128,1024]{2,1,0:T(8,128)(2,1)} %collective-permute-done.15.refs_1_.refs_4_), channel_id=1, source_target_pairs={{2,0},{3,1},{10,8},{11,9},{18,16},{19,17},{26,24},{27,25}} | collective-permute-start | bytes 3145736 | tf_op jit(solution)/shard_map/ppermute | solution.py:235
  207.0 25.2 %collective-permute-start.16 = (bf16[1,4,128,1024]{3,2,1,0:T(8,128)(2,1)}, bf16[1,4,128,1024]{3,2,1,0:T(8,128)(2,1)S(1)}, u32[]{:S(2)}, u32[]{:S(2)}) collective-permute-start(bf16[1,4,128,1024]{3,2,1,0:T(8,128)(2,1)} %get-tuple-element.29), channel_id=1, source_target_pairs={{0,2},{2,4},{1,3},{3,5},{8,10},{10,12},{9,11},{11,13},{16,18},{18,... | collective-permute-start | bytes 3145736 | tf_op jit(solution)/shard_map/ppermute | solution.py:235
  212.4 19.7 %collective-permute-start.17 = (bf16[1,4,128,1024]{3,2,1,0:T(8,128)(2,1)}, bf16[1,4,128,1024]{3,2,1,0:T(8,128)(2,1)}, u32[]{:S(2)}, u32[]{:S(2)}) collective-permute-start(bf16[1,4,128,1024]{3,2,1,0:T(8,128)(2,1)} %get-tuple-element.30), channel_id=1, source_target_pairs={{4,2},{6,4},{5,3},{7,5},{12,10},{14,12},{13,11},{15,13},{20,18},{2... | collective-permute-start | bytes 3145736 | tf_op jit(solution)/shard_map/ppermute | solution.py:235
  235.6 40.0 %collective-permute-start.20 = (bf16[1,4,128,1024]{3,2,1,0:T(8,128)(2,1)S(1)}, bf16[1,4,128,1024]{3,2,1,0:T(8,128)(2,1)S(1)}, u32[]{:S(2)}, u32[]{:S(2)}) collective-permute-start(bf16[1,4,128,1024]{3,2,1,0:T(8,128)(2,1)S(1)} %get-tuple-element.31.refs_6_.after), channel_id=1, source_target_pairs={{0,2},{2,4},{4,6},{1,3},{3,5},{5,7},{8,10},{10,12},{12,14},{9,11},... | collective-permute-start | bytes 3145736 | tf_op jit(solution)/shard_map/ppermute | solution.py:235
  242.1 33.5 %collective-permute-start.21 = (bf16[1,4,128,1024]{3,2,1,0:T(8,128)(2,1)S(1)}, bf16[1,4,128,1024]{3,2,1,0:T(8,128)(2,1)S(1)}, u32[]{:S(2)}, u32[]{:S(2)}) collective-permute-start(bf16[1,4,128,1024]{3,2,1,0:T(8,128)(2,1)S(1)} %get-tuple-element.32), channel_id=1, source_target_pairs={{2,0},{4,2},{6,4},{3,1},{5,3},{7,5},{10,8},{12,10},{14,12},{11,9},... | collective-permute-start | bytes 3145736 | tf_op jit(solution)/shard_map/ppermute | solution.py:235
  268.7 53.9 %collective-permute-start.25 = (bf16[512,1024]{1,0:T(8,128)(2,1)S(1)}, bf16[512,1024]{1,0:T(8,128)(2,1)}, u32[]{:S(2)}, u32[]{:S(2)}) collective-permute-start(bf16[512,1024]{1,0:T(8,128)(2,1)S(1)} %weight.4.after), channel_id=1, source_target_pairs={{0,8},{8,0},{16,24},{24,16},{1,9},{9,1},{17,25},{25,17},{2,10},{10... | collective-permute-start | bytes 3145736 | tf_op jit(solution)/shard_map/ppermute | solution.py:231
  279.2 13.8 %all-to-all-start.1 = ((bf16[4,128,1024]{2,1,0:T(8,128)(2,1)}), bf16[4,128,1024]{2,1,0:T(8,128)(2,1)}, u32[]{:S(2)}, u32[]{:S(2)}) async-start(bf16[4,128,1024]{2,1,0:T(8,128)(2,1)} %sum.1), calls=%async_computation.1 | async-start | bytes 2097152 | tf_op jit(solution)/shard_map/all_to_all | solution.py:379
  288.8 33.8 %collective-permute-start.26 = (bf16[512,1024]{1,0:T(8,128)(2,1)S(1)}, bf16[512,1024]{1,0:T(8,128)(2,1)}, u32[]{:S(2)}, u32[]{:S(2)}) collective-permute-start(bf16[512,1024]{1,0:T(8,128)(2,1)S(1)} %weight.5.after), channel_id=1, source_target_pairs={{0,16},{8,24},{16,0},{24,8},{1,17},{9,25},{17,1},{25,9},{2,18},{10... | collective-permute-start | bytes 3145736 | tf_op jit(solution)/shard_map/ppermute | solution.py:231
  290.8 31.8 %collective-permute-start.27 = (bf16[512,1024]{1,0:T(8,128)(2,1)S(1)}, bf16[512,1024]{1,0:T(8,128)(2,1)}, u32[]{:S(2)}, u32[]{:S(2)}) collective-permute-start(bf16[512,1024]{1,0:T(8,128)(2,1)S(1)} %weight.6.after), channel_id=1, source_target_pairs={{0,24},{8,16},{16,8},{24,0},{1,25},{9,17},{17,9},{25,1},{2,26},{10... | collective-permute-start | bytes 3145736 | tf_op jit(solution)/shard_map/ppermute | solution.py:231
  298.5 7.5 %collective-permute-start.22 = (bf16[16,4096]{1,0:T(8,128)(2,1)S(1)}, bf16[16,4096]{1,0:T(8,128)(2,1)S(1)}, u32[]{:S(2)}, u32[]{:S(2)}) collective-permute-start(bf16[16,4096]{1,0:T(8,128)(2,1)S(1)} %get-tuple-element.36), channel_id=1, source_target_pairs={{2,0},{4,2},{6,4},{3,1},{5,3},{7,5},{10,8},{12,10},{14,12},{11,9},... | collective-permute-start | bytes 393224 | tf_op jit(solution)/shard_map/ppermute | solution.py:235
  299.8 17.7 %collective-permute-start.23 = (bf16[16,4096]{1,0:T(8,128)(2,1)S(1)}, bf16[16,4096]{1,0:T(8,128)(2,1)S(1)}, u32[]{:S(2)}, u32[]{:S(2)}) collective-permute-start(bf16[16,4096]{1,0:T(8,128)(2,1)S(1)} %get-tuple-element.36), channel_id=1, source_target_pairs={{4,0},{6,2},{5,1},{7,3},{12,8},{14,10},{13,9},{15,11},{20,16},{22,... | collective-permute-start | bytes 393224 | tf_op jit(solution)/shard_map/ppermute | solution.py:235
  306.0 11.5 %collective-permute-start.24 = (bf16[16,4096]{1,0:T(8,128)(2,1)S(1)}, bf16[16,4096]{1,0:T(8,128)(2,1)S(1)}, u32[]{:S(2)}, u32[]{:S(2)}) collective-permute-start(bf16[16,4096]{1,0:T(8,128)(2,1)S(1)} %get-tuple-element.36), channel_id=1, source_target_pairs={{6,0},{7,1},{14,8},{15,9},{22,16},{23,17},{30,24},{31,25}} | collective-permute-start | bytes 393224 | tf_op jit(solution)/shard_map/ppermute | solution.py:235
  (29 other events, 172.5 us)
Sparse Core Ops, SparseCore 0:
  75.5 69.1 all-gather.2
where the time goes:
time: 337 us; the launch traced here: 334 us
  Pallas kernels  114 us (34%)
  waiting for transfers between devices  75.2 us (22%)
  starting transfers between devices  73.6 us (22%)
  local copies, waits for them, and re-layouts  24.9 us (7%)
  blocking collectives  20.6 us (6%)
  between operations  14.6 us (4%)
  other arithmetic  11.6 us (3%)
    ppermute x19, waiting for transfers between devices, shift(): return lax.ppermute(value, 'ctx', ends)  74.5 us
    ppermute x19, starting transfers between devices, shift(): return lax.ppermute(value, 'ctx', ends)  51.6 us
    pallas_call x4, Pallas kernels, on_device(): call(weight_body, 'weight', 2 * tokens * feats * quarter, 2 * tokens * (f...  21.4 us
    all_to_all x1, blocking collectives, on_device(): gated_far = lax.all_to_all(gated, 'dp', 0, 0, tiled=True)  20.6 us
    pallas_call x2, Pallas kernels, project(): call(functools.partial(delta_body, n_dp), 'delta', 2 * count * n_dp * row...  19 us
    ppermute x9, starting transfers between devices, swap(): lax.ppermute(value, axis, [(i, i ^ k) for i in range(lax.axis_size(axis))])  17.7 us
    unnamed x63, local copies, waits for them, and re-layouts  16.7 us
    pallas_call x1, Pallas kernels, on_device(): call(flip_body, 'flip', 0, 4 * tokens * depth, grid_spec=pltpu.PrefetchSc...  13.8 us
  transfers between devices with their start and end apart: 30, of which 7 were waited for; matrix products, arithmetic and copies ran while one was open for 5% of the time, Pallas kernels for 31%

commit v1 on v0

--- a/solution.py
+++ b/solution.py
@@ -139,7 +139,8 @@
         conv_grad[:, cols] = (out * query[:, cols].astype(F32)).astype(BF16)
 
 
-def pack_body(count, place, *refs):
+def pack_body(place, *refs):
+    count = len(refs) // 2
     for source, target in zip(refs[:count], refs[-count:]):
         target[...] = source[...]
 
@@ -150,18 +151,16 @@
         out[k] = refs[k][...]
 
 
-def delta_body(count, place, dest, grad, *refs):
-    weights, out = refs[:count], refs[-1]
-    depth = weights[0].shape[1]
+def delta_body(place, dest, grad, weights, *refs):
+    depth = weights.shape[2]
     total = None
-    for k, weight in enumerate(weights):
-        start = pl.multiple_of((place[0] ^ k) * depth, depth)
-        rows = grad[:, :, :, :, pl.ds(start, depth)].reshape(-1, depth)
+    for k in range(weights.shape[0]):
+        rows = grad[:, :, :, :, k * depth : (k + 1) * depth].reshape(-1, depth)
         term = lax.dot_general(
-            rows, weight[...], (((1,), (1,)), ((), ())), preferred_element_type=F32
+            rows, weights[k], (((1,), (1,)), ((), ())), preferred_element_type=F32
         )
         total = term if total is None else total + term
-    out[...] = total.astype(out.dtype).reshape(out.shape)
+    refs[-1][...] = total.astype(BF16).reshape(refs[-1].shape)
 
 
 def flip_body(place, grad, after, out):
@@ -237,20 +236,16 @@
     def piece(k):
         return pl.BlockSpec((part, feats), lambda j, p: (p[2], j * n_ctx + (p[1] ^ k)))
 
-    sent = [
-        lax.dynamic_slice_in_dim(proj_weight, (place[0] ^ k) * quarter, quarter)
-        for k in range(1, n_dp)
-    ]
-    weights = [proj_weight] + [swap(value, "dp", k) for k, value in enumerate(sent, 1)]
+    weights = lax.all_to_all(proj_weight.reshape(n_dp, quarter, feats), "dp", 0, 0, tiled=True)
     mine = call(
-        functools.partial(pack_body, n_ctx), "pack", 0, 4 * part * depth * n_ctx,
+        pack_body, "pack", 0, 4 * part * depth * n_ctx,
         grid_spec=pltpu.PrefetchScalarGridSpec(
             num_scalar_prefetch=1, grid=(n_dp,),
-            in_specs=[piece(k) for k in range(n_ctx)] + [ANY] * len(sent),
+            in_specs=[piece(k) for k in range(n_ctx)],
             out_specs=[pl.BlockSpec((part, feats), lambda j, p: (0, j))] * n_ctx,
         ),
         out_shape=[shape(part, depth)] * n_ctx,
-    )(place, *[out_grad] * n_ctx, *sent)
+    )(place, *[out_grad] * n_ctx)
     mine = [mine[0]] + [swap(mine[k], "ctx", k) for k in range(1, n_ctx)]
     product = (key_in.astype(F32) * value_in.astype(F32)).astype(BF16)
     rim = shift(product, 1)
@@ -283,7 +278,9 @@
             out_shape=shape(rows, width, dtype=F32),
         )(table, x, *after)
 
-    conv_own = local(False, taps, product)
+    conv_own = local(
+        False, taps, product, ends_coef, starts_coef, carry_coef, back_coef, kernel_rev, kernel
+    )
     conv, mixed, ends = call(
         conv_body, "conv", 2 * rows * 128 * width * 8, rows * width * 14,
         grid=(steps,),
@@ -295,10 +292,10 @@
     mine = call(
         join_body, "join", 0, 4 * part * depth * n_ctx,
         grid=(n_dp,),
-        in_specs=[wide(part, feats)] * n_ctx + [ANY] * n_dp,
+        in_specs=[wide(part, feats)] * n_ctx + [ANY] * 2,
         out_specs=deep(n_ctx, part, feats),
         out_shape=shape(n_ctx, part, depth),
-    )(*mine, *weights[1:], mixed)
+    )(*mine, weights, mixed)
     grad = lax.all_gather(mine, ("dp", "tp"), axis=0, tiled=False)
     grad = grad.reshape(n_dp, n_tp, n_ctx, part, depth)
 
@@ -327,7 +324,7 @@
 
     def project(count, dest, *after):
         return call(
-            functools.partial(delta_body, n_dp), "delta", 2 * count * n_dp * rows * depth * quarter,
+            delta_body, "delta", 2 * count * n_dp * rows * depth * quarter,
             2 * tokens * depth + 2 * depth * quarter + 2 * count * n_dp * rows * quarter,
             grid_spec=pltpu.PrefetchScalarGridSpec(
                 num_scalar_prefetch=2, grid=(count,),
@@ -335,49 +332,15 @@
                     pl.BlockSpec(
                         (n_dp, n_tp, 1, part, depth), lambda i, p, q: (0, 0, p[1] ^ q[i], 0, 0)
                     ),
-                    pl.BlockSpec((quarter, feats), lambda i, p, q: (p[0], 0)),
-                ] + [pl.BlockSpec((quarter, feats), lambda i, p, q: (0, 0))] * (n_dp - 1)
-                + [ANY] * len(after),
+                    pl.BlockSpec((n_dp, quarter, feats), lambda i, p, q: (0, 0, 0)),
+                ] + [ANY] * len(after),
                 out_specs=pl.BlockSpec(chunk, lambda i, p, q: (i, 0, 0, 0)),
             ),
             out_shape=shape(count, n_dp, rows, quarter),
-        )(place, dest, grad, *weights, *after)
+        )(place, dest, grad, weights, *after)
 
     first = project(1, first_dest[None], from_left[0], from_right[0])
     partial = project(n_ctx, jnp.arange(n_ctx, dtype=jnp.int32), first)
-    right, left = shift(first, 1, [0]), shift(first, -1, [last])
-
-    def pick(ahead):
-        return pl.BlockSpec(
-            (1, 1, rows, quarter), lambda i, q: (q[ahead], i, 0, 0)
-        )
-
-    piece_of = pl.BlockSpec((1, 1, rows, quarter), lambda i, q: (0, i, 0, 0))
-    for t in range(1, last):
-        dests = jnp.clip(jnp.stack([last - t + place[1], t - last + place[1]]), 0, last)
-        right, left = call(
-            add_body, "add", 0, 12 * n_dp * rows * quarter,
-            grid_spec=pltpu.PrefetchScalarGridSpec(
-                num_scalar_prefetch=1, grid=(n_dp,),
-                in_specs=[pick(0), pick(1), piece_of, piece_of, ANY, ANY],
-                out_specs=[piece_of] * 2,
-            ),
-            out_shape=[shape(*chunk)] * 2,
-        )(dests, partial, partial, right, left, from_left[t], from_right[t])
-        token = right
-        right = shift(right, 1, range(t + 1))
-        left = shift(left, -1, range(last - t, n_ctx))
-    delta = call(
-        sum_body, "sum", 0, 8 * n_dp * rows * quarter,
-        grid_spec=pltpu.PrefetchScalarGridSpec(
-            num_scalar_prefetch=1, grid=(n_dp,),
-            in_specs=[pick(0), piece_of, piece_of],
-            out_specs=pl.BlockSpec((1, rows, quarter), lambda i, q: (i, 0, 0)),
-        ),
-        out_shape=shape(n_dp, rows, quarter),
-    )(place[1:2], partial, right, left)
-    delta_far = lax.all_to_all(delta, "dp", 0, 0, tiled=True)
-
     grad_t = call(
         flip_body, "flip", 0, 4 * tokens * depth,
         grid_spec=pltpu.PrefetchScalarGridSpec(
@@ -393,6 +356,40 @@
         ),
         out_shape=shape(depth, tokens),
     )(place, grad, partial)
+    right, left = shift(first, 1, [0]), shift(first, -1, [last])
+
+    def pick(ahead):
+        return pl.BlockSpec(
+            (1, 1, rows, quarter), lambda i, q: (q[ahead], i, 0, 0)
+        )
+
+    piece_of = pl.BlockSpec((1, 1, rows, quarter), lambda i, q: (0, i, 0, 0))
+    for t in range(1, last):
+        after = (from_left[t], from_right[t]) + ((grad_t,) if t == last - 1 else ())
+        dests = jnp.clip(jnp.stack([last - t + place[1], t - last + place[1]]), 0, last)
+        right, left = call(
+            add_body, "add", 0, 12 * n_dp * rows * quarter,
+            grid_spec=pltpu.PrefetchScalarGridSpec(
+                num_scalar_prefetch=1, grid=(n_dp,),
+                in_specs=[pick(0), pick(1), piece_of, piece_of] + [ANY] * len(after),
+                out_specs=[piece_of] * 2,
+            ),
+            out_shape=[shape(*chunk)] * 2,
+        )(dests, partial, partial, right, left, *after)
+        token = right
+        right = shift(right, 1, range(t + 1))
+        left = shift(left, -1, range(last - t, n_ctx))
+    delta = call(
+        sum_body, "sum", 0, 8 * n_dp * rows * quarter,
+        grid_spec=pltpu.PrefetchScalarGridSpec(
+            num_scalar_prefetch=1, grid=(n_dp,),
+            in_specs=[pick(0), piece_of, piece_of],
+            out_specs=pl.BlockSpec((1, rows, quarter), lambda i, q: (i, 0, 0)),
+        ),
+        out_shape=shape(n_dp, rows, quarter),
+    )(place[1:2], partial, right, left)
+    delta_far = lax.all_to_all(delta, "dp", 0, 0, tiled=True)
+
     gated_all = call(
         merge_body, "merge", 0, 2 * (2 * n_ctx + last) * n_dp * rows * quarter,
         grid=(n_dp,),

time: 337 us -> 312 us (0.926)
  local copies, waits for them, and re-layouts: 24.9 us -> 6.45 us
    ppermute x19, waiting for transfers between devices: 74.5 us -> 40.1 us  [shift(): return lax.ppermute(value, 'ctx', ends)]
    all_to_all x1, waiting for transfers between devices: 0.63 us -> 19.3 us  [on_device(): delta_far = lax.all_to_all(delta, 'dp', 0, 0, tiled=True)]
    unnamed x63 -> x45, local copies, waits for them, and re-layouts: 16.7 us -> 5.59 us
    ppermute x9 -> x6, waiting for transfers between devices: 0.03 us -> 10.1 us  [swap(): lax.ppermute(value, axis, [(i, i ^ k) for i in range(lax.axis_size(axis))])]
    ppermute x9 -> x6, starting transfers between devices: 17.7 us -> 8.92 us  [swap(): lax.ppermute(value, axis, [(i, i ^ k) for i in range(lax.axis_size(axis))])]
    all_to_all x0 -> x1, starting transfers between devices: none -> 5.18 us  [on_device(): lax.all_to_all(proj_weight.reshape(n_dp, quarter, feats), 'dp', 0, 0, til...]
    dynamic_slice x1 -> x0, local copies, waits for them, and re-layouts: 3.59 us -> none  [on_device(): lax.dynamic_slice_in_dim(proj_weight, (place[0] ^ k) * quarter, quarter)]
  transfers between devices with their start and end apart: 30 -> 28, of which waited for: 7 -> 11; matrix products, arithmetic and copies ran while one was open for 5% -> 3% of each run, Pallas kernels for 31% -> 32%
where the time goes in v1:
time: 312 us; the launch traced here: 307 us
  Pallas kernels  114 us (37%)
  starting transfers between devices  73.8 us (24%)
  waiting for transfers between devices  72.1 us (23%)
  blocking collectives  17.9 us (6%)
  between operations  14.5 us (5%)
  other arithmetic  8.51 us (3%)
  local copies, waits for them, and re-layouts  6.45 us (2%)
    ppermute x19, starting transfers between devices, shift(): return lax.ppermute(value, 'ctx', ends)  53 us
    ppermute x19, waiting for transfers between devices, shift(): return lax.ppermute(value, 'ctx', ends)  40.1 us
    pallas_call x4, Pallas kernels, on_device(): call(weight_body, 'weight', 2 * tokens * feats * quarter, 2 * tokens * (f...  21.4 us
    pallas_call x2, Pallas kernels, project(): call(delta_body, 'delta', 2 * count * n_dp * rows * depth * quarter, 2 *...  20.6 us
    all_to_all x1, waiting for transfers between devices, on_device(): delta_far = lax.all_to_all(delta, 'dp', 0, 0, tiled=True)  19.3 us
    all_to_all x1, blocking collectives, on_device(): gated_far = lax.all_to_all(gated, 'dp', 0, 0, tiled=True)  17.9 us
    pallas_call x1, Pallas kernels, on_device(): call(flip_body, 'flip', 0, 4 * tokens * depth, grid_spec=pltpu.PrefetchSc...  13.8 us
    pallas_call x3, Pallas kernels, local(): call(functools.partial(local_body, transposed), 'local_t' if transposed e...  11.8 us
  transfers between devices with their start and end apart: 28, of which 11 were waited for; matrix products, arithmetic and copies ran while one was open for 3% of the time, Pallas kernels for 32%

profile of v1, /device:TPU:0, one launch (start us, length us, event | category | flops | bytes accessed | tf_op | source)
XLA Modules:
  0.0 307.0 jit_solution(10180115335844088806)
XLA Ops:
  7.2 5.2 %all-to-all-start = ((bf16[4,1024,512]{2,1,0:T(8,128)(2,1)}), bf16[4,1024,512]{2,1,0:T(8,128)(2,1)}, u32[]{:S(2)}, u32[]{:S(2)}) async-start(bf16[4,1024,512]{2,1,0:T(8,128)(2,1)} %bitcast.20), calls=%async_computation | async-start | bytes 8388608 | tf_op jit(solution)/shard_map/all_to_all | solution.py:239
  14.3 5.6 %collective-permute-start.3 = (bf16[128,4096]{1,0:T(8,128)(2,1)S(1)}, bf16[128,4096]{1,0:T(8,128)(2,1)}, u32[]{:S(2)}, u32[]{:S(2)}) collective-permute-start(bf16[128,4096]{1,0:T(8,128)(2,1)S(1)} %multiply_convert_fusion.2.x), channel_id=1, source_target_pairs={{0,2},{2,4},{4,6},{1,3},{3,5},{5,7},{8,10},{10,12},{12,14},{9,11},... | collective-permute-start | bytes 3145736 | tf_op jit(solution)/shard_map/ppermute | solution.py:234
  30.2 3.7 %multiply_convert_fusion = (bf16[384,4096]{1,0:T(8,128)(2,1)}, bf16[384,4096]{1,0:T(8,128)(2,1)}) fusion(f32[384]{0:T(512)S(1)} %get-tuple-element.44, f32[4096]{0:T(1024)S(1)} %neg.22, f32[4096]{0:T(1024)S(1)} %mul.110, f32[384]{0:T(512)S(1)} %get-tuple-element.45), kind=kLoop, calls=%fused_computation | loop fusion | flops 9437184 | bytes 6327296 | tf_op jit(solution)/shard_map/convert_element_type | solution.py:260
  34.7 4.2 %local.2.own_part = f32[128,4096]{1,0:T(8,128)} custom-call(f32[256,128]{1,0:T(8,128)S(1)} %pad_maximum_fusion.rows.taps, bf16[128,4096]{1,0:T(8,128)(2,1)S(1)} %multiply_convert_fusion.2.x, bf16[4096,128]{1,0:T(8,128)(2,1)S(1)} %get-tuple-element.43.refs_0_.ends_coef, bf16[4096,128]{1,0:T(8,128)(2,1)S(1)} %get-tuple-element.42.refs_1_.starts_coef, ...), custom_call_target="tpu_custom_call" | custom-call | flops 1073741824 | bytes 3145728 | tf_op jit(solution)/shard_map/local/pallas_call | solution.py:271
  42.5 5.7 %conv.1 = (bf16[128,4096]{1,0:T(8,128)(2,1)S(1)}, bf16[128,4096]{1,0:T(8,128)(2,1)S(1)}, bf16[16,4096]{1,0:T(8,128)(2,1)S(1)}) custom-call(bf16[128,4096]{1,0:T(8,128)(2,1)} %collective-permute-done.3.rim, f32[128,4096]{1,0:T(8,128)} %local.2.own_part, bf16[128,4096]{1,0:T(8,128)(2,1)} %query.3, f32[256,128]{1,0:T(8,128)S(1)} %pad_maximum_fusion.rows.taps, ...), custom_call_target="tpu_custom_call" | custom-call | flops 1073741824 | bytes 7340032 | tf_op jit(solution)/shard_map/conv/pallas_call | solution.py:284
  48.3 5.6 %collective-permute-done.1.refs_2_ = bf16[64,2048]{1,0:T(8,128)(2,1)} collective-permute-done((bf16[64,2048]{1,0:T(8,128)(2,1)}, bf16[64,2048]{1,0:T(8,128)(2,1)}, u32[]{:S(2)}, u32[]{:S(2)}) %collective-permute-start.1) | collective-permute-done | bytes 262176 | tf_op jit(solution)/shard_map/ppermute | solution.py:230
  53.9 4.5 %collective-permute-done.2.refs_3_ = bf16[64,2048]{1,0:T(8,128)(2,1)} collective-permute-done((bf16[64,2048]{1,0:T(8,128)(2,1)}, bf16[64,2048]{1,0:T(8,128)(2,1)}, u32[]{:S(2)}, u32[]{:S(2)}) %collective-permute-start.2) | collective-permute-done | bytes 262176 | tf_op jit(solution)/shard_map/ppermute | solution.py:230
  64.2 6.7 %collective-permute-start.4 = (bf16[16,4096]{1,0:T(8,128)(2,1)S(1)}, bf16[16,4096]{1,0:T(8,128)(2,1)S(1)}, u32[]{:S(2)}, u32[]{:S(2)}) collective-permute-start(bf16[16,4096]{1,0:T(8,128)(2,1)S(1)} %get-tuple-element.27), channel_id=1, source_target_pairs={{0,2},{2,4},{4,6},{1,3},{3,5},{5,7},{8,10},{10,12},{12,14},{9,11},... | collective-permute-start | bytes 393224 | tf_op jit(solution)/shard_map/ppermute | solution.py:234
  70.9 3.8 %collective-permute-start.5 = (bf16[16,4096]{1,0:T(8,128)(2,1)S(1)}, bf16[16,4096]{1,0:T(8,128)(2,1)S(1)}, u32[]{:S(2)}, u32[]{:S(2)}) collective-permute-start(bf16[16,4096]{1,0:T(8,128)(2,1)S(1)} %get-tuple-element.27), channel_id=1, source_target_pairs={{0,4},{2,6},{1,5},{3,7},{8,12},{10,14},{9,13},{11,15},{16,20},{18,... | collective-permute-start | bytes 393224 | tf_op jit(solution)/shard_map/ppermute | solution.py:234
  76.1 4.2 %local.3 = f32[128,4096]{1,0:T(8,128)} custom-call(f32[256,128]{1,0:T(8,128)S(1)} %pad_maximum_fusion.1.refs_4_.rows, bf16[128,4096]{1,0:T(8,128)(2,1)S(1)} %get-tuple-element.26.refs_5_.x, bf16[4,64,2048]{2,1,0:T(8,128)(2,1)} %join.1.refs_0_), custom_call_target="tpu_custom_call" | custom-call | flops 1073741824 | bytes 3145728 | tf_op jit(solution)/shard_map/local/pallas_call | solution.py:271
  80.3 4.0 %long.1 = (bf16[128,4096]{1,0:T(8,128)(2,1)S(1)}, bf16[4,128,1024]{2,1,0:T(8,128)(2,1)S(1)}) custom-call(f32[128,4096]{1,0:T(8,128)} %local.3, bf16[384,4096]{1,0:T(8,128)(2,1)} %get-tuple-element.41.refs_2_.coef, bf16[128,4096]{1,0:T(8,128)(2,1)S(1)} %copy-done.10, bf16[16,4096]{1,0:T(8,128)(2,1)S(1)} %collective-permute-done.4.refs_0_, ...), custom_call_target="tpu_custom_call" | custom-call | flops 134217728 | bytes 5242880 | tf_op jit(solution)/shard_map/long/pallas_call | solution.py:304
  84.3 17.9 %all_to_all.15.own = bf16[4,128,1024]{2,1,0:T(8,128)(2,1)S(1)} all-to-all(bf16[4,128,1024]{2,1,0:T(8,128)(2,1)S(1)} %get-tuple-element.28), channel_id=1, replica_groups=mesh['dp'=4,'ctx'=4,'tp'=2] {'dp'}, dimensions={0} | all-to-all | bytes 2097152 | tf_op jit(solution)/shard_map/all_to_all | solution.py:311
  107.9 17.5 %collective-permute-done.7.refs_0_ = bf16[4,128,1024]{2,1,0:T(8,128)(2,1)S(1)} collective-permute-done((bf16[4,128,1024]{2,1,0:T(8,128)(2,1)S(1)}, bf16[4,128,1024]{2,1,0:T(8,128)(2,1)S(1)}, u32[]{:S(2)}, u32[]{:S(2)}) %collective-permute-start.7) | collective-permute-done | bytes 1048608 | tf_op jit(solution)/shard_map/ppermute | solution.py:234
  131.0 6.7 %delta.2.refs_0_ = bf16[1,4,128,1024]{3,2,1,0:T(8,128)(2,1)} custom-call(s32[3]{0:T(128)S(1)} %pad_add_fusion.place, s32[1]{0:T(128)} %bitcast.5.dest, bf16[4,2,4,64,2048]{4,3,2,1,0:T(8,128)(2,1)} %bitcast.17, bf16[4,1024,512]{2,1,0:T(8,128)(2,1)} %all-to-all-done.refs_4_.weights, bf16[4,128,1024]{2,1,0:T(8,128)(2,1)S(1)} %collective-permute-done.7.refs_0_, ...), custom_call_target="tpu_custom_call" | custom-call | flops 2147483648 | bytes 13631488 | tf_op jit(solution)/shard_map/delta/pallas_call | solution.py:326
  139.3 5.5 %collective-permute-start.9 = (bf16[1,4,128,1024]{3,2,1,0:T(8,128)(2,1)}, bf16[1,4,128,1024]{3,2,1,0:T(8,128)(2,1)}, u32[]{:S(2)}, u32[]{:S(2)}) collective-permute-start(bf16[1,4,128,1024]{3,2,1,0:T(8,128)(2,1)} %delta.2.refs_0_), channel_id=1, source_target_pairs={{0,2},{1,3},{8,10},{9,11},{16,18},{17,19},{24,26},{25,27}} | collective-permute-start | bytes 3145736 | tf_op jit(solution)/shard_map/ppermute | solution.py:234
  146.5 6.4 %collective-permute-done.12.refs_1_.refs_4_ = bf16[4,128,1024]{2,1,0:T(8,128)(2,1)} collective-permute-done((bf16[4,128,1024]{2,1,0:T(8,128)(2,1)S(1)}, bf16[4,128,1024]{2,1,0:T(8,128)(2,1)}, u32[]{:S(2)}, u32[]{:S(2)}) %collective-permute-start.12) | collective-permute-done | bytes 1048608 | tf_op jit(solution)/shard_map/ppermute | solution.py:234
  154.2 13.9 %delta.3.partial_right.partial_left.after.partial = bf16[4,4,128,1024]{3,2,1,0:T(8,128)(2,1)} custom-call(s32[3]{0:T(128)S(1)} %pad_add_fusion.place, s32[4]{0:T(128)S(1)} %iota.21.dest, bf16[4,2,4,64,2048]{4,3,2,1,0:T(8,128)(2,1)} %bitcast.18, bf16[4,1024,512]{2,1,0:T(8,128)(2,1)} %all-to-all-done.refs_4_.weights, bf16[1,4,128,1024]{3,2,1,0:T(8,128)(2,1)} %delta.2.refs_0_), custom_call_target="tpu_custom_call" | custom-call | flops 8589934592 | bytes 16777216 | tf_op jit(solution)/shard_map/delta/pallas_call | solution.py:326
  168.1 4.7 %add.63 = (bf16[1,4,128,1024]{3,2,1,0:T(8,128)(2,1)}, bf16[1,4,128,1024]{3,2,1,0:T(8,128)(2,1)}) custom-call(s32[2]{0:T(128)S(1)} %add_clamp_fusion.1.dests, bf16[4,4,128,1024]{3,2,1,0:T(8,128)(2,1)} %delta.3.partial_right.partial_left.after.partial, bf16[4,4,128,1024]{3,2,1,0:T(8,128)(2,1)} %delta.3.partial_right.partial_left.after.partial, ...), custom_call_target="tpu_custom_call" | custom-call | bytes 6291456 | tf_op jit(solution)/shard_map/add/pallas_call | solution.py:370
  172.8 5.6 %collective-permute-start.13 = (bf16[1,4,128,1024]{3,2,1,0:T(8,128)(2,1)}, bf16[1,4,128,1024]{3,2,1,0:T(8,128)(2,1)S(1)}, u32[]{:S(2)}, u32[]{:S(2)}) collective-permute-start(bf16[1,4,128,1024]{3,2,1,0:T(8,128)(2,1)} %get-tuple-element.29), channel_id=1, source_target_pairs={{0,2},{2,4},{1,3},{3,5},{8,10},{10,12},{9,11},{11,13},{16,18},{18,... | collective-permute-start | bytes 3145736 | tf_op jit(solution)/shard_map/ppermute | solution.py:234
  180.2 13.8 %flip.1.refs_2_.grad_t = bf16[2048,2048]{1,0:T(8,128)(2,1)} custom-call(s32[3]{0:T(128)S(1)} %pad_add_fusion.place, bf16[4,2,4,64,2048]{4,3,2,1,0:T(8,128)(2,1)} %bitcast.19, bf16[4,4,128,1024]{3,2,1,0:T(8,128)(2,1)} %delta.3.partial_right.partial_left.after.partial), custom_call_target="tpu_custom_call" | custom-call | bytes 16777216 | tf_op jit(solution)/shard_map/flip/pallas_call | solution.py:344
  199.6 6.4 %collective-permute-start.17 = (bf16[1,4,128,1024]{3,2,1,0:T(8,128)(2,1)S(1)}, bf16[1,4,128,1024]{3,2,1,0:T(8,128)(2,1)S(1)}, u32[]{:S(2)}, u32[]{:S(2)}) collective-permute-start(bf16[1,4,128,1024]{3,2,1,0:T(8,128)(2,1)S(1)} %get-tuple-element.31.refs_6_.after), channel_id=1, source_target_pairs={{0,2},{2,4},{4,6},{1,3},{3,5},{5,7},{8,10},{10,12},{12,14},{9,11},... | collective-permute-start | bytes 3145736 | tf_op jit(solution)/shard_map/ppermute | solution.py:234
  207.3 4.7 %merge.1 = bf16[4,4,128,1024]{3,2,1,0:T(8,128)(2,1)} custom-call(bf16[4,128,1024]{2,1,0:T(8,128)(2,1)S(1)} %copy-done.9, bf16[4,128,1024]{2,1,0:T(8,128)(2,1)S(1)} %collective-permute-done.7.refs_0_, bf16[4,128,1024]{2,1,0:T(8,128)(2,1)S(1)} %copy-done.5, bf16[4,128,1024]{2,1,0:T(8,128)(2,1)} %collective-permute-done.15.refs_0_.refs_2_, ...), custom_call_target="tpu_custom_call" | custom-call | bytes 11534336 | tf_op jit(solution)/shard_map/merge/pallas_call | solution.py:393
  213.2 5.4 %weight.4.after = bf16[512,1024]{1,0:T(8,128)(2,1)S(1)} custom-call(s32[3]{0:T(128)S(1)} %pad_add_fusion.place, bf16[2048,2048]{1,0:T(8,128)(2,1)} %flip.1.refs_2_.grad_t, bf16[2048,1024]{1,0:T(8,128)(2,1)} %bitcast.13, bf16[1,4,128,1024]{3,2,1,0:T(8,128)(2,1)S(1)} %copy-done.7), custom_call_target="tpu_custom_call" | custom-call | flops 2147483648 | bytes 6291456 | tf_op jit(solution)/shard_map/weight/pallas_call | solution.py:402
  218.6 5.4 %weight.5.after = bf16[512,1024]{1,0:T(8,128)(2,1)S(1)} custom-call(s32[3]{0:T(128)S(1)} %pad_add_fusion.place, bf16[2048,2048]{1,0:T(8,128)(2,1)} %flip.1.refs_2_.grad_t, bf16[2048,1024]{1,0:T(8,128)(2,1)} %bitcast.14, bf16[512,1024]{1,0:T(8,128)(2,1)S(1)} %weight.4.after), custom_call_target="tpu_custom_call" | custom-call | flops 2147483648 | bytes 6291456 | tf_op jit(solution)/shard_map/weight/pallas_call | solution.py:402
  230.3 6.7 %all-to-all-start.2 = ((bf16[4,128,1024]{2,1,0:T(8,128)(2,1)}), bf16[4,128,1024]{2,1,0:T(8,128)(2,1)}, u32[]{:S(2)}, u32[]{:S(2)}) async-start(bf16[4,128,1024]{2,1,0:T(8,128)(2,1)} %sum.1), calls=%async_computation.2 | async-start | bytes 2097152 | tf_op jit(solution)/shard_map/all_to_all | solution.py:391
  237.0 5.4 %weight.6.after = bf16[512,1024]{1,0:T(8,128)(2,1)S(1)} custom-call(s32[3]{0:T(128)S(1)} %pad_add_fusion.place, bf16[2048,2048]{1,0:T(8,128)(2,1)} %flip.1.refs_2_.grad_t, bf16[2048,1024]{1,0:T(8,128)(2,1)} %bitcast.15, bf16[512,1024]{1,0:T(8,128)(2,1)S(1)} %weight.5.after), custom_call_target="tpu_custom_call" | custom-call | flops 2147483648 | bytes 6291456 | tf_op jit(solution)/shard_map/weight/pallas_call | solution.py:402
  246.9 19.3 %all-to-all-done.2.delta = bf16[4,128,1024]{2,1,0:T(8,128)(2,1)} async-done(((bf16[4,128,1024]{2,1,0:T(8,128)(2,1)}), bf16[4,128,1024]{2,1,0:T(8,128)(2,1)}, u32[]{:S(2)}, u32[]{:S(2)}) %all-to-all-start.2) | async-done | bytes 1048608 | tf_op jit(solution)/shard_map/all_to_all | solution.py:391
  267.3 4.4 %seed.1 = (bf16[128,4096]{1,0:T(8,128)(2,1)S(1)}, bf16[16,4096]{1,0:T(8,128)(2,1)S(1)}, bf16[128,4096]{1,0:T(8,128)(2,1)}) custom-call(bf16[4,128,1024]{2,1,0:T(8,128)(2,1)} %all-to-all-done.2.delta, bf16[128,4096]{1,0:T(8,128)(2,1)S(1)} %copy-done.11, bf16[128,4096]{1,0:T(8,128)(2,1)} %copy-done.14, bf16[4096,128]{1,0:T(8,128)(2,1)} %copy-done.1), custom_call_target="tpu_custom_call" | custom-call | flops 134217728 | bytes 5242880 | tf_op jit(solution)/shard_map/seed/pallas_call | solution.py:417
  274.3 4.3 %collective-permute-done.19.refs_0_ = bf16[16,4096]{1,0:T(8,128)(2,1)S(1)} collective-permute-done((bf16[16,4096]{1,0:T(8,128)(2,1)S(1)}, bf16[16,4096]{1,0:T(8,128)(2,1)S(1)}, u32[]{:S(2)}, u32[]{:S(2)}) %collective-permute-start.19) | collective-permute-done | bytes 131104 | tf_op jit(solution)/shard_map/ppermute | solution.py:234
  279.8 5.4 %weight.7.refs_0_ = bf16[512,1024]{1,0:T(8,128)(2,1)S(1)} custom-call(s32[3]{0:T(128)S(1)} %pad_add_fusion.place, bf16[2048,2048]{1,0:T(8,128)(2,1)} %flip.1.refs_2_.grad_t, bf16[2048,1024]{1,0:T(8,128)(2,1)} %bitcast.16, bf16[512,1024]{1,0:T(8,128)(2,1)S(1)} %weight.6.after), custom_call_target="tpu_custom_call" | custom-call | flops 2147483648 | bytes 6291456 | tf_op jit(solution)/shard_map/weight/pallas_call | solution.py:402
  290.1 5.1 %back.1 = (bf16[128,4096]{1,0:T(8,128)(2,1)}, bf16[128,4096]{1,0:T(8,128)(2,1)}) custom-call(f32[128,4096]{1,0:T(8,128)} %copy-done.13, bf16[384,4096]{1,0:T(8,128)(2,1)} %get-tuple-element.40.refs_3_.coef, bf16[128,4096]{1,0:T(8,128)(2,1)S(1)} %copy-done.16, bf16[128,4096]{1,0:T(8,128)(2,1)S(1)} %copy-done.12, ...), custom_call_target="tpu_custom_call" | custom-call | flops 134217728 | bytes 6291456 | tf_op jit(solution)/shard_map/back/pallas_call | solution.py:429
  295.2 4.9 %lay.1 = bf16[512,4096]{1,0:T(8,128)(2,1)} custom-call(s32[3]{0:T(128)S(1)} %pad_add_fusion.place, bf16[512,1024]{1,0:T(8,128)(2,1)S(1)} %weight.7.refs_0_, bf16[512,1024]{1,0:T(8,128)(2,1)} %collective-permute-done.22.refs_1_, bf16[512,1024]{1,0:T(8,128)(2,1)} %collective-permute-done.23.refs_2_, bf16[512,1024]{1,0:T(8,128)(2,1)} %collective-permute-done.24.refs_3_, ...), custom_call_target="tpu_custom_call" | custom-call | bytes 8388608 | tf_op jit(solution)/shard_map/lay/pallas_call | solution.py:439
  (113 shorter events, 70.0 us)
Async XLA Ops:
  7.2 53.8 %all-to-all-start = ((bf16[4,1024,512]{2,1,0:T(8,128)(2,1)}), bf16[4,1024,512]{2,1,0:T(8,128)(2,1)}, u32[]{:S(2)}, u32[]{:S(2)}) async-start(bf16[4,1024,512]{2,1,0:T(8,128)(2,1)} %bitcast.20), calls=%async_computation | async-start | bytes 8388608 | tf_op jit(solution)/shard_map/all_to_all | solution.py:239
  12.3 118.6 %all-gather.3.cloned.1.call-start = ((), (), s32[]{:S(2)}) async-start(), calls=%async_computation.3 | async-start | bytes 9437184 | tf_op jit(solution)/shard_map/all_gather | solution.py:299
  14.3 28.2 %collective-permute-start.3 = (bf16[128,4096]{1,0:T(8,128)(2,1)S(1)}, bf16[128,4096]{1,0:T(8,128)(2,1)}, u32[]{:S(2)}, u32[]{:S(2)}) collective-permute-start(bf16[128,4096]{1,0:T(8,128)(2,1)S(1)} %multiply_convert_fusion.2.x), channel_id=1, source_target_pairs={{0,2},{2,4},{4,6},{1,3},{3,5},{5,7},{8,10},{10,12},{12,14},{9,11},... | collective-permute-start | bytes 3145736 | tf_op jit(solution)/shard_map/ppermute | solution.py:234
  22.9 25.3 %collective-permute-start = (bf16[64,2048]{1,0:T(8,128)(2,1)}, bf16[64,2048]{1,0:T(8,128)(2,1)}, u32[]{:S(2)}, u32[]{:S(2)}) collective-permute-start(bf16[64,2048]{1,0:T(8,128)(2,1)} %get-tuple-element.23), channel_id=1, source_target_pairs={{0,2},{2,0},{4,6},{6,4},{1,3},{3,1},{5,7},{7,5},{8,10},{10,8},{12,... | collective-permute-start | bytes 786440 | tf_op jit(solution)/shard_map/ppermute | solution.py:230
  23.6 30.3 %collective-permute-start.1 = (bf16[64,2048]{1,0:T(8,128)(2,1)}, bf16[64,2048]{1,0:T(8,128)(2,1)}, u32[]{:S(2)}, u32[]{:S(2)}) collective-permute-start(bf16[64,2048]{1,0:T(8,128)(2,1)} %get-tuple-element.24), channel_id=1, source_target_pairs={{0,4},{2,6},{4,0},{6,2},{1,5},{3,7},{5,1},{7,3},{8,12},{10,14},{12... | collective-permute-start | bytes 786440 | tf_op jit(solution)/shard_map/ppermute | solution.py:230
  24.6 33.8 %collective-permute-start.2 = (bf16[64,2048]{1,0:T(8,128)(2,1)}, bf16[64,2048]{1,0:T(8,128)(2,1)}, u32[]{:S(2)}, u32[]{:S(2)}) collective-permute-start(bf16[64,2048]{1,0:T(8,128)(2,1)} %get-tuple-element.25), channel_id=1, source_target_pairs={{0,6},{2,4},{4,2},{6,0},{1,7},{3,5},{5,3},{7,1},{8,14},{10,12},{12... | collective-permute-start | bytes 786440 | tf_op jit(solution)/shard_map/ppermute | solution.py:230
  42.5 18.4 %copy-start.18 = (bf16[64,2048]{1,0:T(8,128)(2,1)S(1)}, bf16[64,2048]{1,0:T(8,128)(2,1)}, u32[]{:S(2)}) copy-start(bf16[64,2048]{1,0:T(8,128)(2,1)} %copy-done.17) | copy-start | bytes 786436
  64.2 16.1 %copy-start.10 = (bf16[128,4096]{1,0:T(8,128)(2,1)S(1)}, bf16[128,4096]{1,0:T(8,128)(2,1)}, u32[]{:S(2)}) copy-start(bf16[128,4096]{1,0:T(8,128)(2,1)} %gate.3) | copy-start | bytes 3145732
  64.2 16.0 %collective-permute-start.4 = (bf16[16,4096]{1,0:T(8,128)(2,1)S(1)}, bf16[16,4096]{1,0:T(8,128)(2,1)S(1)}, u32[]{:S(2)}, u32[]{:S(2)}) collective-permute-start(bf16[16,4096]{1,0:T(8,128)(2,1)S(1)} %get-tuple-element.27), channel_id=1, source_target_pairs={{0,2},{2,4},{4,6},{1,3},{3,5},{5,7},{8,10},{10,12},{12,14},{9,11},... | collective-permute-start | bytes 393224 | tf_op jit(solution)/shard_map/ppermute | solution.py:234
  70.9 9.3 %collective-permute-start.5 = (bf16[16,4096]{1,0:T(8,128)(2,1)S(1)}, bf16[16,4096]{1,0:T(8,128)(2,1)S(1)}, u32[]{:S(2)}, u32[]{:S(2)}) collective-permute-start(bf16[16,4096]{1,0:T(8,128)(2,1)S(1)} %get-tuple-element.27), channel_id=1, source_target_pairs={{0,4},{2,6},{1,5},{3,7},{8,12},{10,14},{9,13},{11,15},{16,20},{18,... | collective-permute-start | bytes 393224 | tf_op jit(solution)/shard_map/ppermute | solution.py:234
  74.8 5.5 %collective-permute-start.6 = (bf16[16,4096]{1,0:T(8,128)(2,1)S(1)}, bf16[16,4096]{1,0:T(8,128)(2,1)S(1)}, u32[]{:S(2)}, u32[]{:S(2)}) collective-permute-start(bf16[16,4096]{1,0:T(8,128)(2,1)S(1)} %get-tuple-element.27), channel_id=1, source_target_pairs={{0,6},{1,7},{8,14},{9,15},{16,22},{17,23},{24,30},{25,31}} | collective-permute-start | bytes 393224 | tf_op jit(solution)/shard_map/ppermute | solution.py:234
  84.3 17.9 %copy-start.14 = (bf16[128,4096]{1,0:T(8,128)(2,1)}, bf16[128,4096]{1,0:T(8,128)(2,1)S(1)}, u32[]{:S(2)}) copy-start(bf16[128,4096]{1,0:T(8,128)(2,1)S(1)} %get-tuple-element.33.long_out) | copy-start | bytes 3145732
  102.2 23.2 %collective-permute-start.7 = (bf16[4,128,1024]{2,1,0:T(8,128)(2,1)S(1)}, bf16[4,128,1024]{2,1,0:T(8,128)(2,1)S(1)}, u32[]{:S(2)}, u32[]{:S(2)}) collective-permute-start(bf16[4,128,1024]{2,1,0:T(8,128)(2,1)S(1)} %all_to_all.15.own), channel_id=1, source_target_pairs={{0,2},{2,4},{4,6},{1,3},{3,5},{5,7},{8,10},{10,12},{12,14},{9,11},... | collective-permute-start | bytes 3145736 | tf_op jit(solution)/shard_map/ppermute | solution.py:234
  105.7 24.0 %collective-permute-start.8 = (bf16[4,128,1024]{2,1,0:T(8,128)(2,1)S(1)}, bf16[4,128,1024]{2,1,0:T(8,128)(2,1)S(1)}, u32[]{:S(2)}, u32[]{:S(2)}) collective-permute-start(bf16[4,128,1024]{2,1,0:T(8,128)(2,1)S(1)} %all_to_all.15.own), channel_id=1, source_target_pairs={{2,0},{4,2},{6,4},{3,1},{5,3},{7,5},{10,8},{12,10},{14,12},{11,9},... | collective-permute-start | bytes 3145736 | tf_op jit(solution)/shard_map/ppermute | solution.py:234
  125.5 19.4 %collective-permute-start.11 = (bf16[4,128,1024]{2,1,0:T(8,128)(2,1)S(1)}, bf16[4,128,1024]{2,1,0:T(8,128)(2,1)S(1)}, u32[]{:S(2)}, u32[]{:S(2)}) collective-permute-start(bf16[4,128,1024]{2,1,0:T(8,128)(2,1)S(1)} %collective-permute-done.7.refs_0_), channel_id=1, source_target_pairs={{2,4},{4,6},{3,5},{5,7},{10,12},{12,14},{11,13},{13,15},{18,20},{2... | collective-permute-start | bytes 3145736 | tf_op jit(solution)/shard_map/ppermute | solution.py:234
  129.6 23.3 %collective-permute-start.12 = (bf16[4,128,1024]{2,1,0:T(8,128)(2,1)S(1)}, bf16[4,128,1024]{2,1,0:T(8,128)(2,1)}, u32[]{:S(2)}, u32[]{:S(2)}) collective-permute-start(bf16[4,128,1024]{2,1,0:T(8,128)(2,1)S(1)} %collective-permute-done.8.refs_1_.refs_5_), channel_id=1, source_target_pairs={{2,0},{4,2},{3,1},{5,3},{10,8},{12,10},{11,9},{13,11},{18,16},{20,... | collective-permute-start | bytes 3145736 | tf_op jit(solution)/shard_map/ppermute | solution.py:234
  137.7 30.4 %collective-permute-start.10 = (bf16[1,4,128,1024]{3,2,1,0:T(8,128)(2,1)}, bf16[1,4,128,1024]{3,2,1,0:T(8,128)(2,1)}, u32[]{:S(2)}, u32[]{:S(2)}) collective-permute-start(bf16[1,4,128,1024]{3,2,1,0:T(8,128)(2,1)} %delta.2.refs_0_), channel_id=1, source_target_pairs={{6,4},{7,5},{14,12},{15,13},{22,20},{23,21},{30,28},{31,29}} | collective-permute-start | bytes 3145736 | tf_op jit(solution)/shard_map/ppermute | solution.py:234
  139.3 28.8 %collective-permute-start.9 = (bf16[1,4,128,1024]{3,2,1,0:T(8,128)(2,1)}, bf16[1,4,128,1024]{3,2,1,0:T(8,128)(2,1)}, u32[]{:S(2)}, u32[]{:S(2)}) collective-permute-start(bf16[1,4,128,1024]{3,2,1,0:T(8,128)(2,1)} %delta.2.refs_0_), channel_id=1, source_target_pairs={{0,2},{1,3},{8,10},{9,11},{16,18},{17,19},{24,26},{25,27}} | collective-permute-start | bytes 3145736 | tf_op jit(solution)/shard_map/ppermute | solution.py:234
  144.9 23.2 %copy-start.4 = (bf16[4,128,1024]{2,1,0:T(8,128)(2,1)}, bf16[4,128,1024]{2,1,0:T(8,128)(2,1)S(1)}, u32[]{:S(2)}) copy-start(bf16[4,128,1024]{2,1,0:T(8,128)(2,1)S(1)} %collective-permute-done.11.refs_0_.refs_1_) | copy-start | bytes 3145732
  144.9 49.1 %collective-permute-start.15 = (bf16[4,128,1024]{2,1,0:T(8,128)(2,1)S(1)}, bf16[4,128,1024]{2,1,0:T(8,128)(2,1)}, u32[]{:S(2)}, u32[]{:S(2)}) collective-permute-start(bf16[4,128,1024]{2,1,0:T(8,128)(2,1)S(1)} %collective-permute-done.11.refs_0_.refs_1_), channel_id=1, source_target_pairs={{4,6},{5,7},{12,14},{13,15},{20,22},{21,23},{28,30},{29,31}} | collective-permute-start | bytes 3145736 | tf_op jit(solution)/shard_map/ppermute | solution.py:234
  152.9 41.1 %collective-permute-start.16 = (bf16[4,128,1024]{2,1,0:T(8,128)(2,1)}, bf16[4,128,1024]{2,1,0:T(8,128)(2,1)}, u32[]{:S(2)}, u32[]{:S(2)}) collective-permute-start(bf16[4,128,1024]{2,1,0:T(8,128)(2,1)} %collective-permute-done.12.refs_1_.refs_4_), channel_id=1, source_target_pairs={{2,0},{3,1},{10,8},{11,9},{18,16},{19,17},{26,24},{27,25}} | collective-permute-start | bytes 3145736 | tf_op jit(solution)/shard_map/ppermute | solution.py:234
  172.8 23.4 %collective-permute-start.13 = (bf16[1,4,128,1024]{3,2,1,0:T(8,128)(2,1)}, bf16[1,4,128,1024]{3,2,1,0:T(8,128)(2,1)S(1)}, u32[]{:S(2)}, u32[]{:S(2)}) collective-permute-start(bf16[1,4,128,1024]{3,2,1,0:T(8,128)(2,1)} %get-tuple-element.29), channel_id=1, source_target_pairs={{0,2},{2,4},{1,3},{3,5},{8,10},{10,12},{9,11},{11,13},{16,18},{18,... | collective-permute-start | bytes 3145736 | tf_op jit(solution)/shard_map/ppermute | solution.py:234
  178.4 17.8 %collective-permute-start.14 = (bf16[1,4,128,1024]{3,2,1,0:T(8,128)(2,1)}, bf16[1,4,128,1024]{3,2,1,0:T(8,128)(2,1)}, u32[]{:S(2)}, u32[]{:S(2)}) collective-permute-start(bf16[1,4,128,1024]{3,2,1,0:T(8,128)(2,1)} %get-tuple-element.30), channel_id=1, source_target_pairs={{4,2},{6,4},{5,3},{7,5},{12,10},{14,12},{13,11},{15,13},{20,18},{2... | collective-permute-start | bytes 3145736 | tf_op jit(solution)/shard_map/ppermute | solution.py:234
  199.6 24.4 %collective-permute-start.17 = (bf16[1,4,128,1024]{3,2,1,0:T(8,128)(2,1)S(1)}, bf16[1,4,128,1024]{3,2,1,0:T(8,128)(2,1)S(1)}, u32[]{:S(2)}, u32[]{:S(2)}) collective-permute-start(bf16[1,4,128,1024]{3,2,1,0:T(8,128)(2,1)S(1)} %get-tuple-element.31.refs_6_.after), channel_id=1, source_target_pairs={{0,2},{2,4},{4,6},{1,3},{3,5},{5,7},{8,10},{10,12},{12,14},{9,11},... | collective-permute-start | bytes 3145736 | tf_op jit(solution)/shard_map/ppermute | solution.py:234
  206.0 20.7 %collective-permute-start.18 = (bf16[1,4,128,1024]{3,2,1,0:T(8,128)(2,1)S(1)}, bf16[1,4,128,1024]{3,2,1,0:T(8,128)(2,1)S(1)}, u32[]{:S(2)}, u32[]{:S(2)}) collective-permute-start(bf16[1,4,128,1024]{3,2,1,0:T(8,128)(2,1)S(1)} %get-tuple-element.32), channel_id=1, source_target_pairs={{2,0},{4,2},{6,4},{3,1},{5,3},{7,5},{10,8},{12,10},{14,12},{11,9},... | collective-permute-start | bytes 3145736 | tf_op jit(solution)/shard_map/ppermute | solution.py:234
  230.3 35.9 %all-to-all-start.2 = ((bf16[4,128,1024]{2,1,0:T(8,128)(2,1)}), bf16[4,128,1024]{2,1,0:T(8,128)(2,1)}, u32[]{:S(2)}, u32[]{:S(2)}) async-start(bf16[4,128,1024]{2,1,0:T(8,128)(2,1)} %sum.1), calls=%async_computation.2 | async-start | bytes 2097152 | tf_op jit(solution)/shard_map/all_to_all | solution.py:391
  242.3 52.8 %collective-permute-start.24 = (bf16[512,1024]{1,0:T(8,128)(2,1)S(1)}, bf16[512,1024]{1,0:T(8,128)(2,1)}, u32[]{:S(2)}, u32[]{:S(2)}) collective-permute-start(bf16[512,1024]{1,0:T(8,128)(2,1)S(1)} %weight.6.after), channel_id=1, source_target_pairs={{0,24},{8,16},{16,8},{24,0},{1,25},{9,17},{17,9},{25,1},{2,26},{10... | collective-permute-start | bytes 3145736 | tf_op jit(solution)/shard_map/ppermute | solution.py:230
  245.3 49.9 %collective-permute-start.23 = (bf16[512,1024]{1,0:T(8,128)(2,1)S(1)}, bf16[512,1024]{1,0:T(8,128)(2,1)}, u32[]{:S(2)}, u32[]{:S(2)}) collective-permute-start(bf16[512,1024]{1,0:T(8,128)(2,1)S(1)} %weight.5.after), channel_id=1, source_target_pairs={{0,16},{8,24},{16,0},{24,8},{1,17},{9,25},{17,1},{25,9},{2,18},{10... | collective-permute-start | bytes 3145736 | tf_op jit(solution)/shard_map/ppermute | solution.py:230
  246.9 48.3 %collective-permute-start.22 = (bf16[512,1024]{1,0:T(8,128)(2,1)S(1)}, bf16[512,1024]{1,0:T(8,128)(2,1)}, u32[]{:S(2)}, u32[]{:S(2)}) collective-permute-start(bf16[512,1024]{1,0:T(8,128)(2,1)S(1)} %weight.4.after), channel_id=1, source_target_pairs={{0,8},{8,0},{16,24},{24,16},{1,9},{9,1},{17,25},{25,17},{2,10},{10... | collective-permute-start | bytes 3145736 | tf_op jit(solution)/shard_map/ppermute | solution.py:230
  271.7 6.8 %collective-permute-start.19 = (bf16[16,4096]{1,0:T(8,128)(2,1)S(1)}, bf16[16,4096]{1,0:T(8,128)(2,1)S(1)}, u32[]{:S(2)}, u32[]{:S(2)}) collective-permute-start(bf16[16,4096]{1,0:T(8,128)(2,1)S(1)} %get-tuple-element.36), channel_id=1, source_target_pairs={{2,0},{4,2},{6,4},{3,1},{5,3},{7,5},{10,8},{12,10},{14,12},{11,9},... | collective-permute-start | bytes 393224 | tf_op jit(solution)/shard_map/ppermute | solution.py:234
  273.0 17.1 %collective-permute-start.20 = (bf16[16,4096]{1,0:T(8,128)(2,1)S(1)}, bf16[16,4096]{1,0:T(8,128)(2,1)S(1)}, u32[]{:S(2)}, u32[]{:S(2)}) collective-permute-start(bf16[16,4096]{1,0:T(8,128)(2,1)S(1)} %get-tuple-element.36), channel_id=1, source_target_pairs={{4,0},{6,2},{5,1},{7,3},{12,8},{14,10},{13,9},{15,11},{20,16},{22,... | collective-permute-start | bytes 393224 | tf_op jit(solution)/shard_map/ppermute | solution.py:234
  278.6 11.5 %collective-permute-start.21 = (bf16[16,4096]{1,0:T(8,128)(2,1)S(1)}, bf16[16,4096]{1,0:T(8,128)(2,1)S(1)}, u32[]{:S(2)}, u32[]{:S(2)}) collective-permute-start(bf16[16,4096]{1,0:T(8,128)(2,1)S(1)} %get-tuple-element.36), channel_id=1, source_target_pairs={{6,0},{7,1},{14,8},{15,9},{22,16},{23,17},{30,24},{31,25}} | collective-permute-start | bytes 393224 | tf_op jit(solution)/shard_map/ppermute | solution.py:234
  (18 other events, 111.9 us)
Sparse Core Ops, SparseCore 0:
  64.4 64.1 all-gather.2

commit v2 on v1

--- a/solution.py
+++ b/solution.py
@@ -151,16 +151,27 @@
         out[k] = refs[k][...]
 
 
-def delta_body(place, dest, grad, weights, *refs):
-    depth = weights.shape[2]
-    total = None
-    for k in range(weights.shape[0]):
-        rows = grad[:, :, :, :, k * depth : (k + 1) * depth].reshape(-1, depth)
-        term = lax.dot_general(
-            rows, weights[k], (((1,), (1,)), ((), ())), preferred_element_type=F32
-        )
-        total = term if total is None else total + term
-    refs[-1][...] = total.astype(BF16).reshape(refs[-1].shape)
+def delta_body(whole, place, dest, grad, weights, *refs):
+    depth, out = weights.shape[2], refs[-1]
+
+    def multiply():
+        total = None
+        for k in range(weights.shape[0]):
+            rows = grad[:, :, :, :, k * depth : (k + 1) * depth].reshape(-1, depth)
+            term = lax.dot_general(
+                rows, weights[k], (((1,), (1,)), ((), ())), preferred_element_type=F32
+            )
+            total = term if total is None else total + term
+        out[...] = total.astype(BF16).reshape(out.shape)
+
+    if not whole:
+        return multiply()
+    is_last = pl.program_id(0) == pl.num_programs(0) - 1
+    pl.when(jnp.logical_not(is_last))(multiply)
+
+    @pl.when(is_last)
+    def _():
+        out[...] = refs[0][...]
 
 
 def flip_body(place, grad, after, out):
@@ -172,6 +183,10 @@
     for k, source in enumerate(sources):
         lanes = source.shape[1]
         out[:, pl.ds(pl.multiple_of((place[0] ^ k) * lanes, lanes), lanes)] = source[...]
+
+
+def wait_body(*refs):
+    pass
 
 
 def add_body(dests, partial_right, partial_left, right, left, *refs):
@@ -289,25 +304,25 @@
         out_shape=[shape(rows, width), shape(rows, width), shape(ORDER, width)],
     )(rim, conv_own, query, taps, ends_coef)
     ends_far = [shift(ends, k) for k in range(1, n_ctx)]
+
+
+    local_fwd = local(False, kernel_rev, mixed)
     mine = call(
         join_body, "join", 0, 4 * part * depth * n_ctx,
         grid=(n_dp,),
         in_specs=[wide(part, feats)] * n_ctx + [ANY] * 2,
         out_specs=deep(n_ctx, part, feats),
         out_shape=shape(n_ctx, part, depth),
-    )(*mine, weights, mixed)
+    )(*mine, weights, local_fwd)
     grad = lax.all_gather(mine, ("dp", "tp"), axis=0, tiled=False)
     grad = grad.reshape(n_dp, n_tp, n_ctx, part, depth)
-
-
-    local_fwd = local(False, kernel_rev, mixed, mine)
     long_out, gated = call(
         functools.partial(long_body, n_ctx - 1), "long", 2 * rows * 128 * width, rows * width * 10,
         grid=(steps,),
-        in_specs=[wide(rows, block), wide((n_ctx - 1) * rows, block), wide(rows, block)] + [wide(ORDER, block)] * (n_ctx - 1),
+        in_specs=[wide(rows, block), wide((n_ctx - 1) * rows, block), wide(rows, block)] + [wide(ORDER, block)] * (n_ctx - 1) + [ANY],
         out_specs=[wide(rows, block), pl.BlockSpec((1, rows, block), lambda i: (i, 0, 0))],
         out_shape=[shape(rows, width), shape(n_dp, rows, quarter)],
-    )(local_fwd, carry_coef, gate, *ends_far)
+    )(local_fwd, carry_coef, gate, *ends_far, mine)
     gated_far = lax.all_to_all(gated, "dp", 0, 0, tiled=True)
     tokens = n_ctx * n_dp * rows
     last = n_ctx - 1
@@ -322,9 +337,12 @@
     first_dest = jnp.where(place[1] < n_ctx // 2, last, 0)
     chunk = (1, n_dp, rows, quarter)
 
-    def project(count, dest, *after):
+    def project(dests, *after):
+        count = dests.shape[0]
+        whole = count > 1
         return call(
-            delta_body, "delta", 2 * count * n_dp * rows * depth * quarter,
+            functools.partial(delta_body, whole), "delta",
+            2 * max(count - 1, 1) * n_dp * rows * depth * quarter,
             2 * tokens * depth + 2 * depth * quarter + 2 * count * n_dp * rows * quarter,
             grid_spec=pltpu.PrefetchScalarGridSpec(
                 num_scalar_prefetch=2, grid=(count,),
@@ -333,14 +351,18 @@
                         (n_dp, n_tp, 1, part, depth), lambda i, p, q: (0, 0, p[1] ^ q[i], 0, 0)
                     ),
                     pl.BlockSpec((n_dp, quarter, feats), lambda i, p, q: (0, 0, 0)),
-                ] + [ANY] * len(after),
-                out_specs=pl.BlockSpec(chunk, lambda i, p, q: (i, 0, 0, 0)),
+                ] + ([pl.BlockSpec(chunk, lambda i, p, q: (0, 0, 0, 0))] if whole
+                     else [ANY] * len(after)),
+                out_specs=pl.BlockSpec(
+                    chunk, lambda i, p, q: (q[i] if whole else 0, 0, 0, 0)
+                ),
             ),
             out_shape=shape(count, n_dp, rows, quarter),
-        )(place, dest, grad, weights, *after)
-
-    first = project(1, first_dest[None], from_left[0], from_right[0])
-    partial = project(n_ctx, jnp.arange(n_ctx, dtype=jnp.int32), first)
+        )(place, dests, grad, weights, *after)
+
+    first = project(first_dest[None], from_left[0], from_right[0])
+    others = (first_dest + 1 + jnp.arange(n_ctx, dtype=jnp.int32)) % n_ctx
+    partial = project(others.astype(jnp.int32), first)
     grad_t = call(
         flip_body, "flip", 0, 4 * tokens * depth,
         grid_spec=pltpu.PrefetchScalarGridSpec(
@@ -397,9 +419,9 @@
         out_specs=pl.BlockSpec((n_ctx, 1, rows, quarter), lambda i: (0, i, 0, 0)),
         out_shape=shape(n_ctx, n_dp, rows, quarter),
     )(gated_far, *from_left, *from_right[::-1], token).reshape(tokens, quarter)
-    weight_far = []
-    for k in list(range(1, n_dp)) + [0]:
-        token = call(
+    pieces = {}
+    for k in list(range(n_dp - 1, -1, -1)):
+        token = pieces[k] = call(
             weight_body, "weight", 2 * tokens * feats * quarter, 2 * tokens * (feats + quarter),
             grid_spec=pltpu.PrefetchScalarGridSpec(
                 num_scalar_prefetch=1, grid=(2,),
@@ -412,7 +434,18 @@
             ),
             out_shape=shape(feats, quarter),
         )(place, grad_t, gated_all, token)
-        weight_far.append(swap(token, "dp", k) if k else token)
+
+    def hold(value, after):
+        return call(
+            wait_body, "hold", 0, 0,
+            in_specs=[ANY] * 2, out_specs=ANY,
+            out_shape=shape(*value.shape), input_output_aliases={0: 0},
+        )(value, after)
+
+    weight_far = [pieces[0]] + [
+        swap(pieces[k] if k == n_dp - 1 else hold(pieces[k], delta_far), "dp", k)
+        for k in range(1, n_dp)
+    ]
 
     seed, starts, gate_grad = call(
         seed_body, "seed", 2 * rows * 128 * width, rows * width * 10,
@@ -444,7 +477,7 @@
             out_specs=pl.BlockSpec((cut, width), lambda i, p: (i, 0)),
         ),
         out_shape=shape(feats, width),
-    )(place, weight_far[-1], *weight_far[:-1], query_grad)
+    )(place, *weight_far, query_grad)
     return query_grad, conv_grad, gate_grad, weight_grad
 
 

time: 312 us -> 306 us (0.981); the launches traced: 307 us -> 305 us
  waiting for transfers between devices: 72.1 us -> 66 us
  starting transfers between devices: 73.8 us -> 77.9 us
    all_to_all x1, waiting for transfers between devices: 19.3 us -> 0.01 us  [on_device(): delta_far = lax.all_to_all(delta, 'dp', 0, 0, tiled=True)]
    ppermute x19, waiting for transfers between devices: 40.1 us -> 59 us  [shift(): return lax.ppermute(value, 'ctx', ends)]
    ppermute x6, waiting for transfers between devices: 10.1 us -> 4.37 us  [swap(): lax.ppermute(value, axis, [(i, i ^ k) for i in range(lax.axis_size(axis))])]
    ppermute x6, starting transfers between devices: 8.92 us -> 13.2 us  [swap(): lax.ppermute(value, axis, [(i, i ^ k) for i in range(lax.axis_size(axis))])]
    pallas_call x2 -> x4, Pallas kernels: 20.6 us -> 18.8 us  [the longest x2 18.8 us: project(): call(functools.partial(delta_body, whole), 'delta', 2 * max(count - 1, 1)...]
  transfers between devices with their start and end apart: 28 -> 28, of which waited for: 11 -> 13; matrix products, arithmetic and copies ran while one was open for 3% -> 3% of each run, Pallas kernels for 32% -> 32%
where the time goes in v2:
time: 306 us; the launch traced here: 305 us
  Pallas kernels  111 us (36%)
  starting transfers between devices  77.9 us (25%)
  waiting for transfers between devices  66 us (22%)
  blocking collectives  18.8 us (6%)
  between operations  14.5 us (5%)
  other arithmetic  8.53 us (3%)
  local copies, waits for them, and re-layouts  7.55 us (2%)
    ppermute x19, waiting for transfers between devices, shift(): return lax.ppermute(value, 'ctx', ends)  59 us
    ppermute x19, starting transfers between devices, shift(): return lax.ppermute(value, 'ctx', ends)  52.9 us
    pallas_call x4, Pallas kernels, on_device(): call(weight_body, 'weight', 2 * tokens * feats * quarter, 2 * tokens * (f...  22.2 us
    pallas_call x2, Pallas kernels, project(): call(functools.partial(delta_body, whole), 'delta', 2 * max(count - 1, 1)...  18.8 us
    all_to_all x1, blocking collectives, on_device(): gated_far = lax.all_to_all(gated, 'dp', 0, 0, tiled=True)  18.8 us
    pallas_call x1, Pallas kernels, on_device(): call(flip_body, 'flip', 0, 4 * tokens * depth, grid_spec=pltpu.PrefetchSc...  13.8 us
    ppermute x6, starting transfers between devices, swap(): lax.ppermute(value, axis, [(i, i ^ k) for i in range(lax.axis_size(axis))])  13.2 us
    pallas_call x3, Pallas kernels, local(): call(functools.partial(local_body, transposed), 'local_t' if transposed e...  11.2 us
  transfers between devices with their start and end apart: 28, of which 13 were waited for; matrix products, arithmetic and copies ran while one was open for 3% of the time, Pallas kernels for 32%

profile of v2, /device:TPU:0, one launch (start us, length us, event | category | flops | bytes accessed | tf_op | source)
XLA Modules:
  0.0 304.5 jit_solution(2694584952938276194)
XLA Ops:
  7.2 5.2 %all-to-all-start = ((bf16[4,1024,512]{2,1,0:T(8,128)(2,1)}), bf16[4,1024,512]{2,1,0:T(8,128)(2,1)}, u32[]{:S(2)}, u32[]{:S(2)}) async-start(bf16[4,1024,512]{2,1,0:T(8,128)(2,1)} %bitcast.20), calls=%async_computation | async-start | bytes 8388608 | tf_op jit(solution)/shard_map/all_to_all | solution.py:254
  14.3 5.7 %collective-permute-start.3 = (bf16[128,4096]{1,0:T(8,128)(2,1)S(1)}, bf16[128,4096]{1,0:T(8,128)(2,1)}, u32[]{:S(2)}, u32[]{:S(2)}) collective-permute-start(bf16[128,4096]{1,0:T(8,128)(2,1)S(1)} %multiply_convert_fusion.2.x), channel_id=1, source_target_pairs={{0,2},{2,4},{4,6},{1,3},{3,5},{5,7},{8,10},{10,12},{12,14},{9,11},... | collective-permute-start | bytes 3145736 | tf_op jit(solution)/shard_map/ppermute | solution.py:249
  34.1 4.2 %local.2.own_part = f32[128,4096]{1,0:T(8,128)} custom-call(f32[256,128]{1,0:T(8,128)S(1)} %pad_maximum_fusion.1.rows.taps, bf16[128,4096]{1,0:T(8,128)(2,1)S(1)} %multiply_convert_fusion.2.x, bf16[4096,128]{1,0:T(8,128)(2,1)S(1)} %get-tuple-element.43.refs_0_.ends_coef, bf16[4096,128]{1,0:T(8,128)(2,1)S(1)} %get-tuple-element.42.refs_1_.starts_coef, ...), custom_call_target="tpu_custom_call" | custom-call | flops 1073741824 | bytes 3145728 | tf_op jit(solution)/shard_map/local/pallas_call | solution.py:286
  38.3 4.2 %collective-permute-done.3.rim = bf16[128,4096]{1,0:T(8,128)(2,1)} collective-permute-done((bf16[128,4096]{1,0:T(8,128)(2,1)S(1)}, bf16[128,4096]{1,0:T(8,128)(2,1)}, u32[]{:S(2)}, u32[]{:S(2)}) %collective-permute-start.3) | collective-permute-done | bytes 1048608 | tf_op jit(solution)/shard_map/ppermute | solution.py:249
  42.5 5.7 %conv.1 = (bf16[128,4096]{1,0:T(8,128)(2,1)S(1)}, bf16[128,4096]{1,0:T(8,128)(2,1)S(1)}, bf16[16,4096]{1,0:T(8,128)(2,1)S(1)}) custom-call(bf16[128,4096]{1,0:T(8,128)(2,1)} %collective-permute-done.3.rim, f32[128,4096]{1,0:T(8,128)} %local.2.own_part, bf16[128,4096]{1,0:T(8,128)(2,1)} %query.3, f32[256,128]{1,0:T(8,128)S(1)} %pad_maximum_fusion.1.rows.taps, ...), custom_call_target="tpu_custom_call" | custom-call | flops 1073741824 | bytes 7340032 | tf_op jit(solution)/shard_map/conv/pallas_call | solution.py:299
  54.0 4.4 %collective-permute-done.2.refs_3_ = bf16[64,2048]{1,0:T(8,128)(2,1)S(1)} collective-permute-done((bf16[64,2048]{1,0:T(8,128)(2,1)}, bf16[64,2048]{1,0:T(8,128)(2,1)S(1)}, u32[]{:S(2)}, u32[]{:S(2)}) %collective-permute-start.2) | collective-permute-done | bytes 262176 | tf_op jit(solution)/shard_map/ppermute | solution.py:245
  62.6 6.5 %collective-permute-start.4 = (bf16[16,4096]{1,0:T(8,128)(2,1)S(1)}, bf16[16,4096]{1,0:T(8,128)(2,1)S(1)}, u32[]{:S(2)}, u32[]{:S(2)}) collective-permute-start(bf16[16,4096]{1,0:T(8,128)(2,1)S(1)} %get-tuple-element.27), channel_id=1, source_target_pairs={{0,2},{2,4},{4,6},{1,3},{3,5},{5,7},{8,10},{10,12},{12,14},{9,11},... | collective-permute-start | bytes 393224 | tf_op jit(solution)/shard_map/ppermute | solution.py:249
  77.6 4.0 %long.1 = (bf16[128,4096]{1,0:T(8,128)(2,1)S(1)}, bf16[4,128,1024]{2,1,0:T(8,128)(2,1)S(1)}) custom-call(f32[128,4096]{1,0:T(8,128)} %copy-done.3, bf16[384,4096]{1,0:T(8,128)(2,1)} %get-tuple-element.41.refs_2_.coef, bf16[128,4096]{1,0:T(8,128)(2,1)S(1)} %copy-done.11, bf16[16,4096]{1,0:T(8,128)(2,1)S(1)} %collective-permute-done.4.refs_0_, ...), custom_call_target="tpu_custom_call" | custom-call | flops 134217728 | bytes 5242880 | tf_op jit(solution)/shard_map/long/pallas_call | solution.py:319
  81.6 18.8 %all_to_all.15.own = bf16[4,128,1024]{2,1,0:T(8,128)(2,1)S(1)} all-to-all(bf16[4,128,1024]{2,1,0:T(8,128)(2,1)S(1)} %get-tuple-element.28), channel_id=1, replica_groups=mesh['dp'=4,'ctx'=4,'tp'=2] {'dp'}, dimensions={0} | all-to-all | bytes 2097152 | tf_op jit(solution)/shard_map/all_to_all | solution.py:326
  106.1 17.7 %collective-permute-done.7.refs_0_ = bf16[4,128,1024]{2,1,0:T(8,128)(2,1)S(1)} collective-permute-done((bf16[4,128,1024]{2,1,0:T(8,128)(2,1)S(1)}, bf16[4,128,1024]{2,1,0:T(8,128)(2,1)S(1)}, u32[]{:S(2)}, u32[]{:S(2)}) %collective-permute-start.7) | collective-permute-done | bytes 1048608 | tf_op jit(solution)/shard_map/ppermute | solution.py:249
  129.3 6.7 %delta.2.refs_0_ = bf16[1,4,128,1024]{3,2,1,0:T(8,128)(2,1)} custom-call(s32[3]{0:T(128)S(1)} %pad_add_fusion.place, s32[1]{0:T(128)} %bitcast.5.dest, bf16[4,2,4,64,2048]{4,3,2,1,0:T(8,128)(2,1)} %bitcast.17, bf16[4,1024,512]{2,1,0:T(8,128)(2,1)} %all-to-all-done.refs_4_.weights, bf16[4,128,1024]{2,1,0:T(8,128)(2,1)S(1)} %collective-permute-done.7.refs_0_, ...), custom_call_target="tpu_custom_call" | custom-call | flops 2147483648 | bytes 13631488 | tf_op jit(solution)/shard_map/delta/pallas_call | solution.py:343
  137.7 5.5 %collective-permute-start.9 = (bf16[1,4,128,1024]{3,2,1,0:T(8,128)(2,1)}, bf16[1,4,128,1024]{3,2,1,0:T(8,128)(2,1)}, u32[]{:S(2)}, u32[]{:S(2)}) collective-permute-start(bf16[1,4,128,1024]{3,2,1,0:T(8,128)(2,1)} %delta.2.refs_0_), channel_id=1, source_target_pairs={{0,2},{1,3},{8,10},{9,11},{16,18},{17,19},{24,26},{25,27}} | collective-permute-start | bytes 3145736 | tf_op jit(solution)/shard_map/ppermute | solution.py:249
  144.9 6.5 %collective-permute-done.12.refs_1_.refs_4_ = bf16[4,128,1024]{2,1,0:T(8,128)(2,1)} collective-permute-done((bf16[4,128,1024]{2,1,0:T(8,128)(2,1)S(1)}, bf16[4,128,1024]{2,1,0:T(8,128)(2,1)}, u32[]{:S(2)}, u32[]{:S(2)}) %collective-permute-start.12) | collective-permute-done | bytes 1048608 | tf_op jit(solution)/shard_map/ppermute | solution.py:249
  152.7 12.1 %delta.3.partial_right.partial_left.after.partial = bf16[4,4,128,1024]{3,2,1,0:T(8,128)(2,1)} custom-call(s32[3]{0:T(128)S(1)} %pad_add_fusion.place, s32[4]{0:T(128)S(1)} %and_select_fusion.dest, bf16[4,2,4,64,2048]{4,3,2,1,0:T(8,128)(2,1)} %bitcast.18, bf16[4,1024,512]{2,1,0:T(8,128)(2,1)} %all-to-all-done.refs_4_.weights, ...), custom_call_target="tpu_custom_call" | custom-call | flops 6442450944 | bytes 16777216 | tf_op jit(solution)/shard_map/delta/pallas_call | solution.py:343
  164.8 4.7 %add.89 = (bf16[1,4,128,1024]{3,2,1,0:T(8,128)(2,1)}, bf16[1,4,128,1024]{3,2,1,0:T(8,128)(2,1)}) custom-call(s32[2]{0:T(128)S(1)} %add_clamp_fusion.1.dests, bf16[4,4,128,1024]{3,2,1,0:T(8,128)(2,1)} %delta.3.partial_right.partial_left.after.partial, bf16[4,4,128,1024]{3,2,1,0:T(8,128)(2,1)} %delta.3.partial_right.partial_left.after.partial, ...), custom_call_target="tpu_custom_call" | custom-call | bytes 6291456 | tf_op jit(solution)/shard_map/add/pallas_call | solution.py:392
  169.5 6.6 %collective-permute-start.13 = (bf16[1,4,128,1024]{3,2,1,0:T(8,128)(2,1)}, bf16[1,4,128,1024]{3,2,1,0:T(8,128)(2,1)}, u32[]{:S(2)}, u32[]{:S(2)}) collective-permute-start(bf16[1,4,128,1024]{3,2,1,0:T(8,128)(2,1)} %get-tuple-element.29), channel_id=1, source_target_pairs={{0,2},{2,4},{1,3},{3,5},{8,10},{10,12},{9,11},{11,13},{16,18},{18,... | collective-permute-start | bytes 3145736 | tf_op jit(solution)/shard_map/ppermute | solution.py:249
  177.1 13.8 %flip.1.refs_2_.grad_t = bf16[2048,2048]{1,0:T(8,128)(2,1)} custom-call(s32[3]{0:T(128)S(1)} %pad_add_fusion.place, bf16[4,2,4,64,2048]{4,3,2,1,0:T(8,128)(2,1)} %bitcast.19, bf16[4,4,128,1024]{3,2,1,0:T(8,128)(2,1)} %delta.3.partial_right.partial_left.after.partial), custom_call_target="tpu_custom_call" | custom-call | bytes 16777216 | tf_op jit(solution)/shard_map/flip/pallas_call | solution.py:366
  194.0 4.5 %add.90 = (bf16[1,4,128,1024]{3,2,1,0:T(8,128)(2,1)}, bf16[1,4,128,1024]{3,2,1,0:T(8,128)(2,1)S(1)}) custom-call(s32[2]{0:T(128)S(1)} %add_clamp_fusion.dests, bf16[4,4,128,1024]{3,2,1,0:T(8,128)(2,1)} %delta.3.partial_right.partial_left.after.partial, bf16[4,4,128,1024]{3,2,1,0:T(8,128)(2,1)} %delta.3.partial_right.partial_left.after.partial, ...), custom_call_target="tpu_custom_call" | custom-call | bytes 6291456 | tf_op jit(solution)/shard_map/add/pallas_call | solution.py:392
  198.6 6.3 %collective-permute-start.17 = (bf16[1,4,128,1024]{3,2,1,0:T(8,128)(2,1)}, bf16[1,4,128,1024]{3,2,1,0:T(8,128)(2,1)S(1)}, u32[]{:S(2)}, u32[]{:S(2)}) collective-permute-start(bf16[1,4,128,1024]{3,2,1,0:T(8,128)(2,1)} %get-tuple-element.31.refs_6_.after), channel_id=1, source_target_pairs={{0,2},{2,4},{4,6},{1,3},{3,5},{5,7},{8,10},{10,12},{12,14},{9,11},... | collective-permute-start | bytes 3145736 | tf_op jit(solution)/shard_map/ppermute | solution.py:249
  206.1 4.8 %merge.1 = bf16[4,4,128,1024]{3,2,1,0:T(8,128)(2,1)} custom-call(bf16[4,128,1024]{2,1,0:T(8,128)(2,1)S(1)} %copy-done.10, bf16[4,128,1024]{2,1,0:T(8,128)(2,1)S(1)} %collective-permute-done.7.refs_0_, bf16[4,128,1024]{2,1,0:T(8,128)(2,1)S(1)} %copy-done.6, bf16[4,128,1024]{2,1,0:T(8,128)(2,1)} %collective-permute-done.15.refs_0_.refs_2_, ...), custom_call_target="tpu_custom_call" | custom-call | bytes 11534336 | tf_op jit(solution)/shard_map/merge/pallas_call | solution.py:415
  210.9 11.0 %collective-permute-done.17.right = bf16[1,4,128,1024]{3,2,1,0:T(8,128)(2,1)S(1)} collective-permute-done((bf16[1,4,128,1024]{3,2,1,0:T(8,128)(2,1)}, bf16[1,4,128,1024]{3,2,1,0:T(8,128)(2,1)S(1)}, u32[]{:S(2)}, u32[]{:S(2)}) %collective-permute-start.17) | collective-permute-done | bytes 1048608 | tf_op jit(solution)/shard_map/ppermute | solution.py:249
  221.9 3.9 %collective-permute-done.18.left = bf16[1,4,128,1024]{3,2,1,0:T(8,128)(2,1)S(1)} collective-permute-done((bf16[1,4,128,1024]{3,2,1,0:T(8,128)(2,1)S(1)}, bf16[1,4,128,1024]{3,2,1,0:T(8,128)(2,1)S(1)}, u32[]{:S(2)}, u32[]{:S(2)}) %collective-permute-start.18) | collective-permute-done | bytes 1048608 | tf_op jit(solution)/shard_map/ppermute | solution.py:249
  229.3 6.6 %all-to-all-start.2 = ((bf16[4,128,1024]{2,1,0:T(8,128)(2,1)}), bf16[4,128,1024]{2,1,0:T(8,128)(2,1)S(1)}, u32[]{:S(2)}, u32[]{:S(2)}) async-start(bf16[4,128,1024]{2,1,0:T(8,128)(2,1)} %sum.1), calls=%async_computation.2 | async-start | bytes 2097152 | tf_op jit(solution)/shard_map/all_to_all | solution.py:413
  235.9 6.1 %weight.4.after = bf16[512,1024]{1,0:T(8,128)(2,1)} custom-call(s32[3]{0:T(128)S(1)} %pad_add_fusion.place, bf16[2048,2048]{1,0:T(8,128)(2,1)} %flip.1.refs_2_.grad_t, bf16[2048,1024]{1,0:T(8,128)(2,1)} %bitcast.13, bf16[1,4,128,1024]{3,2,1,0:T(8,128)(2,1)} %get-tuple-element.31.refs_6_.after), custom_call_target="tpu_custom_call" | custom-call | flops 2147483648 | bytes 6291456 | tf_op jit(solution)/shard_map/weight/pallas_call | solution.py:424
  245.0 5.4 %weight.5.after.refs_0_ = bf16[512,1024]{1,0:T(8,128)(2,1)S(1)} custom-call(s32[3]{0:T(128)S(1)} %pad_add_fusion.place, bf16[2048,2048]{1,0:T(8,128)(2,1)} %flip.1.refs_2_.grad_t, bf16[2048,1024]{1,0:T(8,128)(2,1)} %bitcast.14, bf16[512,1024]{1,0:T(8,128)(2,1)} %weight.4.after), custom_call_target="tpu_custom_call" | custom-call | flops 2147483648 | bytes 6291456 | tf_op jit(solution)/shard_map/weight/pallas_call | solution.py:424
  250.3 5.4 %weight.6.after.refs_0_ = bf16[512,1024]{1,0:T(8,128)(2,1)S(1)} custom-call(s32[3]{0:T(128)S(1)} %pad_add_fusion.place, bf16[2048,2048]{1,0:T(8,128)(2,1)} %flip.1.refs_2_.grad_t, bf16[2048,1024]{1,0:T(8,128)(2,1)} %bitcast.15, bf16[512,1024]{1,0:T(8,128)(2,1)S(1)} %weight.5.after.refs_0_), custom_call_target="tpu_custom_call" | custom-call | flops 2147483648 | bytes 6291456 | tf_op jit(solution)/shard_map/weight/pallas_call | solution.py:424
  255.7 5.4 %weight.7.refs_0_ = bf16[512,1024]{1,0:T(8,128)(2,1)S(1)} custom-call(s32[3]{0:T(128)S(1)} %pad_add_fusion.place, bf16[2048,2048]{1,0:T(8,128)(2,1)} %flip.1.refs_2_.grad_t, bf16[2048,1024]{1,0:T(8,128)(2,1)} %bitcast.16, bf16[512,1024]{1,0:T(8,128)(2,1)S(1)} %weight.6.after.refs_0_), custom_call_target="tpu_custom_call" | custom-call | flops 2147483648 | bytes 6291456 | tf_op jit(solution)/shard_map/weight/pallas_call | solution.py:424
  262.9 5.1 %collective-permute-start.22 = (bf16[512,1024]{1,0:T(8,128)(2,1)S(1)}, bf16[512,1024]{1,0:T(8,128)(2,1)S(1)}, u32[]{:S(2)}, u32[]{:S(2)}) collective-permute-start(bf16[512,1024]{1,0:T(8,128)(2,1)S(1)} %hold.2), channel_id=1, source_target_pairs={{0,8},{8,0},{16,24},{24,16},{1,9},{9,1},{17,25},{25,17},{2,10},{10... | collective-permute-start | bytes 3145736 | tf_op jit(solution)/shard_map/ppermute | solution.py:245
  268.0 4.4 %seed.1 = (bf16[128,4096]{1,0:T(8,128)(2,1)S(1)}, bf16[16,4096]{1,0:T(8,128)(2,1)S(1)}, bf16[128,4096]{1,0:T(8,128)(2,1)}) custom-call(bf16[4,128,1024]{2,1,0:T(8,128)(2,1)S(1)} %all-to-all-done.2.delta.refs_1_, bf16[128,4096]{1,0:T(8,128)(2,1)S(1)} %copy-done.12, bf16[128,4096]{1,0:T(8,128)(2,1)} %copy-done.15, bf16[4096,128]{1,0:T(8,128)(2,1)} %copy-done.1), custom_call_target="tpu_custom_call" | custom-call | flops 134217728 | bytes 5242880 | tf_op jit(solution)/shard_map/seed/pallas_call | solution.py:450
  275.0 4.3 %collective-permute-done.19.refs_0_ = bf16[16,4096]{1,0:T(8,128)(2,1)S(1)} collective-permute-done((bf16[16,4096]{1,0:T(8,128)(2,1)S(1)}, bf16[16,4096]{1,0:T(8,128)(2,1)S(1)}, u32[]{:S(2)}, u32[]{:S(2)}) %collective-permute-start.19) | collective-permute-done | bytes 131104 | tf_op jit(solution)/shard_map/ppermute | solution.py:249
  287.9 5.2 %back.1 = (bf16[128,4096]{1,0:T(8,128)(2,1)}, bf16[128,4096]{1,0:T(8,128)(2,1)}) custom-call(f32[128,4096]{1,0:T(8,128)} %copy-done.14, bf16[384,4096]{1,0:T(8,128)(2,1)} %get-tuple-element.40.refs_3_.coef, bf16[128,4096]{1,0:T(8,128)(2,1)S(1)} %copy-done.17, bf16[128,4096]{1,0:T(8,128)(2,1)S(1)} %copy-done.13, ...), custom_call_target="tpu_custom_call" | custom-call | flops 134217728 | bytes 6291456 | tf_op jit(solution)/shard_map/back/pallas_call | solution.py:462
  293.1 4.5 %lay.1 = bf16[512,4096]{1,0:T(8,128)(2,1)} custom-call(s32[3]{0:T(128)S(1)} %pad_add_fusion.place, bf16[512,1024]{1,0:T(8,128)(2,1)S(1)} %copy-done.8, bf16[512,1024]{1,0:T(8,128)(2,1)S(1)} %collective-permute-done.22.refs_1_, bf16[512,1024]{1,0:T(8,128)(2,1)S(1)} %collective-permute-done.23.refs_2_, bf16[512,1024]{1,0:T(8,128)(2,1)} %collective-permute-done.24.refs_3_, ...), custom_call_target="tpu_custom_call" | custom-call | bytes 8388608 | tf_op jit(solution)/shard_map/lay/pallas_call | solution.py:472
  (115 shorter events, 75.0 us)
Async XLA Ops:
  7.2 53.8 %all-to-all-start = ((bf16[4,1024,512]{2,1,0:T(8,128)(2,1)}), bf16[4,1024,512]{2,1,0:T(8,128)(2,1)}, u32[]{:S(2)}, u32[]{:S(2)}) async-start(bf16[4,1024,512]{2,1,0:T(8,128)(2,1)} %bitcast.20), calls=%async_computation | async-start | bytes 8388608 | tf_op jit(solution)/shard_map/all_to_all | solution.py:254
  12.3 117.0 %all-gather.3.cloned.1.call-start = ((), (), s32[]{:S(2)}) async-start(), calls=%async_computation.3 | async-start | bytes 9437184 | tf_op jit(solution)/shard_map/all_gather | solution.py:317
  14.3 28.2 %collective-permute-start.3 = (bf16[128,4096]{1,0:T(8,128)(2,1)S(1)}, bf16[128,4096]{1,0:T(8,128)(2,1)}, u32[]{:S(2)}, u32[]{:S(2)}) collective-permute-start(bf16[128,4096]{1,0:T(8,128)(2,1)S(1)} %multiply_convert_fusion.2.x), channel_id=1, source_target_pairs={{0,2},{2,4},{4,6},{1,3},{3,5},{5,7},{8,10},{10,12},{12,14},{9,11},... | collective-permute-start | bytes 3145736 | tf_op jit(solution)/shard_map/ppermute | solution.py:249
  22.3 31.7 %collective-permute-start = (bf16[64,2048]{1,0:T(8,128)(2,1)}, bf16[64,2048]{1,0:T(8,128)(2,1)S(1)}, u32[]{:S(2)}, u32[]{:S(2)}) collective-permute-start(bf16[64,2048]{1,0:T(8,128)(2,1)} %get-tuple-element.23), channel_id=1, source_target_pairs={{0,2},{2,0},{4,6},{6,4},{1,3},{3,1},{5,7},{7,5},{8,10},{10,8},{12,... | collective-permute-start | bytes 786440 | tf_op jit(solution)/shard_map/ppermute | solution.py:245
  22.9 31.1 %collective-permute-start.1 = (bf16[64,2048]{1,0:T(8,128)(2,1)}, bf16[64,2048]{1,0:T(8,128)(2,1)S(1)}, u32[]{:S(2)}, u32[]{:S(2)}) collective-permute-start(bf16[64,2048]{1,0:T(8,128)(2,1)} %get-tuple-element.24), channel_id=1, source_target_pairs={{0,4},{2,6},{4,0},{6,2},{1,5},{3,7},{5,1},{7,3},{8,12},{10,14},{12... | collective-permute-start | bytes 786440 | tf_op jit(solution)/shard_map/ppermute | solution.py:245
  23.9 34.5 %collective-permute-start.2 = (bf16[64,2048]{1,0:T(8,128)(2,1)}, bf16[64,2048]{1,0:T(8,128)(2,1)S(1)}, u32[]{:S(2)}, u32[]{:S(2)}) collective-permute-start(bf16[64,2048]{1,0:T(8,128)(2,1)} %get-tuple-element.25), channel_id=1, source_target_pairs={{0,6},{2,4},{4,2},{6,0},{1,7},{3,5},{5,3},{7,1},{8,14},{10,12},{12... | collective-permute-start | bytes 786440 | tf_op jit(solution)/shard_map/ppermute | solution.py:245
  62.6 11.6 %collective-permute-start.4 = (bf16[16,4096]{1,0:T(8,128)(2,1)S(1)}, bf16[16,4096]{1,0:T(8,128)(2,1)S(1)}, u32[]{:S(2)}, u32[]{:S(2)}) collective-permute-start(bf16[16,4096]{1,0:T(8,128)(2,1)S(1)} %get-tuple-element.27), channel_id=1, source_target_pairs={{0,2},{2,4},{4,6},{1,3},{3,5},{5,7},{8,10},{10,12},{12,14},{9,11},... | collective-permute-start | bytes 393224 | tf_op jit(solution)/shard_map/ppermute | solution.py:249
  69.1 7.1 %collective-permute-start.5 = (bf16[16,4096]{1,0:T(8,128)(2,1)S(1)}, bf16[16,4096]{1,0:T(8,128)(2,1)S(1)}, u32[]{:S(2)}, u32[]{:S(2)}) collective-permute-start(bf16[16,4096]{1,0:T(8,128)(2,1)S(1)} %get-tuple-element.27), channel_id=1, source_target_pairs={{0,4},{2,6},{1,5},{3,7},{8,12},{10,14},{9,13},{11,15},{16,20},{18,... | collective-permute-start | bytes 393224 | tf_op jit(solution)/shard_map/ppermute | solution.py:249
  72.9 4.7 %collective-permute-start.6 = (bf16[16,4096]{1,0:T(8,128)(2,1)S(1)}, bf16[16,4096]{1,0:T(8,128)(2,1)S(1)}, u32[]{:S(2)}, u32[]{:S(2)}) collective-permute-start(bf16[16,4096]{1,0:T(8,128)(2,1)S(1)} %get-tuple-element.27), channel_id=1, source_target_pairs={{0,6},{1,7},{8,14},{9,15},{16,22},{17,23},{24,30},{25,31}} | collective-permute-start | bytes 393224 | tf_op jit(solution)/shard_map/ppermute | solution.py:249
  81.6 18.8 %copy-start.15 = (bf16[128,4096]{1,0:T(8,128)(2,1)}, bf16[128,4096]{1,0:T(8,128)(2,1)S(1)}, u32[]{:S(2)}) copy-start(bf16[128,4096]{1,0:T(8,128)(2,1)S(1)} %get-tuple-element.33.long_out) | copy-start | bytes 3145732
  100.4 23.4 %collective-permute-start.7 = (bf16[4,128,1024]{2,1,0:T(8,128)(2,1)S(1)}, bf16[4,128,1024]{2,1,0:T(8,128)(2,1)S(1)}, u32[]{:S(2)}, u32[]{:S(2)}) collective-permute-start(bf16[4,128,1024]{2,1,0:T(8,128)(2,1)S(1)} %all_to_all.15.own), channel_id=1, source_target_pairs={{0,2},{2,4},{4,6},{1,3},{3,5},{5,7},{8,10},{10,12},{12,14},{9,11},... | collective-permute-start | bytes 3145736 | tf_op jit(solution)/shard_map/ppermute | solution.py:249
  103.9 24.1 %collective-permute-start.8 = (bf16[4,128,1024]{2,1,0:T(8,128)(2,1)S(1)}, bf16[4,128,1024]{2,1,0:T(8,128)(2,1)S(1)}, u32[]{:S(2)}, u32[]{:S(2)}) collective-permute-start(bf16[4,128,1024]{2,1,0:T(8,128)(2,1)S(1)} %all_to_all.15.own), channel_id=1, source_target_pairs={{2,0},{4,2},{6,4},{3,1},{5,3},{7,5},{10,8},{12,10},{14,12},{11,9},... | collective-permute-start | bytes 3145736 | tf_op jit(solution)/shard_map/ppermute | solution.py:249
  123.8 19.5 %collective-permute-start.11 = (bf16[4,128,1024]{2,1,0:T(8,128)(2,1)S(1)}, bf16[4,128,1024]{2,1,0:T(8,128)(2,1)S(1)}, u32[]{:S(2)}, u32[]{:S(2)}) collective-permute-start(bf16[4,128,1024]{2,1,0:T(8,128)(2,1)S(1)} %collective-permute-done.7.refs_0_), channel_id=1, source_target_pairs={{2,4},{4,6},{3,5},{5,7},{10,12},{12,14},{11,13},{13,15},{18,20},{2... | collective-permute-start | bytes 3145736 | tf_op jit(solution)/shard_map/ppermute | solution.py:249
  128.0 23.4 %collective-permute-start.12 = (bf16[4,128,1024]{2,1,0:T(8,128)(2,1)S(1)}, bf16[4,128,1024]{2,1,0:T(8,128)(2,1)}, u32[]{:S(2)}, u32[]{:S(2)}) collective-permute-start(bf16[4,128,1024]{2,1,0:T(8,128)(2,1)S(1)} %collective-permute-done.8.refs_1_.refs_5_), channel_id=1, source_target_pairs={{2,0},{4,2},{3,1},{5,3},{10,8},{12,10},{11,9},{13,11},{18,16},{20,... | collective-permute-start | bytes 3145736 | tf_op jit(solution)/shard_map/ppermute | solution.py:249
  136.0 28.8 %collective-permute-start.10 = (bf16[1,4,128,1024]{3,2,1,0:T(8,128)(2,1)}, bf16[1,4,128,1024]{3,2,1,0:T(8,128)(2,1)}, u32[]{:S(2)}, u32[]{:S(2)}) collective-permute-start(bf16[1,4,128,1024]{3,2,1,0:T(8,128)(2,1)} %delta.2.refs_0_), channel_id=1, source_target_pairs={{6,4},{7,5},{14,12},{15,13},{22,20},{23,21},{30,28},{31,29}} | collective-permute-start | bytes 3145736 | tf_op jit(solution)/shard_map/ppermute | solution.py:249
  137.7 27.2 %collective-permute-start.9 = (bf16[1,4,128,1024]{3,2,1,0:T(8,128)(2,1)}, bf16[1,4,128,1024]{3,2,1,0:T(8,128)(2,1)}, u32[]{:S(2)}, u32[]{:S(2)}) collective-permute-start(bf16[1,4,128,1024]{3,2,1,0:T(8,128)(2,1)} %delta.2.refs_0_), channel_id=1, source_target_pairs={{0,2},{1,3},{8,10},{9,11},{16,18},{17,19},{24,26},{25,27}} | collective-permute-start | bytes 3145736 | tf_op jit(solution)/shard_map/ppermute | solution.py:249
  143.3 21.5 %copy-start.5 = (bf16[4,128,1024]{2,1,0:T(8,128)(2,1)}, bf16[4,128,1024]{2,1,0:T(8,128)(2,1)S(1)}, u32[]{:S(2)}) copy-start(bf16[4,128,1024]{2,1,0:T(8,128)(2,1)S(1)} %collective-permute-done.11.refs_0_.refs_1_) | copy-start | bytes 3145732
  143.3 47.7 %collective-permute-start.15 = (bf16[4,128,1024]{2,1,0:T(8,128)(2,1)S(1)}, bf16[4,128,1024]{2,1,0:T(8,128)(2,1)}, u32[]{:S(2)}, u32[]{:S(2)}) collective-permute-start(bf16[4,128,1024]{2,1,0:T(8,128)(2,1)S(1)} %collective-permute-done.11.refs_0_.refs_1_), channel_id=1, source_target_pairs={{4,6},{5,7},{12,14},{13,15},{20,22},{21,23},{28,30},{29,31}} | collective-permute-start | bytes 3145736 | tf_op jit(solution)/shard_map/ppermute | solution.py:249
  151.4 39.6 %collective-permute-start.16 = (bf16[4,128,1024]{2,1,0:T(8,128)(2,1)}, bf16[4,128,1024]{2,1,0:T(8,128)(2,1)}, u32[]{:S(2)}, u32[]{:S(2)}) collective-permute-start(bf16[4,128,1024]{2,1,0:T(8,128)(2,1)} %collective-permute-done.12.refs_1_.refs_4_), channel_id=1, source_target_pairs={{2,0},{3,1},{10,8},{11,9},{18,16},{19,17},{26,24},{27,25}} | collective-permute-start | bytes 3145736 | tf_op jit(solution)/shard_map/ppermute | solution.py:249
  169.5 23.5 %collective-permute-start.13 = (bf16[1,4,128,1024]{3,2,1,0:T(8,128)(2,1)}, bf16[1,4,128,1024]{3,2,1,0:T(8,128)(2,1)}, u32[]{:S(2)}, u32[]{:S(2)}) collective-permute-start(bf16[1,4,128,1024]{3,2,1,0:T(8,128)(2,1)} %get-tuple-element.29), channel_id=1, source_target_pairs={{0,2},{2,4},{1,3},{3,5},{8,10},{10,12},{9,11},{11,13},{16,18},{18,... | collective-permute-start | bytes 3145736 | tf_op jit(solution)/shard_map/ppermute | solution.py:249
  176.1 17.0 %collective-permute-start.14 = (bf16[1,4,128,1024]{3,2,1,0:T(8,128)(2,1)}, bf16[1,4,128,1024]{3,2,1,0:T(8,128)(2,1)S(1)}, u32[]{:S(2)}, u32[]{:S(2)}) collective-permute-start(bf16[1,4,128,1024]{3,2,1,0:T(8,128)(2,1)} %get-tuple-element.30), channel_id=1, source_target_pairs={{4,2},{6,4},{5,3},{7,5},{12,10},{14,12},{13,11},{15,13},{20,18},{2... | collective-permute-start | bytes 3145736 | tf_op jit(solution)/shard_map/ppermute | solution.py:249
  198.6 23.4 %collective-permute-start.17 = (bf16[1,4,128,1024]{3,2,1,0:T(8,128)(2,1)}, bf16[1,4,128,1024]{3,2,1,0:T(8,128)(2,1)S(1)}, u32[]{:S(2)}, u32[]{:S(2)}) collective-permute-start(bf16[1,4,128,1024]{3,2,1,0:T(8,128)(2,1)} %get-tuple-element.31.refs_6_.after), channel_id=1, source_target_pairs={{0,2},{2,4},{4,6},{1,3},{3,5},{5,7},{8,10},{10,12},{12,14},{9,11},... | collective-permute-start | bytes 3145736 | tf_op jit(solution)/shard_map/ppermute | solution.py:249
  204.8 21.0 %collective-permute-start.18 = (bf16[1,4,128,1024]{3,2,1,0:T(8,128)(2,1)S(1)}, bf16[1,4,128,1024]{3,2,1,0:T(8,128)(2,1)S(1)}, u32[]{:S(2)}, u32[]{:S(2)}) collective-permute-start(bf16[1,4,128,1024]{3,2,1,0:T(8,128)(2,1)S(1)} %get-tuple-element.32), channel_id=1, source_target_pairs={{2,0},{4,2},{6,4},{3,1},{5,3},{7,5},{10,8},{12,10},{14,12},{11,9},... | collective-permute-start | bytes 3145736 | tf_op jit(solution)/shard_map/ppermute | solution.py:249
  229.3 32.8 %all-to-all-start.2 = ((bf16[4,128,1024]{2,1,0:T(8,128)(2,1)}), bf16[4,128,1024]{2,1,0:T(8,128)(2,1)S(1)}, u32[]{:S(2)}, u32[]{:S(2)}) async-start(bf16[4,128,1024]{2,1,0:T(8,128)(2,1)} %sum.1), calls=%async_computation.2 | async-start | bytes 2097152 | tf_op jit(solution)/shard_map/all_to_all | solution.py:413
  242.0 51.0 %collective-permute-start.24 = (bf16[512,1024]{1,0:T(8,128)(2,1)}, bf16[512,1024]{1,0:T(8,128)(2,1)}, u32[]{:S(2)}, u32[]{:S(2)}) collective-permute-start(bf16[512,1024]{1,0:T(8,128)(2,1)} %weight.4.after), channel_id=1, source_target_pairs={{0,24},{8,16},{16,8},{24,0},{1,25},{9,17},{17,9},{25,1},{2,26},{10... | collective-permute-start | bytes 3145736 | tf_op jit(solution)/shard_map/ppermute | solution.py:245
  262.1 31.0 %collective-permute-start.23 = (bf16[512,1024]{1,0:T(8,128)(2,1)S(1)}, bf16[512,1024]{1,0:T(8,128)(2,1)S(1)}, u32[]{:S(2)}, u32[]{:S(2)}) collective-permute-start(bf16[512,1024]{1,0:T(8,128)(2,1)S(1)} %hold.3), channel_id=1, source_target_pairs={{0,16},{8,24},{16,0},{24,8},{1,17},{9,25},{17,1},{25,9},{2,18},{10... | collective-permute-start | bytes 3145736 | tf_op jit(solution)/shard_map/ppermute | solution.py:245
  262.9 30.2 %collective-permute-start.22 = (bf16[512,1024]{1,0:T(8,128)(2,1)S(1)}, bf16[512,1024]{1,0:T(8,128)(2,1)S(1)}, u32[]{:S(2)}, u32[]{:S(2)}) collective-permute-start(bf16[512,1024]{1,0:T(8,128)(2,1)S(1)} %hold.2), channel_id=1, source_target_pairs={{0,8},{8,0},{16,24},{24,16},{1,9},{9,1},{17,25},{25,17},{2,10},{10... | collective-permute-start | bytes 3145736 | tf_op jit(solution)/shard_map/ppermute | solution.py:245
  268.0 19.9 %copy-start.13 = (bf16[128,4096]{1,0:T(8,128)(2,1)S(1)}, bf16[128,4096]{1,0:T(8,128)(2,1)}, u32[]{:S(2)}) copy-start(bf16[128,4096]{1,0:T(8,128)(2,1)} %query.3) | copy-start | bytes 3145732
  268.0 19.9 %copy-start.17 = (bf16[128,4096]{1,0:T(8,128)(2,1)S(1)}, bf16[128,4096]{1,0:T(8,128)(2,1)}, u32[]{:S(2)}) copy-start(bf16[128,4096]{1,0:T(8,128)(2,1)} %copy-done.16) | copy-start | bytes 3145732
  272.4 6.8 %collective-permute-start.19 = (bf16[16,4096]{1,0:T(8,128)(2,1)S(1)}, bf16[16,4096]{1,0:T(8,128)(2,1)S(1)}, u32[]{:S(2)}, u32[]{:S(2)}) collective-permute-start(bf16[16,4096]{1,0:T(8,128)(2,1)S(1)} %get-tuple-element.36), channel_id=1, source_target_pairs={{2,0},{4,2},{6,4},{3,1},{5,3},{7,5},{10,8},{12,10},{14,12},{11,9},... | collective-permute-start | bytes 393224 | tf_op jit(solution)/shard_map/ppermute | solution.py:249
  273.7 11.7 %collective-permute-start.20 = (bf16[16,4096]{1,0:T(8,128)(2,1)S(1)}, bf16[16,4096]{1,0:T(8,128)(2,1)S(1)}, u32[]{:S(2)}, u32[]{:S(2)}) collective-permute-start(bf16[16,4096]{1,0:T(8,128)(2,1)S(1)} %get-tuple-element.36), channel_id=1, source_target_pairs={{4,0},{6,2},{5,1},{7,3},{12,8},{14,10},{13,9},{15,11},{20,16},{22,... | collective-permute-start | bytes 393224 | tf_op jit(solution)/shard_map/ppermute | solution.py:249
  279.3 8.6 %collective-permute-start.21 = (bf16[16,4096]{1,0:T(8,128)(2,1)S(1)}, bf16[16,4096]{1,0:T(8,128)(2,1)S(1)}, u32[]{:S(2)}, u32[]{:S(2)}) collective-permute-start(bf16[16,4096]{1,0:T(8,128)(2,1)S(1)} %get-tuple-element.36), channel_id=1, source_target_pairs={{6,0},{7,1},{14,8},{15,9},{22,16},{23,17},{30,24},{31,25}} | collective-permute-start | bytes 393224 | tf_op jit(solution)/shard_map/ppermute | solution.py:249
  (18 other events, 109.1 us)
Sparse Core Ops, SparseCore 0:
  62.7 64.1 all-gather.2

commit v3 on v2

--- a/solution.py
+++ b/solution.py
@@ -117,7 +117,7 @@
         gated[0, :, cols] = (gate[:, cols].astype(F32) * out).astype(BF16)
 
 
-def seed_body(delta, gate, long_out, starts_coef, seed, starts, gate_grad):
+def seed_body(delta, gate, long_out, starts_coef, after, seed, starts, gate_grad):
     for s in range(gate.shape[1] // LANES):
         cols = slice(s * LANES, (s + 1) * LANES)
         out = delta[0, :, cols].astype(F32)
@@ -203,7 +203,7 @@
         out[k + 1] = refs[k][...] + refs[count + k][...]
 
 
-def sum_body(dest, partial, right, left, out):
+def sum_body(dest, partial, right, left, after, out):
     total = partial[0].astype(F32) + right[0].astype(F32) + left[0].astype(F32)
     out[...] = total.astype(BF16)
 
@@ -310,10 +310,10 @@
     mine = call(
         join_body, "join", 0, 4 * part * depth * n_ctx,
         grid=(n_dp,),
-        in_specs=[wide(part, feats)] * n_ctx + [ANY] * 2,
+        in_specs=[wide(part, feats)] * n_ctx + [ANY] * (n_ctx + 1),
         out_specs=deep(n_ctx, part, feats),
         out_shape=shape(n_ctx, part, depth),
-    )(*mine, weights, local_fwd)
+    )(*mine, weights, local_fwd, *ends_far)
     grad = lax.all_gather(mine, ("dp", "tp"), axis=0, tiled=False)
     grad = grad.reshape(n_dp, n_tp, n_ctx, part, depth)
     long_out, gated = call(
@@ -401,17 +401,6 @@
         token = right
         right = shift(right, 1, range(t + 1))
         left = shift(left, -1, range(last - t, n_ctx))
-    delta = call(
-        sum_body, "sum", 0, 8 * n_dp * rows * quarter,
-        grid_spec=pltpu.PrefetchScalarGridSpec(
-            num_scalar_prefetch=1, grid=(n_dp,),
-            in_specs=[pick(0), piece_of, piece_of],
-            out_specs=pl.BlockSpec((1, rows, quarter), lambda i, q: (i, 0, 0)),
-        ),
-        out_shape=shape(n_dp, rows, quarter),
-    )(place[1:2], partial, right, left)
-    delta_far = lax.all_to_all(delta, "dp", 0, 0, tiled=True)
-
     gated_all = call(
         merge_body, "merge", 0, 2 * (2 * n_ctx + last) * n_dp * rows * quarter,
         grid=(n_dp,),
@@ -435,6 +424,17 @@
             out_shape=shape(feats, quarter),
         )(place, grad_t, gated_all, token)
 
+    delta = call(
+        sum_body, "sum", 0, 8 * n_dp * rows * quarter,
+        grid_spec=pltpu.PrefetchScalarGridSpec(
+            num_scalar_prefetch=1, grid=(n_dp,),
+            in_specs=[pick(0), piece_of, piece_of, ANY],
+            out_specs=pl.BlockSpec((1, rows, quarter), lambda i, q: (i, 0, 0)),
+        ),
+        out_shape=shape(n_dp, rows, quarter),
+    )(place[1:2], partial, right, left, pieces[n_dp // 2])
+    delta_far = lax.all_to_all(delta, "dp", 0, 0, tiled=True)
+
     def hold(value, after):
         return call(
             wait_body, "hold", 0, 0,
@@ -452,11 +452,11 @@
         grid=(steps,),
         in_specs=[
             pl.BlockSpec((1, rows, block), lambda i: (i, 0, 0)),
-            wide(rows, block), wide(rows, block), tall(block, rows),
+            wide(rows, block), wide(rows, block), tall(block, rows), ANY,
         ],
         out_specs=[wide(rows, block), wide(ORDER, block), wide(rows, block)],
         out_shape=[shape(rows, width), shape(ORDER, width), shape(rows, width)],
-    )(delta_far, gate, long_out, starts_coef)
+    )(delta_far, gate, long_out, starts_coef, weight_far[-1])
     starts_far = [shift(starts, -k) for k in range(1, n_ctx)]
     local_bwd = local(True, kernel, seed)
     query_grad, conv_grad = call(

time: 306 us -> 324 us (1.059)
  starting transfers between devices: 77.9 us -> 106 us
  waiting for transfers between devices: 66 us -> 58.5 us
  blocking collectives: 18.8 us -> 13.7 us
    ppermute x19, starting transfers between devices: 52.9 us -> 72.5 us  [shift(): return lax.ppermute(value, 'ctx', ends)]
    ppermute x19, waiting for transfers between devices: 59 us -> 46.3 us  [shift(): return lax.ppermute(value, 'ctx', ends)]
    ppermute x6, starting transfers between devices: 13.2 us -> 25.1 us  [swap(): lax.ppermute(value, axis, [(i, i ^ k) for i in range(lax.axis_size(axis))])]
    all_gather x1, waiting for transfers between devices: 0.02 us -> 6.12 us  [on_device(): grad = lax.all_gather(mine, ('dp', 'tp'), axis=0, tiled=False)]
    all_to_all x1, blocking collectives: 18.8 us -> 13.7 us  [on_device(): gated_far = lax.all_to_all(gated, 'dp', 0, 0, tiled=True)]
    unnamed x45 -> x53, local copies, waits for them, and re-layouts: 6.7 us -> 7.95 us
  transfers between devices with their start and end apart: 28 -> 28, of which waited for: 13 -> 12; matrix products, arithmetic and copies ran while one was open for 3% -> 3% of each run, Pallas kernels for 32% -> 30%
where the time goes in v3:
time: 324 us; the launch traced here: 323 us
  Pallas kernels  111 us (34%)
  starting transfers between devices  106 us (33%)
  waiting for transfers between devices  58.5 us (18%)
  between operations  14.5 us (4%)
  blocking collectives  13.7 us (4%)
  other arithmetic  9.29 us (3%)
  local copies, waits for them, and re-layouts  8.8 us (3%)
    ppermute x19, starting transfers between devices, shift(): return lax.ppermute(value, 'ctx', ends)  72.5 us
    ppermute x19, waiting for transfers between devices, shift(): return lax.ppermute(value, 'ctx', ends)  46.3 us
    ppermute x6, starting transfers between devices, swap(): lax.ppermute(value, axis, [(i, i ^ k) for i in range(lax.axis_size(axis))])  25.1 us
    pallas_call x4, Pallas kernels, on_device(): call(weight_body, 'weight', 2 * tokens * feats * quarter, 2 * tokens * (f...  22.2 us
    pallas_call x2, Pallas kernels, project(): call(functools.partial(delta_body, whole), 'delta', 2 * max(count - 1, 1)...  18.8 us
    pallas_call x1, Pallas kernels, on_device(): call(flip_body, 'flip', 0, 4 * tokens * depth, grid_spec=pltpu.PrefetchSc...  13.8 us
    all_to_all x1, blocking collectives, on_device(): gated_far = lax.all_to_all(gated, 'dp', 0, 0, tiled=True)  13.7 us
    pallas_call x3, Pallas kernels, local(): call(functools.partial(local_body, transposed), 'local_t' if transposed e...  12.5 us
  transfers between devices with their start and end apart: 28, of which 12 were waited for; matrix products, arithmetic and copies ran while one was open for 3% of the time, Pallas kernels for 30%

profile of v3, /device:TPU:0, one launch (start us, length us, event | category | flops | bytes accessed | tf_op | source)
XLA Modules:
  0.0 322.6 jit_solution(5090648576489188891)
XLA Ops:
  7.2 5.3 %all-to-all-start = ((bf16[4,1024,512]{2,1,0:T(8,128)(2,1)}), bf16[4,1024,512]{2,1,0:T(8,128)(2,1)}, u32[]{:S(2)}, u32[]{:S(2)}) async-start(bf16[4,1024,512]{2,1,0:T(8,128)(2,1)} %bitcast.20), calls=%async_computation | async-start | bytes 8388608 | tf_op jit(solution)/shard_map/all_to_all | solution.py:254
  15.2 5.6 %collective-permute-start.3 = (bf16[128,4096]{1,0:T(8,128)(2,1)}, bf16[128,4096]{1,0:T(8,128)(2,1)}, u32[]{:S(2)}, u32[]{:S(2)}) collective-permute-start(bf16[128,4096]{1,0:T(8,128)(2,1)} %multiply_convert_fusion.2.x), channel_id=1, source_target_pairs={{0,2},{2,4},{4,6},{1,3},{3,5},{5,7},{8,10},{10,12},{12,14},{9,11},... | collective-permute-start | bytes 3145736 | tf_op jit(solution)/shard_map/ppermute | solution.py:249
  35.0 5.6 %local.2.own_part = f32[128,4096]{1,0:T(8,128)} custom-call(f32[256,128]{1,0:T(8,128)S(1)} %pad_maximum_fusion.1.rows.taps, bf16[128,4096]{1,0:T(8,128)(2,1)} %multiply_convert_fusion.2.x, bf16[4096,128]{1,0:T(8,128)(2,1)S(1)} %get-tuple-element.43.refs_0_.ends_coef, bf16[4096,128]{1,0:T(8,128)(2,1)S(1)} %get-tuple-element.42.refs_1_.starts_coef, ...), custom_call_target="tpu_custom_call" | custom-call | flops 1073741824 | bytes 3145728 | tf_op jit(solution)/shard_map/local/pallas_call | solution.py:286
  43.7 5.7 %conv.1 = (bf16[128,4096]{1,0:T(8,128)(2,1)S(1)}, bf16[128,4096]{1,0:T(8,128)(2,1)S(1)}, bf16[16,4096]{1,0:T(8,128)(2,1)S(1)}) custom-call(bf16[128,4096]{1,0:T(8,128)(2,1)} %collective-permute-done.3.rim, f32[128,4096]{1,0:T(8,128)} %local.2.own_part, bf16[128,4096]{1,0:T(8,128)(2,1)} %query.3, f32[256,128]{1,0:T(8,128)S(1)} %pad_maximum_fusion.1.rows.taps, ...), custom_call_target="tpu_custom_call" | custom-call | flops 1073741824 | bytes 7340032 | tf_op jit(solution)/shard_map/conv/pallas_call | solution.py:299
  50.4 4.4 %collective-permute-start.4 = (bf16[16,4096]{1,0:T(8,128)(2,1)S(1)}, bf16[16,4096]{1,0:T(8,128)(2,1)S(1)}, u32[]{:S(2)}, u32[]{:S(2)}) collective-permute-start(bf16[16,4096]{1,0:T(8,128)(2,1)S(1)} %get-tuple-element.27), channel_id=1, source_target_pairs={{0,2},{2,4},{4,6},{1,3},{3,5},{5,7},{8,10},{10,12},{12,14},{9,11},... | collective-permute-start | bytes 393224 | tf_op jit(solution)/shard_map/ppermute | solution.py:249
  54.8 9.3 %collective-permute-start.5 = (bf16[16,4096]{1,0:T(8,128)(2,1)S(1)}, bf16[16,4096]{1,0:T(8,128)(2,1)S(1)}, u32[]{:S(2)}, u32[]{:S(2)}) collective-permute-start(bf16[16,4096]{1,0:T(8,128)(2,1)S(1)} %get-tuple-element.27), channel_id=1, source_target_pairs={{0,4},{2,6},{1,5},{3,7},{8,12},{10,14},{9,13},{11,15},{16,20},{18,... | collective-permute-start | bytes 393224 | tf_op jit(solution)/shard_map/ppermute | solution.py:249
  72.0 4.0 %long.1 = (bf16[128,4096]{1,0:T(8,128)(2,1)S(1)}, bf16[4,128,1024]{2,1,0:T(8,128)(2,1)S(1)}) custom-call(f32[128,4096]{1,0:T(8,128)} %copy-done.5, bf16[384,4096]{1,0:T(8,128)(2,1)} %get-tuple-element.41.refs_2_.coef, bf16[128,4096]{1,0:T(8,128)(2,1)S(1)} %copy-done.15, bf16[16,4096]{1,0:T(8,128)(2,1)S(1)} %collective-permute-done.4.refs_6_.refs_0_, ...), custom_call_target="tpu_custom_call" | custom-call | flops 134217728 | bytes 5242880 | tf_op jit(solution)/shard_map/long/pallas_call | solution.py:319
  76.0 13.7 %all_to_all.15.own = bf16[4,128,1024]{2,1,0:T(8,128)(2,1)S(1)} all-to-all(bf16[4,128,1024]{2,1,0:T(8,128)(2,1)S(1)} %get-tuple-element.28), channel_id=1, replica_groups=mesh['dp'=4,'ctx'=4,'tp'=2] {'dp'}, dimensions={0} | all-to-all | bytes 2097152 | tf_op jit(solution)/shard_map/all_to_all | solution.py:326
  89.7 21.8 %collective-permute-start.7 = (bf16[4,128,1024]{2,1,0:T(8,128)(2,1)S(1)}, bf16[4,128,1024]{2,1,0:T(8,128)(2,1)S(1)}, u32[]{:S(2)}, u32[]{:S(2)}) collective-permute-start(bf16[4,128,1024]{2,1,0:T(8,128)(2,1)S(1)} %all_to_all.15.own), channel_id=1, source_target_pairs={{0,2},{2,4},{4,6},{1,3},{3,5},{5,7},{8,10},{10,12},{12,14},{9,11},... | collective-permute-start | bytes 3145736 | tf_op jit(solution)/shard_map/ppermute | solution.py:249
  113.8 12.4 %collective-permute-done.7.refs_0_ = bf16[4,128,1024]{2,1,0:T(8,128)(2,1)S(1)} collective-permute-done((bf16[4,128,1024]{2,1,0:T(8,128)(2,1)S(1)}, bf16[4,128,1024]{2,1,0:T(8,128)(2,1)S(1)}, u32[]{:S(2)}, u32[]{:S(2)}) %collective-permute-start.7) | collective-permute-done | bytes 1048608 | tf_op jit(solution)/shard_map/ppermute | solution.py:249
  126.9 7.8 %collective-permute-done.8.refs_1_.refs_5_ = bf16[4,128,1024]{2,1,0:T(8,128)(2,1)S(1)} collective-permute-done((bf16[4,128,1024]{2,1,0:T(8,128)(2,1)S(1)}, bf16[4,128,1024]{2,1,0:T(8,128)(2,1)S(1)}, u32[]{:S(2)}, u32[]{:S(2)}) %collective-permute-start.8) | collective-permute-done | bytes 1048608 | tf_op jit(solution)/shard_map/ppermute | solution.py:249
  136.0 6.1 %all-gather.3.cloned.1.call-done = bf16[32,64,2048]{2,1,0:T(8,128)(2,1)} async-done(((bf16[4,64,2048]{2,1,0:T(8,128)(2,1)}), bf16[32,64,2048]{2,1,0:T(8,128)(2,1)}) %all-gather.3.cloned.1.call-update) | async-done | bytes 8388624 | tf_op jit(solution)/shard_map/all_gather | solution.py:317
  142.1 6.7 %delta.2.refs_0_ = bf16[1,4,128,1024]{3,2,1,0:T(8,128)(2,1)} custom-call(s32[3]{0:T(128)S(1)} %pad_add_fusion.place, s32[1]{0:T(128)} %bitcast.5.dest, bf16[4,2,4,64,2048]{4,3,2,1,0:T(8,128)(2,1)} %bitcast.17, bf16[4,1024,512]{2,1,0:T(8,128)(2,1)} %all-to-all-done.refs_4_.weights, bf16[4,128,1024]{2,1,0:T(8,128)(2,1)S(1)} %collective-permute-done.7.refs_0_, ...), custom_call_target="tpu_custom_call" | custom-call | flops 2147483648 | bytes 13631488 | tf_op jit(solution)/shard_map/delta/pallas_call | solution.py:343
  150.5 4.4 %collective-permute-start.9 = (bf16[1,4,128,1024]{3,2,1,0:T(8,128)(2,1)}, bf16[1,4,128,1024]{3,2,1,0:T(8,128)(2,1)}, u32[]{:S(2)}, u32[]{:S(2)}) collective-permute-start(bf16[1,4,128,1024]{3,2,1,0:T(8,128)(2,1)} %delta.2.refs_0_), channel_id=1, source_target_pairs={{0,2},{1,3},{8,10},{9,11},{16,18},{17,19},{24,26},{25,27}} | collective-permute-start | bytes 3145736 | tf_op jit(solution)/shard_map/ppermute | solution.py:249
  157.9 12.1 %delta.3.partial_right.partial_left.after.partial = bf16[4,4,128,1024]{3,2,1,0:T(8,128)(2,1)} custom-call(s32[3]{0:T(128)S(1)} %pad_add_fusion.place, s32[4]{0:T(128)S(1)} %and_select_fusion.dest, bf16[4,2,4,64,2048]{4,3,2,1,0:T(8,128)(2,1)} %bitcast.18, bf16[4,1024,512]{2,1,0:T(8,128)(2,1)} %all-to-all-done.refs_4_.weights, ...), custom_call_target="tpu_custom_call" | custom-call | flops 6442450944 | bytes 16777216 | tf_op jit(solution)/shard_map/delta/pallas_call | solution.py:343
  170.0 7.0 %collective-permute-done.9.right = bf16[1,4,128,1024]{3,2,1,0:T(8,128)(2,1)} collective-permute-done((bf16[1,4,128,1024]{3,2,1,0:T(8,128)(2,1)}, bf16[1,4,128,1024]{3,2,1,0:T(8,128)(2,1)}, u32[]{:S(2)}, u32[]{:S(2)}) %collective-permute-start.9) | collective-permute-done | bytes 1048608 | tf_op jit(solution)/shard_map/ppermute | solution.py:249
  177.0 4.7 %add.89 = (bf16[1,4,128,1024]{3,2,1,0:T(8,128)(2,1)}, bf16[1,4,128,1024]{3,2,1,0:T(8,128)(2,1)}) custom-call(s32[2]{0:T(128)S(1)} %add_clamp_fusion.1.dests, bf16[4,4,128,1024]{3,2,1,0:T(8,128)(2,1)} %delta.3.partial_right.partial_left.after.partial, bf16[4,4,128,1024]{3,2,1,0:T(8,128)(2,1)} %delta.3.partial_right.partial_left.after.partial, ...), custom_call_target="tpu_custom_call" | custom-call | bytes 6291456 | tf_op jit(solution)/shard_map/add/pallas_call | solution.py:392
  181.7 4.4 %collective-permute-start.13 = (bf16[1,4,128,1024]{3,2,1,0:T(8,128)(2,1)}, bf16[1,4,128,1024]{3,2,1,0:T(8,128)(2,1)S(1)}, u32[]{:S(2)}, u32[]{:S(2)}) collective-permute-start(bf16[1,4,128,1024]{3,2,1,0:T(8,128)(2,1)} %get-tuple-element.29), channel_id=1, source_target_pairs={{0,2},{2,4},{1,3},{3,5},{8,10},{10,12},{9,11},{11,13},{16,18},{18,... | collective-permute-start | bytes 3145736 | tf_op jit(solution)/shard_map/ppermute | solution.py:249
  188.0 13.8 %flip.1.refs_2_.grad_t = bf16[2048,2048]{1,0:T(8,128)(2,1)} custom-call(s32[3]{0:T(128)S(1)} %pad_add_fusion.place, bf16[4,2,4,64,2048]{4,3,2,1,0:T(8,128)(2,1)} %bitcast.19, bf16[4,4,128,1024]{3,2,1,0:T(8,128)(2,1)} %delta.3.partial_right.partial_left.after.partial), custom_call_target="tpu_custom_call" | custom-call | bytes 16777216 | tf_op jit(solution)/shard_map/flip/pallas_call | solution.py:366
  201.8 6.6 %collective-permute-done.13.right = bf16[1,4,128,1024]{3,2,1,0:T(8,128)(2,1)S(1)} collective-permute-done((bf16[1,4,128,1024]{3,2,1,0:T(8,128)(2,1)}, bf16[1,4,128,1024]{3,2,1,0:T(8,128)(2,1)S(1)}, u32[]{:S(2)}, u32[]{:S(2)}) %collective-permute-start.13) | collective-permute-done | bytes 1048608 | tf_op jit(solution)/shard_map/ppermute | solution.py:249
  211.9 6.4 %collective-permute-start.17 = (bf16[1,4,128,1024]{3,2,1,0:T(8,128)(2,1)S(1)}, bf16[1,4,128,1024]{3,2,1,0:T(8,128)(2,1)S(1)}, u32[]{:S(2)}, u32[]{:S(2)}) collective-permute-start(bf16[1,4,128,1024]{3,2,1,0:T(8,128)(2,1)S(1)} %get-tuple-element.31.refs_6_.after), channel_id=1, source_target_pairs={{0,2},{2,4},{4,6},{1,3},{3,5},{5,7},{8,10},{10,12},{12,14},{9,11},... | collective-permute-start | bytes 3145736 | tf_op jit(solution)/shard_map/ppermute | solution.py:249
  219.6 4.8 %merge.1 = bf16[4,4,128,1024]{3,2,1,0:T(8,128)(2,1)} custom-call(bf16[4,128,1024]{2,1,0:T(8,128)(2,1)S(1)} %copy-done.14, bf16[4,128,1024]{2,1,0:T(8,128)(2,1)S(1)} %collective-permute-done.7.refs_0_, bf16[4,128,1024]{2,1,0:T(8,128)(2,1)S(1)} %copy-done.8, bf16[4,128,1024]{2,1,0:T(8,128)(2,1)} %collective-permute-done.15.refs_0_.refs_2_, ...), custom_call_target="tpu_custom_call" | custom-call | bytes 11534336 | tf_op jit(solution)/shard_map/merge/pallas_call | solution.py:404
  225.6 6.1 %weight.4.after = bf16[512,1024]{1,0:T(8,128)(2,1)} custom-call(s32[3]{0:T(128)S(1)} %pad_add_fusion.place, bf16[2048,2048]{1,0:T(8,128)(2,1)} %flip.1.refs_2_.grad_t, bf16[2048,1024]{1,0:T(8,128)(2,1)} %bitcast.13, bf16[1,4,128,1024]{3,2,1,0:T(8,128)(2,1)S(1)} %copy-done.12), custom_call_target="tpu_custom_call" | custom-call | flops 2147483648 | bytes 6291456 | tf_op jit(solution)/shard_map/weight/pallas_call | solution.py:413
  231.7 5.4 %weight.5.after.refs_0_ = bf16[512,1024]{1,0:T(8,128)(2,1)S(1)} custom-call(s32[3]{0:T(128)S(1)} %pad_add_fusion.place, bf16[2048,2048]{1,0:T(8,128)(2,1)} %flip.1.refs_2_.grad_t, bf16[2048,1024]{1,0:T(8,128)(2,1)} %bitcast.14, bf16[512,1024]{1,0:T(8,128)(2,1)} %weight.4.after), custom_call_target="tpu_custom_call" | custom-call | flops 2147483648 | bytes 6291456 | tf_op jit(solution)/shard_map/weight/pallas_call | solution.py:413
  239.3 4.2 %collective-permute-done.18.left = bf16[1,4,128,1024]{3,2,1,0:T(8,128)(2,1)S(1)} collective-permute-done((bf16[1,4,128,1024]{3,2,1,0:T(8,128)(2,1)S(1)}, bf16[1,4,128,1024]{3,2,1,0:T(8,128)(2,1)S(1)}, u32[]{:S(2)}, u32[]{:S(2)}) %collective-permute-start.18) | collective-permute-done | bytes 1048608 | tf_op jit(solution)/shard_map/ppermute | solution.py:249
  253.4 5.4 %weight.6.after.refs_0_ = bf16[512,1024]{1,0:T(8,128)(2,1)S(1)} custom-call(s32[3]{0:T(128)S(1)} %pad_add_fusion.place, bf16[2048,2048]{1,0:T(8,128)(2,1)} %flip.1.refs_2_.grad_t, bf16[2048,1024]{1,0:T(8,128)(2,1)} %bitcast.15, bf16[512,1024]{1,0:T(8,128)(2,1)S(1)} %copy-done.2), custom_call_target="tpu_custom_call" | custom-call | flops 2147483648 | bytes 6291456 | tf_op jit(solution)/shard_map/weight/pallas_call | solution.py:413
  258.7 5.4 %weight.7.refs_0_ = bf16[512,1024]{1,0:T(8,128)(2,1)S(1)} custom-call(s32[3]{0:T(128)S(1)} %pad_add_fusion.place, bf16[2048,2048]{1,0:T(8,128)(2,1)} %flip.1.refs_2_.grad_t, bf16[2048,1024]{1,0:T(8,128)(2,1)} %bitcast.16, bf16[512,1024]{1,0:T(8,128)(2,1)S(1)} %weight.6.after.refs_0_), custom_call_target="tpu_custom_call" | custom-call | flops 2147483648 | bytes 6291456 | tf_op jit(solution)/shard_map/weight/pallas_call | solution.py:413
  267.0 16.4 %collective-permute-start.23 = (bf16[512,1024]{1,0:T(8,128)(2,1)S(1)}, bf16[512,1024]{1,0:T(8,128)(2,1)S(1)}, u32[]{:S(2)}, u32[]{:S(2)}) collective-permute-start(bf16[512,1024]{1,0:T(8,128)(2,1)S(1)} %hold.2), channel_id=1, source_target_pairs={{0,8},{8,0},{16,24},{24,16},{1,9},{9,1},{17,25},{25,17},{2,10},{10... | collective-permute-start | bytes 3145736 | tf_op jit(solution)/shard_map/ppermute | solution.py:245
  283.4 5.6 %collective-permute-done.19.after.refs_3_ = bf16[512,1024]{1,0:T(8,128)(2,1)} collective-permute-done((bf16[512,1024]{1,0:T(8,128)(2,1)}, bf16[512,1024]{1,0:T(8,128)(2,1)}, u32[]{:S(2)}, u32[]{:S(2)}) %collective-permute-start.19) | collective-permute-done | bytes 1048608 | tf_op jit(solution)/shard_map/ppermute | solution.py:245
  289.0 4.3 %seed.1 = (bf16[128,4096]{1,0:T(8,128)(2,1)S(1)}, bf16[16,4096]{1,0:T(8,128)(2,1)S(1)}, bf16[128,4096]{1,0:T(8,128)(2,1)}) custom-call(bf16[4,128,1024]{2,1,0:T(8,128)(2,1)S(1)} %all-to-all-done.2.delta.refs_1_, bf16[128,4096]{1,0:T(8,128)(2,1)S(1)} %copy-done.16, bf16[128,4096]{1,0:T(8,128)(2,1)} %copy-done.19, bf16[4096,128]{1,0:T(8,128)(2,1)} %copy-done.3, ...), custom_call_target="tpu_custom_call" | custom-call | flops 134217728 | bytes 5242880 | tf_op jit(solution)/shard_map/seed/pallas_call | solution.py:450
  306.0 5.2 %back.1 = (bf16[128,4096]{1,0:T(8,128)(2,1)}, bf16[128,4096]{1,0:T(8,128)(2,1)}) custom-call(f32[128,4096]{1,0:T(8,128)} %copy-done.18, bf16[384,4096]{1,0:T(8,128)(2,1)} %get-tuple-element.40.refs_3_.coef, bf16[128,4096]{1,0:T(8,128)(2,1)S(1)} %copy-done.21, bf16[128,4096]{1,0:T(8,128)(2,1)S(1)} %copy-done.17, ...), custom_call_target="tpu_custom_call" | custom-call | flops 134217728 | bytes 6291456 | tf_op jit(solution)/shard_map/back/pallas_call | solution.py:462
  311.2 4.5 %lay.1 = bf16[512,4096]{1,0:T(8,128)(2,1)} custom-call(s32[3]{0:T(128)S(1)} %pad_add_fusion.place, bf16[512,1024]{1,0:T(8,128)(2,1)S(1)} %copy-done.10, bf16[512,1024]{1,0:T(8,128)(2,1)S(1)} %collective-permute-done.23.refs_1_, bf16[512,1024]{1,0:T(8,128)(2,1)S(1)} %collective-permute-done.24.refs_2_, ...), custom_call_target="tpu_custom_call" | custom-call | bytes 8388608 | tf_op jit(solution)/shard_map/lay/pallas_call | solution.py:472
  (123 shorter events, 73.0 us)
Async XLA Ops:
  7.2 63.1 %all-to-all-start = ((bf16[4,1024,512]{2,1,0:T(8,128)(2,1)}), bf16[4,1024,512]{2,1,0:T(8,128)(2,1)}, u32[]{:S(2)}, u32[]{:S(2)}) async-start(bf16[4,1024,512]{2,1,0:T(8,128)(2,1)} %bitcast.20), calls=%async_computation | async-start | bytes 8388608 | tf_op jit(solution)/shard_map/all_to_all | solution.py:254
  12.5 129.7 %all-gather.3.cloned.1.call-start = ((), (), s32[]{:S(2)}) async-start(), calls=%async_computation.3 | async-start | bytes 9437184 | tf_op jit(solution)/shard_map/all_gather | solution.py:317
  15.2 28.5 %collective-permute-start.3 = (bf16[128,4096]{1,0:T(8,128)(2,1)}, bf16[128,4096]{1,0:T(8,128)(2,1)}, u32[]{:S(2)}, u32[]{:S(2)}) collective-permute-start(bf16[128,4096]{1,0:T(8,128)(2,1)} %multiply_convert_fusion.2.x), channel_id=1, source_target_pairs={{0,2},{2,4},{4,6},{1,3},{3,5},{5,7},{8,10},{10,12},{12,14},{9,11},... | collective-permute-start | bytes 3145736 | tf_op jit(solution)/shard_map/ppermute | solution.py:249
  23.1 41.0 %collective-permute-start = (bf16[64,2048]{1,0:T(8,128)(2,1)}, bf16[64,2048]{1,0:T(8,128)(2,1)S(1)}, u32[]{:S(2)}, u32[]{:S(2)}) collective-permute-start(bf16[64,2048]{1,0:T(8,128)(2,1)} %get-tuple-element.23), channel_id=1, source_target_pairs={{0,2},{2,0},{4,6},{6,4},{1,3},{3,1},{5,7},{7,5},{8,10},{10,8},{12,... | collective-permute-start | bytes 786440 | tf_op jit(solution)/shard_map/ppermute | solution.py:245
  23.7 46.5 %collective-permute-start.1 = (bf16[64,2048]{1,0:T(8,128)(2,1)}, bf16[64,2048]{1,0:T(8,128)(2,1)S(1)}, u32[]{:S(2)}, u32[]{:S(2)}) collective-permute-start(bf16[64,2048]{1,0:T(8,128)(2,1)} %get-tuple-element.24), channel_id=1, source_target_pairs={{0,4},{2,6},{4,0},{6,2},{1,5},{3,7},{5,1},{7,3},{8,12},{10,14},{12... | collective-permute-start | bytes 786440 | tf_op jit(solution)/shard_map/ppermute | solution.py:245
  24.8 45.5 %collective-permute-start.2 = (bf16[64,2048]{1,0:T(8,128)(2,1)}, bf16[64,2048]{1,0:T(8,128)(2,1)S(1)}, u32[]{:S(2)}, u32[]{:S(2)}) collective-permute-start(bf16[64,2048]{1,0:T(8,128)(2,1)} %get-tuple-element.25), channel_id=1, source_target_pairs={{0,6},{2,4},{4,2},{6,0},{1,7},{3,5},{5,3},{7,1},{8,14},{10,12},{12... | collective-permute-start | bytes 786440 | tf_op jit(solution)/shard_map/ppermute | solution.py:245
  50.4 19.8 %collective-permute-start.4 = (bf16[16,4096]{1,0:T(8,128)(2,1)S(1)}, bf16[16,4096]{1,0:T(8,128)(2,1)S(1)}, u32[]{:S(2)}, u32[]{:S(2)}) collective-permute-start(bf16[16,4096]{1,0:T(8,128)(2,1)S(1)} %get-tuple-element.27), channel_id=1, source_target_pairs={{0,2},{2,4},{4,6},{1,3},{3,5},{5,7},{8,10},{10,12},{12,14},{9,11},... | collective-permute-start | bytes 393224 | tf_op jit(solution)/shard_map/ppermute | solution.py:249
  54.8 15.5 %collective-permute-start.5 = (bf16[16,4096]{1,0:T(8,128)(2,1)S(1)}, bf16[16,4096]{1,0:T(8,128)(2,1)S(1)}, u32[]{:S(2)}, u32[]{:S(2)}) collective-permute-start(bf16[16,4096]{1,0:T(8,128)(2,1)S(1)} %get-tuple-element.27), channel_id=1, source_target_pairs={{0,4},{2,6},{1,5},{3,7},{8,12},{10,14},{9,13},{11,15},{16,20},{18,... | collective-permute-start | bytes 393224 | tf_op jit(solution)/shard_map/ppermute | solution.py:249
  64.1 6.1 %collective-permute-start.6 = (bf16[16,4096]{1,0:T(8,128)(2,1)S(1)}, bf16[16,4096]{1,0:T(8,128)(2,1)S(1)}, u32[]{:S(2)}, u32[]{:S(2)}) collective-permute-start(bf16[16,4096]{1,0:T(8,128)(2,1)S(1)} %get-tuple-element.27), channel_id=1, source_target_pairs={{0,6},{1,7},{8,14},{9,15},{16,22},{17,23},{24,30},{25,31}} | collective-permute-start | bytes 393224 | tf_op jit(solution)/shard_map/ppermute | solution.py:249
  76.0 58.7 %copy-start.19 = (bf16[128,4096]{1,0:T(8,128)(2,1)}, bf16[128,4096]{1,0:T(8,128)(2,1)S(1)}, u32[]{:S(2)}) copy-start(bf16[128,4096]{1,0:T(8,128)(2,1)S(1)} %get-tuple-element.33.long_out) | copy-start | bytes 3145732
  89.7 36.5 %collective-permute-start.7 = (bf16[4,128,1024]{2,1,0:T(8,128)(2,1)S(1)}, bf16[4,128,1024]{2,1,0:T(8,128)(2,1)S(1)}, u32[]{:S(2)}, u32[]{:S(2)}) collective-permute-start(bf16[4,128,1024]{2,1,0:T(8,128)(2,1)S(1)} %all_to_all.15.own), channel_id=1, source_target_pairs={{0,2},{2,4},{4,6},{1,3},{3,5},{5,7},{8,10},{10,12},{12,14},{9,11},... | collective-permute-start | bytes 3145736 | tf_op jit(solution)/shard_map/ppermute | solution.py:249
  111.5 23.2 %collective-permute-start.8 = (bf16[4,128,1024]{2,1,0:T(8,128)(2,1)S(1)}, bf16[4,128,1024]{2,1,0:T(8,128)(2,1)S(1)}, u32[]{:S(2)}, u32[]{:S(2)}) collective-permute-start(bf16[4,128,1024]{2,1,0:T(8,128)(2,1)S(1)} %all_to_all.15.own), channel_id=1, source_target_pairs={{2,0},{4,2},{6,4},{3,1},{5,3},{7,5},{10,8},{12,10},{14,12},{11,9},... | collective-permute-start | bytes 3145736 | tf_op jit(solution)/shard_map/ppermute | solution.py:249
  126.2 28.8 %collective-permute-start.11 = (bf16[4,128,1024]{2,1,0:T(8,128)(2,1)S(1)}, bf16[4,128,1024]{2,1,0:T(8,128)(2,1)S(1)}, u32[]{:S(2)}, u32[]{:S(2)}) collective-permute-start(bf16[4,128,1024]{2,1,0:T(8,128)(2,1)S(1)} %collective-permute-done.7.refs_0_), channel_id=1, source_target_pairs={{2,4},{4,6},{3,5},{5,7},{10,12},{12,14},{11,13},{13,15},{18,20},{2... | collective-permute-start | bytes 3145736 | tf_op jit(solution)/shard_map/ppermute | solution.py:249
  134.7 21.8 %collective-permute-start.12 = (bf16[4,128,1024]{2,1,0:T(8,128)(2,1)S(1)}, bf16[4,128,1024]{2,1,0:T(8,128)(2,1)}, u32[]{:S(2)}, u32[]{:S(2)}) collective-permute-start(bf16[4,128,1024]{2,1,0:T(8,128)(2,1)S(1)} %collective-permute-done.8.refs_1_.refs_5_), channel_id=1, source_target_pairs={{2,0},{4,2},{3,1},{5,3},{10,8},{12,10},{11,9},{13,11},{18,16},{20,... | collective-permute-start | bytes 3145736 | tf_op jit(solution)/shard_map/ppermute | solution.py:249
  148.8 21.2 %collective-permute-start.10 = (bf16[1,4,128,1024]{3,2,1,0:T(8,128)(2,1)}, bf16[1,4,128,1024]{3,2,1,0:T(8,128)(2,1)}, u32[]{:S(2)}, u32[]{:S(2)}) collective-permute-start(bf16[1,4,128,1024]{3,2,1,0:T(8,128)(2,1)} %delta.2.refs_0_), channel_id=1, source_target_pairs={{6,4},{7,5},{14,12},{15,13},{22,20},{23,21},{30,28},{31,29}} | collective-permute-start | bytes 3145736 | tf_op jit(solution)/shard_map/ppermute | solution.py:249
  150.5 26.5 %collective-permute-start.9 = (bf16[1,4,128,1024]{3,2,1,0:T(8,128)(2,1)}, bf16[1,4,128,1024]{3,2,1,0:T(8,128)(2,1)}, u32[]{:S(2)}, u32[]{:S(2)}) collective-permute-start(bf16[1,4,128,1024]{3,2,1,0:T(8,128)(2,1)} %delta.2.refs_0_), channel_id=1, source_target_pairs={{0,2},{1,3},{8,10},{9,11},{16,18},{17,19},{24,26},{25,27}} | collective-permute-start | bytes 3145736 | tf_op jit(solution)/shard_map/ppermute | solution.py:249
  154.9 46.9 %collective-permute-start.15 = (bf16[4,128,1024]{2,1,0:T(8,128)(2,1)S(1)}, bf16[4,128,1024]{2,1,0:T(8,128)(2,1)}, u32[]{:S(2)}, u32[]{:S(2)}) collective-permute-start(bf16[4,128,1024]{2,1,0:T(8,128)(2,1)S(1)} %collective-permute-done.11.refs_0_.refs_1_), channel_id=1, source_target_pairs={{4,6},{5,7},{12,14},{13,15},{20,22},{21,23},{28,30},{29,31}} | collective-permute-start | bytes 3145736 | tf_op jit(solution)/shard_map/ppermute | solution.py:249
  156.6 45.2 %collective-permute-start.16 = (bf16[4,128,1024]{2,1,0:T(8,128)(2,1)}, bf16[4,128,1024]{2,1,0:T(8,128)(2,1)}, u32[]{:S(2)}, u32[]{:S(2)}) collective-permute-start(bf16[4,128,1024]{2,1,0:T(8,128)(2,1)} %collective-permute-done.12.refs_1_.refs_4_), channel_id=1, source_target_pairs={{2,0},{3,1},{10,8},{11,9},{18,16},{19,17},{26,24},{27,25}} | collective-permute-start | bytes 3145736 | tf_op jit(solution)/shard_map/ppermute | solution.py:249
  181.7 26.7 %collective-permute-start.13 = (bf16[1,4,128,1024]{3,2,1,0:T(8,128)(2,1)}, bf16[1,4,128,1024]{3,2,1,0:T(8,128)(2,1)S(1)}, u32[]{:S(2)}, u32[]{:S(2)}) collective-permute-start(bf16[1,4,128,1024]{3,2,1,0:T(8,128)(2,1)} %get-tuple-element.29), channel_id=1, source_target_pairs={{0,2},{2,4},{1,3},{3,5},{8,10},{10,12},{9,11},{11,13},{16,18},{18,... | collective-permute-start | bytes 3145736 | tf_op jit(solution)/shard_map/ppermute | solution.py:249
  186.2 22.3 %collective-permute-start.14 = (bf16[1,4,128,1024]{3,2,1,0:T(8,128)(2,1)}, bf16[1,4,128,1024]{3,2,1,0:T(8,128)(2,1)}, u32[]{:S(2)}, u32[]{:S(2)}) collective-permute-start(bf16[1,4,128,1024]{3,2,1,0:T(8,128)(2,1)} %get-tuple-element.30), channel_id=1, source_target_pairs={{4,2},{6,4},{5,3},{7,5},{12,10},{14,12},{13,11},{15,13},{20,18},{2... | collective-permute-start | bytes 3145736 | tf_op jit(solution)/shard_map/ppermute | solution.py:249
  201.8 17.8 %copy-start.8 = (bf16[4,128,1024]{2,1,0:T(8,128)(2,1)S(1)}, bf16[4,128,1024]{2,1,0:T(8,128)(2,1)}, u32[]{:S(2)}) copy-start(bf16[4,128,1024]{2,1,0:T(8,128)(2,1)} %copy-done.7) | copy-start | bytes 3145732
  201.8 17.8 %copy-start.14 = (bf16[4,128,1024]{2,1,0:T(8,128)(2,1)S(1)}, bf16[4,128,1024]{2,1,0:T(8,128)(2,1)}, u32[]{:S(2)}) copy-start(bf16[4,128,1024]{2,1,0:T(8,128)(2,1)} %copy-done.13) | copy-start | bytes 3145732
  211.9 27.4 %collective-permute-start.17 = (bf16[1,4,128,1024]{3,2,1,0:T(8,128)(2,1)S(1)}, bf16[1,4,128,1024]{3,2,1,0:T(8,128)(2,1)S(1)}, u32[]{:S(2)}, u32[]{:S(2)}) collective-permute-start(bf16[1,4,128,1024]{3,2,1,0:T(8,128)(2,1)S(1)} %get-tuple-element.31.refs_6_.after), channel_id=1, source_target_pairs={{0,2},{2,4},{4,6},{1,3},{3,5},{5,7},{8,10},{10,12},{12,14},{9,11},... | collective-permute-start | bytes 3145736 | tf_op jit(solution)/shard_map/ppermute | solution.py:249
  218.2 25.2 %collective-permute-start.18 = (bf16[1,4,128,1024]{3,2,1,0:T(8,128)(2,1)S(1)}, bf16[1,4,128,1024]{3,2,1,0:T(8,128)(2,1)S(1)}, u32[]{:S(2)}, u32[]{:S(2)}) collective-permute-start(bf16[1,4,128,1024]{3,2,1,0:T(8,128)(2,1)S(1)} %get-tuple-element.32), channel_id=1, source_target_pairs={{2,0},{4,2},{6,4},{3,1},{5,3},{7,5},{10,8},{12,10},{14,12},{11,9},... | collective-permute-start | bytes 3145736 | tf_op jit(solution)/shard_map/ppermute | solution.py:249
  247.0 18.6 %all-to-all-start.2 = ((bf16[4,128,1024]{2,1,0:T(8,128)(2,1)}), bf16[4,128,1024]{2,1,0:T(8,128)(2,1)S(1)}, u32[]{:S(2)}, u32[]{:S(2)}) async-start(bf16[4,128,1024]{2,1,0:T(8,128)(2,1)} %sum.1), calls=%async_computation.2 | async-start | bytes 2097152 | tf_op jit(solution)/shard_map/all_to_all | solution.py:436
  250.5 38.6 %collective-permute-start.19 = (bf16[512,1024]{1,0:T(8,128)(2,1)}, bf16[512,1024]{1,0:T(8,128)(2,1)}, u32[]{:S(2)}, u32[]{:S(2)}) collective-permute-start(bf16[512,1024]{1,0:T(8,128)(2,1)} %weight.4.after), channel_id=1, source_target_pairs={{0,24},{8,16},{16,8},{24,0},{1,25},{9,17},{17,9},{25,1},{2,26},{10... | collective-permute-start | bytes 3145736 | tf_op jit(solution)/shard_map/ppermute | solution.py:245
  265.6 23.5 %copy-start.16 = (bf16[128,4096]{1,0:T(8,128)(2,1)S(1)}, bf16[128,4096]{1,0:T(8,128)(2,1)}, u32[]{:S(2)}) copy-start(bf16[128,4096]{1,0:T(8,128)(2,1)} %gate.3) | copy-start | bytes 3145732
  265.6 45.6 %collective-permute-start.24 = (bf16[512,1024]{1,0:T(8,128)(2,1)S(1)}, bf16[512,1024]{1,0:T(8,128)(2,1)S(1)}, u32[]{:S(2)}, u32[]{:S(2)}) collective-permute-start(bf16[512,1024]{1,0:T(8,128)(2,1)S(1)} %hold.3), channel_id=1, source_target_pairs={{0,16},{8,24},{16,0},{24,8},{1,17},{9,25},{17,1},{25,9},{2,18},{10... | collective-permute-start | bytes 3145736 | tf_op jit(solution)/shard_map/ppermute | solution.py:245
  267.0 44.1 %collective-permute-start.23 = (bf16[512,1024]{1,0:T(8,128)(2,1)S(1)}, bf16[512,1024]{1,0:T(8,128)(2,1)S(1)}, u32[]{:S(2)}, u32[]{:S(2)}) collective-permute-start(bf16[512,1024]{1,0:T(8,128)(2,1)S(1)} %hold.2), channel_id=1, source_target_pairs={{0,8},{8,0},{16,24},{24,16},{1,9},{9,1},{17,25},{25,17},{2,10},{10... | collective-permute-start | bytes 3145736 | tf_op jit(solution)/shard_map/ppermute | solution.py:245
  293.3 8.8 %collective-permute-start.20 = (bf16[16,4096]{1,0:T(8,128)(2,1)S(1)}, bf16[16,4096]{1,0:T(8,128)(2,1)S(1)}, u32[]{:S(2)}, u32[]{:S(2)}) collective-permute-start(bf16[16,4096]{1,0:T(8,128)(2,1)S(1)} %get-tuple-element.36), channel_id=1, source_target_pairs={{2,0},{4,2},{6,4},{3,1},{5,3},{7,5},{10,8},{12,10},{14,12},{11,9},... | collective-permute-start | bytes 393224 | tf_op jit(solution)/shard_map/ppermute | solution.py:249
  294.7 7.8 %collective-permute-start.21 = (bf16[16,4096]{1,0:T(8,128)(2,1)S(1)}, bf16[16,4096]{1,0:T(8,128)(2,1)S(1)}, u32[]{:S(2)}, u32[]{:S(2)}) collective-permute-start(bf16[16,4096]{1,0:T(8,128)(2,1)S(1)} %get-tuple-element.36), channel_id=1, source_target_pairs={{4,0},{6,2},{5,1},{7,3},{12,8},{14,10},{13,9},{15,11},{20,16},{22,... | collective-permute-start | bytes 393224 | tf_op jit(solution)/shard_map/ppermute | solution.py:249
  296.0 9.9 %collective-permute-start.22 = (bf16[16,4096]{1,0:T(8,128)(2,1)S(1)}, bf16[16,4096]{1,0:T(8,128)(2,1)S(1)}, u32[]{:S(2)}, u32[]{:S(2)}) collective-permute-start(bf16[16,4096]{1,0:T(8,128)(2,1)S(1)} %get-tuple-element.36), channel_id=1, source_target_pairs={{6,0},{7,1},{14,8},{15,9},{22,16},{23,17},{30,24},{31,25}} | collective-permute-start | bytes 393224 | tf_op jit(solution)/shard_map/ppermute | solution.py:249
  (22 other events, 136.3 us)
Sparse Core Ops, SparseCore 0:
  72.1 70.0 all-gather.2

commit v4 on v3

--- a/solution.py
+++ b/solution.py
@@ -141,7 +141,7 @@
 
 def pack_body(place, *refs):
     count = len(refs) // 2
-    for source, target in zip(refs[:count], refs[-count:]):
+    for source, target in zip(refs[:count], refs[count + 1 :]):
         target[...] = source[...]
 
 
@@ -151,7 +151,7 @@
         out[k] = refs[k][...]
 
 
-def delta_body(whole, place, dest, grad, weights, *refs):
+def delta_body(computed, grad, weights, *refs):
     depth, out = weights.shape[2], refs[-1]
 
     def multiply():
@@ -164,18 +164,25 @@
             total = term if total is None else total + term
         out[...] = total.astype(BF16).reshape(out.shape)
 
-    if not whole:
+    if computed is None:
         return multiply()
-    is_last = pl.program_id(0) == pl.num_programs(0) - 1
-    pl.when(jnp.logical_not(is_last))(multiply)
-
-    @pl.when(is_last)
+    pl.when(pl.program_id(0) < computed)(multiply)
+
+    @pl.when(pl.program_id(0) >= computed)
     def _():
         out[...] = refs[0][...]
 
 
-def flip_body(place, grad, after, out):
-    out[...] = grad[...].reshape(-1, grad.shape[-1]).T
+def flip_body(place_of, side, place, far, near, after, out):
+    is_far = place_of(pl.program_id(0), place) >= side
+
+    @pl.when(is_far)
+    def _():
+        out[...] = far[...].reshape(-1, far.shape[-1]).T
+
+    @pl.when(jnp.logical_not(is_far))
+    def _():
+        out[...] = near[...].reshape(-1, near.shape[-1]).T
 
 
 def lay_body(place, *refs):
@@ -252,18 +259,19 @@
         return pl.BlockSpec((part, feats), lambda j, p: (p[2], j * n_ctx + (p[1] ^ k)))
 
     weights = lax.all_to_all(proj_weight.reshape(n_dp, quarter, feats), "dp", 0, 0, tiled=True)
+    product = (key_in.astype(F32) * value_in.astype(F32)).astype(BF16)
+    rim = shift(product, 1)
     mine = call(
         pack_body, "pack", 0, 4 * part * depth * n_ctx,
         grid_spec=pltpu.PrefetchScalarGridSpec(
             num_scalar_prefetch=1, grid=(n_dp,),
-            in_specs=[piece(k) for k in range(n_ctx)],
+            in_specs=[piece(k) for k in range(n_ctx)] + [ANY],
             out_specs=[pl.BlockSpec((part, feats), lambda j, p: (0, j))] * n_ctx,
         ),
         out_shape=[shape(part, depth)] * n_ctx,
-    )(place, *[out_grad] * n_ctx)
+    )(place, *[out_grad] * n_ctx, rim)
     mine = [mine[0]] + [swap(mine[k], "ctx", k) for k in range(1, n_ctx)]
-    product = (key_in.astype(F32) * value_in.astype(F32)).astype(BF16)
-    rim = shift(product, 1)
+
     rate = lr_rate.reshape(-1, 1)
     residue = lr_residue.reshape(-1, 1)
     counts = jnp.arange(rows, dtype=F32)[None, :]
@@ -307,22 +315,31 @@
 
 
     local_fwd = local(False, kernel_rev, mixed)
-    mine = call(
-        join_body, "join", 0, 4 * part * depth * n_ctx,
-        grid=(n_dp,),
-        in_specs=[wide(part, feats)] * n_ctx + [ANY] * (n_ctx + 1),
-        out_specs=deep(n_ctx, part, feats),
-        out_shape=shape(n_ctx, part, depth),
-    )(*mine, weights, local_fwd, *ends_far)
-    grad = lax.all_gather(mine, ("dp", "tp"), axis=0, tiled=False)
-    grad = grad.reshape(n_dp, n_tp, n_ctx, part, depth)
+    side = n_ctx // 2
+
+    def join(pieces, *after):
+        return call(
+            join_body, "join", 0, 4 * part * depth * side,
+            grid=(n_dp,),
+            in_specs=[wide(part, feats)] * side + [ANY] * len(after),
+            out_specs=deep(side, part, feats),
+            out_shape=shape(side, part, depth),
+        )(*pieces, *after)
+
+    def gather(value):
+        value = lax.all_gather(value, ("dp", "tp"), axis=0, tiled=False)
+        return value.reshape(n_dp, n_tp, side, part, depth)
+
+    far = join(mine[side:], weights, local_fwd, *ends_far, *mine[1:side])
+    near = join(mine[:side], far)
+    grad_far, grad_near = gather(far), gather(near)
     long_out, gated = call(
         functools.partial(long_body, n_ctx - 1), "long", 2 * rows * 128 * width, rows * width * 10,
         grid=(steps,),
-        in_specs=[wide(rows, block), wide((n_ctx - 1) * rows, block), wide(rows, block)] + [wide(ORDER, block)] * (n_ctx - 1) + [ANY],
+        in_specs=[wide(rows, block), wide((n_ctx - 1) * rows, block), wide(rows, block)] + [wide(ORDER, block)] * (n_ctx - 1) + [ANY] * 2,
         out_specs=[wide(rows, block), pl.BlockSpec((1, rows, block), lambda i: (i, 0, 0))],
         out_shape=[shape(rows, width), shape(n_dp, rows, quarter)],
-    )(local_fwd, carry_coef, gate, *ends_far, mine)
+    )(local_fwd, carry_coef, gate, *ends_far, far, near)
     gated_far = lax.all_to_all(gated, "dp", 0, 0, tiled=True)
     tokens = n_ctx * n_dp * rows
     last = n_ctx - 1
@@ -334,50 +351,54 @@
         from_left.append(right)
         from_right.append(left)
 
-    first_dest = jnp.where(place[1] < n_ctx // 2, last, 0)
     chunk = (1, n_dp, rows, quarter)
-
-    def project(dests, *after):
-        count = dests.shape[0]
-        whole = count > 1
-        return call(
-            functools.partial(delta_body, whole), "delta",
-            2 * max(count - 1, 1) * n_dp * rows * depth * quarter,
-            2 * tokens * depth + 2 * depth * quarter + 2 * count * n_dp * rows * quarter,
-            grid_spec=pltpu.PrefetchScalarGridSpec(
-                num_scalar_prefetch=2, grid=(count,),
-                in_specs=[
-                    pl.BlockSpec(
-                        (n_dp, n_tp, 1, part, depth), lambda i, p, q: (0, 0, p[1] ^ q[i], 0, 0)
-                    ),
-                    pl.BlockSpec((n_dp, quarter, feats), lambda i, p, q: (0, 0, 0)),
-                ] + ([pl.BlockSpec(chunk, lambda i, p, q: (0, 0, 0, 0))] if whole
-                     else [ANY] * len(after)),
-                out_specs=pl.BlockSpec(
-                    chunk, lambda i, p, q: (q[i] if whole else 0, 0, 0, 0)
-                ),
-            ),
-            out_shape=shape(count, n_dp, rows, quarter),
-        )(place, dests, grad, weights, *after)
-
-    first = project(first_dest[None], from_left[0], from_right[0])
-    others = (first_dest + 1 + jnp.arange(n_ctx, dtype=jnp.int32)) % n_ctx
-    partial = project(others.astype(jnp.int32), first)
+    grad_block = (n_dp, n_tp, 1, part, depth)
+    all_weights = pl.BlockSpec((n_dp, quarter, feats), lambda i: (0, 0, 0))
+    far_part = call(
+        functools.partial(delta_body, None), "delta", tokens * depth * quarter,
+        tokens * depth + 2 * depth * quarter + tokens * quarter,
+        grid=(side,),
+        in_specs=[pl.BlockSpec(grad_block, lambda i: (0, 0, i, 0, 0)), all_weights, ANY, ANY],
+        out_specs=pl.BlockSpec(chunk, lambda i: (i, 0, 0, 0)),
+        out_shape=shape(side, n_dp, rows, quarter),
+    )(grad_far, weights, from_left[0], from_right[0])
+    partial = call(
+        functools.partial(delta_body, side), "delta", tokens * depth * quarter,
+        tokens * depth + 2 * depth * quarter + 3 * tokens * quarter,
+        grid=(n_ctx,),
+        in_specs=[
+            pl.BlockSpec(grad_block, lambda i: (0, 0, jnp.minimum(i, side - 1), 0, 0)),
+            all_weights,
+            pl.BlockSpec(chunk, lambda i: (jnp.maximum(i - side, 0), 0, 0, 0)),
+        ],
+        out_specs=pl.BlockSpec(chunk, lambda i: (i, 0, 0, 0)),
+        out_shape=shape(n_ctx, n_dp, rows, quarter),
+    )(grad_near, weights, far_part)
+    def place_of(i, p):
+        return p[1] ^ ((p[1] + n_ctx - i) % n_ctx)
+
     grad_t = call(
-        flip_body, "flip", 0, 4 * tokens * depth,
+        functools.partial(flip_body, place_of, side), "flip", 0, 6 * tokens * depth,
         grid_spec=pltpu.PrefetchScalarGridSpec(
             num_scalar_prefetch=1, grid=(n_ctx, n_dp),
             in_specs=[
                 pl.BlockSpec(
                     (1, n_tp, 1, part, depth),
-                    lambda i, j, p: (j, 0, p[1] ^ ((p[1] + n_ctx - i) % n_ctx), 0, 0),
+                    lambda i, j, p: (j, 0, jnp.maximum(place_of(i, p) - side, 0), 0, 0),
+                ),
+                pl.BlockSpec(
+                    (1, n_tp, 1, part, depth),
+                    lambda i, j, p: (j, 0, jnp.minimum(place_of(i, p), side - 1), 0, 0),
                 ),
                 ANY,
             ],
             out_specs=pl.BlockSpec((depth, rows), lambda i, j, p: (0, i * n_dp + j)),
         ),
         out_shape=shape(depth, tokens),
-    )(place, grad, partial)
+    )(place, grad_far, grad_near, partial)
+    own = place[1]
+    start = jnp.where(own < side, own ^ last, own) - side
+    first = lax.dynamic_slice_in_dim(far_part, start, 1)
     right, left = shift(first, 1, [0]), shift(first, -1, [last])
 
     def pick(ahead):
@@ -388,7 +409,11 @@
     piece_of = pl.BlockSpec((1, 1, rows, quarter), lambda i, q: (0, i, 0, 0))
     for t in range(1, last):
         after = (from_left[t], from_right[t]) + ((grad_t,) if t == last - 1 else ())
-        dests = jnp.clip(jnp.stack([last - t + place[1], t - last + place[1]]), 0, last)
+        dests = jnp.clip(jnp.stack([last - t + own, t - last + own]), 0, last) ^ own
+        if t < side:
+            table, dests = far_part, jnp.maximum(dests - side, 0)
+        else:
+            table = partial
         right, left = call(
             add_body, "add", 0, 12 * n_dp * rows * quarter,
             grid_spec=pltpu.PrefetchScalarGridSpec(
@@ -397,7 +422,7 @@
                 out_specs=[piece_of] * 2,
             ),
             out_shape=[shape(*chunk)] * 2,
-        )(dests, partial, partial, right, left, *after)
+        )(dests, table, table, right, left, *after)
         token = right
         right = shift(right, 1, range(t + 1))
         left = shift(left, -1, range(last - t, n_ctx))
@@ -432,7 +457,7 @@
             out_specs=pl.BlockSpec((1, rows, quarter), lambda i, q: (i, 0, 0)),
         ),
         out_shape=shape(n_dp, rows, quarter),
-    )(place[1:2], partial, right, left, pieces[n_dp // 2])
+    )(own[None] * 0, partial, right, left, pieces[n_dp // 2])
     delta_far = lax.all_to_all(delta, "dp", 0, 0, tiled=True)
 
     def hold(value, after):
@@ -456,7 +481,7 @@
         ],
         out_specs=[wide(rows, block), wide(ORDER, block), wide(rows, block)],
         out_shape=[shape(rows, width), shape(ORDER, width), shape(rows, width)],
-    )(delta_far, gate, long_out, starts_coef, weight_far[-1])
+    )(delta_far, gate, long_out, starts_coef, delta)
     starts_far = [shift(starts, -k) for k in range(1, n_ctx)]
     local_bwd = local(True, kernel, seed)
     query_grad, conv_grad = call(

time: 324 us -> 319 us (0.985)
  starting transfers between devices: 106 us -> 78 us
  waiting for transfers between devices: 58.5 us -> 77.7 us
    ppermute x6, starting transfers between devices: 25.1 us -> 7.41 us  [swap(): lax.ppermute(value, axis, [(i, i ^ k) for i in range(lax.axis_size(axis))])]
    ppermute x19, waiting for transfers between devices: 46.3 us -> 62.3 us  [shift(): return lax.ppermute(value, 'ctx', ends)]
    all_to_all x1, waiting for transfers between devices: 0.43 us -> 15.4 us  [on_device(): delta_far = lax.all_to_all(delta, 'dp', 0, 0, tiled=True)]
    ppermute x19, starting transfers between devices: 72.5 us -> 61.9 us  [shift(): return lax.ppermute(value, 'ctx', ends)]
    all_gather x1 -> x2, waiting for transfers between devices: 6.12 us -> 0.02 us  [gather(): value = lax.all_gather(value, ('dp', 'tp'), axis=0, tiled=False)]
    ppermute x6, waiting for transfers between devices: 5.62 us -> 0.02 us  [swap(): lax.ppermute(value, axis, [(i, i ^ k) for i in range(lax.axis_size(axis))])]
    pallas_call x4 -> x5, Pallas kernels: 34.3 us -> 36.4 us  [the longest x1 15.3 us: on_device(): call(functools.partial(flip_body, place_of, side), 'flip', 0, 6 * tokens...]
    unnamed x53 -> x51, local copies, waits for them, and re-layouts: 7.95 us -> 6.76 us
  transfers between devices with their start and end apart: 28 -> 29, of which waited for: 12 -> 11; matrix products, arithmetic and copies ran while one was open for 3% -> 3% of each run, Pallas kernels for 30% -> 32%
where the time goes in v4:
time: 319 us; the launch traced here: 317 us
  Pallas kernels  113 us (35%)
  starting transfers between devices  78 us (24%)
  waiting for transfers between devices  77.7 us (24%)
  blocking collectives  15.7 us (5%)
  between operations  14.6 us (5%)
  local copies, waits for them, and re-layouts  9.87 us (3%)
  other arithmetic  8.37 us (3%)
    ppermute x19, waiting for transfers between devices, shift(): return lax.ppermute(value, 'ctx', ends)  62.3 us
    ppermute x19, starting transfers between devices, shift(): return lax.ppermute(value, 'ctx', ends)  61.9 us
    pallas_call x4, Pallas kernels, on_device(): call(weight_body, 'weight', 2 * tokens * feats * quarter, 2 * tokens * (f...  22.2 us
    all_to_all x1, blocking collectives, on_device(): gated_far = lax.all_to_all(gated, 'dp', 0, 0, tiled=True)  15.7 us
    all_to_all x1, waiting for transfers between devices, on_device(): delta_far = lax.all_to_all(delta, 'dp', 0, 0, tiled=True)  15.4 us
    pallas_call x1, Pallas kernels, on_device(): call(functools.partial(flip_body, place_of, side), 'flip', 0, 6 * tokens...  15.3 us
    pallas_call x3, Pallas kernels, local(): call(functools.partial(local_body, transposed), 'local_t' if transposed e...  11.2 us
    pallas_call x1, Pallas kernels, on_device(): call(functools.partial(delta_body, side), 'delta', tokens * depth * quart...  9.62 us
  transfers between devices with their start and end apart: 29, of which 11 were waited for; matrix products, arithmetic and copies ran while one was open for 3% of the time, Pallas kernels for 32%

profile of v4, /device:TPU:0, one launch (start us, length us, event | category | flops | bytes accessed | tf_op | source)
XLA Modules:
  0.0 317.3 jit_solution(10625386482035512140)
XLA Ops:
  9.0 5.0 %collective-permute-start = (bf16[128,4096]{1,0:T(8,128)(2,1)S(1)}, bf16[128,4096]{1,0:T(8,128)(2,1)S(1)}, u32[]{:S(2)}, u32[]{:S(2)}) collective-permute-start(bf16[128,4096]{1,0:T(8,128)(2,1)S(1)} %multiply_convert_fusion.2.x), channel_id=1, source_target_pairs={{0,2},{2,4},{4,6},{1,3},{3,5},{5,7},{8,10},{10,12},{12,14},{9,11},... | collective-permute-start | bytes 3145736 | tf_op jit(solution)/shard_map/ppermute | solution.py:256
  14.0 5.0 %all-to-all-start = ((bf16[4,1024,512]{2,1,0:T(8,128)(2,1)}), bf16[4,1024,512]{2,1,0:T(8,128)(2,1)}, u32[]{:S(2)}, u32[]{:S(2)}) async-start(bf16[4,1024,512]{2,1,0:T(8,128)(2,1)} %bitcast.17), calls=%async_computation | async-start | bytes 8388608 | tf_op jit(solution)/shard_map/all_to_all | solution.py:261
  22.0 3.7 %multiply_convert_fusion = (bf16[384,4096]{1,0:T(8,128)(2,1)}, bf16[384,4096]{1,0:T(8,128)(2,1)}) fusion(f32[384]{0:T(512)S(1)} %get-tuple-element.44, f32[4096]{0:T(1024)S(1)} %neg.22, f32[4096]{0:T(1024)S(1)} %mul.110, f32[384]{0:T(512)S(1)} %get-tuple-element.45), kind=kLoop, calls=%fused_computation | loop fusion | flops 9437184 | bytes 6327296 | tf_op jit(solution)/shard_map/convert_element_type | solution.py:283
  26.5 4.2 %local.2.own_part = f32[128,4096]{1,0:T(8,128)} custom-call(f32[256,128]{1,0:T(8,128)S(1)} %pad_maximum_fusion.1.rows.taps, bf16[128,4096]{1,0:T(8,128)(2,1)S(1)} %multiply_convert_fusion.2.x, bf16[4096,128]{1,0:T(8,128)(2,1)S(1)} %get-tuple-element.43.refs_0_.ends_coef, bf16[4096,128]{1,0:T(8,128)(2,1)S(1)} %get-tuple-element.42.refs_1_.starts_coef, ...), custom_call_target="tpu_custom_call" | custom-call | flops 1073741824 | bytes 3145728 | tf_op jit(solution)/shard_map/local/pallas_call | solution.py:294
  30.8 5.5 %collective-permute-done.refs_4_.rim = bf16[128,4096]{1,0:T(8,128)(2,1)S(1)} collective-permute-done((bf16[128,4096]{1,0:T(8,128)(2,1)S(1)}, bf16[128,4096]{1,0:T(8,128)(2,1)S(1)}, u32[]{:S(2)}, u32[]{:S(2)}) %collective-permute-start) | collective-permute-done | bytes 1048608 | tf_op jit(solution)/shard_map/ppermute | solution.py:256
  36.3 5.6 %conv.1 = (bf16[128,4096]{1,0:T(8,128)(2,1)S(1)}, bf16[128,4096]{1,0:T(8,128)(2,1)S(1)}, bf16[16,4096]{1,0:T(8,128)(2,1)S(1)}) custom-call(bf16[128,4096]{1,0:T(8,128)(2,1)S(1)} %collective-permute-done.refs_4_.rim, f32[128,4096]{1,0:T(8,128)} %local.2.own_part, bf16[128,4096]{1,0:T(8,128)(2,1)} %query.3, f32[256,128]{1,0:T(8,128)S(1)} %pad_maximum_fusion.1.rows.taps, ...), custom_call_target="tpu_custom_call" | custom-call | flops 1073741824 | bytes 7340032 | tf_op jit(solution)/shard_map/conv/pallas_call | solution.py:307
  41.9 4.4 %collective-permute-start.4 = (bf16[16,4096]{1,0:T(8,128)(2,1)S(1)}, bf16[16,4096]{1,0:T(8,128)(2,1)S(1)}, u32[]{:S(2)}, u32[]{:S(2)}) collective-permute-start(bf16[16,4096]{1,0:T(8,128)(2,1)S(1)} %get-tuple-element.27), channel_id=1, source_target_pairs={{0,2},{2,4},{4,6},{1,3},{3,5},{5,7},{8,10},{10,12},{12,14},{9,11},... | collective-permute-start | bytes 393224 | tf_op jit(solution)/shard_map/ppermute | solution.py:256
  53.6 3.6 %collective-permute-start.5 = (bf16[16,4096]{1,0:T(8,128)(2,1)S(1)}, bf16[16,4096]{1,0:T(8,128)(2,1)S(1)}, u32[]{:S(2)}, u32[]{:S(2)}) collective-permute-start(bf16[16,4096]{1,0:T(8,128)(2,1)S(1)} %get-tuple-element.27), channel_id=1, source_target_pairs={{0,4},{2,6},{1,5},{3,7},{8,12},{10,14},{9,13},{11,15},{16,20},{18,... | collective-permute-start | bytes 393224 | tf_op jit(solution)/shard_map/ppermute | solution.py:256
  62.4 8.4 %collective-permute-done.5.refs_5_.refs_1_ = bf16[16,4096]{1,0:T(8,128)(2,1)S(1)} collective-permute-done((bf16[16,4096]{1,0:T(8,128)(2,1)S(1)}, bf16[16,4096]{1,0:T(8,128)(2,1)S(1)}, u32[]{:S(2)}, u32[]{:S(2)}) %collective-permute-start.5) | collective-permute-done | bytes 131104 | tf_op jit(solution)/shard_map/ppermute | solution.py:256
  76.2 4.2 %long.1 = (bf16[128,4096]{1,0:T(8,128)(2,1)S(1)}, bf16[4,128,1024]{2,1,0:T(8,128)(2,1)S(1)}) custom-call(f32[128,4096]{1,0:T(8,128)} %copy-done.5, bf16[384,4096]{1,0:T(8,128)(2,1)} %get-tuple-element.41.refs_2_.coef, bf16[128,4096]{1,0:T(8,128)(2,1)} %gate.3, bf16[16,4096]{1,0:T(8,128)(2,1)S(1)} %collective-permute-done.4.refs_4_.refs_0_, ...), custom_call_target="tpu_custom_call" | custom-call | flops 134217728 | bytes 5242880 | tf_op jit(solution)/shard_map/long/pallas_call | solution.py:336
  80.3 15.7 %all_to_all.15.own = bf16[4,128,1024]{2,1,0:T(8,128)(2,1)S(1)} all-to-all(bf16[4,128,1024]{2,1,0:T(8,128)(2,1)S(1)} %get-tuple-element.28), channel_id=1, replica_groups=mesh['dp'=4,'ctx'=4,'tp'=2] {'dp'}, dimensions={0} | all-to-all | bytes 2097152 | tf_op jit(solution)/shard_map/all_to_all | solution.py:343
  96.0 19.7 %collective-permute-start.7 = (bf16[4,128,1024]{2,1,0:T(8,128)(2,1)S(1)}, bf16[4,128,1024]{2,1,0:T(8,128)(2,1)}, u32[]{:S(2)}, u32[]{:S(2)}) collective-permute-start(bf16[4,128,1024]{2,1,0:T(8,128)(2,1)S(1)} %all_to_all.15.own), channel_id=1, source_target_pairs={{0,2},{2,4},{4,6},{1,3},{3,5},{5,7},{8,10},{10,12},{12,14},{9,11},... | collective-permute-start | bytes 3145736 | tf_op jit(solution)/shard_map/ppermute | solution.py:256
  117.0 17.7 %collective-permute-done.7.refs_0_ = bf16[4,128,1024]{2,1,0:T(8,128)(2,1)} collective-permute-done((bf16[4,128,1024]{2,1,0:T(8,128)(2,1)S(1)}, bf16[4,128,1024]{2,1,0:T(8,128)(2,1)}, u32[]{:S(2)}, u32[]{:S(2)}) %collective-permute-start.7) | collective-permute-done | bytes 1048608 | tf_op jit(solution)/shard_map/ppermute | solution.py:256
  135.4 4.5 %collective-permute-done.8.refs_1_.refs_5_ = bf16[4,128,1024]{2,1,0:T(8,128)(2,1)} collective-permute-done((bf16[4,128,1024]{2,1,0:T(8,128)(2,1)S(1)}, bf16[4,128,1024]{2,1,0:T(8,128)(2,1)}, u32[]{:S(2)}, u32[]{:S(2)}) %collective-permute-start.8) | collective-permute-done | bytes 1048608 | tf_op jit(solution)/shard_map/ppermute | solution.py:256
  141.2 8.6 %delta.2.refs_0_.partial_right.partial_left = bf16[2,4,128,1024]{3,2,1,0:T(8,128)(2,1)} custom-call(bf16[4,2,2,64,2048]{4,3,2,1,0:T(8,128)(2,1)} %bitcast.18, bf16[4,1024,512]{2,1,0:T(8,128)(2,1)} %all-to-all-done.refs_2_.weights, bf16[4,128,1024]{2,1,0:T(8,128)(2,1)} %collective-permute-done.7.refs_0_, ...), custom_call_target="tpu_custom_call" | custom-call | flops 4294967296 | bytes 10485760 | tf_op jit(solution)/shard_map/delta/pallas_call | solution.py:357
  153.7 5.5 %collective-permute-start.9 = (bf16[1,4,128,1024]{3,2,1,0:T(8,128)(2,1)}, bf16[1,4,128,1024]{3,2,1,0:T(8,128)(2,1)}, u32[]{:S(2)}, u32[]{:S(2)}) collective-permute-start(bf16[1,4,128,1024]{3,2,1,0:T(8,128)(2,1)} %constant_dynamic-slice_fusion), channel_id=1, source_target_pairs={{0,2},{1,3},{8,10},{9,11},{16,18},{17,19},{24,26},{25,27}} | collective-permute-start | bytes 3145736 | tf_op jit(solution)/shard_map/ppermute | solution.py:256
  164.7 12.7 %collective-permute-done.9.right = bf16[1,4,128,1024]{3,2,1,0:T(8,128)(2,1)} collective-permute-done((bf16[1,4,128,1024]{3,2,1,0:T(8,128)(2,1)}, bf16[1,4,128,1024]{3,2,1,0:T(8,128)(2,1)}, u32[]{:S(2)}, u32[]{:S(2)}) %collective-permute-start.9) | collective-permute-done | bytes 1048608 | tf_op jit(solution)/shard_map/ppermute | solution.py:256
  177.5 4.7 %add.74 = (bf16[1,4,128,1024]{3,2,1,0:T(8,128)(2,1)}, bf16[1,4,128,1024]{3,2,1,0:T(8,128)(2,1)}) custom-call(s32[2]{0:T(128)S(1)} %add_maximum_fusion.dests, bf16[2,4,128,1024]{3,2,1,0:T(8,128)(2,1)} %delta.2.refs_0_.partial_right.partial_left, bf16[2,4,128,1024]{3,2,1,0:T(8,128)(2,1)} %delta.2.refs_0_.partial_right.partial_left, ...), custom_call_target="tpu_custom_call" | custom-call | bytes 6291456 | tf_op jit(solution)/shard_map/add/pallas_call | solution.py:417
  182.2 5.4 %collective-permute-start.13 = (bf16[1,4,128,1024]{3,2,1,0:T(8,128)(2,1)}, bf16[1,4,128,1024]{3,2,1,0:T(8,128)(2,1)}, u32[]{:S(2)}, u32[]{:S(2)}) collective-permute-start(bf16[1,4,128,1024]{3,2,1,0:T(8,128)(2,1)} %get-tuple-element.29), channel_id=1, source_target_pairs={{0,2},{2,4},{1,3},{3,5},{8,10},{10,12},{9,11},{11,13},{16,18},{18,... | collective-permute-start | bytes 3145736 | tf_op jit(solution)/shard_map/ppermute | solution.py:256
  189.3 9.6 %delta.3.after.partial_right.partial_left.partial = bf16[4,4,128,1024]{3,2,1,0:T(8,128)(2,1)} custom-call(bf16[4,2,2,64,2048]{4,3,2,1,0:T(8,128)(2,1)} %bitcast.20, bf16[4,1024,512]{2,1,0:T(8,128)(2,1)} %all-to-all-done.refs_2_.weights, bf16[2,4,128,1024]{3,2,1,0:T(8,128)(2,1)S(1)} %copy-done.2), custom_call_target="tpu_custom_call" | custom-call | flops 4294967296 | bytes 14680064 | tf_op jit(solution)/shard_map/delta/pallas_call | solution.py:365
  198.9 15.3 %flip.1.refs_2_.grad_t = bf16[2048,2048]{1,0:T(8,128)(2,1)} custom-call(s32[3]{0:T(128)S(1)} %pad_add_fusion.place, bf16[4,2,2,64,2048]{4,3,2,1,0:T(8,128)(2,1)} %bitcast.19, bf16[4,2,2,64,2048]{4,3,2,1,0:T(8,128)(2,1)} %bitcast.21, bf16[4,4,128,1024]{3,2,1,0:T(8,128)(2,1)} %delta.3.after.partial_right.partial_left.partial), custom_call_target="tpu_custom_call" | custom-call | bytes 25165824 | tf_op jit(solution)/shard_map/flip/pallas_call | solution.py:380
  214.3 3.6 %add.75 = (bf16[1,4,128,1024]{3,2,1,0:T(8,128)(2,1)S(1)}, bf16[1,4,128,1024]{3,2,1,0:T(8,128)(2,1)S(1)}) custom-call(s32[2]{0:T(128)S(1)} %fusion.5.dests, bf16[4,4,128,1024]{3,2,1,0:T(8,128)(2,1)} %delta.3.after.partial_right.partial_left.partial, bf16[4,4,128,1024]{3,2,1,0:T(8,128)(2,1)} %delta.3.after.partial_right.partial_left.partial, ...), custom_call_target="tpu_custom_call" | custom-call | bytes 6291456 | tf_op jit(solution)/shard_map/add/pallas_call | solution.py:417
  221.0 5.0 %merge.1 = bf16[4,4,128,1024]{3,2,1,0:T(8,128)(2,1)} custom-call(bf16[4,128,1024]{2,1,0:T(8,128)(2,1)S(1)} %copy-done.13, bf16[4,128,1024]{2,1,0:T(8,128)(2,1)} %collective-permute-done.7.refs_0_, bf16[4,128,1024]{2,1,0:T(8,128)(2,1)S(1)} %copy-done.7, bf16[4,128,1024]{2,1,0:T(8,128)(2,1)} %collective-permute-done.15.refs_0_.refs_2_, ...), custom_call_target="tpu_custom_call" | custom-call | bytes 11534336 | tf_op jit(solution)/shard_map/merge/pallas_call | solution.py:429
  227.2 6.1 %weight.4.after = bf16[512,1024]{1,0:T(8,128)(2,1)} custom-call(s32[3]{0:T(128)S(1)} %pad_add_fusion.place, bf16[2048,2048]{1,0:T(8,128)(2,1)} %flip.1.refs_2_.grad_t, bf16[2048,1024]{1,0:T(8,128)(2,1)} %bitcast.13, bf16[1,4,128,1024]{3,2,1,0:T(8,128)(2,1)S(1)} %copy-done.11), custom_call_target="tpu_custom_call" | custom-call | flops 2147483648 | bytes 6291456 | tf_op jit(solution)/shard_map/weight/pallas_call | solution.py:438
  233.4 5.4 %weight.5.after.refs_0_ = bf16[512,1024]{1,0:T(8,128)(2,1)S(1)} custom-call(s32[3]{0:T(128)S(1)} %pad_add_fusion.place, bf16[2048,2048]{1,0:T(8,128)(2,1)} %flip.1.refs_2_.grad_t, bf16[2048,1024]{1,0:T(8,128)(2,1)} %bitcast.14, bf16[512,1024]{1,0:T(8,128)(2,1)} %weight.4.after), custom_call_target="tpu_custom_call" | custom-call | flops 2147483648 | bytes 6291456 | tf_op jit(solution)/shard_map/weight/pallas_call | solution.py:438
  252.6 5.4 %weight.6.after.refs_0_ = bf16[512,1024]{1,0:T(8,128)(2,1)S(1)} custom-call(s32[3]{0:T(128)S(1)} %pad_add_fusion.place, bf16[2048,2048]{1,0:T(8,128)(2,1)} %flip.1.refs_2_.grad_t, bf16[2048,1024]{1,0:T(8,128)(2,1)} %bitcast.15, bf16[512,1024]{1,0:T(8,128)(2,1)S(1)} %copy-done.1), custom_call_target="tpu_custom_call" | custom-call | flops 2147483648 | bytes 6291456 | tf_op jit(solution)/shard_map/weight/pallas_call | solution.py:438
  257.9 5.4 %weight.7.refs_0_ = bf16[512,1024]{1,0:T(8,128)(2,1)S(1)} custom-call(s32[3]{0:T(128)S(1)} %pad_add_fusion.place, bf16[2048,2048]{1,0:T(8,128)(2,1)} %flip.1.refs_2_.grad_t, bf16[2048,1024]{1,0:T(8,128)(2,1)} %bitcast.16, bf16[512,1024]{1,0:T(8,128)(2,1)S(1)} %weight.6.after.refs_0_), custom_call_target="tpu_custom_call" | custom-call | flops 2147483648 | bytes 6291456 | tf_op jit(solution)/shard_map/weight/pallas_call | solution.py:438
  264.3 15.4 %all-to-all-done.2.delta.refs_1_ = bf16[4,128,1024]{2,1,0:T(8,128)(2,1)S(1)} async-done(((bf16[4,128,1024]{2,1,0:T(8,128)(2,1)}), bf16[4,128,1024]{2,1,0:T(8,128)(2,1)S(1)}, u32[]{:S(2)}, u32[]{:S(2)}) %all-to-all-start.2) | async-done | bytes 1048608 | tf_op jit(solution)/shard_map/all_to_all | solution.py:461
  280.9 4.3 %seed.1 = (bf16[128,4096]{1,0:T(8,128)(2,1)S(1)}, bf16[16,4096]{1,0:T(8,128)(2,1)S(1)}, bf16[128,4096]{1,0:T(8,128)(2,1)}) custom-call(bf16[4,128,1024]{2,1,0:T(8,128)(2,1)S(1)} %all-to-all-done.2.delta.refs_1_, bf16[128,4096]{1,0:T(8,128)(2,1)S(1)} %copy-done.14, bf16[128,4096]{1,0:T(8,128)(2,1)} %copy-done.17, bf16[4096,128]{1,0:T(8,128)(2,1)} %copy-done.3, ...), custom_call_target="tpu_custom_call" | custom-call | flops 134217728 | bytes 5242880 | tf_op jit(solution)/shard_map/seed/pallas_call | solution.py:475
  287.8 4.3 %collective-permute-done.19.refs_0_ = bf16[16,4096]{1,0:T(8,128)(2,1)S(1)} collective-permute-done((bf16[16,4096]{1,0:T(8,128)(2,1)S(1)}, bf16[16,4096]{1,0:T(8,128)(2,1)S(1)}, u32[]{:S(2)}, u32[]{:S(2)}) %collective-permute-start.19) | collective-permute-done | bytes 131104 | tf_op jit(solution)/shard_map/ppermute | solution.py:256
  300.8 5.2 %back.1 = (bf16[128,4096]{1,0:T(8,128)(2,1)}, bf16[128,4096]{1,0:T(8,128)(2,1)}) custom-call(f32[128,4096]{1,0:T(8,128)} %copy-done.16, bf16[384,4096]{1,0:T(8,128)(2,1)} %get-tuple-element.40.refs_3_.coef, bf16[128,4096]{1,0:T(8,128)(2,1)S(1)} %copy-done.19, bf16[128,4096]{1,0:T(8,128)(2,1)S(1)} %copy-done.15, ...), custom_call_target="tpu_custom_call" | custom-call | flops 134217728 | bytes 6291456 | tf_op jit(solution)/shard_map/back/pallas_call | solution.py:487
  306.0 4.5 %lay.1 = bf16[512,4096]{1,0:T(8,128)(2,1)} custom-call(s32[3]{0:T(128)S(1)} %pad_add_fusion.place, bf16[512,1024]{1,0:T(8,128)(2,1)S(1)} %copy-done.9, bf16[512,1024]{1,0:T(8,128)(2,1)S(1)} %collective-permute-done.22.refs_1_, bf16[512,1024]{1,0:T(8,128)(2,1)S(1)} %collective-permute-done.23.refs_2_, bf16[512,1024]{1,0:T(8,128)(2,1)} %collective-permute-done.24.refs_3_, ...), custom_call_target="tpu_custom_call" | custom-call | bytes 8388608 | tf_op jit(solution)/shard_map/lay/pallas_call | solution.py:497
  (125 shorter events, 69.3 us)
Async XLA Ops:
  9.0 27.3 %collective-permute-start = (bf16[128,4096]{1,0:T(8,128)(2,1)S(1)}, bf16[128,4096]{1,0:T(8,128)(2,1)S(1)}, u32[]{:S(2)}, u32[]{:S(2)}) collective-permute-start(bf16[128,4096]{1,0:T(8,128)(2,1)S(1)} %multiply_convert_fusion.2.x), channel_id=1, source_target_pairs={{0,2},{2,4},{4,6},{1,3},{3,5},{5,7},{8,10},{10,12},{12,14},{9,11},... | collective-permute-start | bytes 3145736 | tf_op jit(solution)/shard_map/ppermute | solution.py:256
  14.0 58.2 %all-to-all-start = ((bf16[4,1024,512]{2,1,0:T(8,128)(2,1)}), bf16[4,1024,512]{2,1,0:T(8,128)(2,1)}, u32[]{:S(2)}, u32[]{:S(2)}) async-start(bf16[4,1024,512]{2,1,0:T(8,128)(2,1)} %bitcast.17), calls=%async_computation | async-start | bytes 8388608 | tf_op jit(solution)/shard_map/all_to_all | solution.py:261
  19.0 122.2 %all-gather.7.cloned.1.call-start = ((), (), s32[]{:S(2)}) async-start(), calls=%async_computation.4 | async-start | bytes 4718592 | tf_op jit(solution)/shard_map/all_gather | solution.py:330
  41.9 15.3 %collective-permute-start.4 = (bf16[16,4096]{1,0:T(8,128)(2,1)S(1)}, bf16[16,4096]{1,0:T(8,128)(2,1)S(1)}, u32[]{:S(2)}, u32[]{:S(2)}) collective-permute-start(bf16[16,4096]{1,0:T(8,128)(2,1)S(1)} %get-tuple-element.27), channel_id=1, source_target_pairs={{0,2},{2,4},{4,6},{1,3},{3,5},{5,7},{8,10},{10,12},{12,14},{9,11},... | collective-permute-start | bytes 393224 | tf_op jit(solution)/shard_map/ppermute | solution.py:256
  49.1 23.1 %copy-start.20 = (bf16[64,2048]{1,0:T(8,128)(2,1)}, bf16[64,2048]{1,0:T(8,128)(2,1)S(1)}, u32[]{:S(2)}) copy-start(bf16[64,2048]{1,0:T(8,128)(2,1)S(1)} %get-tuple-element.22.refs_0_) | copy-start | bytes 786436
  49.1 23.1 %collective-permute-start.1 = (bf16[64,2048]{1,0:T(8,128)(2,1)S(1)}, bf16[64,2048]{1,0:T(8,128)(2,1)S(1)}, u32[]{:S(2)}, u32[]{:S(2)}) collective-permute-start(bf16[64,2048]{1,0:T(8,128)(2,1)S(1)} %get-tuple-element.23), channel_id=1, source_target_pairs={{0,2},{2,0},{4,6},{6,4},{1,3},{3,1},{5,7},{7,5},{8,10},{10,8},{12,... | collective-permute-start | bytes 786440 | tf_op jit(solution)/shard_map/ppermute | solution.py:252
  50.8 21.4 %collective-permute-start.2 = (bf16[64,2048]{1,0:T(8,128)(2,1)S(1)}, bf16[64,2048]{1,0:T(8,128)(2,1)S(1)}, u32[]{:S(2)}, u32[]{:S(2)}) collective-permute-start(bf16[64,2048]{1,0:T(8,128)(2,1)S(1)} %get-tuple-element.24), channel_id=1, source_target_pairs={{0,4},{2,6},{4,0},{6,2},{1,5},{3,7},{5,1},{7,3},{8,12},{10,14},{12... | collective-permute-start | bytes 786440 | tf_op jit(solution)/shard_map/ppermute | solution.py:252
  51.9 20.3 %collective-permute-start.3 = (bf16[64,2048]{1,0:T(8,128)(2,1)S(1)}, bf16[64,2048]{1,0:T(8,128)(2,1)S(1)}, u32[]{:S(2)}, u32[]{:S(2)}) collective-permute-start(bf16[64,2048]{1,0:T(8,128)(2,1)S(1)} %get-tuple-element.25), channel_id=1, source_target_pairs={{0,6},{2,4},{4,2},{6,0},{1,7},{3,5},{5,3},{7,1},{8,14},{10,12},{12... | collective-permute-start | bytes 786440 | tf_op jit(solution)/shard_map/ppermute | solution.py:252
  53.6 17.2 %collective-permute-start.5 = (bf16[16,4096]{1,0:T(8,128)(2,1)S(1)}, bf16[16,4096]{1,0:T(8,128)(2,1)S(1)}, u32[]{:S(2)}, u32[]{:S(2)}) collective-permute-start(bf16[16,4096]{1,0:T(8,128)(2,1)S(1)} %get-tuple-element.27), channel_id=1, source_target_pairs={{0,4},{2,6},{1,5},{3,7},{8,12},{10,14},{9,13},{11,15},{16,20},{18,... | collective-permute-start | bytes 393224 | tf_op jit(solution)/shard_map/ppermute | solution.py:256
  57.2 15.0 %collective-permute-start.6 = (bf16[16,4096]{1,0:T(8,128)(2,1)S(1)}, bf16[16,4096]{1,0:T(8,128)(2,1)S(1)}, u32[]{:S(2)}, u32[]{:S(2)}) collective-permute-start(bf16[16,4096]{1,0:T(8,128)(2,1)S(1)} %get-tuple-element.27), channel_id=1, source_target_pairs={{0,6},{1,7},{8,14},{9,15},{16,22},{17,23},{24,30},{25,31}} | collective-permute-start | bytes 393224 | tf_op jit(solution)/shard_map/ppermute | solution.py:256
  73.7 115.6 %all-gather.5.cloned.1.call-start = ((), (), s32[]{:S(2)}) async-start(), calls=%async_computation.3 | async-start | bytes 4718592 | tf_op jit(solution)/shard_map/all_gather | solution.py:330
  96.0 53.8 %copy-start.12 = (bf16[4,128,1024]{2,1,0:T(8,128)(2,1)}, bf16[4,128,1024]{2,1,0:T(8,128)(2,1)S(1)}, u32[]{:S(2)}) copy-start(bf16[4,128,1024]{2,1,0:T(8,128)(2,1)S(1)} %all_to_all.15.own) | copy-start | bytes 3145732
  96.0 38.7 %collective-permute-start.7 = (bf16[4,128,1024]{2,1,0:T(8,128)(2,1)S(1)}, bf16[4,128,1024]{2,1,0:T(8,128)(2,1)}, u32[]{:S(2)}, u32[]{:S(2)}) collective-permute-start(bf16[4,128,1024]{2,1,0:T(8,128)(2,1)S(1)} %all_to_all.15.own), channel_id=1, source_target_pairs={{0,2},{2,4},{4,6},{1,3},{3,5},{5,7},{8,10},{10,12},{12,14},{9,11},... | collective-permute-start | bytes 3145736 | tf_op jit(solution)/shard_map/ppermute | solution.py:256
  115.7 24.2 %collective-permute-start.8 = (bf16[4,128,1024]{2,1,0:T(8,128)(2,1)S(1)}, bf16[4,128,1024]{2,1,0:T(8,128)(2,1)}, u32[]{:S(2)}, u32[]{:S(2)}) collective-permute-start(bf16[4,128,1024]{2,1,0:T(8,128)(2,1)S(1)} %all_to_all.15.own), channel_id=1, source_target_pairs={{2,0},{4,2},{6,4},{3,1},{5,3},{7,5},{10,8},{12,10},{14,12},{11,9},... | collective-permute-start | bytes 3145736 | tf_op jit(solution)/shard_map/ppermute | solution.py:256
  134.7 24.6 %collective-permute-start.11 = (bf16[4,128,1024]{2,1,0:T(8,128)(2,1)}, bf16[4,128,1024]{2,1,0:T(8,128)(2,1)S(1)}, u32[]{:S(2)}, u32[]{:S(2)}) collective-permute-start(bf16[4,128,1024]{2,1,0:T(8,128)(2,1)} %collective-permute-done.7.refs_0_), channel_id=1, source_target_pairs={{2,4},{4,6},{3,5},{5,7},{10,12},{12,14},{11,13},{13,15},{18,20},{2... | collective-permute-start | bytes 3145736 | tf_op jit(solution)/shard_map/ppermute | solution.py:256
  139.9 23.5 %collective-permute-start.12 = (bf16[4,128,1024]{2,1,0:T(8,128)(2,1)}, bf16[4,128,1024]{2,1,0:T(8,128)(2,1)}, u32[]{:S(2)}, u32[]{:S(2)}) collective-permute-start(bf16[4,128,1024]{2,1,0:T(8,128)(2,1)} %collective-permute-done.8.refs_1_.refs_5_), channel_id=1, source_target_pairs={{2,0},{4,2},{3,1},{5,3},{10,8},{12,10},{11,9},{13,11},{18,16},{20,... | collective-permute-start | bytes 3145736 | tf_op jit(solution)/shard_map/ppermute | solution.py:256
  152.1 12.7 %collective-permute-start.10 = (bf16[1,4,128,1024]{3,2,1,0:T(8,128)(2,1)}, bf16[1,4,128,1024]{3,2,1,0:T(8,128)(2,1)}, u32[]{:S(2)}, u32[]{:S(2)}) collective-permute-start(bf16[1,4,128,1024]{3,2,1,0:T(8,128)(2,1)} %constant_dynamic-slice_fusion), channel_id=1, source_target_pairs={{6,4},{7,5},{14,12},{15,13},{22,20},{23,21},{30,28},{31,29}} | collective-permute-start | bytes 3145736 | tf_op jit(solution)/shard_map/ppermute | solution.py:256
  153.7 23.8 %collective-permute-start.9 = (bf16[1,4,128,1024]{3,2,1,0:T(8,128)(2,1)}, bf16[1,4,128,1024]{3,2,1,0:T(8,128)(2,1)}, u32[]{:S(2)}, u32[]{:S(2)}) collective-permute-start(bf16[1,4,128,1024]{3,2,1,0:T(8,128)(2,1)} %constant_dynamic-slice_fusion), channel_id=1, source_target_pairs={{0,2},{1,3},{8,10},{9,11},{16,18},{17,19},{24,26},{25,27}} | collective-permute-start | bytes 3145736 | tf_op jit(solution)/shard_map/ppermute | solution.py:256
  159.4 29.9 %copy-start.2 = (bf16[2,4,128,1024]{3,2,1,0:T(8,128)(2,1)S(1)}, bf16[2,4,128,1024]{3,2,1,0:T(8,128)(2,1)}, u32[]{:S(2)}) copy-start(bf16[2,4,128,1024]{3,2,1,0:T(8,128)(2,1)} %delta.2.refs_0_.partial_right.partial_left) | copy-start | bytes 6291460
  159.4 54.8 %collective-permute-start.15 = (bf16[4,128,1024]{2,1,0:T(8,128)(2,1)S(1)}, bf16[4,128,1024]{2,1,0:T(8,128)(2,1)}, u32[]{:S(2)}, u32[]{:S(2)}) collective-permute-start(bf16[4,128,1024]{2,1,0:T(8,128)(2,1)S(1)} %collective-permute-done.11.refs_0_.refs_1_), channel_id=1, source_target_pairs={{4,6},{5,7},{12,14},{13,15},{20,22},{21,23},{28,30},{29,31}} | collective-permute-start | bytes 3145736 | tf_op jit(solution)/shard_map/ppermute | solution.py:256
  163.4 50.8 %collective-permute-start.16 = (bf16[4,128,1024]{2,1,0:T(8,128)(2,1)}, bf16[4,128,1024]{2,1,0:T(8,128)(2,1)}, u32[]{:S(2)}, u32[]{:S(2)}) collective-permute-start(bf16[4,128,1024]{2,1,0:T(8,128)(2,1)} %collective-permute-done.12.refs_1_.refs_4_), channel_id=1, source_target_pairs={{2,0},{3,1},{10,8},{11,9},{18,16},{19,17},{26,24},{27,25}} | collective-permute-start | bytes 3145736 | tf_op jit(solution)/shard_map/ppermute | solution.py:256
  182.2 32.0 %collective-permute-start.13 = (bf16[1,4,128,1024]{3,2,1,0:T(8,128)(2,1)}, bf16[1,4,128,1024]{3,2,1,0:T(8,128)(2,1)}, u32[]{:S(2)}, u32[]{:S(2)}) collective-permute-start(bf16[1,4,128,1024]{3,2,1,0:T(8,128)(2,1)} %get-tuple-element.29), channel_id=1, source_target_pairs={{0,2},{2,4},{1,3},{3,5},{8,10},{10,12},{9,11},{11,13},{16,18},{18,... | collective-permute-start | bytes 3145736 | tf_op jit(solution)/shard_map/ppermute | solution.py:256
  187.6 26.7 %collective-permute-start.14 = (bf16[1,4,128,1024]{3,2,1,0:T(8,128)(2,1)}, bf16[1,4,128,1024]{3,2,1,0:T(8,128)(2,1)}, u32[]{:S(2)}, u32[]{:S(2)}) collective-permute-start(bf16[1,4,128,1024]{3,2,1,0:T(8,128)(2,1)} %get-tuple-element.30), channel_id=1, source_target_pairs={{4,2},{6,4},{5,3},{7,5},{12,10},{14,12},{13,11},{15,13},{20,18},{2... | collective-permute-start | bytes 3145736 | tf_op jit(solution)/shard_map/ppermute | solution.py:256
  217.9 21.8 %collective-permute-start.17 = (bf16[1,4,128,1024]{3,2,1,0:T(8,128)(2,1)S(1)}, bf16[1,4,128,1024]{3,2,1,0:T(8,128)(2,1)S(1)}, u32[]{:S(2)}, u32[]{:S(2)}) collective-permute-start(bf16[1,4,128,1024]{3,2,1,0:T(8,128)(2,1)S(1)} %get-tuple-element.31.refs_6_.after), channel_id=1, source_target_pairs={{0,2},{2,4},{4,6},{1,3},{3,5},{5,7},{8,10},{10,12},{12,14},{9,11},... | collective-permute-start | bytes 3145736 | tf_op jit(solution)/shard_map/ppermute | solution.py:256
  219.7 22.9 %collective-permute-start.18 = (bf16[1,4,128,1024]{3,2,1,0:T(8,128)(2,1)S(1)}, bf16[1,4,128,1024]{3,2,1,0:T(8,128)(2,1)S(1)}, u32[]{:S(2)}, u32[]{:S(2)}) collective-permute-start(bf16[1,4,128,1024]{3,2,1,0:T(8,128)(2,1)S(1)} %get-tuple-element.32), channel_id=1, source_target_pairs={{2,0},{4,2},{6,4},{3,1},{5,3},{7,5},{10,8},{12,10},{14,12},{11,9},... | collective-permute-start | bytes 3145736 | tf_op jit(solution)/shard_map/ppermute | solution.py:256
  246.1 33.5 %all-to-all-start.2 = ((bf16[4,128,1024]{2,1,0:T(8,128)(2,1)}), bf16[4,128,1024]{2,1,0:T(8,128)(2,1)S(1)}, u32[]{:S(2)}, u32[]{:S(2)}) async-start(bf16[4,128,1024]{2,1,0:T(8,128)(2,1)} %sum.1.after), calls=%async_computation.2 | async-start | bytes 2097152 | tf_op jit(solution)/shard_map/all_to_all | solution.py:461
  249.7 56.3 %collective-permute-start.24 = (bf16[512,1024]{1,0:T(8,128)(2,1)}, bf16[512,1024]{1,0:T(8,128)(2,1)}, u32[]{:S(2)}, u32[]{:S(2)}) collective-permute-start(bf16[512,1024]{1,0:T(8,128)(2,1)} %weight.4.after), channel_id=1, source_target_pairs={{0,24},{8,16},{16,8},{24,0},{1,25},{9,17},{17,9},{25,1},{2,26},{10... | collective-permute-start | bytes 3145736 | tf_op jit(solution)/shard_map/ppermute | solution.py:252
  279.6 26.3 %collective-permute-start.23 = (bf16[512,1024]{1,0:T(8,128)(2,1)S(1)}, bf16[512,1024]{1,0:T(8,128)(2,1)S(1)}, u32[]{:S(2)}, u32[]{:S(2)}) collective-permute-start(bf16[512,1024]{1,0:T(8,128)(2,1)S(1)} %hold.3), channel_id=1, source_target_pairs={{0,16},{8,24},{16,0},{24,8},{1,17},{9,25},{17,1},{25,9},{2,18},{10... | collective-permute-start | bytes 3145736 | tf_op jit(solution)/shard_map/ppermute | solution.py:252
  279.6 26.3 %collective-permute-start.22 = (bf16[512,1024]{1,0:T(8,128)(2,1)S(1)}, bf16[512,1024]{1,0:T(8,128)(2,1)S(1)}, u32[]{:S(2)}, u32[]{:S(2)}) collective-permute-start(bf16[512,1024]{1,0:T(8,128)(2,1)S(1)} %hold.2), channel_id=1, source_target_pairs={{0,8},{8,0},{16,24},{24,16},{1,9},{9,1},{17,25},{25,17},{2,10},{10... | collective-permute-start | bytes 3145736 | tf_op jit(solution)/shard_map/ppermute | solution.py:252
  285.1 7.0 %collective-permute-start.19 = (bf16[16,4096]{1,0:T(8,128)(2,1)S(1)}, bf16[16,4096]{1,0:T(8,128)(2,1)S(1)}, u32[]{:S(2)}, u32[]{:S(2)}) collective-permute-start(bf16[16,4096]{1,0:T(8,128)(2,1)S(1)} %get-tuple-element.36), channel_id=1, source_target_pairs={{2,0},{4,2},{6,4},{3,1},{5,3},{7,5},{10,8},{12,10},{14,12},{11,9},... | collective-permute-start | bytes 393224 | tf_op jit(solution)/shard_map/ppermute | solution.py:256
  286.5 11.7 %collective-permute-start.20 = (bf16[16,4096]{1,0:T(8,128)(2,1)S(1)}, bf16[16,4096]{1,0:T(8,128)(2,1)S(1)}, u32[]{:S(2)}, u32[]{:S(2)}) collective-permute-start(bf16[16,4096]{1,0:T(8,128)(2,1)S(1)} %get-tuple-element.36), channel_id=1, source_target_pairs={{4,0},{6,2},{5,1},{7,3},{12,8},{14,10},{13,9},{15,11},{20,16},{22,... | collective-permute-start | bytes 393224 | tf_op jit(solution)/shard_map/ppermute | solution.py:256
  292.1 8.6 %collective-permute-start.21 = (bf16[16,4096]{1,0:T(8,128)(2,1)S(1)}, bf16[16,4096]{1,0:T(8,128)(2,1)S(1)}, u32[]{:S(2)}, u32[]{:S(2)}) collective-permute-start(bf16[16,4096]{1,0:T(8,128)(2,1)S(1)} %get-tuple-element.36), channel_id=1, source_target_pairs={{6,0},{7,1},{14,8},{15,9},{22,16},{23,17},{30,24},{31,25}} | collective-permute-start | bytes 393224 | tf_op jit(solution)/shard_map/ppermute | solution.py:256
  (22 other events, 151.0 us)
Sparse Core Ops, SparseCore 0:
  73.8 56.8 all-gather.6
  132.6 36.7 all-gather.4

commit v5 on v4

--- a/solution.py
+++ b/solution.py
@@ -139,9 +139,8 @@
         conv_grad[:, cols] = (out * query[:, cols].astype(F32)).astype(BF16)
 
 
-def pack_body(place, *refs):
-    count = len(refs) // 2
-    for source, target in zip(refs[:count], refs[count + 1 :]):
+def pack_body(count, place, *refs):
+    for source, target in zip(refs[:count], refs[-count:]):
         target[...] = source[...]
 
 
@@ -261,16 +260,6 @@
     weights = lax.all_to_all(proj_weight.reshape(n_dp, quarter, feats), "dp", 0, 0, tiled=True)
     product = (key_in.astype(F32) * value_in.astype(F32)).astype(BF16)
     rim = shift(product, 1)
-    mine = call(
-        pack_body, "pack", 0, 4 * part * depth * n_ctx,
-        grid_spec=pltpu.PrefetchScalarGridSpec(
-            num_scalar_prefetch=1, grid=(n_dp,),
-            in_specs=[piece(k) for k in range(n_ctx)] + [ANY],
-            out_specs=[pl.BlockSpec((part, feats), lambda j, p: (0, j))] * n_ctx,
-        ),
-        out_shape=[shape(part, depth)] * n_ctx,
-    )(place, *[out_grad] * n_ctx, rim)
-    mine = [mine[0]] + [swap(mine[k], "ctx", k) for k in range(1, n_ctx)]
 
     rate = lr_rate.reshape(-1, 1)
     residue = lr_residue.reshape(-1, 1)
@@ -315,6 +304,24 @@
 
 
     local_fwd = local(False, kernel_rev, mixed)
+    mine = call(
+        functools.partial(pack_body, n_ctx), "pack", 0, 4 * part * depth * n_ctx,
+        grid_spec=pltpu.PrefetchScalarGridSpec(
+            num_scalar_prefetch=1, grid=(n_dp,),
+            in_specs=[piece(k) for k in range(n_ctx)] + [ANY] * (n_ctx - 1),
+            out_specs=[pl.BlockSpec((part, feats), lambda j, p: (0, j))] * n_ctx,
+        ),
+        out_shape=[shape(part, depth)] * n_ctx,
+    )(place, *[out_grad] * n_ctx, *ends_far)
+    mine = [mine[0]] + [swap(mine[k], "ctx", k) for k in range(1, n_ctx)]
+    long_out, gated = call(
+        functools.partial(long_body, n_ctx - 1), "long", 2 * rows * 128 * width, rows * width * 10,
+        grid=(steps,),
+        in_specs=[wide(rows, block), wide((n_ctx - 1) * rows, block), wide(rows, block)] + [wide(ORDER, block)] * (n_ctx - 1),
+        out_specs=[wide(rows, block), pl.BlockSpec((1, rows, block), lambda i: (i, 0, 0))],
+        out_shape=[shape(rows, width), shape(n_dp, rows, quarter)],
+    )(local_fwd, carry_coef, gate, *ends_far)
+    gated_far = lax.all_to_all(gated, "dp", 0, 0, tiled=True)
     side = n_ctx // 2
 
     def join(pieces, *after):
@@ -330,17 +337,9 @@
         value = lax.all_gather(value, ("dp", "tp"), axis=0, tiled=False)
         return value.reshape(n_dp, n_tp, side, part, depth)
 
-    far = join(mine[side:], weights, local_fwd, *ends_far, *mine[1:side])
+    far = join(mine[side:], weights, gated_far, *mine[1:side])
     near = join(mine[:side], far)
     grad_far, grad_near = gather(far), gather(near)
-    long_out, gated = call(
-        functools.partial(long_body, n_ctx - 1), "long", 2 * rows * 128 * width, rows * width * 10,
-        grid=(steps,),
-        in_specs=[wide(rows, block), wide((n_ctx - 1) * rows, block), wide(rows, block)] + [wide(ORDER, block)] * (n_ctx - 1) + [ANY] * 2,
-        out_specs=[wide(rows, block), pl.BlockSpec((1, rows, block), lambda i: (i, 0, 0))],
-        out_shape=[shape(rows, width), shape(n_dp, rows, quarter)],
-    )(local_fwd, carry_coef, gate, *ends_far, far, near)
-    gated_far = lax.all_to_all(gated, "dp", 0, 0, tiled=True)
     tokens = n_ctx * n_dp * rows
     last = n_ctx - 1
     from_left, from_right = [], []
@@ -449,6 +448,14 @@
             out_shape=shape(feats, quarter),
         )(place, grad_t, gated_all, token)
 
+    def hold(value, after):
+        return call(
+            wait_body, "hold", 0, 0,
+            in_specs=[ANY] * 2, out_specs=ANY,
+            out_shape=shape(*value.shape), input_output_aliases={0: 0},
+        )(value, after)
+
+    diagonal = swap(pieces[n_dp - 1], "dp", n_dp - 1)
     delta = call(
         sum_body, "sum", 0, 8 * n_dp * rows * quarter,
         grid_spec=pltpu.PrefetchScalarGridSpec(
@@ -457,20 +464,12 @@
             out_specs=pl.BlockSpec((1, rows, quarter), lambda i, q: (i, 0, 0)),
         ),
         out_shape=shape(n_dp, rows, quarter),
-    )(own[None] * 0, partial, right, left, pieces[n_dp // 2])
+    )(own[None] * 0, partial, right, left, diagonal)
     delta_far = lax.all_to_all(delta, "dp", 0, 0, tiled=True)
 
-    def hold(value, after):
-        return call(
-            wait_body, "hold", 0, 0,
-            in_specs=[ANY] * 2, out_specs=ANY,
-            out_shape=shape(*value.shape), input_output_aliases={0: 0},
-        )(value, after)
-
     weight_far = [pieces[0]] + [
-        swap(pieces[k] if k == n_dp - 1 else hold(pieces[k], delta_far), "dp", k)
-        for k in range(1, n_dp)
-    ]
+        swap(hold(pieces[k], delta_far), "dp", k) for k in range(1, n_dp - 1)
+    ] + [diagonal]
 
     seed, starts, gate_grad = call(
         seed_body, "seed", 2 * rows * 128 * width, rows * width * 10,

time: 319 us -> 353 us (1.11)
  waiting for transfers between devices: 77.7 us -> 124 us
  starting transfers between devices: 78 us -> 67.4 us
    ppermute x6, waiting for transfers between devices: 0.02 us -> 40.2 us  [swap(): lax.ppermute(value, axis, [(i, i ^ k) for i in range(lax.axis_size(axis))])]
    all_to_all x1, waiting for transfers between devices: 0.01 us -> 18.4 us  [on_device(): lax.all_to_all(proj_weight.reshape(n_dp, quarter, feats), 'dp', 0, 0, til...]
    all_to_all x1, waiting for transfers between devices: 15.4 us -> 0.01 us  [on_device(): delta_far = lax.all_to_all(delta, 'dp', 0, 0, tiled=True)]
    ppermute x19, starting transfers between devices: 61.9 us -> 48.1 us  [shift(): return lax.ppermute(value, 'ctx', ends)]
    all_gather x2, waiting for transfers between devices: 0.02 us -> 4.89 us  [gather(): value = lax.all_gather(value, ('dp', 'tp'), axis=0, tiled=False)]
  transfers between devices with their start and end apart: 29 -> 29, of which waited for: 11 -> 12; matrix products, arithmetic and copies ran while one was open for 3% -> 3% of each run, Pallas kernels for 32% -> 25%
where the time goes in v5:
time: 353 us; the launch traced here: 351 us
  waiting for transfers between devices  124 us (35%)
  Pallas kernels  111 us (31%)
  starting transfers between devices  67.4 us (19%)
  blocking collectives  16.2 us (5%)
  between operations  14.6 us (4%)
  local copies, waits for them, and re-layouts  9.82 us (3%)
  other arithmetic  8.35 us (2%)
    ppermute x19, waiting for transfers between devices, shift(): return lax.ppermute(value, 'ctx', ends)  60.2 us
    ppermute x19, starting transfers between devices, shift(): return lax.ppermute(value, 'ctx', ends)  48.1 us
    ppermute x6, waiting for transfers between devices, swap(): lax.ppermute(value, axis, [(i, i ^ k) for i in range(lax.axis_size(axis))])  40.2 us
    pallas_call x4, Pallas kernels, on_device(): call(weight_body, 'weight', 2 * tokens * feats * quarter, 2 * tokens * (f...  21.4 us
    all_to_all x1, waiting for transfers between devices, on_device(): lax.all_to_all(proj_weight.reshape(n_dp, quarter, feats), 'dp', 0, 0, til...  18.4 us
    all_to_all x1, blocking collectives, on_device(): gated_far = lax.all_to_all(gated, 'dp', 0, 0, tiled=True)  16.2 us
    pallas_call x1, Pallas kernels, on_device(): call(functools.partial(flip_body, place_of, side), 'flip', 0, 6 * tokens...  15.3 us
    pallas_call x3, Pallas kernels, local(): call(functools.partial(local_body, transposed), 'local_t' if transposed e...  11.2 us
  transfers between devices with their start and end apart: 29, of which 12 were waited for; matrix products, arithmetic and copies ran while one was open for 3% of the time, Pallas kernels for 25%

profile of v5, /device:TPU:0, one launch (start us, length us, event | category | flops | bytes accessed | tf_op | source)
XLA Modules:
  0.0 350.8 jit_solution(8926203845606212881)
XLA Ops:
  9.0 5.0 %collective-permute-start = (bf16[128,4096]{1,0:T(8,128)(2,1)S(1)}, bf16[128,4096]{1,0:T(8,128)(2,1)S(1)}, u32[]{:S(2)}, u32[]{:S(2)}) collective-permute-start(bf16[128,4096]{1,0:T(8,128)(2,1)S(1)} %multiply_convert_fusion.2.x), channel_id=1, source_target_pairs={{0,2},{2,4},{4,6},{1,3},{3,5},{5,7},{8,10},{10,12},{12,14},{9,11},... | collective-permute-start | bytes 3145736 | tf_op jit(solution)/shard_map/ppermute | solution.py:255
  21.4 4.2 %local.2.own_part = f32[128,4096]{1,0:T(8,128)} custom-call(f32[256,128]{1,0:T(8,128)S(1)} %get-tuple-element.46.rows.taps, bf16[128,4096]{1,0:T(8,128)(2,1)S(1)} %multiply_convert_fusion.2.x, bf16[4096,128]{1,0:T(8,128)(2,1)S(1)} %get-tuple-element.43.refs_0_.ends_coef, bf16[4096,128]{1,0:T(8,128)(2,1)S(1)} %get-tuple-element.42.refs_1_.starts_coef, ...), custom_call_target="tpu_custom_call" | custom-call | flops 1073741824 | bytes 3145728 | tf_op jit(solution)/shard_map/local/pallas_call | solution.py:283
  25.6 10.7 %collective-permute-done.rim = bf16[128,4096]{1,0:T(8,128)(2,1)S(1)} collective-permute-done((bf16[128,4096]{1,0:T(8,128)(2,1)S(1)}, bf16[128,4096]{1,0:T(8,128)(2,1)S(1)}, u32[]{:S(2)}, u32[]{:S(2)}) %collective-permute-start) | collective-permute-done | bytes 1048608 | tf_op jit(solution)/shard_map/ppermute | solution.py:255
  36.4 5.6 %conv.1 = (bf16[128,4096]{1,0:T(8,128)(2,1)S(1)}, bf16[128,4096]{1,0:T(8,128)(2,1)S(1)}, bf16[16,4096]{1,0:T(8,128)(2,1)S(1)}) custom-call(bf16[128,4096]{1,0:T(8,128)(2,1)S(1)} %collective-permute-done.rim, f32[128,4096]{1,0:T(8,128)} %local.2.own_part, bf16[128,4096]{1,0:T(8,128)(2,1)} %query.3, f32[256,128]{1,0:T(8,128)S(1)} %get-tuple-element.46.rows.taps, ...), custom_call_target="tpu_custom_call" | custom-call | flops 1073741824 | bytes 7340032 | tf_op jit(solution)/shard_map/conv/pallas_call | solution.py:296
  42.0 4.5 %collective-permute-start.1 = (bf16[16,4096]{1,0:T(8,128)(2,1)S(1)}, bf16[16,4096]{1,0:T(8,128)(2,1)S(1)}, u32[]{:S(2)}, u32[]{:S(2)}) collective-permute-start(bf16[16,4096]{1,0:T(8,128)(2,1)S(1)} %get-tuple-element.22), channel_id=1, source_target_pairs={{0,2},{2,4},{4,6},{1,3},{3,5},{5,7},{8,10},{10,12},{12,14},{9,11},... | collective-permute-start | bytes 393224 | tf_op jit(solution)/shard_map/ppermute | solution.py:255
  46.5 4.5 %collective-permute-start.2 = (bf16[16,4096]{1,0:T(8,128)(2,1)S(1)}, bf16[16,4096]{1,0:T(8,128)(2,1)S(1)}, u32[]{:S(2)}, u32[]{:S(2)}) collective-permute-start(bf16[16,4096]{1,0:T(8,128)(2,1)S(1)} %get-tuple-element.22), channel_id=1, source_target_pairs={{0,4},{2,6},{1,5},{3,7},{8,12},{10,14},{9,13},{11,15},{16,20},{18,... | collective-permute-start | bytes 393224 | tf_op jit(solution)/shard_map/ppermute | solution.py:255
  57.2 4.1 %long.1 = (bf16[128,4096]{1,0:T(8,128)(2,1)S(1)}, bf16[4,128,1024]{2,1,0:T(8,128)(2,1)S(1)}) custom-call(f32[128,4096]{1,0:T(8,128)} %copy-done.11, bf16[384,4096]{1,0:T(8,128)(2,1)} %get-tuple-element.41.refs_2_.coef, bf16[128,4096]{1,0:T(8,128)(2,1)S(1)} %copy-done.4, bf16[16,4096]{1,0:T(8,128)(2,1)S(1)} %collective-permute-done.1.refs_4_.refs_0_, ...), custom_call_target="tpu_custom_call" | custom-call | flops 134217728 | bytes 5242880 | tf_op jit(solution)/shard_map/long/pallas_call | solution.py:317
  61.3 16.2 %all_to_all.15.refs_3_.own = bf16[4,128,1024]{2,1,0:T(8,128)(2,1)S(1)} all-to-all(bf16[4,128,1024]{2,1,0:T(8,128)(2,1)S(1)} %get-tuple-element.28), channel_id=1, replica_groups=mesh['dp'=4,'ctx'=4,'tp'=2] {'dp'}, dimensions={0} | all-to-all | bytes 2097152 | tf_op jit(solution)/shard_map/all_to_all | solution.py:324
  77.5 5.0 %all-to-all-start = ((bf16[4,1024,512]{2,1,0:T(8,128)(2,1)}), bf16[4,1024,512]{2,1,0:T(8,128)(2,1)}, u32[]{:S(2)}, u32[]{:S(2)}) async-start(bf16[4,1024,512]{2,1,0:T(8,128)(2,1)} %bitcast.17), calls=%async_computation | async-start | bytes 8388608 | tf_op jit(solution)/shard_map/all_to_all | solution.py:260
  91.2 4.3 %collective-permute-done.4.refs_4_.refs_1_ = bf16[64,2048]{1,0:T(8,128)(2,1)S(1)} collective-permute-done((bf16[64,2048]{1,0:T(8,128)(2,1)S(1)}, bf16[64,2048]{1,0:T(8,128)(2,1)S(1)}, u32[]{:S(2)}, u32[]{:S(2)}) %collective-permute-start.4) | collective-permute-done | bytes 262176 | tf_op jit(solution)/shard_map/ppermute | solution.py:251
  95.5 13.4 %collective-permute-done.5.refs_0_ = bf16[64,2048]{1,0:T(8,128)(2,1)S(1)} collective-permute-done((bf16[64,2048]{1,0:T(8,128)(2,1)S(1)}, bf16[64,2048]{1,0:T(8,128)(2,1)S(1)}, u32[]{:S(2)}, u32[]{:S(2)}) %collective-permute-start.5) | collective-permute-done | bytes 262176 | tf_op jit(solution)/shard_map/ppermute | solution.py:251
  108.9 18.4 %all-to-all-done.refs_2_.weights = bf16[4,1024,512]{2,1,0:T(8,128)(2,1)} async-done(((bf16[4,1024,512]{2,1,0:T(8,128)(2,1)}), bf16[4,1024,512]{2,1,0:T(8,128)(2,1)}, u32[]{:S(2)}, u32[]{:S(2)}) %all-to-all-start) | async-done | bytes 4194336 | tf_op jit(solution)/shard_map/all_to_all | solution.py:260
  130.2 5.9 %collective-permute-start.7 = (bf16[4,128,1024]{2,1,0:T(8,128)(2,1)S(1)}, bf16[4,128,1024]{2,1,0:T(8,128)(2,1)}, u32[]{:S(2)}, u32[]{:S(2)}) collective-permute-start(bf16[4,128,1024]{2,1,0:T(8,128)(2,1)S(1)} %all_to_all.15.refs_3_.own), channel_id=1, source_target_pairs={{0,2},{2,4},{4,6},{1,3},{3,5},{5,7},{8,10},{10,12},{12,14},{9,11},... | collective-permute-start | bytes 3145736 | tf_op jit(solution)/shard_map/ppermute | solution.py:255
  137.4 19.3 %collective-permute-done.7.refs_0_ = bf16[4,128,1024]{2,1,0:T(8,128)(2,1)} collective-permute-done((bf16[4,128,1024]{2,1,0:T(8,128)(2,1)S(1)}, bf16[4,128,1024]{2,1,0:T(8,128)(2,1)}, u32[]{:S(2)}, u32[]{:S(2)}) %collective-permute-start.7) | collective-permute-done | bytes 1048608 | tf_op jit(solution)/shard_map/ppermute | solution.py:255
  163.1 4.9 %all-gather.7.cloned.1.call-done = bf16[16,64,2048]{2,1,0:T(8,128)(2,1)} async-done(((bf16[2,64,2048]{2,1,0:T(8,128)(2,1)}), bf16[16,64,2048]{2,1,0:T(8,128)(2,1)}) %all-gather.7.cloned.1.call-update) | async-done | bytes 4194320 | tf_op jit(solution)/shard_map/all_gather | solution.py:337
  168.0 8.5 %delta.2.refs_0_.partial_right.partial_left = bf16[2,4,128,1024]{3,2,1,0:T(8,128)(2,1)} custom-call(bf16[4,2,2,64,2048]{4,3,2,1,0:T(8,128)(2,1)} %bitcast.18, bf16[4,1024,512]{2,1,0:T(8,128)(2,1)} %all-to-all-done.refs_2_.weights, bf16[4,128,1024]{2,1,0:T(8,128)(2,1)} %collective-permute-done.7.refs_0_, ...), custom_call_target="tpu_custom_call" | custom-call | flops 4294967296 | bytes 10485760 | tf_op jit(solution)/shard_map/delta/pallas_call | solution.py:356
  180.6 4.4 %collective-permute-start.9 = (bf16[1,4,128,1024]{3,2,1,0:T(8,128)(2,1)}, bf16[1,4,128,1024]{3,2,1,0:T(8,128)(2,1)}, u32[]{:S(2)}, u32[]{:S(2)}) collective-permute-start(bf16[1,4,128,1024]{3,2,1,0:T(8,128)(2,1)} %constant_dynamic-slice_fusion), channel_id=1, source_target_pairs={{0,2},{1,3},{8,10},{9,11},{16,18},{17,19},{24,26},{25,27}} | collective-permute-start | bytes 3145736 | tf_op jit(solution)/shard_map/ppermute | solution.py:255
  188.2 18.9 %collective-permute-done.9.right = bf16[1,4,128,1024]{3,2,1,0:T(8,128)(2,1)} collective-permute-done((bf16[1,4,128,1024]{3,2,1,0:T(8,128)(2,1)}, bf16[1,4,128,1024]{3,2,1,0:T(8,128)(2,1)}, u32[]{:S(2)}, u32[]{:S(2)}) %collective-permute-start.9) | collective-permute-done | bytes 1048608 | tf_op jit(solution)/shard_map/ppermute | solution.py:255
  207.1 4.7 %add.74 = (bf16[1,4,128,1024]{3,2,1,0:T(8,128)(2,1)}, bf16[1,4,128,1024]{3,2,1,0:T(8,128)(2,1)}) custom-call(s32[2]{0:T(128)S(1)} %add_maximum_fusion.dests, bf16[2,4,128,1024]{3,2,1,0:T(8,128)(2,1)} %delta.2.refs_0_.partial_right.partial_left, bf16[2,4,128,1024]{3,2,1,0:T(8,128)(2,1)} %delta.2.refs_0_.partial_right.partial_left, ...), custom_call_target="tpu_custom_call" | custom-call | bytes 6291456 | tf_op jit(solution)/shard_map/add/pallas_call | solution.py:416
  211.8 5.4 %collective-permute-start.13 = (bf16[1,4,128,1024]{3,2,1,0:T(8,128)(2,1)}, bf16[1,4,128,1024]{3,2,1,0:T(8,128)(2,1)}, u32[]{:S(2)}, u32[]{:S(2)}) collective-permute-start(bf16[1,4,128,1024]{3,2,1,0:T(8,128)(2,1)} %get-tuple-element.29), channel_id=1, source_target_pairs={{0,2},{2,4},{1,3},{3,5},{8,10},{10,12},{9,11},{11,13},{16,18},{18,... | collective-permute-start | bytes 3145736 | tf_op jit(solution)/shard_map/ppermute | solution.py:255
  218.9 9.6 %delta.3.after.partial_right.partial_left.partial = bf16[4,4,128,1024]{3,2,1,0:T(8,128)(2,1)} custom-call(bf16[4,2,2,64,2048]{4,3,2,1,0:T(8,128)(2,1)} %bitcast.20, bf16[4,1024,512]{2,1,0:T(8,128)(2,1)} %all-to-all-done.refs_2_.weights, bf16[2,4,128,1024]{3,2,1,0:T(8,128)(2,1)S(1)} %copy-done.1), custom_call_target="tpu_custom_call" | custom-call | flops 4294967296 | bytes 14680064 | tf_op jit(solution)/shard_map/delta/pallas_call | solution.py:364
  228.5 15.3 %flip.1.refs_2_.grad_t = bf16[2048,2048]{1,0:T(8,128)(2,1)} custom-call(s32[3]{0:T(128)S(1)} %pad_add_fusion.place, bf16[4,2,2,64,2048]{4,3,2,1,0:T(8,128)(2,1)} %bitcast.19, bf16[4,2,2,64,2048]{4,3,2,1,0:T(8,128)(2,1)} %bitcast.21, bf16[4,4,128,1024]{3,2,1,0:T(8,128)(2,1)} %delta.3.after.partial_right.partial_left.partial), custom_call_target="tpu_custom_call" | custom-call | bytes 25165824 | tf_op jit(solution)/shard_map/flip/pallas_call | solution.py:379
  248.9 5.2 %merge.1 = bf16[4,4,128,1024]{3,2,1,0:T(8,128)(2,1)} custom-call(bf16[4,128,1024]{2,1,0:T(8,128)(2,1)S(1)} %all_to_all.15.refs_3_.own, bf16[4,128,1024]{2,1,0:T(8,128)(2,1)} %collective-permute-done.7.refs_0_, bf16[4,128,1024]{2,1,0:T(8,128)(2,1)} %collective-permute-done.11.refs_0_.refs_1_, bf16[4,128,1024]{2,1,0:T(8,128)(2,1)} %collective-permute-done.15.refs_0_.refs_2_, ...), custom_call_target="tpu_custom_call" | custom-call | bytes 11534336 | tf_op jit(solution)/shard_map/merge/pallas_call | solution.py:428
  255.3 5.4 %weight.4.after = bf16[512,1024]{1,0:T(8,128)(2,1)S(1)} custom-call(s32[3]{0:T(128)S(1)} %pad_add_fusion.place, bf16[2048,2048]{1,0:T(8,128)(2,1)} %flip.1.refs_2_.grad_t, bf16[2048,1024]{1,0:T(8,128)(2,1)} %bitcast.13, bf16[1,4,128,1024]{3,2,1,0:T(8,128)(2,1)S(1)} %copy-done.9), custom_call_target="tpu_custom_call" | custom-call | flops 2147483648 | bytes 6291456 | tf_op jit(solution)/shard_map/weight/pallas_call | solution.py:437
  263.4 22.4 %collective-permute-done.19.after.refs_3_ = bf16[512,1024]{1,0:T(8,128)(2,1)S(1)} collective-permute-done((bf16[512,1024]{1,0:T(8,128)(2,1)S(1)}, bf16[512,1024]{1,0:T(8,128)(2,1)S(1)}, u32[]{:S(2)}, u32[]{:S(2)}) %collective-permute-start.19) | collective-permute-done | bytes 1048608 | tf_op jit(solution)/shard_map/ppermute | solution.py:251
  295.0 5.4 %weight.5.after.refs_0_ = bf16[512,1024]{1,0:T(8,128)(2,1)S(1)} custom-call(s32[3]{0:T(128)S(1)} %pad_add_fusion.place, bf16[2048,2048]{1,0:T(8,128)(2,1)} %flip.1.refs_2_.grad_t, bf16[2048,1024]{1,0:T(8,128)(2,1)} %bitcast.14, bf16[512,1024]{1,0:T(8,128)(2,1)S(1)} %weight.4.after), custom_call_target="tpu_custom_call" | custom-call | flops 2147483648 | bytes 6291456 | tf_op jit(solution)/shard_map/weight/pallas_call | solution.py:437
  300.4 5.4 %weight.6.after.refs_0_ = bf16[512,1024]{1,0:T(8,128)(2,1)S(1)} custom-call(s32[3]{0:T(128)S(1)} %pad_add_fusion.place, bf16[2048,2048]{1,0:T(8,128)(2,1)} %flip.1.refs_2_.grad_t, bf16[2048,1024]{1,0:T(8,128)(2,1)} %bitcast.15, bf16[512,1024]{1,0:T(8,128)(2,1)S(1)} %weight.5.after.refs_0_), custom_call_target="tpu_custom_call" | custom-call | flops 2147483648 | bytes 6291456 | tf_op jit(solution)/shard_map/weight/pallas_call | solution.py:437
  305.8 5.4 %weight.7.refs_0_ = bf16[512,1024]{1,0:T(8,128)(2,1)S(1)} custom-call(s32[3]{0:T(128)S(1)} %pad_add_fusion.place, bf16[2048,2048]{1,0:T(8,128)(2,1)} %flip.1.refs_2_.grad_t, bf16[2048,1024]{1,0:T(8,128)(2,1)} %bitcast.16, bf16[512,1024]{1,0:T(8,128)(2,1)S(1)} %weight.6.after.refs_0_), custom_call_target="tpu_custom_call" | custom-call | flops 2147483648 | bytes 6291456 | tf_op jit(solution)/shard_map/weight/pallas_call | solution.py:437
  315.6 4.3 %seed.1 = (bf16[128,4096]{1,0:T(8,128)(2,1)S(1)}, bf16[16,4096]{1,0:T(8,128)(2,1)S(1)}, bf16[128,4096]{1,0:T(8,128)(2,1)}) custom-call(bf16[4,128,1024]{2,1,0:T(8,128)(2,1)S(1)} %all-to-all-done.2.delta.refs_1_, bf16[128,4096]{1,0:T(8,128)(2,1)S(1)} %copy-done.5, bf16[128,4096]{1,0:T(8,128)(2,1)} %copy-done.13, bf16[4096,128]{1,0:T(8,128)(2,1)} %copy-done.2, ...), custom_call_target="tpu_custom_call" | custom-call | flops 134217728 | bytes 5242880 | tf_op jit(solution)/shard_map/seed/pallas_call | solution.py:474
  328.7 5.5 %collective-permute-done.21.refs_1_ = bf16[16,4096]{1,0:T(8,128)(2,1)S(1)} collective-permute-done((bf16[16,4096]{1,0:T(8,128)(2,1)S(1)}, bf16[16,4096]{1,0:T(8,128)(2,1)S(1)}, u32[]{:S(2)}, u32[]{:S(2)}) %collective-permute-start.21) | collective-permute-done | bytes 131104 | tf_op jit(solution)/shard_map/ppermute | solution.py:255
  334.2 5.2 %back.1 = (bf16[128,4096]{1,0:T(8,128)(2,1)}, bf16[128,4096]{1,0:T(8,128)(2,1)}) custom-call(f32[128,4096]{1,0:T(8,128)} %copy-done.12, bf16[384,4096]{1,0:T(8,128)(2,1)} %get-tuple-element.40.refs_3_.coef, bf16[128,4096]{1,0:T(8,128)(2,1)S(1)} %copy-done.15, bf16[128,4096]{1,0:T(8,128)(2,1)S(1)} %copy-done.10, ...), custom_call_target="tpu_custom_call" | custom-call | flops 134217728 | bytes 6291456 | tf_op jit(solution)/shard_map/back/pallas_call | solution.py:486
  339.4 4.5 %lay.1 = bf16[512,4096]{1,0:T(8,128)(2,1)} custom-call(s32[3]{0:T(128)S(1)} %pad_add_fusion.place, bf16[512,1024]{1,0:T(8,128)(2,1)S(1)} %copy-done.7, bf16[512,1024]{1,0:T(8,128)(2,1)S(1)} %collective-permute-done.23.refs_1_, bf16[512,1024]{1,0:T(8,128)(2,1)S(1)} %collective-permute-done.24.refs_2_, bf16[512,1024]{1,0:T(8,128)(2,1)} %copy-done.20, ...), custom_call_target="tpu_custom_call" | custom-call | bytes 8388608 | tf_op jit(solution)/shard_map/lay/pallas_call | solution.py:496
  (122 shorter events, 74.9 us)
Async XLA Ops:
  9.0 27.3 %collective-permute-start = (bf16[128,4096]{1,0:T(8,128)(2,1)S(1)}, bf16[128,4096]{1,0:T(8,128)(2,1)S(1)}, u32[]{:S(2)}, u32[]{:S(2)}) collective-permute-start(bf16[128,4096]{1,0:T(8,128)(2,1)S(1)} %multiply_convert_fusion.2.x), channel_id=1, source_target_pairs={{0,2},{2,4},{4,6},{1,3},{3,5},{5,7},{8,10},{10,12},{12,14},{9,11},... | collective-permute-start | bytes 3145736 | tf_op jit(solution)/shard_map/ppermute | solution.py:255
  42.0 19.3 %copy-start.14 = (bf16[128,4096]{1,0:T(8,128)(2,1)}, bf16[128,4096]{1,0:T(8,128)(2,1)S(1)}, u32[]{:S(2)}) copy-start(bf16[128,4096]{1,0:T(8,128)(2,1)S(1)} %get-tuple-element.35.conv) | copy-start | bytes 3145732
  42.0 15.2 %collective-permute-start.1 = (bf16[16,4096]{1,0:T(8,128)(2,1)S(1)}, bf16[16,4096]{1,0:T(8,128)(2,1)S(1)}, u32[]{:S(2)}, u32[]{:S(2)}) collective-permute-start(bf16[16,4096]{1,0:T(8,128)(2,1)S(1)} %get-tuple-element.22), channel_id=1, source_target_pairs={{0,2},{2,4},{4,6},{1,3},{3,5},{5,7},{8,10},{10,12},{12,14},{9,11},... | collective-permute-start | bytes 393224 | tf_op jit(solution)/shard_map/ppermute | solution.py:255
  46.5 10.7 %collective-permute-start.2 = (bf16[16,4096]{1,0:T(8,128)(2,1)S(1)}, bf16[16,4096]{1,0:T(8,128)(2,1)S(1)}, u32[]{:S(2)}, u32[]{:S(2)}) collective-permute-start(bf16[16,4096]{1,0:T(8,128)(2,1)S(1)} %get-tuple-element.22), channel_id=1, source_target_pairs={{0,4},{2,6},{1,5},{3,7},{8,12},{10,14},{9,13},{11,15},{16,20},{18,... | collective-permute-start | bytes 393224 | tf_op jit(solution)/shard_map/ppermute | solution.py:255
  51.0 6.2 %collective-permute-start.3 = (bf16[16,4096]{1,0:T(8,128)(2,1)S(1)}, bf16[16,4096]{1,0:T(8,128)(2,1)S(1)}, u32[]{:S(2)}, u32[]{:S(2)}) collective-permute-start(bf16[16,4096]{1,0:T(8,128)(2,1)S(1)} %get-tuple-element.22), channel_id=1, source_target_pairs={{0,6},{1,7},{8,14},{9,15},{16,22},{17,23},{24,30},{25,31}} | collective-permute-start | bytes 393224 | tf_op jit(solution)/shard_map/ppermute | solution.py:255
  77.5 49.7 %all-to-all-start = ((bf16[4,1024,512]{2,1,0:T(8,128)(2,1)}), bf16[4,1024,512]{2,1,0:T(8,128)(2,1)}, u32[]{:S(2)}, u32[]{:S(2)}) async-start(bf16[4,1024,512]{2,1,0:T(8,128)(2,1)} %bitcast.17), calls=%async_computation | async-start | bytes 8388608 | tf_op jit(solution)/shard_map/all_to_all | solution.py:260
  82.5 85.5 %all-gather.7.cloned.1.call-start = ((), (), s32[]{:S(2)}) async-start(), calls=%async_computation.4 | async-start | bytes 4718592 | tf_op jit(solution)/shard_map/all_gather | solution.py:337
  85.4 10.1 %collective-permute-start.4 = (bf16[64,2048]{1,0:T(8,128)(2,1)S(1)}, bf16[64,2048]{1,0:T(8,128)(2,1)S(1)}, u32[]{:S(2)}, u32[]{:S(2)}) collective-permute-start(bf16[64,2048]{1,0:T(8,128)(2,1)S(1)} %get-tuple-element.24), channel_id=1, source_target_pairs={{0,2},{2,0},{4,6},{6,4},{1,3},{3,1},{5,7},{7,5},{8,10},{10,8},{12,... | collective-permute-start | bytes 786440 | tf_op jit(solution)/shard_map/ppermute | solution.py:251
  87.8 21.1 %collective-permute-start.5 = (bf16[64,2048]{1,0:T(8,128)(2,1)S(1)}, bf16[64,2048]{1,0:T(8,128)(2,1)S(1)}, u32[]{:S(2)}, u32[]{:S(2)}) collective-permute-start(bf16[64,2048]{1,0:T(8,128)(2,1)S(1)} %get-tuple-element.25), channel_id=1, source_target_pairs={{0,4},{2,6},{4,0},{6,2},{1,5},{3,7},{5,1},{7,3},{8,12},{10,14},{12... | collective-permute-start | bytes 786440 | tf_op jit(solution)/shard_map/ppermute | solution.py:251
  91.2 37.6 %copy-start.19 = (bf16[64,2048]{1,0:T(8,128)(2,1)S(1)}, bf16[64,2048]{1,0:T(8,128)(2,1)}, u32[]{:S(2)}) copy-start(bf16[64,2048]{1,0:T(8,128)(2,1)} %copy-done.18) | copy-start | bytes 786436
  91.2 17.7 %collective-permute-start.6 = (bf16[64,2048]{1,0:T(8,128)(2,1)S(1)}, bf16[64,2048]{1,0:T(8,128)(2,1)S(1)}, u32[]{:S(2)}, u32[]{:S(2)}) collective-permute-start(bf16[64,2048]{1,0:T(8,128)(2,1)S(1)} %get-tuple-element.26), channel_id=1, source_target_pairs={{0,6},{2,4},{4,2},{6,0},{1,7},{3,5},{5,3},{7,1},{8,14},{10,12},{12... | collective-permute-start | bytes 786440 | tf_op jit(solution)/shard_map/ppermute | solution.py:251
  128.7 90.2 %all-gather.5.cloned.1.call-start = ((), (), s32[]{:S(2)}) async-start(), calls=%async_computation.3 | async-start | bytes 4718592 | tf_op jit(solution)/shard_map/all_gather | solution.py:337
  130.2 26.4 %collective-permute-start.7 = (bf16[4,128,1024]{2,1,0:T(8,128)(2,1)S(1)}, bf16[4,128,1024]{2,1,0:T(8,128)(2,1)}, u32[]{:S(2)}, u32[]{:S(2)}) collective-permute-start(bf16[4,128,1024]{2,1,0:T(8,128)(2,1)S(1)} %all_to_all.15.refs_3_.own), channel_id=1, source_target_pairs={{0,2},{2,4},{4,6},{1,3},{3,5},{5,7},{8,10},{10,12},{12,14},{9,11},... | collective-permute-start | bytes 3145736 | tf_op jit(solution)/shard_map/ppermute | solution.py:255
  136.1 25.8 %collective-permute-start.8 = (bf16[4,128,1024]{2,1,0:T(8,128)(2,1)S(1)}, bf16[4,128,1024]{2,1,0:T(8,128)(2,1)}, u32[]{:S(2)}, u32[]{:S(2)}) collective-permute-start(bf16[4,128,1024]{2,1,0:T(8,128)(2,1)S(1)} %all_to_all.15.refs_3_.own), channel_id=1, source_target_pairs={{2,0},{4,2},{6,4},{3,1},{5,3},{7,5},{10,8},{12,10},{14,12},{11,9},... | collective-permute-start | bytes 3145736 | tf_op jit(solution)/shard_map/ppermute | solution.py:255
  156.7 28.4 %collective-permute-start.11 = (bf16[4,128,1024]{2,1,0:T(8,128)(2,1)}, bf16[4,128,1024]{2,1,0:T(8,128)(2,1)}, u32[]{:S(2)}, u32[]{:S(2)}) collective-permute-start(bf16[4,128,1024]{2,1,0:T(8,128)(2,1)} %collective-permute-done.7.refs_0_), channel_id=1, source_target_pairs={{2,4},{4,6},{3,5},{5,7},{10,12},{12,14},{11,13},{13,15},{18,20},{2... | collective-permute-start | bytes 3145736 | tf_op jit(solution)/shard_map/ppermute | solution.py:255
  161.9 25.1 %collective-permute-start.12 = (bf16[4,128,1024]{2,1,0:T(8,128)(2,1)}, bf16[4,128,1024]{2,1,0:T(8,128)(2,1)}, u32[]{:S(2)}, u32[]{:S(2)}) collective-permute-start(bf16[4,128,1024]{2,1,0:T(8,128)(2,1)} %collective-permute-done.8.refs_1_.refs_5_), channel_id=1, source_target_pairs={{2,0},{4,2},{3,1},{5,3},{10,8},{12,10},{11,9},{13,11},{18,16},{20,... | collective-permute-start | bytes 3145736 | tf_op jit(solution)/shard_map/ppermute | solution.py:255
  178.9 9.3 %collective-permute-start.10 = (bf16[1,4,128,1024]{3,2,1,0:T(8,128)(2,1)}, bf16[1,4,128,1024]{3,2,1,0:T(8,128)(2,1)}, u32[]{:S(2)}, u32[]{:S(2)}) collective-permute-start(bf16[1,4,128,1024]{3,2,1,0:T(8,128)(2,1)} %constant_dynamic-slice_fusion), channel_id=1, source_target_pairs={{6,4},{7,5},{14,12},{15,13},{22,20},{23,21},{30,28},{31,29}} | collective-permute-start | bytes 3145736 | tf_op jit(solution)/shard_map/ppermute | solution.py:255
  180.6 26.5 %collective-permute-start.9 = (bf16[1,4,128,1024]{3,2,1,0:T(8,128)(2,1)}, bf16[1,4,128,1024]{3,2,1,0:T(8,128)(2,1)}, u32[]{:S(2)}, u32[]{:S(2)}) collective-permute-start(bf16[1,4,128,1024]{3,2,1,0:T(8,128)(2,1)} %constant_dynamic-slice_fusion), channel_id=1, source_target_pairs={{0,2},{1,3},{8,10},{9,11},{16,18},{17,19},{24,26},{25,27}} | collective-permute-start | bytes 3145736 | tf_op jit(solution)/shard_map/ppermute | solution.py:255
  185.0 33.9 %copy-start.1 = (bf16[2,4,128,1024]{3,2,1,0:T(8,128)(2,1)S(1)}, bf16[2,4,128,1024]{3,2,1,0:T(8,128)(2,1)}, u32[]{:S(2)}) copy-start(bf16[2,4,128,1024]{3,2,1,0:T(8,128)(2,1)} %delta.2.refs_0_.partial_right.partial_left) | copy-start | bytes 6291460
  185.0 58.8 %collective-permute-start.15 = (bf16[4,128,1024]{2,1,0:T(8,128)(2,1)}, bf16[4,128,1024]{2,1,0:T(8,128)(2,1)}, u32[]{:S(2)}, u32[]{:S(2)}) collective-permute-start(bf16[4,128,1024]{2,1,0:T(8,128)(2,1)} %collective-permute-done.11.refs_0_.refs_1_), channel_id=1, source_target_pairs={{4,6},{5,7},{12,14},{13,15},{20,22},{21,23},{28,30},{29,31}} | collective-permute-start | bytes 3145736 | tf_op jit(solution)/shard_map/ppermute | solution.py:255
  186.9 56.9 %collective-permute-start.16 = (bf16[4,128,1024]{2,1,0:T(8,128)(2,1)}, bf16[4,128,1024]{2,1,0:T(8,128)(2,1)}, u32[]{:S(2)}, u32[]{:S(2)}) collective-permute-start(bf16[4,128,1024]{2,1,0:T(8,128)(2,1)} %collective-permute-done.12.refs_1_.refs_4_), channel_id=1, source_target_pairs={{2,0},{3,1},{10,8},{11,9},{18,16},{19,17},{26,24},{27,25}} | collective-permute-start | bytes 3145736 | tf_op jit(solution)/shard_map/ppermute | solution.py:255
  211.8 32.0 %collective-permute-start.13 = (bf16[1,4,128,1024]{3,2,1,0:T(8,128)(2,1)}, bf16[1,4,128,1024]{3,2,1,0:T(8,128)(2,1)}, u32[]{:S(2)}, u32[]{:S(2)}) collective-permute-start(bf16[1,4,128,1024]{3,2,1,0:T(8,128)(2,1)} %get-tuple-element.29), channel_id=1, source_target_pairs={{0,2},{2,4},{1,3},{3,5},{8,10},{10,12},{9,11},{11,13},{16,18},{18,... | collective-permute-start | bytes 3145736 | tf_op jit(solution)/shard_map/ppermute | solution.py:255
  217.2 26.7 %collective-permute-start.14 = (bf16[1,4,128,1024]{3,2,1,0:T(8,128)(2,1)}, bf16[1,4,128,1024]{3,2,1,0:T(8,128)(2,1)}, u32[]{:S(2)}, u32[]{:S(2)}) collective-permute-start(bf16[1,4,128,1024]{3,2,1,0:T(8,128)(2,1)} %get-tuple-element.30), channel_id=1, source_target_pairs={{4,2},{6,4},{5,3},{7,5},{12,10},{14,12},{13,11},{15,13},{20,18},{2... | collective-permute-start | bytes 3145736 | tf_op jit(solution)/shard_map/ppermute | solution.py:255
  247.5 38.4 %collective-permute-start.17 = (bf16[1,4,128,1024]{3,2,1,0:T(8,128)(2,1)S(1)}, bf16[1,4,128,1024]{3,2,1,0:T(8,128)(2,1)S(1)}, u32[]{:S(2)}, u32[]{:S(2)}) collective-permute-start(bf16[1,4,128,1024]{3,2,1,0:T(8,128)(2,1)S(1)} %get-tuple-element.31.refs_6_.after), channel_id=1, source_target_pairs={{0,2},{2,4},{4,6},{1,3},{3,5},{5,7},{8,10},{10,12},{12,14},{9,11},... | collective-permute-start | bytes 3145736 | tf_op jit(solution)/shard_map/ppermute | solution.py:255
  260.6 25.2 %collective-permute-start.19 = (bf16[512,1024]{1,0:T(8,128)(2,1)S(1)}, bf16[512,1024]{1,0:T(8,128)(2,1)S(1)}, u32[]{:S(2)}, u32[]{:S(2)}) collective-permute-start(bf16[512,1024]{1,0:T(8,128)(2,1)S(1)} %weight.4.after), channel_id=1, source_target_pairs={{0,24},{8,16},{16,8},{24,0},{1,25},{9,17},{17,9},{25,1},{2,26},{10... | collective-permute-start | bytes 3145736 | tf_op jit(solution)/shard_map/ppermute | solution.py:251
  262.1 25.9 %collective-permute-start.18 = (bf16[1,4,128,1024]{3,2,1,0:T(8,128)(2,1)S(1)}, bf16[1,4,128,1024]{3,2,1,0:T(8,128)(2,1)S(1)}, u32[]{:S(2)}, u32[]{:S(2)}) collective-permute-start(bf16[1,4,128,1024]{3,2,1,0:T(8,128)(2,1)S(1)} %get-tuple-element.32), channel_id=1, source_target_pairs={{2,0},{4,2},{6,4},{3,1},{5,3},{7,5},{10,8},{12,10},{14,12},{11,9},... | collective-permute-start | bytes 3145736 | tf_op jit(solution)/shard_map/ppermute | solution.py:255
  291.5 20.6 %all-to-all-start.2 = ((bf16[4,128,1024]{2,1,0:T(8,128)(2,1)}), bf16[4,128,1024]{2,1,0:T(8,128)(2,1)S(1)}, u32[]{:S(2)}, u32[]{:S(2)}) async-start(bf16[4,128,1024]{2,1,0:T(8,128)(2,1)} %sum.1.after), calls=%async_computation.2 | async-start | bytes 2097152 | tf_op jit(solution)/shard_map/all_to_all | solution.py:468
  312.1 27.2 %collective-permute-start.24 = (bf16[512,1024]{1,0:T(8,128)(2,1)S(1)}, bf16[512,1024]{1,0:T(8,128)(2,1)S(1)}, u32[]{:S(2)}, u32[]{:S(2)}) collective-permute-start(bf16[512,1024]{1,0:T(8,128)(2,1)S(1)} %hold.3), channel_id=1, source_target_pairs={{0,16},{8,24},{16,0},{24,8},{1,17},{9,25},{17,1},{25,9},{2,18},{10... | collective-permute-start | bytes 3145736 | tf_op jit(solution)/shard_map/ppermute | solution.py:251
  314.1 25.2 %collective-permute-start.23 = (bf16[512,1024]{1,0:T(8,128)(2,1)S(1)}, bf16[512,1024]{1,0:T(8,128)(2,1)S(1)}, u32[]{:S(2)}, u32[]{:S(2)}) collective-permute-start(bf16[512,1024]{1,0:T(8,128)(2,1)S(1)} %hold.2), channel_id=1, source_target_pairs={{0,8},{8,0},{16,24},{24,16},{1,9},{9,1},{17,25},{25,17},{2,10},{10... | collective-permute-start | bytes 3145736 | tf_op jit(solution)/shard_map/ppermute | solution.py:251
  319.9 8.8 %collective-permute-start.20 = (bf16[16,4096]{1,0:T(8,128)(2,1)S(1)}, bf16[16,4096]{1,0:T(8,128)(2,1)S(1)}, u32[]{:S(2)}, u32[]{:S(2)}) collective-permute-start(bf16[16,4096]{1,0:T(8,128)(2,1)S(1)} %get-tuple-element.36), channel_id=1, source_target_pairs={{2,0},{4,2},{6,4},{3,1},{5,3},{7,5},{10,8},{12,10},{14,12},{11,9},... | collective-permute-start | bytes 393224 | tf_op jit(solution)/shard_map/ppermute | solution.py:255
  321.3 12.9 %collective-permute-start.21 = (bf16[16,4096]{1,0:T(8,128)(2,1)S(1)}, bf16[16,4096]{1,0:T(8,128)(2,1)S(1)}, u32[]{:S(2)}, u32[]{:S(2)}) collective-permute-start(bf16[16,4096]{1,0:T(8,128)(2,1)S(1)} %get-tuple-element.36), channel_id=1, source_target_pairs={{4,0},{6,2},{5,1},{7,3},{12,8},{14,10},{13,9},{15,11},{20,16},{22,... | collective-permute-start | bytes 393224 | tf_op jit(solution)/shard_map/ppermute | solution.py:255
  322.6 11.6 %collective-permute-start.22 = (bf16[16,4096]{1,0:T(8,128)(2,1)S(1)}, bf16[16,4096]{1,0:T(8,128)(2,1)S(1)}, u32[]{:S(2)}, u32[]{:S(2)}) collective-permute-start(bf16[16,4096]{1,0:T(8,128)(2,1)S(1)} %get-tuple-element.36), channel_id=1, source_target_pairs={{6,0},{7,1},{14,8},{15,9},{22,16},{23,17},{30,24},{31,25}} | collective-permute-start | bytes 393224 | tf_op jit(solution)/shard_map/ppermute | solution.py:255
  (21 other events, 117.4 us)
Sparse Core Ops, SparseCore 0:
  128.8 39.1 all-gather.6
  170.5 36.7 all-gather.4

commit v6 on v3

--- a/solution.py
+++ b/solution.py
@@ -117,10 +117,18 @@
         gated[0, :, cols] = (gate[:, cols].astype(F32) * out).astype(BF16)
 
 
-def seed_body(delta, gate, long_out, starts_coef, after, seed, starts, gate_grad):
+def seed_body(count, place, *refs):
+    sources = refs[:count]
+    gate, long_out, starts_coef, seed, starts, gate_grad, delta = refs[count:]
+    for k, source in enumerate(sources):
+
+        @pl.when(pl.program_id(0) == k)
+        def _(source=source):
+            delta[...] = source[...]
+
     for s in range(gate.shape[1] // LANES):
         cols = slice(s * LANES, (s + 1) * LANES)
-        out = delta[0, :, cols].astype(F32)
+        out = delta[:, cols].astype(F32)
         seed[:, cols] = (out * gate[:, cols].astype(F32)).astype(BF16)
         gate_grad[:, cols] = (out * long_out[:, cols].astype(F32)).astype(BF16)
     for s in range(gate.shape[1] // LANES):
@@ -178,15 +186,8 @@
     out[...] = grad[...].reshape(-1, grad.shape[-1]).T
 
 
-def lay_body(place, *refs):
-    sources, out = refs[:-2], refs[-1]
-    for k, source in enumerate(sources):
-        lanes = source.shape[1]
-        out[:, pl.ds(pl.multiple_of((place[0] ^ k) * lanes, lanes), lanes)] = source[...]
-
-
-def wait_body(*refs):
-    pass
+def lay_body(source, after, target):
+    target[...] = source[0]
 
 
 def add_body(dests, partial_right, partial_left, right, left, *refs):
@@ -203,13 +204,17 @@
         out[k + 1] = refs[k][...] + refs[count + k][...]
 
 
-def sum_body(dest, partial, right, left, after, out):
-    total = partial[0].astype(F32) + right[0].astype(F32) + left[0].astype(F32)
-    out[...] = total.astype(BF16)
-
-
-def weight_body(place, grad_t, gated, after, out):
-    out[...] = dot(grad_t[...], gated[...]).astype(out.dtype)
+def sum_body(place, partial, right, left, after, *outs):
+    total = partial[0, 0].astype(F32) + right[0, 0].astype(F32) + left[0, 0].astype(F32)
+    for k, out in enumerate(outs):
+
+        @pl.when(pl.program_id(0) == k)
+        def _(out=out):
+            out[...] = total.astype(BF16)
+
+
+def weight_body(grad_t, gated, after, out):
+    out[0] = dot(grad_t[...], gated[...]).astype(out.dtype)
 
 
 def wide(rows, lanes):
@@ -310,10 +315,10 @@
     mine = call(
         join_body, "join", 0, 4 * part * depth * n_ctx,
         grid=(n_dp,),
-        in_specs=[wide(part, feats)] * n_ctx + [ANY] * (n_ctx + 1),
+        in_specs=[wide(part, feats)] * n_ctx + [ANY] * 2,
         out_specs=deep(n_ctx, part, feats),
         out_shape=shape(n_ctx, part, depth),
-    )(*mine, weights, local_fwd, *ends_far)
+    )(*mine, weights, local_fwd)
     grad = lax.all_gather(mine, ("dp", "tp"), axis=0, tiled=False)
     grad = grad.reshape(n_dp, n_tp, n_ctx, part, depth)
     long_out, gated = call(
@@ -408,55 +413,47 @@
         out_specs=pl.BlockSpec((n_ctx, 1, rows, quarter), lambda i: (0, i, 0, 0)),
         out_shape=shape(n_ctx, n_dp, rows, quarter),
     )(gated_far, *from_left, *from_right[::-1], token).reshape(tokens, quarter)
-    pieces = {}
-    for k in list(range(n_dp - 1, -1, -1)):
-        token = pieces[k] = call(
-            weight_body, "weight", 2 * tokens * feats * quarter, 2 * tokens * (feats + quarter),
-            grid_spec=pltpu.PrefetchScalarGridSpec(
-                num_scalar_prefetch=1, grid=(2,),
-                in_specs=[
-                    pl.BlockSpec((feats, tokens), lambda i, p, k=k: (p[0] ^ k, 0)),
-                    pl.BlockSpec((tokens, quarter // 2), lambda i, p: (0, i)),
-                    ANY,
-                ],
-                out_specs=pl.BlockSpec((feats, quarter // 2), lambda i, p: (0, i)),
-            ),
-            out_shape=shape(feats, quarter),
-        )(place, grad_t, gated_all, token)
+    weight_part = call(
+        weight_body, "weight", 2 * tokens * depth * quarter, 2 * tokens * (depth + quarter),
+        grid=(n_dp,),
+        in_specs=[
+            pl.BlockSpec((feats, tokens), lambda i: (i, 0)),
+            pl.BlockSpec((tokens, quarter), lambda i: (0, 0)),
+            ANY,
+        ],
+        out_specs=pl.BlockSpec((1, feats, quarter), lambda i: (i, 0, 0)),
+        out_shape=shape(n_dp, feats, quarter),
+    )(grad_t, gated_all, token)
+    weight_far = lax.all_to_all(weight_part, "dp", 0, 0, tiled=True)
 
     delta = call(
         sum_body, "sum", 0, 8 * n_dp * rows * quarter,
         grid_spec=pltpu.PrefetchScalarGridSpec(
             num_scalar_prefetch=1, grid=(n_dp,),
-            in_specs=[pick(0), piece_of, piece_of, ANY],
-            out_specs=pl.BlockSpec((1, rows, quarter), lambda i, q: (i, 0, 0)),
+            in_specs=[
+                pl.BlockSpec((1, 1, rows, quarter), lambda i, p: (p[1], p[0] ^ i, 0, 0)),
+                pl.BlockSpec((1, 1, rows, quarter), lambda i, p: (0, p[0] ^ i, 0, 0)),
+                pl.BlockSpec((1, 1, rows, quarter), lambda i, p: (0, p[0] ^ i, 0, 0)),
+                ANY,
+            ],
+            out_specs=[pl.BlockSpec((rows, quarter), lambda i, p: (0, 0))] * n_dp,
         ),
-        out_shape=shape(n_dp, rows, quarter),
-    )(place[1:2], partial, right, left, pieces[n_dp // 2])
-    delta_far = lax.all_to_all(delta, "dp", 0, 0, tiled=True)
-
-    def hold(value, after):
-        return call(
-            wait_body, "hold", 0, 0,
-            in_specs=[ANY] * 2, out_specs=ANY,
-            out_shape=shape(*value.shape), input_output_aliases={0: 0},
-        )(value, after)
-
-    weight_far = [pieces[0]] + [
-        swap(pieces[k] if k == n_dp - 1 else hold(pieces[k], delta_far), "dp", k)
-        for k in range(1, n_dp)
-    ]
-
+        out_shape=[shape(rows, quarter)] * n_dp,
+    )(place, partial, right, left, weight_part)
+    delta = [delta[0]] + [swap(delta[k], "dp", k) for k in range(1, n_dp)]
+
+    here = pl.BlockSpec((rows, block), lambda i, p: (0, p[0] ^ i))
     seed, starts, gate_grad = call(
-        seed_body, "seed", 2 * rows * 128 * width, rows * width * 10,
-        grid=(steps,),
-        in_specs=[
-            pl.BlockSpec((1, rows, block), lambda i: (i, 0, 0)),
-            wide(rows, block), wide(rows, block), tall(block, rows), ANY,
-        ],
-        out_specs=[wide(rows, block), wide(ORDER, block), wide(rows, block)],
+        functools.partial(seed_body, n_dp), "seed", 2 * rows * 128 * width, rows * width * 10,
+        grid_spec=pltpu.PrefetchScalarGridSpec(
+            num_scalar_prefetch=1, grid=(n_dp,),
+            in_specs=[pl.BlockSpec((rows, quarter), lambda i, p: (0, 0))] * n_dp
+            + [here, here, pl.BlockSpec((block, rows), lambda i, p: (p[0] ^ i, 0))],
+            out_specs=[here, pl.BlockSpec((ORDER, block), lambda i, p: (0, p[0] ^ i)), here],
+            scratch_shapes=[pltpu.VMEM((rows, block), BF16)],
+        ),
         out_shape=[shape(rows, width), shape(ORDER, width), shape(rows, width)],
-    )(delta_far, gate, long_out, starts_coef, weight_far[-1])
+    )(place, *delta, gate, long_out, starts_coef)
     starts_far = [shift(starts, -k) for k in range(1, n_ctx)]
     local_bwd = local(True, kernel, seed)
     query_grad, conv_grad = call(
@@ -468,16 +465,13 @@
         out_shape=[shape(rows, width)] * 2,
     )(local_bwd, back_coef, conv, query, *starts_far)
 
-    cut = feats // n_dp
     weight_grad = call(
         lay_body, "lay", 0, 4 * feats * width,
-        grid_spec=pltpu.PrefetchScalarGridSpec(
-            num_scalar_prefetch=1, grid=(n_dp,),
-            in_specs=[pl.BlockSpec((cut, quarter), lambda i, p: (i, 0))] * n_dp + [ANY],
-            out_specs=pl.BlockSpec((cut, width), lambda i, p: (i, 0)),
-        ),
+        grid=(n_dp,),
+        in_specs=[pl.BlockSpec((1, feats, quarter), lambda i: (i, 0, 0)), ANY],
+        out_specs=pl.BlockSpec((feats, quarter), lambda i: (0, i)),
         out_shape=shape(feats, width),
-    )(place, *weight_far, query_grad)
+    )(weight_far, query_grad)
     return query_grad, conv_grad, gate_grad, weight_grad
 
 

time: 324 us -> 318 us (0.981)
  starting transfers between devices: 106 us -> 73.8 us
  waiting for transfers between devices: 58.5 us -> 88.5 us
  Pallas kernels: 111 us -> 102 us
  blocking collectives: 13.7 us -> 18.8 us
    ppermute x19, starting transfers between devices: 72.5 us -> 52.9 us  [shift(): return lax.ppermute(value, 'ctx', ends)]
    ppermute x6, waiting for transfers between devices: 5.62 us -> 22.8 us  [swap(): lax.ppermute(value, axis, [(i, i ^ k) for i in range(lax.axis_size(axis))])]
    ppermute x19, waiting for transfers between devices: 46.3 us -> 63.1 us  [shift(): return lax.ppermute(value, 'ctx', ends)]
    ppermute x6, starting transfers between devices: 25.1 us -> 9.87 us  [swap(): lax.ppermute(value, axis, [(i, i ^ k) for i in range(lax.axis_size(axis))])]
    pallas_call x8 -> x3, Pallas kernels: 31 us -> 22.8 us  [the longest x1 13.2 us: on_device(): call(weight_body, 'weight', 2 * tokens * depth * quarter, 2 * tokens * (d...]
    all_gather x1, waiting for transfers between devices: 6.12 us -> 0.02 us  [on_device(): grad = lax.all_gather(mine, ('dp', 'tp'), axis=0, tiled=False)]
    all_to_all x1, blocking collectives: 13.7 us -> 18.8 us  [on_device(): gated_far = lax.all_to_all(gated, 'dp', 0, 0, tiled=True)]
    unnamed x53 -> x51, local copies, waits for them, and re-layouts: 7.95 us -> 6.93 us
  transfers between devices with their start and end apart: 28 -> 28, of which waited for: 12 -> 16; matrix products, arithmetic and copies ran while one was open for 3% -> 3% of each run, Pallas kernels for 30% -> 23%
where the time goes in v6:
time: 318 us; the launch traced here: 314 us
  Pallas kernels  102 us (32%)
  waiting for transfers between devices  88.5 us (28%)
  starting transfers between devices  73.8 us (23%)
  blocking collectives  18.8 us (6%)
  between operations  14.5 us (5%)
  other arithmetic  8.53 us (3%)
  local copies, waits for them, and re-layouts  7.78 us (2%)
    ppermute x19, waiting for transfers between devices, shift(): return lax.ppermute(value, 'ctx', ends)  63.1 us
    ppermute x19, starting transfers between devices, shift(): return lax.ppermute(value, 'ctx', ends)  52.9 us
    ppermute x6, waiting for transfers between devices, swap(): lax.ppermute(value, axis, [(i, i ^ k) for i in range(lax.axis_size(axis))])  22.8 us
    pallas_call x2, Pallas kernels, project(): call(functools.partial(delta_body, whole), 'delta', 2 * max(count - 1, 1)...  18.8 us
    all_to_all x1, blocking collectives, on_device(): gated_far = lax.all_to_all(gated, 'dp', 0, 0, tiled=True)  18.8 us
    pallas_call x1, Pallas kernels, on_device(): call(flip_body, 'flip', 0, 4 * tokens * depth, grid_spec=pltpu.PrefetchSc...  13.8 us
    pallas_call x1, Pallas kernels, on_device(): call(weight_body, 'weight', 2 * tokens * depth * quarter, 2 * tokens * (d...  13.2 us
    pallas_call x3, Pallas kernels, local(): call(functools.partial(local_body, transposed), 'local_t' if transposed e...  11.1 us
  transfers between devices with their start and end apart: 28, of which 16 were waited for; matrix products, arithmetic and copies ran while one was open for 3% of the time, Pallas kernels for 23%

profile of v6, /device:TPU:0, one launch (start us, length us, event | category | flops | bytes accessed | tf_op | source)
XLA Modules:
  0.0 313.7 jit_solution(9559359450279772027)
XLA Ops:
  7.2 5.2 %all-to-all-start = ((bf16[4,1024,512]{2,1,0:T(8,128)(2,1)}), bf16[4,1024,512]{2,1,0:T(8,128)(2,1)}, u32[]{:S(2)}, u32[]{:S(2)}) async-start(bf16[4,1024,512]{2,1,0:T(8,128)(2,1)} %bitcast.17), calls=%async_computation | async-start | bytes 8388608 | tf_op jit(solution)/shard_map/all_to_all | solution.py:259
  14.3 5.6 %collective-permute-start.3 = (bf16[128,4096]{1,0:T(8,128)(2,1)S(1)}, bf16[128,4096]{1,0:T(8,128)(2,1)}, u32[]{:S(2)}, u32[]{:S(2)}) collective-permute-start(bf16[128,4096]{1,0:T(8,128)(2,1)S(1)} %multiply_convert_fusion.2.x), channel_id=1, source_target_pairs={{0,2},{2,4},{4,6},{1,3},{3,5},{5,7},{8,10},{10,12},{12,14},{9,11},... | collective-permute-start | bytes 3145736 | tf_op jit(solution)/shard_map/ppermute | solution.py:254
  29.6 3.7 %multiply_convert_fusion = (bf16[384,4096]{1,0:T(8,128)(2,1)}, bf16[384,4096]{1,0:T(8,128)(2,1)}) fusion(f32[384]{0:T(512)S(1)} %get-tuple-element.52, f32[4096]{0:T(1024)S(1)} %neg.22, f32[4096]{0:T(1024)S(1)} %mul.110, f32[384]{0:T(512)S(1)} %get-tuple-element.53), kind=kLoop, calls=%fused_computation | loop fusion | flops 9437184 | bytes 6327296 | tf_op jit(solution)/shard_map/convert_element_type | solution.py:280
  34.1 4.2 %local.2.own_part = f32[128,4096]{1,0:T(8,128)} custom-call(f32[256,128]{1,0:T(8,128)S(1)} %pad_maximum_fusion.1.rows.taps, bf16[128,4096]{1,0:T(8,128)(2,1)S(1)} %multiply_convert_fusion.2.x, bf16[4096,128]{1,0:T(8,128)(2,1)S(1)} %get-tuple-element.51.refs_0_.ends_coef, bf16[4096,128]{1,0:T(8,128)(2,1)S(1)} %get-tuple-element.50.refs_1_.refs_6_, ...), custom_call_target="tpu_custom_call" | custom-call | flops 1073741824 | bytes 3145728 | tf_op jit(solution)/shard_map/local/pallas_call | solution.py:291
  38.3 4.2 %collective-permute-done.3.rim = bf16[128,4096]{1,0:T(8,128)(2,1)} collective-permute-done((bf16[128,4096]{1,0:T(8,128)(2,1)S(1)}, bf16[128,4096]{1,0:T(8,128)(2,1)}, u32[]{:S(2)}, u32[]{:S(2)}) %collective-permute-start.3) | collective-permute-done | bytes 1048608 | tf_op jit(solution)/shard_map/ppermute | solution.py:254
  42.5 5.7 %conv.1 = (bf16[128,4096]{1,0:T(8,128)(2,1)S(1)}, bf16[128,4096]{1,0:T(8,128)(2,1)S(1)}, bf16[16,4096]{1,0:T(8,128)(2,1)S(1)}) custom-call(bf16[128,4096]{1,0:T(8,128)(2,1)} %collective-permute-done.3.rim, f32[128,4096]{1,0:T(8,128)} %local.2.own_part, bf16[128,4096]{1,0:T(8,128)(2,1)} %query.3, f32[256,128]{1,0:T(8,128)S(1)} %pad_maximum_fusion.1.rows.taps, ...), custom_call_target="tpu_custom_call" | custom-call | flops 1073741824 | bytes 7340032 | tf_op jit(solution)/shard_map/conv/pallas_call | solution.py:304
  54.0 4.3 %collective-permute-done.2.refs_3_ = bf16[64,2048]{1,0:T(8,128)(2,1)S(1)} collective-permute-done((bf16[64,2048]{1,0:T(8,128)(2,1)}, bf16[64,2048]{1,0:T(8,128)(2,1)S(1)}, u32[]{:S(2)}, u32[]{:S(2)}) %collective-permute-start.2) | collective-permute-done | bytes 262176 | tf_op jit(solution)/shard_map/ppermute | solution.py:250
  62.6 6.5 %collective-permute-start.4 = (bf16[16,4096]{1,0:T(8,128)(2,1)S(1)}, bf16[16,4096]{1,0:T(8,128)(2,1)S(1)}, u32[]{:S(2)}, u32[]{:S(2)}) collective-permute-start(bf16[16,4096]{1,0:T(8,128)(2,1)S(1)} %get-tuple-element.31), channel_id=1, source_target_pairs={{0,2},{2,4},{4,6},{1,3},{3,5},{5,7},{8,10},{10,12},{12,14},{9,11},... | collective-permute-start | bytes 393224 | tf_op jit(solution)/shard_map/ppermute | solution.py:254
  69.1 3.7 %collective-permute-start.5 = (bf16[16,4096]{1,0:T(8,128)(2,1)S(1)}, bf16[16,4096]{1,0:T(8,128)(2,1)S(1)}, u32[]{:S(2)}, u32[]{:S(2)}) collective-permute-start(bf16[16,4096]{1,0:T(8,128)(2,1)S(1)} %get-tuple-element.31), channel_id=1, source_target_pairs={{0,4},{2,6},{1,5},{3,7},{8,12},{10,14},{9,13},{11,15},{16,20},{18,... | collective-permute-start | bytes 393224 | tf_op jit(solution)/shard_map/ppermute | solution.py:254
  77.6 4.0 %long.1 = (bf16[128,4096]{1,0:T(8,128)(2,1)S(1)}, bf16[4,128,1024]{2,1,0:T(8,128)(2,1)S(1)}) custom-call(f32[128,4096]{1,0:T(8,128)} %copy-done.3, bf16[384,4096]{1,0:T(8,128)(2,1)} %get-tuple-element.49.refs_2_.coef, bf16[128,4096]{1,0:T(8,128)(2,1)S(1)} %copy-done.9, bf16[16,4096]{1,0:T(8,128)(2,1)S(1)} %collective-permute-done.4.refs_0_, ...), custom_call_target="tpu_custom_call" | custom-call | flops 134217728 | bytes 5242880 | tf_op jit(solution)/shard_map/long/pallas_call | solution.py:324
  81.6 18.8 %all_to_all.15.own = bf16[4,128,1024]{2,1,0:T(8,128)(2,1)S(1)} all-to-all(bf16[4,128,1024]{2,1,0:T(8,128)(2,1)S(1)} %get-tuple-element.32), channel_id=1, replica_groups=mesh['dp'=4,'ctx'=4,'tp'=2] {'dp'}, dimensions={0} | all-to-all | bytes 2097152 | tf_op jit(solution)/shard_map/all_to_all | solution.py:331
  106.1 17.7 %collective-permute-done.7.refs_0_ = bf16[4,128,1024]{2,1,0:T(8,128)(2,1)S(1)} collective-permute-done((bf16[4,128,1024]{2,1,0:T(8,128)(2,1)S(1)}, bf16[4,128,1024]{2,1,0:T(8,128)(2,1)S(1)}, u32[]{:S(2)}, u32[]{:S(2)}) %collective-permute-start.7) | collective-permute-done | bytes 1048608 | tf_op jit(solution)/shard_map/ppermute | solution.py:254
  129.3 6.7 %delta.2.refs_0_ = bf16[1,4,128,1024]{3,2,1,0:T(8,128)(2,1)} custom-call(s32[3]{0:T(128)S(1)} %pad_add_fusion.place, s32[1]{0:T(128)} %bitcast.5.dest, bf16[4,2,4,64,2048]{4,3,2,1,0:T(8,128)(2,1)} %bitcast.13, bf16[4,1024,512]{2,1,0:T(8,128)(2,1)} %all-to-all-done.refs_4_.weights, bf16[4,128,1024]{2,1,0:T(8,128)(2,1)S(1)} %collective-permute-done.7.refs_0_, ...), custom_call_target="tpu_custom_call" | custom-call | flops 2147483648 | bytes 13631488 | tf_op jit(solution)/shard_map/delta/pallas_call | solution.py:348
  137.7 5.5 %collective-permute-start.9 = (bf16[1,4,128,1024]{3,2,1,0:T(8,128)(2,1)}, bf16[1,4,128,1024]{3,2,1,0:T(8,128)(2,1)}, u32[]{:S(2)}, u32[]{:S(2)}) collective-permute-start(bf16[1,4,128,1024]{3,2,1,0:T(8,128)(2,1)} %delta.2.refs_0_), channel_id=1, source_target_pairs={{0,2},{1,3},{8,10},{9,11},{16,18},{17,19},{24,26},{25,27}} | collective-permute-start | bytes 3145736 | tf_op jit(solution)/shard_map/ppermute | solution.py:254
  144.9 6.5 %collective-permute-done.12.refs_1_.refs_4_ = bf16[4,128,1024]{2,1,0:T(8,128)(2,1)} collective-permute-done((bf16[4,128,1024]{2,1,0:T(8,128)(2,1)S(1)}, bf16[4,128,1024]{2,1,0:T(8,128)(2,1)}, u32[]{:S(2)}, u32[]{:S(2)}) %collective-permute-start.12) | collective-permute-done | bytes 1048608 | tf_op jit(solution)/shard_map/ppermute | solution.py:254
  152.7 12.1 %delta.3.partial_right.partial_left.after.partial = bf16[4,4,128,1024]{3,2,1,0:T(8,128)(2,1)} custom-call(s32[3]{0:T(128)S(1)} %pad_add_fusion.place, s32[4]{0:T(128)S(1)} %and_select_fusion.dest, bf16[4,2,4,64,2048]{4,3,2,1,0:T(8,128)(2,1)} %bitcast.14, bf16[4,1024,512]{2,1,0:T(8,128)(2,1)} %all-to-all-done.refs_4_.weights, ...), custom_call_target="tpu_custom_call" | custom-call | flops 6442450944 | bytes 16777216 | tf_op jit(solution)/shard_map/delta/pallas_call | solution.py:348
  164.8 4.7 %add.89 = (bf16[1,4,128,1024]{3,2,1,0:T(8,128)(2,1)}, bf16[1,4,128,1024]{3,2,1,0:T(8,128)(2,1)}) custom-call(s32[2]{0:T(128)S(1)} %add_clamp_fusion.1.dests, bf16[4,4,128,1024]{3,2,1,0:T(8,128)(2,1)} %delta.3.partial_right.partial_left.after.partial, bf16[4,4,128,1024]{3,2,1,0:T(8,128)(2,1)} %delta.3.partial_right.partial_left.after.partial, ...), custom_call_target="tpu_custom_call" | custom-call | bytes 6291456 | tf_op jit(solution)/shard_map/add/pallas_call | solution.py:397
  169.5 5.6 %collective-permute-start.13 = (bf16[1,4,128,1024]{3,2,1,0:T(8,128)(2,1)}, bf16[1,4,128,1024]{3,2,1,0:T(8,128)(2,1)}, u32[]{:S(2)}, u32[]{:S(2)}) collective-permute-start(bf16[1,4,128,1024]{3,2,1,0:T(8,128)(2,1)} %get-tuple-element.33), channel_id=1, source_target_pairs={{0,2},{2,4},{1,3},{3,5},{8,10},{10,12},{9,11},{11,13},{16,18},{18,... | collective-permute-start | bytes 3145736 | tf_op jit(solution)/shard_map/ppermute | solution.py:254
  176.9 13.8 %flip.1.refs_2_.grad_t = bf16[2048,2048]{1,0:T(8,128)(2,1)} custom-call(s32[3]{0:T(128)S(1)} %pad_add_fusion.place, bf16[4,2,4,64,2048]{4,3,2,1,0:T(8,128)(2,1)} %bitcast.15, bf16[4,4,128,1024]{3,2,1,0:T(8,128)(2,1)} %delta.3.partial_right.partial_left.after.partial), custom_call_target="tpu_custom_call" | custom-call | bytes 16777216 | tf_op jit(solution)/shard_map/flip/pallas_call | solution.py:371
  192.2 3.6 %add.90 = (bf16[1,4,128,1024]{3,2,1,0:T(8,128)(2,1)S(1)}, bf16[1,4,128,1024]{3,2,1,0:T(8,128)(2,1)S(1)}) custom-call(s32[2]{0:T(128)S(1)} %add_clamp_fusion.dests, bf16[4,4,128,1024]{3,2,1,0:T(8,128)(2,1)} %delta.3.partial_right.partial_left.after.partial, bf16[4,4,128,1024]{3,2,1,0:T(8,128)(2,1)} %delta.3.partial_right.partial_left.after.partial, ...), custom_call_target="tpu_custom_call" | custom-call | bytes 6291456 | tf_op jit(solution)/shard_map/add/pallas_call | solution.py:397
  196.8 5.2 %merge.1 = bf16[4,4,128,1024]{3,2,1,0:T(8,128)(2,1)} custom-call(bf16[4,128,1024]{2,1,0:T(8,128)(2,1)S(1)} %copy-done.8, bf16[4,128,1024]{2,1,0:T(8,128)(2,1)S(1)} %collective-permute-done.7.refs_0_, bf16[4,128,1024]{2,1,0:T(8,128)(2,1)S(1)} %copy-done.6, bf16[4,128,1024]{2,1,0:T(8,128)(2,1)} %collective-permute-done.15.refs_0_.refs_2_, ...), custom_call_target="tpu_custom_call" | custom-call | bytes 11534336 | tf_op jit(solution)/shard_map/merge/pallas_call | solution.py:409
  201.9 13.2 %weight.1.after = bf16[4,512,1024]{2,1,0:T(8,128)(2,1)} custom-call(bf16[2048,2048]{1,0:T(8,128)(2,1)} %flip.1.refs_2_.grad_t, bf16[2048,1024]{1,0:T(8,128)(2,1)} %bitcast.16, bf16[1,4,128,1024]{3,2,1,0:T(8,128)(2,1)S(1)} %copy-done.15), custom_call_target="tpu_custom_call" | custom-call | flops 8589934592 | bytes 12582912 | tf_op jit(solution)/shard_map/weight/pallas_call | solution.py:416
  215.1 5.8 %all-to-all-start.2 = ((bf16[4,512,1024]{2,1,0:T(8,128)(2,1)}), bf16[4,512,1024]{2,1,0:T(8,128)(2,1)}, u32[]{:S(2)}, u32[]{:S(2)}) async-start(bf16[4,512,1024]{2,1,0:T(8,128)(2,1)} %weight.1.after), calls=%async_computation.2 | async-start | bytes 8388608 | tf_op jit(solution)/shard_map/all_to_all | solution.py:427
  220.9 6.4 %collective-permute-start.17 = (bf16[1,4,128,1024]{3,2,1,0:T(8,128)(2,1)S(1)}, bf16[1,4,128,1024]{3,2,1,0:T(8,128)(2,1)S(1)}, u32[]{:S(2)}, u32[]{:S(2)}) collective-permute-start(bf16[1,4,128,1024]{3,2,1,0:T(8,128)(2,1)S(1)} %copy-done.15), channel_id=1, source_target_pairs={{0,2},{2,4},{4,6},{1,3},{3,5},{5,7},{8,10},{10,12},{12,14},{9,11},... | collective-permute-start | bytes 3145736 | tf_op jit(solution)/shard_map/ppermute | solution.py:254
  228.7 15.9 %collective-permute-done.17.right = bf16[1,4,128,1024]{3,2,1,0:T(8,128)(2,1)S(1)} collective-permute-done((bf16[1,4,128,1024]{3,2,1,0:T(8,128)(2,1)S(1)}, bf16[1,4,128,1024]{3,2,1,0:T(8,128)(2,1)S(1)}, u32[]{:S(2)}, u32[]{:S(2)}) %collective-permute-start.17) | collective-permute-done | bytes 1048608 | tf_op jit(solution)/shard_map/ppermute | solution.py:254
  244.6 4.3 %collective-permute-done.18.left = bf16[1,4,128,1024]{3,2,1,0:T(8,128)(2,1)S(1)} collective-permute-done((bf16[1,4,128,1024]{3,2,1,0:T(8,128)(2,1)S(1)}, bf16[1,4,128,1024]{3,2,1,0:T(8,128)(2,1)S(1)}, u32[]{:S(2)}, u32[]{:S(2)}) %collective-permute-start.18) | collective-permute-done | bytes 1048608 | tf_op jit(solution)/shard_map/ppermute | solution.py:254
  252.0 3.9 %collective-permute-start.19 = (bf16[128,1024]{1,0:T(8,128)(2,1)S(1)}, bf16[128,1024]{1,0:T(8,128)(2,1)S(1)}, u32[]{:S(2)}, u32[]{:S(2)}) collective-permute-start(bf16[128,1024]{1,0:T(8,128)(2,1)S(1)} %get-tuple-element.38), channel_id=1, source_target_pairs={{0,8},{8,0},{16,24},{24,16},{1,9},{9,1},{17,25},{25,17},{2,10},{10... | collective-permute-start | bytes 786440 | tf_op jit(solution)/shard_map/ppermute | solution.py:250
  257.5 16.6 %collective-permute-done.19.refs_1_ = bf16[128,1024]{1,0:T(8,128)(2,1)S(1)} collective-permute-done((bf16[128,1024]{1,0:T(8,128)(2,1)S(1)}, bf16[128,1024]{1,0:T(8,128)(2,1)S(1)}, u32[]{:S(2)}, u32[]{:S(2)}) %collective-permute-start.19) | collective-permute-done | bytes 262176 | tf_op jit(solution)/shard_map/ppermute | solution.py:250
  276.0 4.9 %seed.1 = (bf16[128,4096]{1,0:T(8,128)(2,1)S(1)}, bf16[16,4096]{1,0:T(8,128)(2,1)S(1)}, bf16[128,4096]{1,0:T(8,128)(2,1)}) custom-call(s32[3]{0:T(128)S(1)} %pad_add_fusion.place, bf16[128,1024]{1,0:T(8,128)(2,1)S(1)} %get-tuple-element.37.refs_0_, bf16[128,1024]{1,0:T(8,128)(2,1)S(1)} %collective-permute-done.19.refs_1_, ...), custom_call_target="tpu_custom_call" | custom-call | flops 134217728 | bytes 5242880 | tf_op jit(solution)/shard_map/seed/pallas_call | solution.py:446
  284.8 3.5 %local_t.1.local = f32[128,4096]{1,0:T(8,128)S(1)} custom-call(f32[256,128]{1,0:T(8,128)S(1)} %multiply_reduce_fusion.refs_5_.rows, bf16[128,4096]{1,0:T(8,128)(2,1)S(1)} %get-tuple-element.42.x), custom_call_target="tpu_custom_call" | custom-call | flops 1073741824 | bytes 3145728 | tf_op jit(solution)/shard_map/local_t/pallas_call | solution.py:291
  295.8 5.1 %back.1 = (bf16[128,4096]{1,0:T(8,128)(2,1)}, bf16[128,4096]{1,0:T(8,128)(2,1)}) custom-call(f32[128,4096]{1,0:T(8,128)} %copy-done.12, bf16[384,4096]{1,0:T(8,128)(2,1)} %get-tuple-element.48.refs_3_.coef, bf16[128,4096]{1,0:T(8,128)(2,1)S(1)} %copy-done.18, bf16[128,4096]{1,0:T(8,128)(2,1)S(1)} %copy-done.11, ...), custom_call_target="tpu_custom_call" | custom-call | flops 134217728 | bytes 6291456 | tf_op jit(solution)/shard_map/back/pallas_call | solution.py:459
  302.1 4.7 %lay.1 = bf16[512,4096]{1,0:T(8,128)(2,1)} custom-call(bf16[4,512,1024]{2,1,0:T(8,128)(2,1)} %all-to-all-done.2.source, bf16[128,4096]{1,0:T(8,128)(2,1)S(1)} %copy-done.16), custom_call_target="tpu_custom_call" | custom-call | bytes 8388608 | tf_op jit(solution)/shard_map/lay/pallas_call | solution.py:468
  (116 shorter events, 67.4 us)
Async XLA Ops:
  7.2 53.7 %all-to-all-start = ((bf16[4,1024,512]{2,1,0:T(8,128)(2,1)}), bf16[4,1024,512]{2,1,0:T(8,128)(2,1)}, u32[]{:S(2)}, u32[]{:S(2)}) async-start(bf16[4,1024,512]{2,1,0:T(8,128)(2,1)} %bitcast.17), calls=%async_computation | async-start | bytes 8388608 | tf_op jit(solution)/shard_map/all_to_all | solution.py:259
  12.3 117.0 %all-gather.3.cloned.1.call-start = ((), (), s32[]{:S(2)}) async-start(), calls=%async_computation.3 | async-start | bytes 9437184 | tf_op jit(solution)/shard_map/all_gather | solution.py:322
  14.3 28.2 %collective-permute-start.3 = (bf16[128,4096]{1,0:T(8,128)(2,1)S(1)}, bf16[128,4096]{1,0:T(8,128)(2,1)}, u32[]{:S(2)}, u32[]{:S(2)}) collective-permute-start(bf16[128,4096]{1,0:T(8,128)(2,1)S(1)} %multiply_convert_fusion.2.x), channel_id=1, source_target_pairs={{0,2},{2,4},{4,6},{1,3},{3,5},{5,7},{8,10},{10,12},{12,14},{9,11},... | collective-permute-start | bytes 3145736 | tf_op jit(solution)/shard_map/ppermute | solution.py:254
  22.3 31.7 %collective-permute-start = (bf16[64,2048]{1,0:T(8,128)(2,1)}, bf16[64,2048]{1,0:T(8,128)(2,1)S(1)}, u32[]{:S(2)}, u32[]{:S(2)}) collective-permute-start(bf16[64,2048]{1,0:T(8,128)(2,1)} %get-tuple-element.27), channel_id=1, source_target_pairs={{0,2},{2,0},{4,6},{6,4},{1,3},{3,1},{5,7},{7,5},{8,10},{10,8},{12,... | collective-permute-start | bytes 786440 | tf_op jit(solution)/shard_map/ppermute | solution.py:250
  22.9 31.1 %collective-permute-start.1 = (bf16[64,2048]{1,0:T(8,128)(2,1)}, bf16[64,2048]{1,0:T(8,128)(2,1)S(1)}, u32[]{:S(2)}, u32[]{:S(2)}) collective-permute-start(bf16[64,2048]{1,0:T(8,128)(2,1)} %get-tuple-element.28), channel_id=1, source_target_pairs={{0,4},{2,6},{4,0},{6,2},{1,5},{3,7},{5,1},{7,3},{8,12},{10,14},{12... | collective-permute-start | bytes 786440 | tf_op jit(solution)/shard_map/ppermute | solution.py:250
  23.9 34.5 %collective-permute-start.2 = (bf16[64,2048]{1,0:T(8,128)(2,1)}, bf16[64,2048]{1,0:T(8,128)(2,1)S(1)}, u32[]{:S(2)}, u32[]{:S(2)}) collective-permute-start(bf16[64,2048]{1,0:T(8,128)(2,1)} %get-tuple-element.29), channel_id=1, source_target_pairs={{0,6},{2,4},{4,2},{6,0},{1,7},{3,5},{5,3},{7,1},{8,14},{10,12},{12... | collective-permute-start | bytes 786440 | tf_op jit(solution)/shard_map/ppermute | solution.py:250
  62.6 11.6 %collective-permute-start.4 = (bf16[16,4096]{1,0:T(8,128)(2,1)S(1)}, bf16[16,4096]{1,0:T(8,128)(2,1)S(1)}, u32[]{:S(2)}, u32[]{:S(2)}) collective-permute-start(bf16[16,4096]{1,0:T(8,128)(2,1)S(1)} %get-tuple-element.31), channel_id=1, source_target_pairs={{0,2},{2,4},{4,6},{1,3},{3,5},{5,7},{8,10},{10,12},{12,14},{9,11},... | collective-permute-start | bytes 393224 | tf_op jit(solution)/shard_map/ppermute | solution.py:254
  69.1 7.1 %collective-permute-start.5 = (bf16[16,4096]{1,0:T(8,128)(2,1)S(1)}, bf16[16,4096]{1,0:T(8,128)(2,1)S(1)}, u32[]{:S(2)}, u32[]{:S(2)}) collective-permute-start(bf16[16,4096]{1,0:T(8,128)(2,1)S(1)} %get-tuple-element.31), channel_id=1, source_target_pairs={{0,4},{2,6},{1,5},{3,7},{8,12},{10,14},{9,13},{11,15},{16,20},{18,... | collective-permute-start | bytes 393224 | tf_op jit(solution)/shard_map/ppermute | solution.py:254
  72.9 4.7 %collective-permute-start.6 = (bf16[16,4096]{1,0:T(8,128)(2,1)S(1)}, bf16[16,4096]{1,0:T(8,128)(2,1)S(1)}, u32[]{:S(2)}, u32[]{:S(2)}) collective-permute-start(bf16[16,4096]{1,0:T(8,128)(2,1)S(1)} %get-tuple-element.31), channel_id=1, source_target_pairs={{0,6},{1,7},{8,14},{9,15},{16,22},{17,23},{24,30},{25,31}} | collective-permute-start | bytes 393224 | tf_op jit(solution)/shard_map/ppermute | solution.py:254
  81.6 46.4 %copy-start.13 = (bf16[128,4096]{1,0:T(8,128)(2,1)}, bf16[128,4096]{1,0:T(8,128)(2,1)S(1)}, u32[]{:S(2)}) copy-start(bf16[128,4096]{1,0:T(8,128)(2,1)S(1)} %get-tuple-element.41.refs_5_) | copy-start | bytes 3145732
  100.4 23.4 %collective-permute-start.7 = (bf16[4,128,1024]{2,1,0:T(8,128)(2,1)S(1)}, bf16[4,128,1024]{2,1,0:T(8,128)(2,1)S(1)}, u32[]{:S(2)}, u32[]{:S(2)}) collective-permute-start(bf16[4,128,1024]{2,1,0:T(8,128)(2,1)S(1)} %all_to_all.15.own), channel_id=1, source_target_pairs={{0,2},{2,4},{4,6},{1,3},{3,5},{5,7},{8,10},{10,12},{12,14},{9,11},... | collective-permute-start | bytes 3145736 | tf_op jit(solution)/shard_map/ppermute | solution.py:254
  103.9 24.1 %collective-permute-start.8 = (bf16[4,128,1024]{2,1,0:T(8,128)(2,1)S(1)}, bf16[4,128,1024]{2,1,0:T(8,128)(2,1)S(1)}, u32[]{:S(2)}, u32[]{:S(2)}) collective-permute-start(bf16[4,128,1024]{2,1,0:T(8,128)(2,1)S(1)} %all_to_all.15.own), channel_id=1, source_target_pairs={{2,0},{4,2},{6,4},{3,1},{5,3},{7,5},{10,8},{12,10},{14,12},{11,9},... | collective-permute-start | bytes 3145736 | tf_op jit(solution)/shard_map/ppermute | solution.py:254
  123.8 19.5 %collective-permute-start.11 = (bf16[4,128,1024]{2,1,0:T(8,128)(2,1)S(1)}, bf16[4,128,1024]{2,1,0:T(8,128)(2,1)S(1)}, u32[]{:S(2)}, u32[]{:S(2)}) collective-permute-start(bf16[4,128,1024]{2,1,0:T(8,128)(2,1)S(1)} %collective-permute-done.7.refs_0_), channel_id=1, source_target_pairs={{2,4},{4,6},{3,5},{5,7},{10,12},{12,14},{11,13},{13,15},{18,20},{2... | collective-permute-start | bytes 3145736 | tf_op jit(solution)/shard_map/ppermute | solution.py:254
  128.0 23.4 %collective-permute-start.12 = (bf16[4,128,1024]{2,1,0:T(8,128)(2,1)S(1)}, bf16[4,128,1024]{2,1,0:T(8,128)(2,1)}, u32[]{:S(2)}, u32[]{:S(2)}) collective-permute-start(bf16[4,128,1024]{2,1,0:T(8,128)(2,1)S(1)} %collective-permute-done.8.refs_1_.refs_5_), channel_id=1, source_target_pairs={{2,0},{4,2},{3,1},{5,3},{10,8},{12,10},{11,9},{13,11},{18,16},{20,... | collective-permute-start | bytes 3145736 | tf_op jit(solution)/shard_map/ppermute | solution.py:254
  136.0 28.8 %collective-permute-start.10 = (bf16[1,4,128,1024]{3,2,1,0:T(8,128)(2,1)}, bf16[1,4,128,1024]{3,2,1,0:T(8,128)(2,1)}, u32[]{:S(2)}, u32[]{:S(2)}) collective-permute-start(bf16[1,4,128,1024]{3,2,1,0:T(8,128)(2,1)} %delta.2.refs_0_), channel_id=1, source_target_pairs={{6,4},{7,5},{14,12},{15,13},{22,20},{23,21},{30,28},{31,29}} | collective-permute-start | bytes 3145736 | tf_op jit(solution)/shard_map/ppermute | solution.py:254
  137.7 27.2 %collective-permute-start.9 = (bf16[1,4,128,1024]{3,2,1,0:T(8,128)(2,1)}, bf16[1,4,128,1024]{3,2,1,0:T(8,128)(2,1)}, u32[]{:S(2)}, u32[]{:S(2)}) collective-permute-start(bf16[1,4,128,1024]{3,2,1,0:T(8,128)(2,1)} %delta.2.refs_0_), channel_id=1, source_target_pairs={{0,2},{1,3},{8,10},{9,11},{16,18},{17,19},{24,26},{25,27}} | collective-permute-start | bytes 3145736 | tf_op jit(solution)/shard_map/ppermute | solution.py:254
  143.3 21.5 %copy-start.5 = (bf16[4,128,1024]{2,1,0:T(8,128)(2,1)}, bf16[4,128,1024]{2,1,0:T(8,128)(2,1)S(1)}, u32[]{:S(2)}) copy-start(bf16[4,128,1024]{2,1,0:T(8,128)(2,1)S(1)} %collective-permute-done.11.refs_0_.refs_1_) | copy-start | bytes 3145732
  143.3 47.5 %collective-permute-start.15 = (bf16[4,128,1024]{2,1,0:T(8,128)(2,1)S(1)}, bf16[4,128,1024]{2,1,0:T(8,128)(2,1)}, u32[]{:S(2)}, u32[]{:S(2)}) collective-permute-start(bf16[4,128,1024]{2,1,0:T(8,128)(2,1)S(1)} %collective-permute-done.11.refs_0_.refs_1_), channel_id=1, source_target_pairs={{4,6},{5,7},{12,14},{13,15},{20,22},{21,23},{28,30},{29,31}} | collective-permute-start | bytes 3145736 | tf_op jit(solution)/shard_map/ppermute | solution.py:254
  151.4 39.4 %collective-permute-start.16 = (bf16[4,128,1024]{2,1,0:T(8,128)(2,1)}, bf16[4,128,1024]{2,1,0:T(8,128)(2,1)S(1)}, u32[]{:S(2)}, u32[]{:S(2)}) collective-permute-start(bf16[4,128,1024]{2,1,0:T(8,128)(2,1)} %collective-permute-done.12.refs_1_.refs_4_), channel_id=1, source_target_pairs={{2,0},{3,1},{10,8},{11,9},{18,16},{19,17},{26,24},{27,25}} | collective-permute-start | bytes 3145736 | tf_op jit(solution)/shard_map/ppermute | solution.py:254
  169.5 22.6 %collective-permute-start.13 = (bf16[1,4,128,1024]{3,2,1,0:T(8,128)(2,1)}, bf16[1,4,128,1024]{3,2,1,0:T(8,128)(2,1)}, u32[]{:S(2)}, u32[]{:S(2)}) collective-permute-start(bf16[1,4,128,1024]{3,2,1,0:T(8,128)(2,1)} %get-tuple-element.33), channel_id=1, source_target_pairs={{0,2},{2,4},{1,3},{3,5},{8,10},{10,12},{9,11},{11,13},{16,18},{18,... | collective-permute-start | bytes 3145736 | tf_op jit(solution)/shard_map/ppermute | solution.py:254
  175.1 17.0 %collective-permute-start.14 = (bf16[1,4,128,1024]{3,2,1,0:T(8,128)(2,1)}, bf16[1,4,128,1024]{3,2,1,0:T(8,128)(2,1)}, u32[]{:S(2)}, u32[]{:S(2)}) collective-permute-start(bf16[1,4,128,1024]{3,2,1,0:T(8,128)(2,1)} %get-tuple-element.34), channel_id=1, source_target_pairs={{4,2},{6,4},{5,3},{7,5},{12,10},{14,12},{13,11},{15,13},{20,18},{2... | collective-permute-start | bytes 3145736 | tf_op jit(solution)/shard_map/ppermute | solution.py:254
  215.1 85.8 %all-to-all-start.2 = ((bf16[4,512,1024]{2,1,0:T(8,128)(2,1)}), bf16[4,512,1024]{2,1,0:T(8,128)(2,1)}, u32[]{:S(2)}, u32[]{:S(2)}) async-start(bf16[4,512,1024]{2,1,0:T(8,128)(2,1)} %weight.1.after), calls=%async_computation.2 | async-start | bytes 8388608 | tf_op jit(solution)/shard_map/all_to_all | solution.py:427
  220.9 23.7 %collective-permute-start.17 = (bf16[1,4,128,1024]{3,2,1,0:T(8,128)(2,1)S(1)}, bf16[1,4,128,1024]{3,2,1,0:T(8,128)(2,1)S(1)}, u32[]{:S(2)}, u32[]{:S(2)}) collective-permute-start(bf16[1,4,128,1024]{3,2,1,0:T(8,128)(2,1)S(1)} %copy-done.15), channel_id=1, source_target_pairs={{0,2},{2,4},{4,6},{1,3},{3,5},{5,7},{8,10},{10,12},{12,14},{9,11},... | collective-permute-start | bytes 3145736 | tf_op jit(solution)/shard_map/ppermute | solution.py:254
  227.3 48.7 %copy-start.10 = (bf16[128,4096]{1,0:T(8,128)(2,1)S(1)}, bf16[128,4096]{1,0:T(8,128)(2,1)}, u32[]{:S(2)}) copy-start(bf16[128,4096]{1,0:T(8,128)(2,1)} %refs_4_.1) | copy-start | bytes 3145732
  227.3 21.7 %collective-permute-start.18 = (bf16[1,4,128,1024]{3,2,1,0:T(8,128)(2,1)S(1)}, bf16[1,4,128,1024]{3,2,1,0:T(8,128)(2,1)S(1)}, u32[]{:S(2)}, u32[]{:S(2)}) collective-permute-start(bf16[1,4,128,1024]{3,2,1,0:T(8,128)(2,1)S(1)} %copy-done.20), channel_id=1, source_target_pairs={{2,0},{4,2},{6,4},{3,1},{5,3},{7,5},{10,8},{12,10},{14,12},{11,9},... | collective-permute-start | bytes 3145736 | tf_op jit(solution)/shard_map/ppermute | solution.py:254
  252.0 22.1 %collective-permute-start.19 = (bf16[128,1024]{1,0:T(8,128)(2,1)S(1)}, bf16[128,1024]{1,0:T(8,128)(2,1)S(1)}, u32[]{:S(2)}, u32[]{:S(2)}) collective-permute-start(bf16[128,1024]{1,0:T(8,128)(2,1)S(1)} %get-tuple-element.38), channel_id=1, source_target_pairs={{0,8},{8,0},{16,24},{24,16},{1,9},{9,1},{17,25},{25,17},{2,10},{10... | collective-permute-start | bytes 786440 | tf_op jit(solution)/shard_map/ppermute | solution.py:250
  256.0 18.1 %collective-permute-start.20 = (bf16[128,1024]{1,0:T(8,128)(2,1)S(1)}, bf16[128,1024]{1,0:T(8,128)(2,1)S(1)}, u32[]{:S(2)}, u32[]{:S(2)}) collective-permute-start(bf16[128,1024]{1,0:T(8,128)(2,1)S(1)} %get-tuple-element.39), channel_id=1, source_target_pairs={{0,16},{8,24},{16,0},{24,8},{1,17},{9,25},{17,1},{25,9},{2,18},{10... | collective-permute-start | bytes 786440 | tf_op jit(solution)/shard_map/ppermute | solution.py:250
  256.0 20.0 %collective-permute-start.21 = (bf16[128,1024]{1,0:T(8,128)(2,1)S(1)}, bf16[128,1024]{1,0:T(8,128)(2,1)S(1)}, u32[]{:S(2)}, u32[]{:S(2)}) collective-permute-start(bf16[128,1024]{1,0:T(8,128)(2,1)S(1)} %get-tuple-element.40), channel_id=1, source_target_pairs={{0,24},{8,16},{16,8},{24,0},{1,25},{9,17},{17,9},{25,1},{2,26},{10... | collective-permute-start | bytes 786440 | tf_op jit(solution)/shard_map/ppermute | solution.py:250
  276.0 19.8 %copy-start.18 = (bf16[128,4096]{1,0:T(8,128)(2,1)S(1)}, bf16[128,4096]{1,0:T(8,128)(2,1)}, u32[]{:S(2)}) copy-start(bf16[128,4096]{1,0:T(8,128)(2,1)} %copy-done.17) | copy-start | bytes 3145732
  280.9 10.2 %collective-permute-start.22 = (bf16[16,4096]{1,0:T(8,128)(2,1)S(1)}, bf16[16,4096]{1,0:T(8,128)(2,1)S(1)}, u32[]{:S(2)}, u32[]{:S(2)}) collective-permute-start(bf16[16,4096]{1,0:T(8,128)(2,1)S(1)} %get-tuple-element.44), channel_id=1, source_target_pairs={{2,0},{4,2},{6,4},{3,1},{5,3},{7,5},{10,8},{12,10},{14,12},{11,9},... | collective-permute-start | bytes 393224 | tf_op jit(solution)/shard_map/ppermute | solution.py:254
  282.2 10.8 %collective-permute-start.23 = (bf16[16,4096]{1,0:T(8,128)(2,1)S(1)}, bf16[16,4096]{1,0:T(8,128)(2,1)S(1)}, u32[]{:S(2)}, u32[]{:S(2)}) collective-permute-start(bf16[16,4096]{1,0:T(8,128)(2,1)S(1)} %get-tuple-element.44), channel_id=1, source_target_pairs={{4,0},{6,2},{5,1},{7,3},{12,8},{14,10},{13,9},{15,11},{20,16},{22,... | collective-permute-start | bytes 393224 | tf_op jit(solution)/shard_map/ppermute | solution.py:254
  283.5 12.3 %collective-permute-start.24 = (bf16[16,4096]{1,0:T(8,128)(2,1)S(1)}, bf16[16,4096]{1,0:T(8,128)(2,1)S(1)}, u32[]{:S(2)}, u32[]{:S(2)}) collective-permute-start(bf16[16,4096]{1,0:T(8,128)(2,1)S(1)} %get-tuple-element.44), channel_id=1, source_target_pairs={{6,0},{7,1},{14,8},{15,9},{22,16},{23,17},{30,24},{31,25}} | collective-permute-start | bytes 393224 | tf_op jit(solution)/shard_map/ppermute | solution.py:254
  (21 other events, 123.6 us)
Sparse Core Ops, SparseCore 0:
  62.7 64.1 all-gather.2

commit v7 on v6

--- a/solution.py
+++ b/solution.py
@@ -188,6 +188,10 @@
 
 def lay_body(source, after, target):
     target[...] = source[0]
+
+
+def wait_body(*refs):
+    pass
 
 
 def add_body(dests, partial_right, partial_left, right, left, *refs):
@@ -424,7 +428,6 @@
         out_specs=pl.BlockSpec((1, feats, quarter), lambda i: (i, 0, 0)),
         out_shape=shape(n_dp, feats, quarter),
     )(grad_t, gated_all, token)
-    weight_far = lax.all_to_all(weight_part, "dp", 0, 0, tiled=True)
 
     delta = call(
         sum_body, "sum", 0, 8 * n_dp * rows * quarter,
@@ -440,6 +443,12 @@
         ),
         out_shape=[shape(rows, quarter)] * n_dp,
     )(place, partial, right, left, weight_part)
+    held = call(
+        wait_body, "hold", 0, 0,
+        in_specs=[ANY] * 2, out_specs=ANY,
+        out_shape=shape(n_dp, feats, quarter), input_output_aliases={0: 0},
+    )(weight_part, delta[0])
+    weight_far = lax.all_to_all(held, "dp", 0, 0, tiled=True)
     delta = [delta[0]] + [swap(delta[k], "dp", k) for k in range(1, n_dp)]
 
     here = pl.BlockSpec((rows, block), lambda i, p: (0, p[0] ^ i))

time: 318 us -> 324 us (1.019)
  waiting for transfers between devices: 88.5 us -> 96.3 us
    ppermute x6, waiting for transfers between devices: 22.8 us -> 52.7 us  [swap(): lax.ppermute(value, axis, [(i, i ^ k) for i in range(lax.axis_size(axis))])]
    ppermute x19, waiting for transfers between devices: 63.1 us -> 41 us  [shift(): return lax.ppermute(value, 'ctx', ends)]
    unnamed x51 -> x47, local copies, waits for them, and re-layouts: 6.93 us -> 7.19 us
  transfers between devices with their start and end apart: 28 -> 28, of which waited for: 16 -> 14; matrix products, arithmetic and copies ran while one was open for 3% -> 3% of each run, Pallas kernels for 23% -> 27%
where the time goes in v7:
time: 324 us; the launch traced here: 322 us
  Pallas kernels  102 us (31%)
  waiting for transfers between devices  96.3 us (30%)
  starting transfers between devices  74.3 us (23%)
  blocking collectives  18.8 us (6%)
  between operations  14.5 us (4%)
  other arithmetic  8.53 us (3%)
  local copies, waits for them, and re-layouts  8.04 us (2%)
    ppermute x19, starting transfers between devices, shift(): return lax.ppermute(value, 'ctx', ends)  52.9 us
    ppermute x6, waiting for transfers between devices, swap(): lax.ppermute(value, axis, [(i, i ^ k) for i in range(lax.axis_size(axis))])  52.7 us
    ppermute x19, waiting for transfers between devices, shift(): return lax.ppermute(value, 'ctx', ends)  41 us
    pallas_call x2, Pallas kernels, project(): call(functools.partial(delta_body, whole), 'delta', 2 * max(count - 1, 1)...  18.8 us
    all_to_all x1, blocking collectives, on_device(): gated_far = lax.all_to_all(gated, 'dp', 0, 0, tiled=True)  18.8 us
    pallas_call x1, Pallas kernels, on_device(): call(flip_body, 'flip', 0, 4 * tokens * depth, grid_spec=pltpu.PrefetchSc...  13.8 us
    pallas_call x1, Pallas kernels, on_device(): call(weight_body, 'weight', 2 * tokens * depth * quarter, 2 * tokens * (d...  13.3 us
    pallas_call x3, Pallas kernels, local(): call(functools.partial(local_body, transposed), 'local_t' if transposed e...  11.2 us
  transfers between devices with their start and end apart: 28, of which 14 were waited for; matrix products, arithmetic and copies ran while one was open for 3% of the time, Pallas kernels for 27%

profile of v7, /device:TPU:0, one launch (start us, length us, event | category | flops | bytes accessed | tf_op | source)
XLA Modules:
  0.0 322.1 jit_solution(14035148393269638583)
XLA Ops:
  7.2 5.2 %all-to-all-start = ((bf16[4,1024,512]{2,1,0:T(8,128)(2,1)}), bf16[4,1024,512]{2,1,0:T(8,128)(2,1)}, u32[]{:S(2)}, u32[]{:S(2)}) async-start(bf16[4,1024,512]{2,1,0:T(8,128)(2,1)} %bitcast.17), calls=%async_computation | async-start | bytes 8388608 | tf_op jit(solution)/shard_map/all_to_all | solution.py:263
  14.3 5.7 %collective-permute-start.3 = (bf16[128,4096]{1,0:T(8,128)(2,1)S(1)}, bf16[128,4096]{1,0:T(8,128)(2,1)}, u32[]{:S(2)}, u32[]{:S(2)}) collective-permute-start(bf16[128,4096]{1,0:T(8,128)(2,1)S(1)} %multiply_convert_fusion.2.x), channel_id=1, source_target_pairs={{0,2},{2,4},{4,6},{1,3},{3,5},{5,7},{8,10},{10,12},{12,14},{9,11},... | collective-permute-start | bytes 3145736 | tf_op jit(solution)/shard_map/ppermute | solution.py:258
  29.6 3.7 %multiply_convert_fusion = (bf16[384,4096]{1,0:T(8,128)(2,1)}, bf16[384,4096]{1,0:T(8,128)(2,1)}) fusion(f32[384]{0:T(512)S(1)} %get-tuple-element.52, f32[4096]{0:T(1024)S(1)} %neg.22, f32[4096]{0:T(1024)S(1)} %mul.110, f32[384]{0:T(512)S(1)} %get-tuple-element.53), kind=kLoop, calls=%fused_computation | loop fusion | flops 9437184 | bytes 6327296 | tf_op jit(solution)/shard_map/convert_element_type | solution.py:284
  34.1 4.2 %local.2.own_part = f32[128,4096]{1,0:T(8,128)} custom-call(f32[256,128]{1,0:T(8,128)S(1)} %pad_maximum_fusion.1.rows.taps, bf16[128,4096]{1,0:T(8,128)(2,1)S(1)} %multiply_convert_fusion.2.x, bf16[4096,128]{1,0:T(8,128)(2,1)S(1)} %get-tuple-element.51.refs_0_.ends_coef, bf16[4096,128]{1,0:T(8,128)(2,1)S(1)} %get-tuple-element.50.refs_1_.refs_6_, ...), custom_call_target="tpu_custom_call" | custom-call | flops 1073741824 | bytes 3145728 | tf_op jit(solution)/shard_map/local/pallas_call | solution.py:295
  38.3 4.2 %collective-permute-done.3.rim = bf16[128,4096]{1,0:T(8,128)(2,1)} collective-permute-done((bf16[128,4096]{1,0:T(8,128)(2,1)S(1)}, bf16[128,4096]{1,0:T(8,128)(2,1)}, u32[]{:S(2)}, u32[]{:S(2)}) %collective-permute-start.3) | collective-permute-done | bytes 1048608 | tf_op jit(solution)/shard_map/ppermute | solution.py:258
  42.5 5.7 %conv.1 = (bf16[128,4096]{1,0:T(8,128)(2,1)S(1)}, bf16[128,4096]{1,0:T(8,128)(2,1)S(1)}, bf16[16,4096]{1,0:T(8,128)(2,1)S(1)}) custom-call(bf16[128,4096]{1,0:T(8,128)(2,1)} %collective-permute-done.3.rim, f32[128,4096]{1,0:T(8,128)} %local.2.own_part, bf16[128,4096]{1,0:T(8,128)(2,1)} %query.3, f32[256,128]{1,0:T(8,128)S(1)} %pad_maximum_fusion.1.rows.taps, ...), custom_call_target="tpu_custom_call" | custom-call | flops 1073741824 | bytes 7340032 | tf_op jit(solution)/shard_map/conv/pallas_call | solution.py:308
  49.2 3.5 %local.3.refs_5_ = f32[128,4096]{1,0:T(8,128)S(1)} custom-call(f32[256,128]{1,0:T(8,128)S(1)} %pad_maximum_fusion.refs_4_.rows, bf16[128,4096]{1,0:T(8,128)(2,1)S(1)} %get-tuple-element.30.x), custom_call_target="tpu_custom_call" | custom-call | flops 1073741824 | bytes 3145728 | tf_op jit(solution)/shard_map/local/pallas_call | solution.py:295
  54.0 4.3 %collective-permute-done.2.refs_3_ = bf16[64,2048]{1,0:T(8,128)(2,1)S(1)} collective-permute-done((bf16[64,2048]{1,0:T(8,128)(2,1)}, bf16[64,2048]{1,0:T(8,128)(2,1)S(1)}, u32[]{:S(2)}, u32[]{:S(2)}) %collective-permute-start.2) | collective-permute-done | bytes 262176 | tf_op jit(solution)/shard_map/ppermute | solution.py:254
  62.6 6.6 %collective-permute-start.4 = (bf16[16,4096]{1,0:T(8,128)(2,1)S(1)}, bf16[16,4096]{1,0:T(8,128)(2,1)S(1)}, u32[]{:S(2)}, u32[]{:S(2)}) collective-permute-start(bf16[16,4096]{1,0:T(8,128)(2,1)S(1)} %get-tuple-element.31), channel_id=1, source_target_pairs={{0,2},{2,4},{4,6},{1,3},{3,5},{5,7},{8,10},{10,12},{12,14},{9,11},... | collective-permute-start | bytes 393224 | tf_op jit(solution)/shard_map/ppermute | solution.py:258
  69.1 3.7 %collective-permute-start.5 = (bf16[16,4096]{1,0:T(8,128)(2,1)S(1)}, bf16[16,4096]{1,0:T(8,128)(2,1)S(1)}, u32[]{:S(2)}, u32[]{:S(2)}) collective-permute-start(bf16[16,4096]{1,0:T(8,128)(2,1)S(1)} %get-tuple-element.31), channel_id=1, source_target_pairs={{0,4},{2,6},{1,5},{3,7},{8,12},{10,14},{9,13},{11,15},{16,20},{18,... | collective-permute-start | bytes 393224 | tf_op jit(solution)/shard_map/ppermute | solution.py:258
  77.6 4.0 %long.1 = (bf16[128,4096]{1,0:T(8,128)(2,1)S(1)}, bf16[4,128,1024]{2,1,0:T(8,128)(2,1)S(1)}) custom-call(f32[128,4096]{1,0:T(8,128)} %copy-done.3, bf16[384,4096]{1,0:T(8,128)(2,1)} %get-tuple-element.49.refs_2_.coef, bf16[128,4096]{1,0:T(8,128)(2,1)S(1)} %copy-done.9, bf16[16,4096]{1,0:T(8,128)(2,1)S(1)} %collective-permute-done.4.refs_0_, ...), custom_call_target="tpu_custom_call" | custom-call | flops 134217728 | bytes 5242880 | tf_op jit(solution)/shard_map/long/pallas_call | solution.py:328
  81.6 18.8 %all_to_all.15.own = bf16[4,128,1024]{2,1,0:T(8,128)(2,1)S(1)} all-to-all(bf16[4,128,1024]{2,1,0:T(8,128)(2,1)S(1)} %get-tuple-element.32), channel_id=1, replica_groups=mesh['dp'=4,'ctx'=4,'tp'=2] {'dp'}, dimensions={0} | all-to-all | bytes 2097152 | tf_op jit(solution)/shard_map/all_to_all | solution.py:335
  106.2 17.7 %collective-permute-done.7.refs_0_ = bf16[4,128,1024]{2,1,0:T(8,128)(2,1)S(1)} collective-permute-done((bf16[4,128,1024]{2,1,0:T(8,128)(2,1)S(1)}, bf16[4,128,1024]{2,1,0:T(8,128)(2,1)S(1)}, u32[]{:S(2)}, u32[]{:S(2)}) %collective-permute-start.7) | collective-permute-done | bytes 1048608 | tf_op jit(solution)/shard_map/ppermute | solution.py:258
  124.5 3.5 %collective-permute-done.8.refs_1_.refs_5_ = bf16[4,128,1024]{2,1,0:T(8,128)(2,1)S(1)} collective-permute-done((bf16[4,128,1024]{2,1,0:T(8,128)(2,1)S(1)}, bf16[4,128,1024]{2,1,0:T(8,128)(2,1)S(1)}, u32[]{:S(2)}, u32[]{:S(2)}) %collective-permute-start.8) | collective-permute-done | bytes 1048608 | tf_op jit(solution)/shard_map/ppermute | solution.py:258
  129.3 6.7 %delta.2.refs_0_ = bf16[1,4,128,1024]{3,2,1,0:T(8,128)(2,1)} custom-call(s32[3]{0:T(128)S(1)} %pad_add_fusion.place, s32[1]{0:T(128)} %bitcast.5.dest, bf16[4,2,4,64,2048]{4,3,2,1,0:T(8,128)(2,1)} %bitcast.13, bf16[4,1024,512]{2,1,0:T(8,128)(2,1)} %all-to-all-done.refs_4_.weights, bf16[4,128,1024]{2,1,0:T(8,128)(2,1)S(1)} %collective-permute-done.7.refs_0_, ...), custom_call_target="tpu_custom_call" | custom-call | flops 2147483648 | bytes 13631488 | tf_op jit(solution)/shard_map/delta/pallas_call | solution.py:352
  137.7 5.5 %collective-permute-start.9 = (bf16[1,4,128,1024]{3,2,1,0:T(8,128)(2,1)}, bf16[1,4,128,1024]{3,2,1,0:T(8,128)(2,1)}, u32[]{:S(2)}, u32[]{:S(2)}) collective-permute-start(bf16[1,4,128,1024]{3,2,1,0:T(8,128)(2,1)} %delta.2.refs_0_), channel_id=1, source_target_pairs={{0,2},{1,3},{8,10},{9,11},{16,18},{17,19},{24,26},{25,27}} | collective-permute-start | bytes 3145736 | tf_op jit(solution)/shard_map/ppermute | solution.py:258
  144.9 6.5 %collective-permute-done.12.refs_1_.refs_4_ = bf16[4,128,1024]{2,1,0:T(8,128)(2,1)} collective-permute-done((bf16[4,128,1024]{2,1,0:T(8,128)(2,1)S(1)}, bf16[4,128,1024]{2,1,0:T(8,128)(2,1)}, u32[]{:S(2)}, u32[]{:S(2)}) %collective-permute-start.12) | collective-permute-done | bytes 1048608 | tf_op jit(solution)/shard_map/ppermute | solution.py:258
  152.7 12.1 %delta.3.partial_right.partial_left.after.partial = bf16[4,4,128,1024]{3,2,1,0:T(8,128)(2,1)} custom-call(s32[3]{0:T(128)S(1)} %pad_add_fusion.place, s32[4]{0:T(128)S(1)} %and_select_fusion.dest, bf16[4,2,4,64,2048]{4,3,2,1,0:T(8,128)(2,1)} %bitcast.14, bf16[4,1024,512]{2,1,0:T(8,128)(2,1)} %all-to-all-done.refs_4_.weights, ...), custom_call_target="tpu_custom_call" | custom-call | flops 6442450944 | bytes 16777216 | tf_op jit(solution)/shard_map/delta/pallas_call | solution.py:352
  164.8 4.7 %add.89 = (bf16[1,4,128,1024]{3,2,1,0:T(8,128)(2,1)}, bf16[1,4,128,1024]{3,2,1,0:T(8,128)(2,1)}) custom-call(s32[2]{0:T(128)S(1)} %add_clamp_fusion.1.dests, bf16[4,4,128,1024]{3,2,1,0:T(8,128)(2,1)} %delta.3.partial_right.partial_left.after.partial, bf16[4,4,128,1024]{3,2,1,0:T(8,128)(2,1)} %delta.3.partial_right.partial_left.after.partial, ...), custom_call_target="tpu_custom_call" | custom-call | bytes 6291456 | tf_op jit(solution)/shard_map/add/pallas_call | solution.py:401
  169.6 5.6 %collective-permute-start.13 = (bf16[1,4,128,1024]{3,2,1,0:T(8,128)(2,1)}, bf16[1,4,128,1024]{3,2,1,0:T(8,128)(2,1)}, u32[]{:S(2)}, u32[]{:S(2)}) collective-permute-start(bf16[1,4,128,1024]{3,2,1,0:T(8,128)(2,1)} %get-tuple-element.33), channel_id=1, source_target_pairs={{0,2},{2,4},{1,3},{3,5},{8,10},{10,12},{9,11},{11,13},{16,18},{18,... | collective-permute-start | bytes 3145736 | tf_op jit(solution)/shard_map/ppermute | solution.py:258
  176.9 13.8 %flip.1.refs_2_.grad_t = bf16[2048,2048]{1,0:T(8,128)(2,1)} custom-call(s32[3]{0:T(128)S(1)} %pad_add_fusion.place, bf16[4,2,4,64,2048]{4,3,2,1,0:T(8,128)(2,1)} %bitcast.15, bf16[4,4,128,1024]{3,2,1,0:T(8,128)(2,1)} %delta.3.partial_right.partial_left.after.partial), custom_call_target="tpu_custom_call" | custom-call | bytes 16777216 | tf_op jit(solution)/shard_map/flip/pallas_call | solution.py:375
  192.2 3.6 %add.90 = (bf16[1,4,128,1024]{3,2,1,0:T(8,128)(2,1)S(1)}, bf16[1,4,128,1024]{3,2,1,0:T(8,128)(2,1)S(1)}) custom-call(s32[2]{0:T(128)S(1)} %add_clamp_fusion.dests, bf16[4,4,128,1024]{3,2,1,0:T(8,128)(2,1)} %delta.3.partial_right.partial_left.after.partial, bf16[4,4,128,1024]{3,2,1,0:T(8,128)(2,1)} %delta.3.partial_right.partial_left.after.partial, ...), custom_call_target="tpu_custom_call" | custom-call | bytes 6291456 | tf_op jit(solution)/shard_map/add/pallas_call | solution.py:401
  195.8 6.4 %collective-permute-start.17 = (bf16[1,4,128,1024]{3,2,1,0:T(8,128)(2,1)S(1)}, bf16[1,4,128,1024]{3,2,1,0:T(8,128)(2,1)S(1)}, u32[]{:S(2)}, u32[]{:S(2)}) collective-permute-start(bf16[1,4,128,1024]{3,2,1,0:T(8,128)(2,1)S(1)} %get-tuple-element.35.refs_6_.after), channel_id=1, source_target_pairs={{0,2},{2,4},{4,6},{1,3},{3,5},{5,7},{8,10},{10,12},{12,14},{9,11},... | collective-permute-start | bytes 3145736 | tf_op jit(solution)/shard_map/ppermute | solution.py:258
  203.5 4.8 %merge.1 = bf16[4,4,128,1024]{3,2,1,0:T(8,128)(2,1)} custom-call(bf16[4,128,1024]{2,1,0:T(8,128)(2,1)S(1)} %copy-done.8, bf16[4,128,1024]{2,1,0:T(8,128)(2,1)S(1)} %collective-permute-done.7.refs_0_, bf16[4,128,1024]{2,1,0:T(8,128)(2,1)S(1)} %copy-done.6, bf16[4,128,1024]{2,1,0:T(8,128)(2,1)} %collective-permute-done.15.refs_0_.refs_2_, ...), custom_call_target="tpu_custom_call" | custom-call | bytes 11534336 | tf_op jit(solution)/shard_map/merge/pallas_call | solution.py:413
  209.5 13.3 %weight.1.after.refs_0_ = bf16[4,512,1024]{2,1,0:T(8,128)(2,1)} custom-call(bf16[2048,2048]{1,0:T(8,128)(2,1)} %flip.1.refs_2_.grad_t, bf16[2048,1024]{1,0:T(8,128)(2,1)} %bitcast.16, bf16[1,4,128,1024]{3,2,1,0:T(8,128)(2,1)S(1)} %copy-done.16), custom_call_target="tpu_custom_call" | custom-call | flops 8589934592 | bytes 12582912 | tf_op jit(solution)/shard_map/weight/pallas_call | solution.py:420
  226.2 6.7 %all-to-all-start.2 = ((bf16[4,512,1024]{2,1,0:T(8,128)(2,1)}), bf16[4,512,1024]{2,1,0:T(8,128)(2,1)}, u32[]{:S(2)}, u32[]{:S(2)}) async-start(bf16[4,512,1024]{2,1,0:T(8,128)(2,1)} %hold.1), calls=%async_computation.2 | async-start | bytes 8388608 | tf_op jit(solution)/shard_map/all_to_all | solution.py:451
  232.9 3.6 %collective-permute-start.19 = (bf16[128,1024]{1,0:T(8,128)(2,1)S(1)}, bf16[128,1024]{1,0:T(8,128)(2,1)S(1)}, u32[]{:S(2)}, u32[]{:S(2)}) collective-permute-start(bf16[128,1024]{1,0:T(8,128)(2,1)S(1)} %get-tuple-element.38), channel_id=1, source_target_pairs={{0,8},{8,0},{16,24},{24,16},{1,9},{9,1},{17,25},{25,17},{2,10},{10... | collective-permute-start | bytes 786440 | tf_op jit(solution)/shard_map/ppermute | solution.py:254
  238.1 46.8 %collective-permute-done.19.refs_1_ = bf16[128,1024]{1,0:T(8,128)(2,1)S(1)} collective-permute-done((bf16[128,1024]{1,0:T(8,128)(2,1)S(1)}, bf16[128,1024]{1,0:T(8,128)(2,1)S(1)}, u32[]{:S(2)}, u32[]{:S(2)}) %collective-permute-start.19) | collective-permute-done | bytes 262176 | tf_op jit(solution)/shard_map/ppermute | solution.py:254
  286.5 4.9 %seed.1 = (bf16[128,4096]{1,0:T(8,128)(2,1)S(1)}, bf16[16,4096]{1,0:T(8,128)(2,1)S(1)}, bf16[128,4096]{1,0:T(8,128)(2,1)}) custom-call(s32[3]{0:T(128)S(1)} %pad_add_fusion.place, bf16[128,1024]{1,0:T(8,128)(2,1)S(1)} %get-tuple-element.37.refs_0_.refs_1_, bf16[128,1024]{1,0:T(8,128)(2,1)S(1)} %collective-permute-done.19.refs_1_, ...), custom_call_target="tpu_custom_call" | custom-call | flops 134217728 | bytes 5242880 | tf_op jit(solution)/shard_map/seed/pallas_call | solution.py:455
  295.3 3.5 %local_t.1.local = f32[128,4096]{1,0:T(8,128)S(1)} custom-call(f32[256,128]{1,0:T(8,128)S(1)} %multiply_reduce_fusion.refs_5_.rows, bf16[128,4096]{1,0:T(8,128)(2,1)S(1)} %get-tuple-element.42.x), custom_call_target="tpu_custom_call" | custom-call | flops 1073741824 | bytes 3145728 | tf_op jit(solution)/shard_map/local_t/pallas_call | solution.py:295
  304.2 5.1 %back.1 = (bf16[128,4096]{1,0:T(8,128)(2,1)}, bf16[128,4096]{1,0:T(8,128)(2,1)}) custom-call(f32[128,4096]{1,0:T(8,128)} %copy-done.12, bf16[384,4096]{1,0:T(8,128)(2,1)} %get-tuple-element.48.refs_3_.coef, bf16[128,4096]{1,0:T(8,128)(2,1)S(1)} %copy-done.18, bf16[128,4096]{1,0:T(8,128)(2,1)S(1)} %copy-done.11, ...), custom_call_target="tpu_custom_call" | custom-call | flops 134217728 | bytes 6291456 | tf_op jit(solution)/shard_map/back/pallas_call | solution.py:468
  310.5 4.7 %lay.1 = bf16[512,4096]{1,0:T(8,128)(2,1)} custom-call(bf16[4,512,1024]{2,1,0:T(8,128)(2,1)} %all-to-all-done.2.source, bf16[128,4096]{1,0:T(8,128)(2,1)S(1)} %copy-done.14), custom_call_target="tpu_custom_call" | custom-call | bytes 8388608 | tf_op jit(solution)/shard_map/lay/pallas_call | solution.py:477
  (113 shorter events, 58.5 us)
Async XLA Ops:
  7.2 53.7 %all-to-all-start = ((bf16[4,1024,512]{2,1,0:T(8,128)(2,1)}), bf16[4,1024,512]{2,1,0:T(8,128)(2,1)}, u32[]{:S(2)}, u32[]{:S(2)}) async-start(bf16[4,1024,512]{2,1,0:T(8,128)(2,1)} %bitcast.17), calls=%async_computation | async-start | bytes 8388608 | tf_op jit(solution)/shard_map/all_to_all | solution.py:263
  12.3 117.0 %all-gather.3.cloned.1.call-start = ((), (), s32[]{:S(2)}) async-start(), calls=%async_computation.3 | async-start | bytes 9437184 | tf_op jit(solution)/shard_map/all_gather | solution.py:326
  14.3 28.2 %collective-permute-start.3 = (bf16[128,4096]{1,0:T(8,128)(2,1)S(1)}, bf16[128,4096]{1,0:T(8,128)(2,1)}, u32[]{:S(2)}, u32[]{:S(2)}) collective-permute-start(bf16[128,4096]{1,0:T(8,128)(2,1)S(1)} %multiply_convert_fusion.2.x), channel_id=1, source_target_pairs={{0,2},{2,4},{4,6},{1,3},{3,5},{5,7},{8,10},{10,12},{12,14},{9,11},... | collective-permute-start | bytes 3145736 | tf_op jit(solution)/shard_map/ppermute | solution.py:258
  22.3 31.7 %collective-permute-start = (bf16[64,2048]{1,0:T(8,128)(2,1)}, bf16[64,2048]{1,0:T(8,128)(2,1)S(1)}, u32[]{:S(2)}, u32[]{:S(2)}) collective-permute-start(bf16[64,2048]{1,0:T(8,128)(2,1)} %get-tuple-element.27), channel_id=1, source_target_pairs={{0,2},{2,0},{4,6},{6,4},{1,3},{3,1},{5,7},{7,5},{8,10},{10,8},{12,... | collective-permute-start | bytes 786440 | tf_op jit(solution)/shard_map/ppermute | solution.py:254
  22.9 31.1 %collective-permute-start.1 = (bf16[64,2048]{1,0:T(8,128)(2,1)}, bf16[64,2048]{1,0:T(8,128)(2,1)S(1)}, u32[]{:S(2)}, u32[]{:S(2)}) collective-permute-start(bf16[64,2048]{1,0:T(8,128)(2,1)} %get-tuple-element.28), channel_id=1, source_target_pairs={{0,4},{2,6},{4,0},{6,2},{1,5},{3,7},{5,1},{7,3},{8,12},{10,14},{12... | collective-permute-start | bytes 786440 | tf_op jit(solution)/shard_map/ppermute | solution.py:254
  23.9 34.5 %collective-permute-start.2 = (bf16[64,2048]{1,0:T(8,128)(2,1)}, bf16[64,2048]{1,0:T(8,128)(2,1)S(1)}, u32[]{:S(2)}, u32[]{:S(2)}) collective-permute-start(bf16[64,2048]{1,0:T(8,128)(2,1)} %get-tuple-element.29), channel_id=1, source_target_pairs={{0,6},{2,4},{4,2},{6,0},{1,7},{3,5},{5,3},{7,1},{8,14},{10,12},{12... | collective-permute-start | bytes 786440 | tf_op jit(solution)/shard_map/ppermute | solution.py:254
  62.6 11.6 %collective-permute-start.4 = (bf16[16,4096]{1,0:T(8,128)(2,1)S(1)}, bf16[16,4096]{1,0:T(8,128)(2,1)S(1)}, u32[]{:S(2)}, u32[]{:S(2)}) collective-permute-start(bf16[16,4096]{1,0:T(8,128)(2,1)S(1)} %get-tuple-element.31), channel_id=1, source_target_pairs={{0,2},{2,4},{4,6},{1,3},{3,5},{5,7},{8,10},{10,12},{12,14},{9,11},... | collective-permute-start | bytes 393224 | tf_op jit(solution)/shard_map/ppermute | solution.py:258
  69.1 7.1 %collective-permute-start.5 = (bf16[16,4096]{1,0:T(8,128)(2,1)S(1)}, bf16[16,4096]{1,0:T(8,128)(2,1)S(1)}, u32[]{:S(2)}, u32[]{:S(2)}) collective-permute-start(bf16[16,4096]{1,0:T(8,128)(2,1)S(1)} %get-tuple-element.31), channel_id=1, source_target_pairs={{0,4},{2,6},{1,5},{3,7},{8,12},{10,14},{9,13},{11,15},{16,20},{18,... | collective-permute-start | bytes 393224 | tf_op jit(solution)/shard_map/ppermute | solution.py:258
  72.9 4.7 %collective-permute-start.6 = (bf16[16,4096]{1,0:T(8,128)(2,1)S(1)}, bf16[16,4096]{1,0:T(8,128)(2,1)S(1)}, u32[]{:S(2)}, u32[]{:S(2)}) collective-permute-start(bf16[16,4096]{1,0:T(8,128)(2,1)S(1)} %get-tuple-element.31), channel_id=1, source_target_pairs={{0,6},{1,7},{8,14},{9,15},{16,22},{17,23},{24,30},{25,31}} | collective-permute-start | bytes 393224 | tf_op jit(solution)/shard_map/ppermute | solution.py:258
  81.6 46.4 %copy-start.13 = (bf16[128,4096]{1,0:T(8,128)(2,1)}, bf16[128,4096]{1,0:T(8,128)(2,1)S(1)}, u32[]{:S(2)}) copy-start(bf16[128,4096]{1,0:T(8,128)(2,1)S(1)} %get-tuple-element.41.refs_5_) | copy-start | bytes 3145732
  100.4 23.4 %collective-permute-start.7 = (bf16[4,128,1024]{2,1,0:T(8,128)(2,1)S(1)}, bf16[4,128,1024]{2,1,0:T(8,128)(2,1)S(1)}, u32[]{:S(2)}, u32[]{:S(2)}) collective-permute-start(bf16[4,128,1024]{2,1,0:T(8,128)(2,1)S(1)} %all_to_all.15.own), channel_id=1, source_target_pairs={{0,2},{2,4},{4,6},{1,3},{3,5},{5,7},{8,10},{10,12},{12,14},{9,11},... | collective-permute-start | bytes 3145736 | tf_op jit(solution)/shard_map/ppermute | solution.py:258
  103.9 24.1 %collective-permute-start.8 = (bf16[4,128,1024]{2,1,0:T(8,128)(2,1)S(1)}, bf16[4,128,1024]{2,1,0:T(8,128)(2,1)S(1)}, u32[]{:S(2)}, u32[]{:S(2)}) collective-permute-start(bf16[4,128,1024]{2,1,0:T(8,128)(2,1)S(1)} %all_to_all.15.own), channel_id=1, source_target_pairs={{2,0},{4,2},{6,4},{3,1},{5,3},{7,5},{10,8},{12,10},{14,12},{11,9},... | collective-permute-start | bytes 3145736 | tf_op jit(solution)/shard_map/ppermute | solution.py:258
  123.8 19.5 %collective-permute-start.11 = (bf16[4,128,1024]{2,1,0:T(8,128)(2,1)S(1)}, bf16[4,128,1024]{2,1,0:T(8,128)(2,1)S(1)}, u32[]{:S(2)}, u32[]{:S(2)}) collective-permute-start(bf16[4,128,1024]{2,1,0:T(8,128)(2,1)S(1)} %collective-permute-done.7.refs_0_), channel_id=1, source_target_pairs={{2,4},{4,6},{3,5},{5,7},{10,12},{12,14},{11,13},{13,15},{18,20},{2... | collective-permute-start | bytes 3145736 | tf_op jit(solution)/shard_map/ppermute | solution.py:258
  128.0 23.4 %collective-permute-start.12 = (bf16[4,128,1024]{2,1,0:T(8,128)(2,1)S(1)}, bf16[4,128,1024]{2,1,0:T(8,128)(2,1)}, u32[]{:S(2)}, u32[]{:S(2)}) collective-permute-start(bf16[4,128,1024]{2,1,0:T(8,128)(2,1)S(1)} %collective-permute-done.8.refs_1_.refs_5_), channel_id=1, source_target_pairs={{2,0},{4,2},{3,1},{5,3},{10,8},{12,10},{11,9},{13,11},{18,16},{20,... | collective-permute-start | bytes 3145736 | tf_op jit(solution)/shard_map/ppermute | solution.py:258
  136.0 28.8 %collective-permute-start.10 = (bf16[1,4,128,1024]{3,2,1,0:T(8,128)(2,1)}, bf16[1,4,128,1024]{3,2,1,0:T(8,128)(2,1)}, u32[]{:S(2)}, u32[]{:S(2)}) collective-permute-start(bf16[1,4,128,1024]{3,2,1,0:T(8,128)(2,1)} %delta.2.refs_0_), channel_id=1, source_target_pairs={{6,4},{7,5},{14,12},{15,13},{22,20},{23,21},{30,28},{31,29}} | collective-permute-start | bytes 3145736 | tf_op jit(solution)/shard_map/ppermute | solution.py:258
  137.7 27.2 %collective-permute-start.9 = (bf16[1,4,128,1024]{3,2,1,0:T(8,128)(2,1)}, bf16[1,4,128,1024]{3,2,1,0:T(8,128)(2,1)}, u32[]{:S(2)}, u32[]{:S(2)}) collective-permute-start(bf16[1,4,128,1024]{3,2,1,0:T(8,128)(2,1)} %delta.2.refs_0_), channel_id=1, source_target_pairs={{0,2},{1,3},{8,10},{9,11},{16,18},{17,19},{24,26},{25,27}} | collective-permute-start | bytes 3145736 | tf_op jit(solution)/shard_map/ppermute | solution.py:258
  143.3 21.6 %copy-start.5 = (bf16[4,128,1024]{2,1,0:T(8,128)(2,1)}, bf16[4,128,1024]{2,1,0:T(8,128)(2,1)S(1)}, u32[]{:S(2)}) copy-start(bf16[4,128,1024]{2,1,0:T(8,128)(2,1)S(1)} %collective-permute-done.11.refs_0_.refs_1_) | copy-start | bytes 3145732
  143.3 47.5 %collective-permute-start.15 = (bf16[4,128,1024]{2,1,0:T(8,128)(2,1)S(1)}, bf16[4,128,1024]{2,1,0:T(8,128)(2,1)}, u32[]{:S(2)}, u32[]{:S(2)}) collective-permute-start(bf16[4,128,1024]{2,1,0:T(8,128)(2,1)S(1)} %collective-permute-done.11.refs_0_.refs_1_), channel_id=1, source_target_pairs={{4,6},{5,7},{12,14},{13,15},{20,22},{21,23},{28,30},{29,31}} | collective-permute-start | bytes 3145736 | tf_op jit(solution)/shard_map/ppermute | solution.py:258
  151.4 39.4 %collective-permute-start.16 = (bf16[4,128,1024]{2,1,0:T(8,128)(2,1)}, bf16[4,128,1024]{2,1,0:T(8,128)(2,1)S(1)}, u32[]{:S(2)}, u32[]{:S(2)}) collective-permute-start(bf16[4,128,1024]{2,1,0:T(8,128)(2,1)} %collective-permute-done.12.refs_1_.refs_4_), channel_id=1, source_target_pairs={{2,0},{3,1},{10,8},{11,9},{18,16},{19,17},{26,24},{27,25}} | collective-permute-start | bytes 3145736 | tf_op jit(solution)/shard_map/ppermute | solution.py:258
  169.6 22.6 %collective-permute-start.13 = (bf16[1,4,128,1024]{3,2,1,0:T(8,128)(2,1)}, bf16[1,4,128,1024]{3,2,1,0:T(8,128)(2,1)}, u32[]{:S(2)}, u32[]{:S(2)}) collective-permute-start(bf16[1,4,128,1024]{3,2,1,0:T(8,128)(2,1)} %get-tuple-element.33), channel_id=1, source_target_pairs={{0,2},{2,4},{1,3},{3,5},{8,10},{10,12},{9,11},{11,13},{16,18},{18,... | collective-permute-start | bytes 3145736 | tf_op jit(solution)/shard_map/ppermute | solution.py:258
  175.1 17.0 %collective-permute-start.14 = (bf16[1,4,128,1024]{3,2,1,0:T(8,128)(2,1)}, bf16[1,4,128,1024]{3,2,1,0:T(8,128)(2,1)}, u32[]{:S(2)}, u32[]{:S(2)}) collective-permute-start(bf16[1,4,128,1024]{3,2,1,0:T(8,128)(2,1)} %get-tuple-element.34), channel_id=1, source_target_pairs={{4,2},{6,4},{5,3},{7,5},{12,10},{14,12},{13,11},{15,13},{20,18},{2... | collective-permute-start | bytes 3145736 | tf_op jit(solution)/shard_map/ppermute | solution.py:258
  195.8 27.0 %collective-permute-start.17 = (bf16[1,4,128,1024]{3,2,1,0:T(8,128)(2,1)S(1)}, bf16[1,4,128,1024]{3,2,1,0:T(8,128)(2,1)S(1)}, u32[]{:S(2)}, u32[]{:S(2)}) collective-permute-start(bf16[1,4,128,1024]{3,2,1,0:T(8,128)(2,1)S(1)} %get-tuple-element.35.refs_6_.after), channel_id=1, source_target_pairs={{0,2},{2,4},{4,6},{1,3},{3,5},{5,7},{8,10},{10,12},{12,14},{9,11},... | collective-permute-start | bytes 3145736 | tf_op jit(solution)/shard_map/ppermute | solution.py:258
  202.2 20.9 %collective-permute-start.18 = (bf16[1,4,128,1024]{3,2,1,0:T(8,128)(2,1)S(1)}, bf16[1,4,128,1024]{3,2,1,0:T(8,128)(2,1)S(1)}, u32[]{:S(2)}, u32[]{:S(2)}) collective-permute-start(bf16[1,4,128,1024]{3,2,1,0:T(8,128)(2,1)S(1)} %get-tuple-element.36), channel_id=1, source_target_pairs={{2,0},{4,2},{6,4},{3,1},{5,3},{7,5},{10,8},{12,10},{14,12},{11,9},... | collective-permute-start | bytes 3145736 | tf_op jit(solution)/shard_map/ppermute | solution.py:258
  226.1 60.3 %copy-start.10 = (bf16[128,4096]{1,0:T(8,128)(2,1)S(1)}, bf16[128,4096]{1,0:T(8,128)(2,1)}, u32[]{:S(2)}) copy-start(bf16[128,4096]{1,0:T(8,128)(2,1)} %refs_4_.1) | copy-start | bytes 3145732
  226.2 83.1 %all-to-all-start.2 = ((bf16[4,512,1024]{2,1,0:T(8,128)(2,1)}), bf16[4,512,1024]{2,1,0:T(8,128)(2,1)}, u32[]{:S(2)}, u32[]{:S(2)}) async-start(bf16[4,512,1024]{2,1,0:T(8,128)(2,1)} %hold.1), calls=%async_computation.2 | async-start | bytes 8388608 | tf_op jit(solution)/shard_map/all_to_all | solution.py:451
  232.9 52.0 %collective-permute-start.19 = (bf16[128,1024]{1,0:T(8,128)(2,1)S(1)}, bf16[128,1024]{1,0:T(8,128)(2,1)S(1)}, u32[]{:S(2)}, u32[]{:S(2)}) collective-permute-start(bf16[128,1024]{1,0:T(8,128)(2,1)S(1)} %get-tuple-element.38), channel_id=1, source_target_pairs={{0,8},{8,0},{16,24},{24,16},{1,9},{9,1},{17,25},{25,17},{2,10},{10... | collective-permute-start | bytes 786440 | tf_op jit(solution)/shard_map/ppermute | solution.py:254
  236.5 48.3 %collective-permute-start.20 = (bf16[128,1024]{1,0:T(8,128)(2,1)S(1)}, bf16[128,1024]{1,0:T(8,128)(2,1)S(1)}, u32[]{:S(2)}, u32[]{:S(2)}) collective-permute-start(bf16[128,1024]{1,0:T(8,128)(2,1)S(1)} %get-tuple-element.39), channel_id=1, source_target_pairs={{0,16},{8,24},{16,0},{24,8},{1,17},{9,25},{17,1},{25,9},{2,18},{10... | collective-permute-start | bytes 786440 | tf_op jit(solution)/shard_map/ppermute | solution.py:254
  236.5 49.9 %collective-permute-start.21 = (bf16[128,1024]{1,0:T(8,128)(2,1)S(1)}, bf16[128,1024]{1,0:T(8,128)(2,1)S(1)}, u32[]{:S(2)}, u32[]{:S(2)}) collective-permute-start(bf16[128,1024]{1,0:T(8,128)(2,1)S(1)} %get-tuple-element.40), channel_id=1, source_target_pairs={{0,24},{8,16},{16,8},{24,0},{1,25},{9,17},{17,9},{25,1},{2,26},{10... | collective-permute-start | bytes 786440 | tf_op jit(solution)/shard_map/ppermute | solution.py:254
  286.5 17.7 %copy-start.18 = (bf16[128,4096]{1,0:T(8,128)(2,1)S(1)}, bf16[128,4096]{1,0:T(8,128)(2,1)}, u32[]{:S(2)}) copy-start(bf16[128,4096]{1,0:T(8,128)(2,1)} %copy-done.17) | copy-start | bytes 3145732
  291.4 8.7 %collective-permute-start.22 = (bf16[16,4096]{1,0:T(8,128)(2,1)S(1)}, bf16[16,4096]{1,0:T(8,128)(2,1)S(1)}, u32[]{:S(2)}, u32[]{:S(2)}) collective-permute-start(bf16[16,4096]{1,0:T(8,128)(2,1)S(1)} %get-tuple-element.44), channel_id=1, source_target_pairs={{2,0},{4,2},{6,4},{3,1},{5,3},{7,5},{10,8},{12,10},{14,12},{11,9},... | collective-permute-start | bytes 393224 | tf_op jit(solution)/shard_map/ppermute | solution.py:258
  292.7 8.7 %collective-permute-start.23 = (bf16[16,4096]{1,0:T(8,128)(2,1)S(1)}, bf16[16,4096]{1,0:T(8,128)(2,1)S(1)}, u32[]{:S(2)}, u32[]{:S(2)}) collective-permute-start(bf16[16,4096]{1,0:T(8,128)(2,1)S(1)} %get-tuple-element.44), channel_id=1, source_target_pairs={{4,0},{6,2},{5,1},{7,3},{12,8},{14,10},{13,9},{15,11},{20,16},{22,... | collective-permute-start | bytes 393224 | tf_op jit(solution)/shard_map/ppermute | solution.py:258
  294.0 10.2 %collective-permute-start.24 = (bf16[16,4096]{1,0:T(8,128)(2,1)S(1)}, bf16[16,4096]{1,0:T(8,128)(2,1)S(1)}, u32[]{:S(2)}, u32[]{:S(2)}) collective-permute-start(bf16[16,4096]{1,0:T(8,128)(2,1)S(1)} %get-tuple-element.44), channel_id=1, source_target_pairs={{6,0},{7,1},{14,8},{15,9},{22,16},{23,17},{30,24},{31,25}} | collective-permute-start | bytes 393224 | tf_op jit(solution)/shard_map/ppermute | solution.py:258
  (19 other events, 120.5 us)
Sparse Core Ops, SparseCore 0:
  62.7 64.1 all-gather.2

commit v8 on v6

--- a/solution.py
+++ b/solution.py
@@ -186,8 +186,15 @@
     out[...] = grad[...].reshape(-1, grad.shape[-1]).T
 
 
-def lay_body(source, after, target):
-    target[...] = source[0]
+def lay_body(place, *refs):
+    sources, out = refs[:-2], refs[-1]
+    for k, source in enumerate(sources):
+        lanes = source.shape[1]
+        out[:, pl.ds(pl.multiple_of((place[0] ^ k) * lanes, lanes), lanes)] = source[...]
+
+
+def wait_body(*refs):
+    pass
 
 
 def add_body(dests, partial_right, partial_left, right, left, *refs):
@@ -213,8 +220,8 @@
             out[...] = total.astype(BF16)
 
 
-def weight_body(grad_t, gated, after, out):
-    out[0] = dot(grad_t[...], gated[...]).astype(out.dtype)
+def weight_body(place, grad_t, gated, after, out):
+    out[...] = dot(grad_t[...], gated[...]).astype(out.dtype)
 
 
 def wide(rows, lanes):
@@ -413,18 +420,30 @@
         out_specs=pl.BlockSpec((n_ctx, 1, rows, quarter), lambda i: (0, i, 0, 0)),
         out_shape=shape(n_ctx, n_dp, rows, quarter),
     )(gated_far, *from_left, *from_right[::-1], token).reshape(tokens, quarter)
-    weight_part = call(
-        weight_body, "weight", 2 * tokens * depth * quarter, 2 * tokens * (depth + quarter),
-        grid=(n_dp,),
-        in_specs=[
-            pl.BlockSpec((feats, tokens), lambda i: (i, 0)),
-            pl.BlockSpec((tokens, quarter), lambda i: (0, 0)),
-            ANY,
-        ],
-        out_specs=pl.BlockSpec((1, feats, quarter), lambda i: (i, 0, 0)),
-        out_shape=shape(n_dp, feats, quarter),
-    )(grad_t, gated_all, token)
-    weight_far = lax.all_to_all(weight_part, "dp", 0, 0, tiled=True)
+    pieces = {}
+    for k in range(n_dp - 1, -1, -1):
+        token = pieces[k] = call(
+            weight_body, "weight", 2 * tokens * feats * quarter, 2 * tokens * (feats + quarter),
+            grid_spec=pltpu.PrefetchScalarGridSpec(
+                num_scalar_prefetch=1, grid=(2,),
+                in_specs=[
+                    pl.BlockSpec((feats, tokens), lambda i, p, k=k: (p[0] ^ k, 0)),
+                    pl.BlockSpec((tokens, quarter // 2), lambda i, p: (0, i)),
+                    ANY,
+                ],
+                out_specs=pl.BlockSpec((feats, quarter // 2), lambda i, p: (0, i)),
+            ),
+            out_shape=shape(feats, quarter),
+        )(place, grad_t, gated_all, token)
+
+    def hold(value, *after):
+        return call(
+            wait_body, "hold", 0, 0,
+            in_specs=[ANY] * (1 + len(after)), out_specs=ANY,
+            out_shape=shape(*value.shape), input_output_aliases={0: 0},
+        )(value, *after)
+
+    diagonal = swap(pieces[n_dp - 1], "dp", n_dp - 1)
 
     delta = call(
         sum_body, "sum", 0, 8 * n_dp * rows * quarter,
@@ -439,8 +458,11 @@
             out_specs=[pl.BlockSpec((rows, quarter), lambda i, p: (0, 0))] * n_dp,
         ),
         out_shape=[shape(rows, quarter)] * n_dp,
-    )(place, partial, right, left, weight_part)
-    delta = [delta[0]] + [swap(delta[k], "dp", k) for k in range(1, n_dp)]
+    )(place, partial, right, left, pieces[n_dp // 2])
+    delta = [delta[0]] + [swap(hold(delta[k], diagonal), "dp", k) for k in range(1, n_dp)]
+    weight_far = [pieces[0]] + [
+        swap(hold(pieces[k], *delta[1:]), "dp", k) for k in range(1, n_dp - 1)
+    ] + [diagonal]
 
     here = pl.BlockSpec((rows, block), lambda i, p: (0, p[0] ^ i))
     seed, starts, gate_grad = call(
@@ -465,13 +487,16 @@
         out_shape=[shape(rows, width)] * 2,
     )(local_bwd, back_coef, conv, query, *starts_far)
 
+    cut = feats // n_dp
     weight_grad = call(
         lay_body, "lay", 0, 4 * feats * width,
-        grid=(n_dp,),
-        in_specs=[pl.BlockSpec((1, feats, quarter), lambda i: (i, 0, 0)), ANY],
-        out_specs=pl.BlockSpec((feats, quarter), lambda i: (0, i)),
+        grid_spec=pltpu.PrefetchScalarGridSpec(
+            num_scalar_prefetch=1, grid=(n_dp,),
+            in_specs=[pl.BlockSpec((cut, quarter), lambda i, p: (i, 0))] * n_dp + [ANY],
+            out_specs=pl.BlockSpec((cut, width), lambda i, p: (i, 0)),
+        ),
         out_shape=shape(feats, width),
-    )(weight_far, query_grad)
+    )(place, *weight_far, query_grad)
     return query_grad, conv_grad, gate_grad, weight_grad
 
 

time: 318 us -> 294 us (0.925)
  waiting for transfers between devices: 88.5 us -> 60.1 us
  Pallas kernels: 102 us -> 109 us
    ppermute x19, waiting for transfers between devices: 63.1 us -> 42 us  [shift(): return lax.ppermute(value, 'ctx', ends)]
    pallas_call x2 -> x10, Pallas kernels: 17.9 us -> 26 us  [the longest x4 21.4 us: on_device(): call(weight_body, 'weight', 2 * tokens * feats * quarter, 2 * tokens * (f...]
    ppermute x6 -> x9, waiting for transfers between devices: 22.8 us -> 15.4 us  [swap(): lax.ppermute(value, axis, [(i, i ^ k) for i in range(lax.axis_size(axis))])]
    all_to_all x1 -> x0, starting transfers between devices: 5.78 us -> none  [on_device(): weight_far = lax.all_to_all(weight_part, 'dp', 0, 0, tiled=True)]
    ppermute x6 -> x9, starting transfers between devices: 9.87 us -> 15.4 us  [swap(): lax.ppermute(value, axis, [(i, i ^ k) for i in range(lax.axis_size(axis))])]
    unnamed x51 -> x49, local copies, waits for them, and re-layouts: 6.93 us -> 6.93 us
  transfers between devices with their start and end apart: 28 -> 30, of which waited for: 16 -> 12; matrix products, arithmetic and copies ran while one was open for 3% -> 3% of each run, Pallas kernels for 23% -> 34%
where the time goes in v8:
time: 294 us; the launch traced here: 292 us
  Pallas kernels  109 us (37%)
  starting transfers between devices  73.4 us (25%)
  waiting for transfers between devices  60.1 us (20%)
  blocking collectives  18.8 us (6%)
  between operations  14.6 us (5%)
  other arithmetic  8.53 us (3%)
  local copies, waits for them, and re-layouts  7.78 us (3%)
    ppermute x19, starting transfers between devices, shift(): return lax.ppermute(value, 'ctx', ends)  52.8 us
    ppermute x19, waiting for transfers between devices, shift(): return lax.ppermute(value, 'ctx', ends)  42 us
    pallas_call x4, Pallas kernels, on_device(): call(weight_body, 'weight', 2 * tokens * feats * quarter, 2 * tokens * (f...  21.4 us
    pallas_call x2, Pallas kernels, project(): call(functools.partial(delta_body, whole), 'delta', 2 * max(count - 1, 1)...  18.8 us
    all_to_all x1, blocking collectives, on_device(): gated_far = lax.all_to_all(gated, 'dp', 0, 0, tiled=True)  18.8 us
    ppermute x9, waiting for transfers between devices, swap(): lax.ppermute(value, axis, [(i, i ^ k) for i in range(lax.axis_size(axis))])  15.4 us
    ppermute x9, starting transfers between devices, swap(): lax.ppermute(value, axis, [(i, i ^ k) for i in range(lax.axis_size(axis))])  15.4 us
    pallas_call x1, Pallas kernels, on_device(): call(flip_body, 'flip', 0, 4 * tokens * depth, grid_spec=pltpu.PrefetchSc...  13.8 us
  transfers between devices with their start and end apart: 30, of which 12 were waited for; matrix products, arithmetic and copies ran while one was open for 3% of the time, Pallas kernels for 34%

profile of v8, /device:TPU:0, one launch (start us, length us, event | category | flops | bytes accessed | tf_op | source)
XLA Modules:
  0.0 292.4 jit_solution(5064146851253981932)
XLA Ops:
  7.2 5.2 %all-to-all-start = ((bf16[4,1024,512]{2,1,0:T(8,128)(2,1)}), bf16[4,1024,512]{2,1,0:T(8,128)(2,1)}, u32[]{:S(2)}, u32[]{:S(2)}) async-start(bf16[4,1024,512]{2,1,0:T(8,128)(2,1)} %bitcast.20), calls=%async_computation | async-start | bytes 8388608 | tf_op jit(solution)/shard_map/all_to_all | solution.py:266
  14.3 5.6 %collective-permute-start.3 = (bf16[128,4096]{1,0:T(8,128)(2,1)S(1)}, bf16[128,4096]{1,0:T(8,128)(2,1)}, u32[]{:S(2)}, u32[]{:S(2)}) collective-permute-start(bf16[128,4096]{1,0:T(8,128)(2,1)S(1)} %multiply_convert_fusion.2.x), channel_id=1, source_target_pairs={{0,2},{2,4},{4,6},{1,3},{3,5},{5,7},{8,10},{10,12},{12,14},{9,11},... | collective-permute-start | bytes 3145736 | tf_op jit(solution)/shard_map/ppermute | solution.py:261
  29.6 3.7 %multiply_convert_fusion = (bf16[384,4096]{1,0:T(8,128)(2,1)}, bf16[384,4096]{1,0:T(8,128)(2,1)}) fusion(f32[384]{0:T(512)S(1)} %get-tuple-element.52, f32[4096]{0:T(1024)S(1)} %neg.22, f32[4096]{0:T(1024)S(1)} %mul.110, f32[384]{0:T(512)S(1)} %get-tuple-element.53), kind=kLoop, calls=%fused_computation | loop fusion | flops 9437184 | bytes 6327296 | tf_op jit(solution)/shard_map/convert_element_type | solution.py:287
  34.1 4.2 %local.2.own_part = f32[128,4096]{1,0:T(8,128)} custom-call(f32[256,128]{1,0:T(8,128)S(1)} %pad_maximum_fusion.1.rows.taps, bf16[128,4096]{1,0:T(8,128)(2,1)S(1)} %multiply_convert_fusion.2.x, bf16[4096,128]{1,0:T(8,128)(2,1)S(1)} %get-tuple-element.51.refs_0_.ends_coef, bf16[4096,128]{1,0:T(8,128)(2,1)S(1)} %get-tuple-element.50.refs_1_.refs_6_, ...), custom_call_target="tpu_custom_call" | custom-call | flops 1073741824 | bytes 3145728 | tf_op jit(solution)/shard_map/local/pallas_call | solution.py:298
  38.3 4.2 %collective-permute-done.3.rim = bf16[128,4096]{1,0:T(8,128)(2,1)} collective-permute-done((bf16[128,4096]{1,0:T(8,128)(2,1)S(1)}, bf16[128,4096]{1,0:T(8,128)(2,1)}, u32[]{:S(2)}, u32[]{:S(2)}) %collective-permute-start.3) | collective-permute-done | bytes 1048608 | tf_op jit(solution)/shard_map/ppermute | solution.py:261
  42.5 5.7 %conv.1 = (bf16[128,4096]{1,0:T(8,128)(2,1)S(1)}, bf16[128,4096]{1,0:T(8,128)(2,1)S(1)}, bf16[16,4096]{1,0:T(8,128)(2,1)S(1)}) custom-call(bf16[128,4096]{1,0:T(8,128)(2,1)} %collective-permute-done.3.rim, f32[128,4096]{1,0:T(8,128)} %local.2.own_part, bf16[128,4096]{1,0:T(8,128)(2,1)} %query.3, f32[256,128]{1,0:T(8,128)S(1)} %pad_maximum_fusion.1.rows.taps, ...), custom_call_target="tpu_custom_call" | custom-call | flops 1073741824 | bytes 7340032 | tf_op jit(solution)/shard_map/conv/pallas_call | solution.py:311
  49.2 3.5 %local.3.refs_5_ = f32[128,4096]{1,0:T(8,128)S(1)} custom-call(f32[256,128]{1,0:T(8,128)S(1)} %pad_maximum_fusion.refs_4_.rows, bf16[128,4096]{1,0:T(8,128)(2,1)S(1)} %get-tuple-element.30.x), custom_call_target="tpu_custom_call" | custom-call | flops 1073741824 | bytes 3145728 | tf_op jit(solution)/shard_map/local/pallas_call | solution.py:298
  54.0 4.3 %collective-permute-done.2.refs_3_ = bf16[64,2048]{1,0:T(8,128)(2,1)S(1)} collective-permute-done((bf16[64,2048]{1,0:T(8,128)(2,1)}, bf16[64,2048]{1,0:T(8,128)(2,1)S(1)}, u32[]{:S(2)}, u32[]{:S(2)}) %collective-permute-start.2) | collective-permute-done | bytes 262176 | tf_op jit(solution)/shard_map/ppermute | solution.py:257
  62.6 6.5 %collective-permute-start.4 = (bf16[16,4096]{1,0:T(8,128)(2,1)S(1)}, bf16[16,4096]{1,0:T(8,128)(2,1)S(1)}, u32[]{:S(2)}, u32[]{:S(2)}) collective-permute-start(bf16[16,4096]{1,0:T(8,128)(2,1)S(1)} %get-tuple-element.31), channel_id=1, source_target_pairs={{0,2},{2,4},{4,6},{1,3},{3,5},{5,7},{8,10},{10,12},{12,14},{9,11},... | collective-permute-start | bytes 393224 | tf_op jit(solution)/shard_map/ppermute | solution.py:261
  69.1 3.7 %collective-permute-start.5 = (bf16[16,4096]{1,0:T(8,128)(2,1)S(1)}, bf16[16,4096]{1,0:T(8,128)(2,1)S(1)}, u32[]{:S(2)}, u32[]{:S(2)}) collective-permute-start(bf16[16,4096]{1,0:T(8,128)(2,1)S(1)} %get-tuple-element.31), channel_id=1, source_target_pairs={{0,4},{2,6},{1,5},{3,7},{8,12},{10,14},{9,13},{11,15},{16,20},{18,... | collective-permute-start | bytes 393224 | tf_op jit(solution)/shard_map/ppermute | solution.py:261
  77.6 4.0 %long.1 = (bf16[128,4096]{1,0:T(8,128)(2,1)S(1)}, bf16[4,128,1024]{2,1,0:T(8,128)(2,1)S(1)}) custom-call(f32[128,4096]{1,0:T(8,128)} %copy-done.6, bf16[384,4096]{1,0:T(8,128)(2,1)} %get-tuple-element.49.refs_2_.coef, bf16[128,4096]{1,0:T(8,128)(2,1)S(1)} %copy-done.14, bf16[16,4096]{1,0:T(8,128)(2,1)S(1)} %collective-permute-done.4.refs_0_, ...), custom_call_target="tpu_custom_call" | custom-call | flops 134217728 | bytes 5242880 | tf_op jit(solution)/shard_map/long/pallas_call | solution.py:331
  81.6 18.8 %all_to_all.10.own = bf16[4,128,1024]{2,1,0:T(8,128)(2,1)S(1)} all-to-all(bf16[4,128,1024]{2,1,0:T(8,128)(2,1)S(1)} %get-tuple-element.32), channel_id=1, replica_groups=mesh['dp'=4,'ctx'=4,'tp'=2] {'dp'}, dimensions={0} | all-to-all | bytes 2097152 | tf_op jit(solution)/shard_map/all_to_all | solution.py:338
  106.1 17.7 %collective-permute-done.7.refs_0_ = bf16[4,128,1024]{2,1,0:T(8,128)(2,1)S(1)} collective-permute-done((bf16[4,128,1024]{2,1,0:T(8,128)(2,1)S(1)}, bf16[4,128,1024]{2,1,0:T(8,128)(2,1)S(1)}, u32[]{:S(2)}, u32[]{:S(2)}) %collective-permute-start.7) | collective-permute-done | bytes 1048608 | tf_op jit(solution)/shard_map/ppermute | solution.py:261
  129.3 6.7 %delta.2.refs_0_ = bf16[1,4,128,1024]{3,2,1,0:T(8,128)(2,1)} custom-call(s32[3]{0:T(128)S(1)} %pad_add_fusion.place, s32[1]{0:T(128)} %bitcast.5.dest, bf16[4,2,4,64,2048]{4,3,2,1,0:T(8,128)(2,1)} %bitcast.17, bf16[4,1024,512]{2,1,0:T(8,128)(2,1)} %all-to-all-done.refs_4_.weights, bf16[4,128,1024]{2,1,0:T(8,128)(2,1)S(1)} %collective-permute-done.7.refs_0_, ...), custom_call_target="tpu_custom_call" | custom-call | flops 2147483648 | bytes 13631488 | tf_op jit(solution)/shard_map/delta/pallas_call | solution.py:355
  137.7 5.5 %collective-permute-start.9 = (bf16[1,4,128,1024]{3,2,1,0:T(8,128)(2,1)}, bf16[1,4,128,1024]{3,2,1,0:T(8,128)(2,1)}, u32[]{:S(2)}, u32[]{:S(2)}) collective-permute-start(bf16[1,4,128,1024]{3,2,1,0:T(8,128)(2,1)} %delta.2.refs_0_), channel_id=1, source_target_pairs={{0,2},{1,3},{8,10},{9,11},{16,18},{17,19},{24,26},{25,27}} | collective-permute-start | bytes 3145736 | tf_op jit(solution)/shard_map/ppermute | solution.py:261
  144.9 6.5 %collective-permute-done.12.refs_1_.refs_4_ = bf16[4,128,1024]{2,1,0:T(8,128)(2,1)} collective-permute-done((bf16[4,128,1024]{2,1,0:T(8,128)(2,1)S(1)}, bf16[4,128,1024]{2,1,0:T(8,128)(2,1)}, u32[]{:S(2)}, u32[]{:S(2)}) %collective-permute-start.12) | collective-permute-done | bytes 1048608 | tf_op jit(solution)/shard_map/ppermute | solution.py:261
  152.7 12.1 %delta.3.partial_right.partial_left.after.partial = bf16[4,4,128,1024]{3,2,1,0:T(8,128)(2,1)} custom-call(s32[3]{0:T(128)S(1)} %pad_add_fusion.place, s32[4]{0:T(128)S(1)} %and_select_fusion.dest, bf16[4,2,4,64,2048]{4,3,2,1,0:T(8,128)(2,1)} %bitcast.18, bf16[4,1024,512]{2,1,0:T(8,128)(2,1)} %all-to-all-done.refs_4_.weights, ...), custom_call_target="tpu_custom_call" | custom-call | flops 6442450944 | bytes 16777216 | tf_op jit(solution)/shard_map/delta/pallas_call | solution.py:355
  164.8 4.7 %add.89 = (bf16[1,4,128,1024]{3,2,1,0:T(8,128)(2,1)}, bf16[1,4,128,1024]{3,2,1,0:T(8,128)(2,1)}) custom-call(s32[2]{0:T(128)S(1)} %add_clamp_fusion.1.dests, bf16[4,4,128,1024]{3,2,1,0:T(8,128)(2,1)} %delta.3.partial_right.partial_left.after.partial, bf16[4,4,128,1024]{3,2,1,0:T(8,128)(2,1)} %delta.3.partial_right.partial_left.after.partial, ...), custom_call_target="tpu_custom_call" | custom-call | bytes 6291456 | tf_op jit(solution)/shard_map/add/pallas_call | solution.py:404
  169.5 5.6 %collective-permute-start.13 = (bf16[1,4,128,1024]{3,2,1,0:T(8,128)(2,1)}, bf16[1,4,128,1024]{3,2,1,0:T(8,128)(2,1)S(1)}, u32[]{:S(2)}, u32[]{:S(2)}) collective-permute-start(bf16[1,4,128,1024]{3,2,1,0:T(8,128)(2,1)} %get-tuple-element.33), channel_id=1, source_target_pairs={{0,2},{2,4},{1,3},{3,5},{8,10},{10,12},{9,11},{11,13},{16,18},{18,... | collective-permute-start | bytes 3145736 | tf_op jit(solution)/shard_map/ppermute | solution.py:261
  176.9 13.8 %flip.1.refs_2_.grad_t = bf16[2048,2048]{1,0:T(8,128)(2,1)} custom-call(s32[3]{0:T(128)S(1)} %pad_add_fusion.place, bf16[4,2,4,64,2048]{4,3,2,1,0:T(8,128)(2,1)} %bitcast.19, bf16[4,4,128,1024]{3,2,1,0:T(8,128)(2,1)} %delta.3.partial_right.partial_left.after.partial), custom_call_target="tpu_custom_call" | custom-call | bytes 16777216 | tf_op jit(solution)/shard_map/flip/pallas_call | solution.py:378
  196.5 6.4 %collective-permute-start.17 = (bf16[1,4,128,1024]{3,2,1,0:T(8,128)(2,1)S(1)}, bf16[1,4,128,1024]{3,2,1,0:T(8,128)(2,1)S(1)}, u32[]{:S(2)}, u32[]{:S(2)}) collective-permute-start(bf16[1,4,128,1024]{3,2,1,0:T(8,128)(2,1)S(1)} %get-tuple-element.35.refs_6_.after), channel_id=1, source_target_pairs={{0,2},{2,4},{4,6},{1,3},{3,5},{5,7},{8,10},{10,12},{12,14},{9,11},... | collective-permute-start | bytes 3145736 | tf_op jit(solution)/shard_map/ppermute | solution.py:261
  204.2 4.8 %merge.1 = bf16[4,4,128,1024]{3,2,1,0:T(8,128)(2,1)} custom-call(bf16[4,128,1024]{2,1,0:T(8,128)(2,1)S(1)} %copy-done.13, bf16[4,128,1024]{2,1,0:T(8,128)(2,1)S(1)} %collective-permute-done.7.refs_0_, bf16[4,128,1024]{2,1,0:T(8,128)(2,1)S(1)} %copy-done.9, bf16[4,128,1024]{2,1,0:T(8,128)(2,1)} %collective-permute-done.15.refs_0_.refs_2_, ...), custom_call_target="tpu_custom_call" | custom-call | bytes 11534336 | tf_op jit(solution)/shard_map/merge/pallas_call | solution.py:416
  210.2 5.4 %weight.4.after = bf16[512,1024]{1,0:T(8,128)(2,1)S(1)} custom-call(s32[3]{0:T(128)S(1)} %pad_add_fusion.place, bf16[2048,2048]{1,0:T(8,128)(2,1)} %flip.1.refs_2_.grad_t, bf16[2048,1024]{1,0:T(8,128)(2,1)} %bitcast.13, bf16[1,4,128,1024]{3,2,1,0:T(8,128)(2,1)S(1)} %copy-done.11), custom_call_target="tpu_custom_call" | custom-call | flops 2147483648 | bytes 6291456 | tf_op jit(solution)/shard_map/weight/pallas_call | solution.py:425
  215.6 3.7 %collective-permute-start.19 = (bf16[512,1024]{1,0:T(8,128)(2,1)S(1)}, bf16[512,1024]{1,0:T(8,128)(2,1)S(1)}, u32[]{:S(2)}, u32[]{:S(2)}) collective-permute-start(bf16[512,1024]{1,0:T(8,128)(2,1)S(1)} %weight.4.after), channel_id=1, source_target_pairs={{0,24},{8,16},{16,8},{24,0},{1,25},{9,17},{17,9},{25,1},{2,26},{10... | collective-permute-start | bytes 3145736 | tf_op jit(solution)/shard_map/ppermute | solution.py:257
  219.3 5.4 %weight.5.after.refs_0_ = bf16[512,1024]{1,0:T(8,128)(2,1)S(1)} custom-call(s32[3]{0:T(128)S(1)} %pad_add_fusion.place, bf16[2048,2048]{1,0:T(8,128)(2,1)} %flip.1.refs_2_.grad_t, bf16[2048,1024]{1,0:T(8,128)(2,1)} %bitcast.14, bf16[512,1024]{1,0:T(8,128)(2,1)S(1)} %weight.4.after), custom_call_target="tpu_custom_call" | custom-call | flops 2147483648 | bytes 6291456 | tf_op jit(solution)/shard_map/weight/pallas_call | solution.py:425
  228.7 11.1 %collective-permute-done.19.refs_1_.refs_3_ = bf16[512,1024]{1,0:T(8,128)(2,1)S(1)} collective-permute-done((bf16[512,1024]{1,0:T(8,128)(2,1)S(1)}, bf16[512,1024]{1,0:T(8,128)(2,1)S(1)}, u32[]{:S(2)}, u32[]{:S(2)}) %collective-permute-start.19) | collective-permute-done | bytes 1048608 | tf_op jit(solution)/shard_map/ppermute | solution.py:257
  244.9 5.4 %weight.6.after.refs_0_ = bf16[512,1024]{1,0:T(8,128)(2,1)S(1)} custom-call(s32[3]{0:T(128)S(1)} %pad_add_fusion.place, bf16[2048,2048]{1,0:T(8,128)(2,1)} %flip.1.refs_2_.grad_t, bf16[2048,1024]{1,0:T(8,128)(2,1)} %bitcast.15, bf16[512,1024]{1,0:T(8,128)(2,1)S(1)} %copy-done.3), custom_call_target="tpu_custom_call" | custom-call | flops 2147483648 | bytes 6291456 | tf_op jit(solution)/shard_map/weight/pallas_call | solution.py:425
  250.3 5.4 %weight.7.refs_0_ = bf16[512,1024]{1,0:T(8,128)(2,1)S(1)} custom-call(s32[3]{0:T(128)S(1)} %pad_add_fusion.place, bf16[2048,2048]{1,0:T(8,128)(2,1)} %flip.1.refs_2_.grad_t, bf16[2048,1024]{1,0:T(8,128)(2,1)} %bitcast.16, bf16[512,1024]{1,0:T(8,128)(2,1)S(1)} %weight.6.after.refs_0_), custom_call_target="tpu_custom_call" | custom-call | flops 2147483648 | bytes 6291456 | tf_op jit(solution)/shard_map/weight/pallas_call | solution.py:425
  257.9 4.9 %seed.1 = (bf16[128,4096]{1,0:T(8,128)(2,1)S(1)}, bf16[16,4096]{1,0:T(8,128)(2,1)S(1)}, bf16[128,4096]{1,0:T(8,128)(2,1)}) custom-call(s32[3]{0:T(128)S(1)} %pad_add_fusion.place, bf16[128,1024]{1,0:T(8,128)(2,1)S(1)} %get-tuple-element.37.refs_0_, bf16[128,1024]{1,0:T(8,128)(2,1)S(1)} %collective-permute-done.20.refs_1_, ...), custom_call_target="tpu_custom_call" | custom-call | flops 134217728 | bytes 5242880 | tf_op jit(solution)/shard_map/seed/pallas_call | solution.py:468
  266.7 3.5 %local_t.1.local = f32[128,4096]{1,0:T(8,128)S(1)} custom-call(f32[256,128]{1,0:T(8,128)S(1)} %multiply_reduce_fusion.refs_5_.rows, bf16[128,4096]{1,0:T(8,128)(2,1)S(1)} %get-tuple-element.42.x), custom_call_target="tpu_custom_call" | custom-call | flops 1073741824 | bytes 3145728 | tf_op jit(solution)/shard_map/local_t/pallas_call | solution.py:298
  276.0 5.1 %back.1 = (bf16[128,4096]{1,0:T(8,128)(2,1)}, bf16[128,4096]{1,0:T(8,128)(2,1)}) custom-call(f32[128,4096]{1,0:T(8,128)} %copy-done.17, bf16[384,4096]{1,0:T(8,128)(2,1)} %get-tuple-element.48.refs_3_.coef, bf16[128,4096]{1,0:T(8,128)(2,1)S(1)} %copy-done.20, bf16[128,4096]{1,0:T(8,128)(2,1)S(1)} %copy-done.16, ...), custom_call_target="tpu_custom_call" | custom-call | flops 134217728 | bytes 6291456 | tf_op jit(solution)/shard_map/back/pallas_call | solution.py:481
  281.0 4.5 %lay.1 = bf16[512,4096]{1,0:T(8,128)(2,1)} custom-call(s32[3]{0:T(128)S(1)} %pad_add_fusion.place, bf16[512,1024]{1,0:T(8,128)(2,1)S(1)} %weight.7.refs_0_, bf16[512,1024]{1,0:T(8,128)(2,1)S(1)} %collective-permute-done.26.refs_1_, bf16[512,1024]{1,0:T(8,128)(2,1)S(1)} %collective-permute-done.27.refs_2_, bf16[512,1024]{1,0:T(8,128)(2,1)} %copy-done.1, ...), custom_call_target="tpu_custom_call" | custom-call | bytes 8388608 | tf_op jit(solution)/shard_map/lay/pallas_call | solution.py:491
  (126 shorter events, 70.2 us)
Async XLA Ops:
  7.2 53.7 %all-to-all-start = ((bf16[4,1024,512]{2,1,0:T(8,128)(2,1)}), bf16[4,1024,512]{2,1,0:T(8,128)(2,1)}, u32[]{:S(2)}, u32[]{:S(2)}) async-start(bf16[4,1024,512]{2,1,0:T(8,128)(2,1)} %bitcast.20), calls=%async_computation | async-start | bytes 8388608 | tf_op jit(solution)/shard_map/all_to_all | solution.py:266
  12.3 117.0 %all-gather.3.cloned.1.call-start = ((), (), s32[]{:S(2)}) async-start(), calls=%async_computation.2 | async-start | bytes 9437184 | tf_op jit(solution)/shard_map/all_gather | solution.py:329
  14.3 28.2 %collective-permute-start.3 = (bf16[128,4096]{1,0:T(8,128)(2,1)S(1)}, bf16[128,4096]{1,0:T(8,128)(2,1)}, u32[]{:S(2)}, u32[]{:S(2)}) collective-permute-start(bf16[128,4096]{1,0:T(8,128)(2,1)S(1)} %multiply_convert_fusion.2.x), channel_id=1, source_target_pairs={{0,2},{2,4},{4,6},{1,3},{3,5},{5,7},{8,10},{10,12},{12,14},{9,11},... | collective-permute-start | bytes 3145736 | tf_op jit(solution)/shard_map/ppermute | solution.py:261
  22.3 31.7 %collective-permute-start = (bf16[64,2048]{1,0:T(8,128)(2,1)}, bf16[64,2048]{1,0:T(8,128)(2,1)S(1)}, u32[]{:S(2)}, u32[]{:S(2)}) collective-permute-start(bf16[64,2048]{1,0:T(8,128)(2,1)} %get-tuple-element.27), channel_id=1, source_target_pairs={{0,2},{2,0},{4,6},{6,4},{1,3},{3,1},{5,7},{7,5},{8,10},{10,8},{12,... | collective-permute-start | bytes 786440 | tf_op jit(solution)/shard_map/ppermute | solution.py:257
  22.9 31.1 %collective-permute-start.1 = (bf16[64,2048]{1,0:T(8,128)(2,1)}, bf16[64,2048]{1,0:T(8,128)(2,1)S(1)}, u32[]{:S(2)}, u32[]{:S(2)}) collective-permute-start(bf16[64,2048]{1,0:T(8,128)(2,1)} %get-tuple-element.28), channel_id=1, source_target_pairs={{0,4},{2,6},{4,0},{6,2},{1,5},{3,7},{5,1},{7,3},{8,12},{10,14},{12... | collective-permute-start | bytes 786440 | tf_op jit(solution)/shard_map/ppermute | solution.py:257
  23.9 34.5 %collective-permute-start.2 = (bf16[64,2048]{1,0:T(8,128)(2,1)}, bf16[64,2048]{1,0:T(8,128)(2,1)S(1)}, u32[]{:S(2)}, u32[]{:S(2)}) collective-permute-start(bf16[64,2048]{1,0:T(8,128)(2,1)} %get-tuple-element.29), channel_id=1, source_target_pairs={{0,6},{2,4},{4,2},{6,0},{1,7},{3,5},{5,3},{7,1},{8,14},{10,12},{12... | collective-permute-start | bytes 786440 | tf_op jit(solution)/shard_map/ppermute | solution.py:257
  62.6 11.6 %collective-permute-start.4 = (bf16[16,4096]{1,0:T(8,128)(2,1)S(1)}, bf16[16,4096]{1,0:T(8,128)(2,1)S(1)}, u32[]{:S(2)}, u32[]{:S(2)}) collective-permute-start(bf16[16,4096]{1,0:T(8,128)(2,1)S(1)} %get-tuple-element.31), channel_id=1, source_target_pairs={{0,2},{2,4},{4,6},{1,3},{3,5},{5,7},{8,10},{10,12},{12,14},{9,11},... | collective-permute-start | bytes 393224 | tf_op jit(solution)/shard_map/ppermute | solution.py:261
  69.1 7.1 %collective-permute-start.5 = (bf16[16,4096]{1,0:T(8,128)(2,1)S(1)}, bf16[16,4096]{1,0:T(8,128)(2,1)S(1)}, u32[]{:S(2)}, u32[]{:S(2)}) collective-permute-start(bf16[16,4096]{1,0:T(8,128)(2,1)S(1)} %get-tuple-element.31), channel_id=1, source_target_pairs={{0,4},{2,6},{1,5},{3,7},{8,12},{10,14},{9,13},{11,15},{16,20},{18,... | collective-permute-start | bytes 393224 | tf_op jit(solution)/shard_map/ppermute | solution.py:261
  72.9 4.7 %collective-permute-start.6 = (bf16[16,4096]{1,0:T(8,128)(2,1)S(1)}, bf16[16,4096]{1,0:T(8,128)(2,1)S(1)}, u32[]{:S(2)}, u32[]{:S(2)}) collective-permute-start(bf16[16,4096]{1,0:T(8,128)(2,1)S(1)} %get-tuple-element.31), channel_id=1, source_target_pairs={{0,6},{1,7},{8,14},{9,15},{16,22},{17,23},{24,30},{25,31}} | collective-permute-start | bytes 393224 | tf_op jit(solution)/shard_map/ppermute | solution.py:261
  81.6 46.4 %copy-start.18 = (bf16[128,4096]{1,0:T(8,128)(2,1)}, bf16[128,4096]{1,0:T(8,128)(2,1)S(1)}, u32[]{:S(2)}) copy-start(bf16[128,4096]{1,0:T(8,128)(2,1)S(1)} %get-tuple-element.41.refs_5_) | copy-start | bytes 3145732
  100.4 23.4 %collective-permute-start.7 = (bf16[4,128,1024]{2,1,0:T(8,128)(2,1)S(1)}, bf16[4,128,1024]{2,1,0:T(8,128)(2,1)S(1)}, u32[]{:S(2)}, u32[]{:S(2)}) collective-permute-start(bf16[4,128,1024]{2,1,0:T(8,128)(2,1)S(1)} %all_to_all.10.own), channel_id=1, source_target_pairs={{0,2},{2,4},{4,6},{1,3},{3,5},{5,7},{8,10},{10,12},{12,14},{9,11},... | collective-permute-start | bytes 3145736 | tf_op jit(solution)/shard_map/ppermute | solution.py:261
  103.9 24.1 %collective-permute-start.8 = (bf16[4,128,1024]{2,1,0:T(8,128)(2,1)S(1)}, bf16[4,128,1024]{2,1,0:T(8,128)(2,1)S(1)}, u32[]{:S(2)}, u32[]{:S(2)}) collective-permute-start(bf16[4,128,1024]{2,1,0:T(8,128)(2,1)S(1)} %all_to_all.10.own), channel_id=1, source_target_pairs={{2,0},{4,2},{6,4},{3,1},{5,3},{7,5},{10,8},{12,10},{14,12},{11,9},... | collective-permute-start | bytes 3145736 | tf_op jit(solution)/shard_map/ppermute | solution.py:261
  123.8 19.5 %collective-permute-start.11 = (bf16[4,128,1024]{2,1,0:T(8,128)(2,1)S(1)}, bf16[4,128,1024]{2,1,0:T(8,128)(2,1)S(1)}, u32[]{:S(2)}, u32[]{:S(2)}) collective-permute-start(bf16[4,128,1024]{2,1,0:T(8,128)(2,1)S(1)} %collective-permute-done.7.refs_0_), channel_id=1, source_target_pairs={{2,4},{4,6},{3,5},{5,7},{10,12},{12,14},{11,13},{13,15},{18,20},{2... | collective-permute-start | bytes 3145736 | tf_op jit(solution)/shard_map/ppermute | solution.py:261
  128.0 23.4 %collective-permute-start.12 = (bf16[4,128,1024]{2,1,0:T(8,128)(2,1)S(1)}, bf16[4,128,1024]{2,1,0:T(8,128)(2,1)}, u32[]{:S(2)}, u32[]{:S(2)}) collective-permute-start(bf16[4,128,1024]{2,1,0:T(8,128)(2,1)S(1)} %collective-permute-done.8.refs_1_.refs_5_), channel_id=1, source_target_pairs={{2,0},{4,2},{3,1},{5,3},{10,8},{12,10},{11,9},{13,11},{18,16},{20,... | collective-permute-start | bytes 3145736 | tf_op jit(solution)/shard_map/ppermute | solution.py:261
  136.0 28.8 %collective-permute-start.10 = (bf16[1,4,128,1024]{3,2,1,0:T(8,128)(2,1)}, bf16[1,4,128,1024]{3,2,1,0:T(8,128)(2,1)}, u32[]{:S(2)}, u32[]{:S(2)}) collective-permute-start(bf16[1,4,128,1024]{3,2,1,0:T(8,128)(2,1)} %delta.2.refs_0_), channel_id=1, source_target_pairs={{6,4},{7,5},{14,12},{15,13},{22,20},{23,21},{30,28},{31,29}} | collective-permute-start | bytes 3145736 | tf_op jit(solution)/shard_map/ppermute | solution.py:261
  137.7 27.2 %collective-permute-start.9 = (bf16[1,4,128,1024]{3,2,1,0:T(8,128)(2,1)}, bf16[1,4,128,1024]{3,2,1,0:T(8,128)(2,1)}, u32[]{:S(2)}, u32[]{:S(2)}) collective-permute-start(bf16[1,4,128,1024]{3,2,1,0:T(8,128)(2,1)} %delta.2.refs_0_), channel_id=1, source_target_pairs={{0,2},{1,3},{8,10},{9,11},{16,18},{17,19},{24,26},{25,27}} | collective-permute-start | bytes 3145736 | tf_op jit(solution)/shard_map/ppermute | solution.py:261
  143.3 21.5 %copy-start.8 = (bf16[4,128,1024]{2,1,0:T(8,128)(2,1)}, bf16[4,128,1024]{2,1,0:T(8,128)(2,1)S(1)}, u32[]{:S(2)}) copy-start(bf16[4,128,1024]{2,1,0:T(8,128)(2,1)S(1)} %collective-permute-done.11.refs_0_.refs_1_) | copy-start | bytes 3145732
  143.3 47.5 %collective-permute-start.15 = (bf16[4,128,1024]{2,1,0:T(8,128)(2,1)S(1)}, bf16[4,128,1024]{2,1,0:T(8,128)(2,1)}, u32[]{:S(2)}, u32[]{:S(2)}) collective-permute-start(bf16[4,128,1024]{2,1,0:T(8,128)(2,1)S(1)} %collective-permute-done.11.refs_0_.refs_1_), channel_id=1, source_target_pairs={{4,6},{5,7},{12,14},{13,15},{20,22},{21,23},{28,30},{29,31}} | collective-permute-start | bytes 3145736 | tf_op jit(solution)/shard_map/ppermute | solution.py:261
  151.4 39.4 %collective-permute-start.16 = (bf16[4,128,1024]{2,1,0:T(8,128)(2,1)}, bf16[4,128,1024]{2,1,0:T(8,128)(2,1)}, u32[]{:S(2)}, u32[]{:S(2)}) collective-permute-start(bf16[4,128,1024]{2,1,0:T(8,128)(2,1)} %collective-permute-done.12.refs_1_.refs_4_), channel_id=1, source_target_pairs={{2,0},{3,1},{10,8},{11,9},{18,16},{19,17},{26,24},{27,25}} | collective-permute-start | bytes 3145736 | tf_op jit(solution)/shard_map/ppermute | solution.py:261
  169.5 23.5 %collective-permute-start.13 = (bf16[1,4,128,1024]{3,2,1,0:T(8,128)(2,1)}, bf16[1,4,128,1024]{3,2,1,0:T(8,128)(2,1)S(1)}, u32[]{:S(2)}, u32[]{:S(2)}) collective-permute-start(bf16[1,4,128,1024]{3,2,1,0:T(8,128)(2,1)} %get-tuple-element.33), channel_id=1, source_target_pairs={{0,2},{2,4},{1,3},{3,5},{8,10},{10,12},{9,11},{11,13},{16,18},{18,... | collective-permute-start | bytes 3145736 | tf_op jit(solution)/shard_map/ppermute | solution.py:261
  175.1 18.0 %collective-permute-start.14 = (bf16[1,4,128,1024]{3,2,1,0:T(8,128)(2,1)}, bf16[1,4,128,1024]{3,2,1,0:T(8,128)(2,1)}, u32[]{:S(2)}, u32[]{:S(2)}) collective-permute-start(bf16[1,4,128,1024]{3,2,1,0:T(8,128)(2,1)} %get-tuple-element.34), channel_id=1, source_target_pairs={{4,2},{6,4},{5,3},{7,5},{12,10},{14,12},{13,11},{15,13},{20,18},{2... | collective-permute-start | bytes 3145736 | tf_op jit(solution)/shard_map/ppermute | solution.py:261
  196.5 29.2 %collective-permute-start.17 = (bf16[1,4,128,1024]{3,2,1,0:T(8,128)(2,1)S(1)}, bf16[1,4,128,1024]{3,2,1,0:T(8,128)(2,1)S(1)}, u32[]{:S(2)}, u32[]{:S(2)}) collective-permute-start(bf16[1,4,128,1024]{3,2,1,0:T(8,128)(2,1)S(1)} %get-tuple-element.35.refs_6_.after), channel_id=1, source_target_pairs={{0,2},{2,4},{4,6},{1,3},{3,5},{5,7},{8,10},{10,12},{12,14},{9,11},... | collective-permute-start | bytes 3145736 | tf_op jit(solution)/shard_map/ppermute | solution.py:261
  202.9 22.8 %collective-permute-start.18 = (bf16[1,4,128,1024]{3,2,1,0:T(8,128)(2,1)S(1)}, bf16[1,4,128,1024]{3,2,1,0:T(8,128)(2,1)S(1)}, u32[]{:S(2)}, u32[]{:S(2)}) collective-permute-start(bf16[1,4,128,1024]{3,2,1,0:T(8,128)(2,1)S(1)} %get-tuple-element.36), channel_id=1, source_target_pairs={{2,0},{4,2},{6,4},{3,1},{5,3},{7,5},{10,8},{12,10},{14,12},{11,9},... | collective-permute-start | bytes 3145736 | tf_op jit(solution)/shard_map/ppermute | solution.py:261
  215.6 24.2 %collective-permute-start.19 = (bf16[512,1024]{1,0:T(8,128)(2,1)S(1)}, bf16[512,1024]{1,0:T(8,128)(2,1)S(1)}, u32[]{:S(2)}, u32[]{:S(2)}) collective-permute-start(bf16[512,1024]{1,0:T(8,128)(2,1)S(1)} %weight.4.after), channel_id=1, source_target_pairs={{0,24},{8,16},{16,8},{24,0},{1,25},{9,17},{17,9},{25,1},{2,26},{10... | collective-permute-start | bytes 3145736 | tf_op jit(solution)/shard_map/ppermute | solution.py:257
  239.8 15.9 %collective-permute-start.22 = (bf16[128,1024]{1,0:T(8,128)(2,1)S(1)}, bf16[128,1024]{1,0:T(8,128)(2,1)S(1)}, u32[]{:S(2)}, u32[]{:S(2)}) collective-permute-start(bf16[128,1024]{1,0:T(8,128)(2,1)S(1)} %hold.7), channel_id=1, source_target_pairs={{0,24},{8,16},{16,8},{24,0},{1,25},{9,17},{17,9},{25,1},{2,26},{10... | collective-permute-start | bytes 786440 | tf_op jit(solution)/shard_map/ppermute | solution.py:257
  242.7 13.0 %collective-permute-start.21 = (bf16[128,1024]{1,0:T(8,128)(2,1)S(1)}, bf16[128,1024]{1,0:T(8,128)(2,1)S(1)}, u32[]{:S(2)}, u32[]{:S(2)}) collective-permute-start(bf16[128,1024]{1,0:T(8,128)(2,1)S(1)} %hold.6), channel_id=1, source_target_pairs={{0,16},{8,24},{16,0},{24,8},{1,17},{9,25},{17,1},{25,9},{2,18},{10... | collective-permute-start | bytes 786440 | tf_op jit(solution)/shard_map/ppermute | solution.py:257
  244.9 10.8 %collective-permute-start.20 = (bf16[128,1024]{1,0:T(8,128)(2,1)S(1)}, bf16[128,1024]{1,0:T(8,128)(2,1)S(1)}, u32[]{:S(2)}, u32[]{:S(2)}) collective-permute-start(bf16[128,1024]{1,0:T(8,128)(2,1)S(1)} %hold.5), channel_id=1, source_target_pairs={{0,8},{8,0},{16,24},{24,16},{1,9},{9,1},{17,25},{25,17},{2,10},{10... | collective-permute-start | bytes 786440 | tf_op jit(solution)/shard_map/ppermute | solution.py:257
  255.7 25.3 %collective-permute-start.27 = (bf16[512,1024]{1,0:T(8,128)(2,1)S(1)}, bf16[512,1024]{1,0:T(8,128)(2,1)S(1)}, u32[]{:S(2)}, u32[]{:S(2)}) collective-permute-start(bf16[512,1024]{1,0:T(8,128)(2,1)S(1)} %hold.9), channel_id=1, source_target_pairs={{0,16},{8,24},{16,0},{24,8},{1,17},{9,25},{17,1},{25,9},{2,18},{10... | collective-permute-start | bytes 3145736 | tf_op jit(solution)/shard_map/ppermute | solution.py:257
  256.4 24.6 %collective-permute-start.26 = (bf16[512,1024]{1,0:T(8,128)(2,1)S(1)}, bf16[512,1024]{1,0:T(8,128)(2,1)S(1)}, u32[]{:S(2)}, u32[]{:S(2)}) collective-permute-start(bf16[512,1024]{1,0:T(8,128)(2,1)S(1)} %hold.8), channel_id=1, source_target_pairs={{0,8},{8,0},{16,24},{24,16},{1,9},{9,1},{17,25},{25,17},{2,10},{10... | collective-permute-start | bytes 3145736 | tf_op jit(solution)/shard_map/ppermute | solution.py:257
  262.8 8.7 %collective-permute-start.23 = (bf16[16,4096]{1,0:T(8,128)(2,1)S(1)}, bf16[16,4096]{1,0:T(8,128)(2,1)S(1)}, u32[]{:S(2)}, u32[]{:S(2)}) collective-permute-start(bf16[16,4096]{1,0:T(8,128)(2,1)S(1)} %get-tuple-element.44), channel_id=1, source_target_pairs={{2,0},{4,2},{6,4},{3,1},{5,3},{7,5},{10,8},{12,10},{14,12},{11,9},... | collective-permute-start | bytes 393224 | tf_op jit(solution)/shard_map/ppermute | solution.py:261
  264.1 9.0 %collective-permute-start.24 = (bf16[16,4096]{1,0:T(8,128)(2,1)S(1)}, bf16[16,4096]{1,0:T(8,128)(2,1)S(1)}, u32[]{:S(2)}, u32[]{:S(2)}) collective-permute-start(bf16[16,4096]{1,0:T(8,128)(2,1)S(1)} %get-tuple-element.44), channel_id=1, source_target_pairs={{4,0},{6,2},{5,1},{7,3},{12,8},{14,10},{13,9},{15,11},{20,16},{22,... | collective-permute-start | bytes 393224 | tf_op jit(solution)/shard_map/ppermute | solution.py:261
  265.4 10.6 %collective-permute-start.25 = (bf16[16,4096]{1,0:T(8,128)(2,1)S(1)}, bf16[16,4096]{1,0:T(8,128)(2,1)S(1)}, u32[]{:S(2)}, u32[]{:S(2)}) collective-permute-start(bf16[16,4096]{1,0:T(8,128)(2,1)S(1)} %get-tuple-element.44), channel_id=1, source_target_pairs={{6,0},{7,1},{14,8},{15,9},{22,16},{23,17},{30,24},{31,25}} | collective-permute-start | bytes 393224 | tf_op jit(solution)/shard_map/ppermute | solution.py:261
  (22 other events, 167.4 us)
Sparse Core Ops, SparseCore 0:
  62.7 64.1 all-gather.2

commit v9 on v8

--- a/solution.py
+++ b/solution.py
@@ -459,7 +459,7 @@
         ),
         out_shape=[shape(rows, quarter)] * n_dp,
     )(place, partial, right, left, pieces[n_dp // 2])
-    delta = [delta[0]] + [swap(hold(delta[k], diagonal), "dp", k) for k in range(1, n_dp)]
+    delta = [delta[0]] + [swap(hold(delta[k], diagonal, pieces[0]), "dp", k) for k in range(1, n_dp)]
     weight_far = [pieces[0]] + [
         swap(hold(pieces[k], *delta[1:]), "dp", k) for k in range(1, n_dp - 1)
     ] + [diagonal]

time: 294 us -> 294 us (level)
  transfers between devices with their start and end apart: 30 -> 30, of which waited for: 12 -> 15; matrix products, arithmetic and copies ran while one was open for 3% -> 3% of each run, Pallas kernels for 34% -> 34%
where the time goes in v9:
time: 294 us; the launch traced here: 292 us
  Pallas kernels  109 us (37%)
  starting transfers between devices  75.2 us (26%)
  waiting for transfers between devices  59.2 us (20%)
  blocking collectives  18.8 us (6%)
  between operations  14.5 us (5%)
  other arithmetic  8.53 us (3%)
  local copies, waits for them, and re-layouts  6.82 us (2%)
    ppermute x19, starting transfers between devices, shift(): return lax.ppermute(value, 'ctx', ends)  52.8 us
    ppermute x19, waiting for transfers between devices, shift(): return lax.ppermute(value, 'ctx', ends)  42.3 us
    pallas_call x4, Pallas kernels, on_device(): call(weight_body, 'weight', 2 * tokens * feats * quarter, 2 * tokens * (f...  21.4 us
    pallas_call x2, Pallas kernels, project(): call(functools.partial(delta_body, whole), 'delta', 2 * max(count - 1, 1)...  18.8 us
    all_to_all x1, blocking collectives, on_device(): gated_far = lax.all_to_all(gated, 'dp', 0, 0, tiled=True)  18.8 us
    ppermute x9, starting transfers between devices, swap(): lax.ppermute(value, axis, [(i, i ^ k) for i in range(lax.axis_size(axis))])  17.2 us
    ppermute x9, waiting for transfers between devices, swap(): lax.ppermute(value, axis, [(i, i ^ k) for i in range(lax.axis_size(axis))])  14.3 us
    pallas_call x1, Pallas kernels, on_device(): call(flip_body, 'flip', 0, 4 * tokens * depth, grid_spec=pltpu.PrefetchSc...  13.8 us
  transfers between devices with their start and end apart: 30, of which 15 were waited for; matrix products, arithmetic and copies ran while one was open for 3% of the time, Pallas kernels for 34%

profile of v9, /device:TPU:0, one launch (start us, length us, event | category | flops | bytes accessed | tf_op | source)
XLA Modules:
  0.0 292.4 jit_solution(5868072369107496155)
XLA Ops:
  7.2 5.2 %all-to-all-start = ((bf16[4,1024,512]{2,1,0:T(8,128)(2,1)}), bf16[4,1024,512]{2,1,0:T(8,128)(2,1)}, u32[]{:S(2)}, u32[]{:S(2)}) async-start(bf16[4,1024,512]{2,1,0:T(8,128)(2,1)} %bitcast.20), calls=%async_computation | async-start | bytes 8388608 | tf_op jit(solution)/shard_map/all_to_all | solution.py:266
  14.3 5.6 %collective-permute-start.3 = (bf16[128,4096]{1,0:T(8,128)(2,1)S(1)}, bf16[128,4096]{1,0:T(8,128)(2,1)}, u32[]{:S(2)}, u32[]{:S(2)}) collective-permute-start(bf16[128,4096]{1,0:T(8,128)(2,1)S(1)} %multiply_convert_fusion.2.x), channel_id=1, source_target_pairs={{0,2},{2,4},{4,6},{1,3},{3,5},{5,7},{8,10},{10,12},{12,14},{9,11},... | collective-permute-start | bytes 3145736 | tf_op jit(solution)/shard_map/ppermute | solution.py:261
  29.6 3.7 %multiply_convert_fusion = (bf16[384,4096]{1,0:T(8,128)(2,1)}, bf16[384,4096]{1,0:T(8,128)(2,1)}) fusion(f32[384]{0:T(512)S(1)} %get-tuple-element.52, f32[4096]{0:T(1024)S(1)} %neg.22, f32[4096]{0:T(1024)S(1)} %mul.110, f32[384]{0:T(512)S(1)} %get-tuple-element.53), kind=kLoop, calls=%fused_computation | loop fusion | flops 9437184 | bytes 6327296 | tf_op jit(solution)/shard_map/convert_element_type | solution.py:287
  34.1 4.2 %local.2.own_part = f32[128,4096]{1,0:T(8,128)} custom-call(f32[256,128]{1,0:T(8,128)S(1)} %pad_maximum_fusion.1.rows.taps, bf16[128,4096]{1,0:T(8,128)(2,1)S(1)} %multiply_convert_fusion.2.x, bf16[4096,128]{1,0:T(8,128)(2,1)S(1)} %get-tuple-element.51.refs_0_.ends_coef, bf16[4096,128]{1,0:T(8,128)(2,1)S(1)} %get-tuple-element.50.refs_1_.refs_6_, ...), custom_call_target="tpu_custom_call" | custom-call | flops 1073741824 | bytes 3145728 | tf_op jit(solution)/shard_map/local/pallas_call | solution.py:298
  38.3 4.2 %collective-permute-done.3.rim = bf16[128,4096]{1,0:T(8,128)(2,1)} collective-permute-done((bf16[128,4096]{1,0:T(8,128)(2,1)S(1)}, bf16[128,4096]{1,0:T(8,128)(2,1)}, u32[]{:S(2)}, u32[]{:S(2)}) %collective-permute-start.3) | collective-permute-done | bytes 1048608 | tf_op jit(solution)/shard_map/ppermute | solution.py:261
  42.5 5.7 %conv.1 = (bf16[128,4096]{1,0:T(8,128)(2,1)S(1)}, bf16[128,4096]{1,0:T(8,128)(2,1)S(1)}, bf16[16,4096]{1,0:T(8,128)(2,1)S(1)}) custom-call(bf16[128,4096]{1,0:T(8,128)(2,1)} %collective-permute-done.3.rim, f32[128,4096]{1,0:T(8,128)} %local.2.own_part, bf16[128,4096]{1,0:T(8,128)(2,1)} %query.3, f32[256,128]{1,0:T(8,128)S(1)} %pad_maximum_fusion.1.rows.taps, ...), custom_call_target="tpu_custom_call" | custom-call | flops 1073741824 | bytes 7340032 | tf_op jit(solution)/shard_map/conv/pallas_call | solution.py:311
  49.2 3.5 %local.3.refs_5_ = f32[128,4096]{1,0:T(8,128)S(1)} custom-call(f32[256,128]{1,0:T(8,128)S(1)} %pad_maximum_fusion.refs_4_.rows, bf16[128,4096]{1,0:T(8,128)(2,1)S(1)} %get-tuple-element.30.x), custom_call_target="tpu_custom_call" | custom-call | flops 1073741824 | bytes 3145728 | tf_op jit(solution)/shard_map/local/pallas_call | solution.py:298
  54.0 4.3 %collective-permute-done.2.refs_3_ = bf16[64,2048]{1,0:T(8,128)(2,1)S(1)} collective-permute-done((bf16[64,2048]{1,0:T(8,128)(2,1)}, bf16[64,2048]{1,0:T(8,128)(2,1)S(1)}, u32[]{:S(2)}, u32[]{:S(2)}) %collective-permute-start.2) | collective-permute-done | bytes 262176 | tf_op jit(solution)/shard_map/ppermute | solution.py:257
  62.6 6.5 %collective-permute-start.4 = (bf16[16,4096]{1,0:T(8,128)(2,1)S(1)}, bf16[16,4096]{1,0:T(8,128)(2,1)S(1)}, u32[]{:S(2)}, u32[]{:S(2)}) collective-permute-start(bf16[16,4096]{1,0:T(8,128)(2,1)S(1)} %get-tuple-element.31), channel_id=1, source_target_pairs={{0,2},{2,4},{4,6},{1,3},{3,5},{5,7},{8,10},{10,12},{12,14},{9,11},... | collective-permute-start | bytes 393224 | tf_op jit(solution)/shard_map/ppermute | solution.py:261
  69.1 3.7 %collective-permute-start.5 = (bf16[16,4096]{1,0:T(8,128)(2,1)S(1)}, bf16[16,4096]{1,0:T(8,128)(2,1)S(1)}, u32[]{:S(2)}, u32[]{:S(2)}) collective-permute-start(bf16[16,4096]{1,0:T(8,128)(2,1)S(1)} %get-tuple-element.31), channel_id=1, source_target_pairs={{0,4},{2,6},{1,5},{3,7},{8,12},{10,14},{9,13},{11,15},{16,20},{18,... | collective-permute-start | bytes 393224 | tf_op jit(solution)/shard_map/ppermute | solution.py:261
  77.6 4.0 %long.1 = (bf16[128,4096]{1,0:T(8,128)(2,1)S(1)}, bf16[4,128,1024]{2,1,0:T(8,128)(2,1)S(1)}) custom-call(f32[128,4096]{1,0:T(8,128)} %copy-done.6, bf16[384,4096]{1,0:T(8,128)(2,1)} %get-tuple-element.49.refs_2_.coef, bf16[128,4096]{1,0:T(8,128)(2,1)S(1)} %copy-done.14, bf16[16,4096]{1,0:T(8,128)(2,1)S(1)} %collective-permute-done.4.refs_0_, ...), custom_call_target="tpu_custom_call" | custom-call | flops 134217728 | bytes 5242880 | tf_op jit(solution)/shard_map/long/pallas_call | solution.py:331
  81.6 18.8 %all_to_all.10.own = bf16[4,128,1024]{2,1,0:T(8,128)(2,1)S(1)} all-to-all(bf16[4,128,1024]{2,1,0:T(8,128)(2,1)S(1)} %get-tuple-element.32), channel_id=1, replica_groups=mesh['dp'=4,'ctx'=4,'tp'=2] {'dp'}, dimensions={0} | all-to-all | bytes 2097152 | tf_op jit(solution)/shard_map/all_to_all | solution.py:338
  106.1 17.7 %collective-permute-done.7.refs_0_ = bf16[4,128,1024]{2,1,0:T(8,128)(2,1)S(1)} collective-permute-done((bf16[4,128,1024]{2,1,0:T(8,128)(2,1)S(1)}, bf16[4,128,1024]{2,1,0:T(8,128)(2,1)S(1)}, u32[]{:S(2)}, u32[]{:S(2)}) %collective-permute-start.7) | collective-permute-done | bytes 1048608 | tf_op jit(solution)/shard_map/ppermute | solution.py:261
  129.3 6.7 %delta.2.refs_0_ = bf16[1,4,128,1024]{3,2,1,0:T(8,128)(2,1)} custom-call(s32[3]{0:T(128)S(1)} %pad_add_fusion.place, s32[1]{0:T(128)} %bitcast.5.dest, bf16[4,2,4,64,2048]{4,3,2,1,0:T(8,128)(2,1)} %bitcast.17, bf16[4,1024,512]{2,1,0:T(8,128)(2,1)} %all-to-all-done.refs_4_.weights, bf16[4,128,1024]{2,1,0:T(8,128)(2,1)S(1)} %collective-permute-done.7.refs_0_, ...), custom_call_target="tpu_custom_call" | custom-call | flops 2147483648 | bytes 13631488 | tf_op jit(solution)/shard_map/delta/pallas_call | solution.py:355
  137.7 5.5 %collective-permute-start.9 = (bf16[1,4,128,1024]{3,2,1,0:T(8,128)(2,1)}, bf16[1,4,128,1024]{3,2,1,0:T(8,128)(2,1)}, u32[]{:S(2)}, u32[]{:S(2)}) collective-permute-start(bf16[1,4,128,1024]{3,2,1,0:T(8,128)(2,1)} %delta.2.refs_0_), channel_id=1, source_target_pairs={{0,2},{1,3},{8,10},{9,11},{16,18},{17,19},{24,26},{25,27}} | collective-permute-start | bytes 3145736 | tf_op jit(solution)/shard_map/ppermute | solution.py:261
  144.9 6.5 %collective-permute-done.12.refs_1_.refs_4_ = bf16[4,128,1024]{2,1,0:T(8,128)(2,1)} collective-permute-done((bf16[4,128,1024]{2,1,0:T(8,128)(2,1)S(1)}, bf16[4,128,1024]{2,1,0:T(8,128)(2,1)}, u32[]{:S(2)}, u32[]{:S(2)}) %collective-permute-start.12) | collective-permute-done | bytes 1048608 | tf_op jit(solution)/shard_map/ppermute | solution.py:261
  152.7 12.1 %delta.3.partial_right.partial_left.after.partial = bf16[4,4,128,1024]{3,2,1,0:T(8,128)(2,1)} custom-call(s32[3]{0:T(128)S(1)} %pad_add_fusion.place, s32[4]{0:T(128)S(1)} %and_select_fusion.dest, bf16[4,2,4,64,2048]{4,3,2,1,0:T(8,128)(2,1)} %bitcast.18, bf16[4,1024,512]{2,1,0:T(8,128)(2,1)} %all-to-all-done.refs_4_.weights, ...), custom_call_target="tpu_custom_call" | custom-call | flops 6442450944 | bytes 16777216 | tf_op jit(solution)/shard_map/delta/pallas_call | solution.py:355
  164.8 4.7 %add.89 = (bf16[1,4,128,1024]{3,2,1,0:T(8,128)(2,1)}, bf16[1,4,128,1024]{3,2,1,0:T(8,128)(2,1)}) custom-call(s32[2]{0:T(128)S(1)} %add_clamp_fusion.1.dests, bf16[4,4,128,1024]{3,2,1,0:T(8,128)(2,1)} %delta.3.partial_right.partial_left.after.partial, bf16[4,4,128,1024]{3,2,1,0:T(8,128)(2,1)} %delta.3.partial_right.partial_left.after.partial, ...), custom_call_target="tpu_custom_call" | custom-call | bytes 6291456 | tf_op jit(solution)/shard_map/add/pallas_call | solution.py:404
  169.5 5.6 %collective-permute-start.13 = (bf16[1,4,128,1024]{3,2,1,0:T(8,128)(2,1)}, bf16[1,4,128,1024]{3,2,1,0:T(8,128)(2,1)S(1)}, u32[]{:S(2)}, u32[]{:S(2)}) collective-permute-start(bf16[1,4,128,1024]{3,2,1,0:T(8,128)(2,1)} %get-tuple-element.33), channel_id=1, source_target_pairs={{0,2},{2,4},{1,3},{3,5},{8,10},{10,12},{9,11},{11,13},{16,18},{18,... | collective-permute-start | bytes 3145736 | tf_op jit(solution)/shard_map/ppermute | solution.py:261
  176.9 13.8 %flip.1.refs_2_.grad_t = bf16[2048,2048]{1,0:T(8,128)(2,1)} custom-call(s32[3]{0:T(128)S(1)} %pad_add_fusion.place, bf16[4,2,4,64,2048]{4,3,2,1,0:T(8,128)(2,1)} %bitcast.19, bf16[4,4,128,1024]{3,2,1,0:T(8,128)(2,1)} %delta.3.partial_right.partial_left.after.partial), custom_call_target="tpu_custom_call" | custom-call | bytes 16777216 | tf_op jit(solution)/shard_map/flip/pallas_call | solution.py:378
  196.5 6.4 %collective-permute-start.17 = (bf16[1,4,128,1024]{3,2,1,0:T(8,128)(2,1)S(1)}, bf16[1,4,128,1024]{3,2,1,0:T(8,128)(2,1)S(1)}, u32[]{:S(2)}, u32[]{:S(2)}) collective-permute-start(bf16[1,4,128,1024]{3,2,1,0:T(8,128)(2,1)S(1)} %get-tuple-element.35.refs_6_.after), channel_id=1, source_target_pairs={{0,2},{2,4},{4,6},{1,3},{3,5},{5,7},{8,10},{10,12},{12,14},{9,11},... | collective-permute-start | bytes 3145736 | tf_op jit(solution)/shard_map/ppermute | solution.py:261
  204.2 4.8 %merge.1 = bf16[4,4,128,1024]{3,2,1,0:T(8,128)(2,1)} custom-call(bf16[4,128,1024]{2,1,0:T(8,128)(2,1)S(1)} %copy-done.13, bf16[4,128,1024]{2,1,0:T(8,128)(2,1)S(1)} %collective-permute-done.7.refs_0_, bf16[4,128,1024]{2,1,0:T(8,128)(2,1)S(1)} %copy-done.9, bf16[4,128,1024]{2,1,0:T(8,128)(2,1)} %collective-permute-done.15.refs_0_.refs_2_, ...), custom_call_target="tpu_custom_call" | custom-call | bytes 11534336 | tf_op jit(solution)/shard_map/merge/pallas_call | solution.py:416
  210.2 5.4 %weight.4.after = bf16[512,1024]{1,0:T(8,128)(2,1)S(1)} custom-call(s32[3]{0:T(128)S(1)} %pad_add_fusion.place, bf16[2048,2048]{1,0:T(8,128)(2,1)} %flip.1.refs_2_.grad_t, bf16[2048,1024]{1,0:T(8,128)(2,1)} %bitcast.13, bf16[1,4,128,1024]{3,2,1,0:T(8,128)(2,1)S(1)} %copy-done.11), custom_call_target="tpu_custom_call" | custom-call | flops 2147483648 | bytes 6291456 | tf_op jit(solution)/shard_map/weight/pallas_call | solution.py:425
  215.6 3.7 %collective-permute-start.19 = (bf16[512,1024]{1,0:T(8,128)(2,1)S(1)}, bf16[512,1024]{1,0:T(8,128)(2,1)S(1)}, u32[]{:S(2)}, u32[]{:S(2)}) collective-permute-start(bf16[512,1024]{1,0:T(8,128)(2,1)S(1)} %weight.4.after), channel_id=1, source_target_pairs={{0,24},{8,16},{16,8},{24,0},{1,25},{9,17},{17,9},{25,1},{2,26},{10... | collective-permute-start | bytes 3145736 | tf_op jit(solution)/shard_map/ppermute | solution.py:257
  219.3 5.4 %weight.5.after.refs_0_ = bf16[512,1024]{1,0:T(8,128)(2,1)S(1)} custom-call(s32[3]{0:T(128)S(1)} %pad_add_fusion.place, bf16[2048,2048]{1,0:T(8,128)(2,1)} %flip.1.refs_2_.grad_t, bf16[2048,1024]{1,0:T(8,128)(2,1)} %bitcast.14, bf16[512,1024]{1,0:T(8,128)(2,1)S(1)} %weight.4.after), custom_call_target="tpu_custom_call" | custom-call | flops 2147483648 | bytes 6291456 | tf_op jit(solution)/shard_map/weight/pallas_call | solution.py:425
  224.7 5.4 %weight.6.after.refs_0_ = bf16[512,1024]{1,0:T(8,128)(2,1)S(1)} custom-call(s32[3]{0:T(128)S(1)} %pad_add_fusion.place, bf16[2048,2048]{1,0:T(8,128)(2,1)} %flip.1.refs_2_.grad_t, bf16[2048,1024]{1,0:T(8,128)(2,1)} %bitcast.15, bf16[512,1024]{1,0:T(8,128)(2,1)S(1)} %weight.5.after.refs_0_), custom_call_target="tpu_custom_call" | custom-call | flops 2147483648 | bytes 6291456 | tf_op jit(solution)/shard_map/weight/pallas_call | solution.py:425
  230.1 5.4 %weight.7.refs_2_.refs_0_ = bf16[512,1024]{1,0:T(8,128)(2,1)S(1)} custom-call(s32[3]{0:T(128)S(1)} %pad_add_fusion.place, bf16[2048,2048]{1,0:T(8,128)(2,1)} %flip.1.refs_2_.grad_t, bf16[2048,1024]{1,0:T(8,128)(2,1)} %bitcast.16, bf16[512,1024]{1,0:T(8,128)(2,1)S(1)} %weight.6.after.refs_0_), custom_call_target="tpu_custom_call" | custom-call | flops 2147483648 | bytes 6291456 | tf_op jit(solution)/shard_map/weight/pallas_call | solution.py:425
  247.2 5.5 %collective-permute-done.21.refs_2_ = bf16[128,1024]{1,0:T(8,128)(2,1)S(1)} collective-permute-done((bf16[128,1024]{1,0:T(8,128)(2,1)S(1)}, bf16[128,1024]{1,0:T(8,128)(2,1)S(1)}, u32[]{:S(2)}, u32[]{:S(2)}) %collective-permute-start.21) | collective-permute-done | bytes 262176 | tf_op jit(solution)/shard_map/ppermute | solution.py:257
  257.6 4.9 %seed.1 = (bf16[128,4096]{1,0:T(8,128)(2,1)S(1)}, bf16[16,4096]{1,0:T(8,128)(2,1)S(1)}, bf16[128,4096]{1,0:T(8,128)(2,1)}) custom-call(s32[3]{0:T(128)S(1)} %pad_add_fusion.place, bf16[128,1024]{1,0:T(8,128)(2,1)S(1)} %get-tuple-element.37.refs_0_, bf16[128,1024]{1,0:T(8,128)(2,1)S(1)} %collective-permute-done.20.refs_1_, ...), custom_call_target="tpu_custom_call" | custom-call | flops 134217728 | bytes 5242880 | tf_op jit(solution)/shard_map/seed/pallas_call | solution.py:468
  266.4 3.5 %local_t.1.local = f32[128,4096]{1,0:T(8,128)S(1)} custom-call(f32[256,128]{1,0:T(8,128)S(1)} %multiply_reduce_fusion.refs_5_.rows, bf16[128,4096]{1,0:T(8,128)(2,1)S(1)} %get-tuple-element.42.x), custom_call_target="tpu_custom_call" | custom-call | flops 1073741824 | bytes 3145728 | tf_op jit(solution)/shard_map/local_t/pallas_call | solution.py:298
  275.9 5.1 %back.1 = (bf16[128,4096]{1,0:T(8,128)(2,1)}, bf16[128,4096]{1,0:T(8,128)(2,1)}) custom-call(f32[128,4096]{1,0:T(8,128)} %copy-done.17, bf16[384,4096]{1,0:T(8,128)(2,1)} %get-tuple-element.48.refs_3_.coef, bf16[128,4096]{1,0:T(8,128)(2,1)S(1)} %copy-done.20, bf16[128,4096]{1,0:T(8,128)(2,1)S(1)} %copy-done.16, ...), custom_call_target="tpu_custom_call" | custom-call | flops 134217728 | bytes 6291456 | tf_op jit(solution)/shard_map/back/pallas_call | solution.py:481
  281.0 4.5 %lay.1 = bf16[512,4096]{1,0:T(8,128)(2,1)} custom-call(s32[3]{0:T(128)S(1)} %pad_add_fusion.place, bf16[512,1024]{1,0:T(8,128)(2,1)S(1)} %weight.7.refs_2_.refs_0_, bf16[512,1024]{1,0:T(8,128)(2,1)S(1)} %collective-permute-done.26.refs_1_, bf16[512,1024]{1,0:T(8,128)(2,1)S(1)} %collective-permute-done.27.refs_2_, bf16[512,1024]{1,0:T(8,128)(2,1)} %copy-done.1, ...), custom_call_target="tpu_custom_call" | custom-call | bytes 8388608 | tf_op jit(solution)/shard_map/lay/pallas_call | solution.py:491
  (126 shorter events, 75.8 us)
Async XLA Ops:
  7.2 53.7 %all-to-all-start = ((bf16[4,1024,512]{2,1,0:T(8,128)(2,1)}), bf16[4,1024,512]{2,1,0:T(8,128)(2,1)}, u32[]{:S(2)}, u32[]{:S(2)}) async-start(bf16[4,1024,512]{2,1,0:T(8,128)(2,1)} %bitcast.20), calls=%async_computation | async-start | bytes 8388608 | tf_op jit(solution)/shard_map/all_to_all | solution.py:266
  12.3 117.0 %all-gather.3.cloned.1.call-start = ((), (), s32[]{:S(2)}) async-start(), calls=%async_computation.2 | async-start | bytes 9437184 | tf_op jit(solution)/shard_map/all_gather | solution.py:329
  14.3 28.2 %collective-permute-start.3 = (bf16[128,4096]{1,0:T(8,128)(2,1)S(1)}, bf16[128,4096]{1,0:T(8,128)(2,1)}, u32[]{:S(2)}, u32[]{:S(2)}) collective-permute-start(bf16[128,4096]{1,0:T(8,128)(2,1)S(1)} %multiply_convert_fusion.2.x), channel_id=1, source_target_pairs={{0,2},{2,4},{4,6},{1,3},{3,5},{5,7},{8,10},{10,12},{12,14},{9,11},... | collective-permute-start | bytes 3145736 | tf_op jit(solution)/shard_map/ppermute | solution.py:261
  22.3 31.7 %collective-permute-start = (bf16[64,2048]{1,0:T(8,128)(2,1)}, bf16[64,2048]{1,0:T(8,128)(2,1)S(1)}, u32[]{:S(2)}, u32[]{:S(2)}) collective-permute-start(bf16[64,2048]{1,0:T(8,128)(2,1)} %get-tuple-element.27), channel_id=1, source_target_pairs={{0,2},{2,0},{4,6},{6,4},{1,3},{3,1},{5,7},{7,5},{8,10},{10,8},{12,... | collective-permute-start | bytes 786440 | tf_op jit(solution)/shard_map/ppermute | solution.py:257
  22.9 31.1 %collective-permute-start.1 = (bf16[64,2048]{1,0:T(8,128)(2,1)}, bf16[64,2048]{1,0:T(8,128)(2,1)S(1)}, u32[]{:S(2)}, u32[]{:S(2)}) collective-permute-start(bf16[64,2048]{1,0:T(8,128)(2,1)} %get-tuple-element.28), channel_id=1, source_target_pairs={{0,4},{2,6},{4,0},{6,2},{1,5},{3,7},{5,1},{7,3},{8,12},{10,14},{12... | collective-permute-start | bytes 786440 | tf_op jit(solution)/shard_map/ppermute | solution.py:257
  23.9 34.5 %collective-permute-start.2 = (bf16[64,2048]{1,0:T(8,128)(2,1)}, bf16[64,2048]{1,0:T(8,128)(2,1)S(1)}, u32[]{:S(2)}, u32[]{:S(2)}) collective-permute-start(bf16[64,2048]{1,0:T(8,128)(2,1)} %get-tuple-element.29), channel_id=1, source_target_pairs={{0,6},{2,4},{4,2},{6,0},{1,7},{3,5},{5,3},{7,1},{8,14},{10,12},{12... | collective-permute-start | bytes 786440 | tf_op jit(solution)/shard_map/ppermute | solution.py:257
  62.6 11.6 %collective-permute-start.4 = (bf16[16,4096]{1,0:T(8,128)(2,1)S(1)}, bf16[16,4096]{1,0:T(8,128)(2,1)S(1)}, u32[]{:S(2)}, u32[]{:S(2)}) collective-permute-start(bf16[16,4096]{1,0:T(8,128)(2,1)S(1)} %get-tuple-element.31), channel_id=1, source_target_pairs={{0,2},{2,4},{4,6},{1,3},{3,5},{5,7},{8,10},{10,12},{12,14},{9,11},... | collective-permute-start | bytes 393224 | tf_op jit(solution)/shard_map/ppermute | solution.py:261
  69.1 7.1 %collective-permute-start.5 = (bf16[16,4096]{1,0:T(8,128)(2,1)S(1)}, bf16[16,4096]{1,0:T(8,128)(2,1)S(1)}, u32[]{:S(2)}, u32[]{:S(2)}) collective-permute-start(bf16[16,4096]{1,0:T(8,128)(2,1)S(1)} %get-tuple-element.31), channel_id=1, source_target_pairs={{0,4},{2,6},{1,5},{3,7},{8,12},{10,14},{9,13},{11,15},{16,20},{18,... | collective-permute-start | bytes 393224 | tf_op jit(solution)/shard_map/ppermute | solution.py:261
  72.9 4.7 %collective-permute-start.6 = (bf16[16,4096]{1,0:T(8,128)(2,1)S(1)}, bf16[16,4096]{1,0:T(8,128)(2,1)S(1)}, u32[]{:S(2)}, u32[]{:S(2)}) collective-permute-start(bf16[16,4096]{1,0:T(8,128)(2,1)S(1)} %get-tuple-element.31), channel_id=1, source_target_pairs={{0,6},{1,7},{8,14},{9,15},{16,22},{17,23},{24,30},{25,31}} | collective-permute-start | bytes 393224 | tf_op jit(solution)/shard_map/ppermute | solution.py:261
  81.6 46.4 %copy-start.18 = (bf16[128,4096]{1,0:T(8,128)(2,1)}, bf16[128,4096]{1,0:T(8,128)(2,1)S(1)}, u32[]{:S(2)}) copy-start(bf16[128,4096]{1,0:T(8,128)(2,1)S(1)} %get-tuple-element.41.refs_5_) | copy-start | bytes 3145732
  100.4 23.4 %collective-permute-start.7 = (bf16[4,128,1024]{2,1,0:T(8,128)(2,1)S(1)}, bf16[4,128,1024]{2,1,0:T(8,128)(2,1)S(1)}, u32[]{:S(2)}, u32[]{:S(2)}) collective-permute-start(bf16[4,128,1024]{2,1,0:T(8,128)(2,1)S(1)} %all_to_all.10.own), channel_id=1, source_target_pairs={{0,2},{2,4},{4,6},{1,3},{3,5},{5,7},{8,10},{10,12},{12,14},{9,11},... | collective-permute-start | bytes 3145736 | tf_op jit(solution)/shard_map/ppermute | solution.py:261
  103.9 24.1 %collective-permute-start.8 = (bf16[4,128,1024]{2,1,0:T(8,128)(2,1)S(1)}, bf16[4,128,1024]{2,1,0:T(8,128)(2,1)S(1)}, u32[]{:S(2)}, u32[]{:S(2)}) collective-permute-start(bf16[4,128,1024]{2,1,0:T(8,128)(2,1)S(1)} %all_to_all.10.own), channel_id=1, source_target_pairs={{2,0},{4,2},{6,4},{3,1},{5,3},{7,5},{10,8},{12,10},{14,12},{11,9},... | collective-permute-start | bytes 3145736 | tf_op jit(solution)/shard_map/ppermute | solution.py:261
  123.8 19.5 %collective-permute-start.11 = (bf16[4,128,1024]{2,1,0:T(8,128)(2,1)S(1)}, bf16[4,128,1024]{2,1,0:T(8,128)(2,1)S(1)}, u32[]{:S(2)}, u32[]{:S(2)}) collective-permute-start(bf16[4,128,1024]{2,1,0:T(8,128)(2,1)S(1)} %collective-permute-done.7.refs_0_), channel_id=1, source_target_pairs={{2,4},{4,6},{3,5},{5,7},{10,12},{12,14},{11,13},{13,15},{18,20},{2... | collective-permute-start | bytes 3145736 | tf_op jit(solution)/shard_map/ppermute | solution.py:261
  128.0 23.4 %collective-permute-start.12 = (bf16[4,128,1024]{2,1,0:T(8,128)(2,1)S(1)}, bf16[4,128,1024]{2,1,0:T(8,128)(2,1)}, u32[]{:S(2)}, u32[]{:S(2)}) collective-permute-start(bf16[4,128,1024]{2,1,0:T(8,128)(2,1)S(1)} %collective-permute-done.8.refs_1_.refs_5_), channel_id=1, source_target_pairs={{2,0},{4,2},{3,1},{5,3},{10,8},{12,10},{11,9},{13,11},{18,16},{20,... | collective-permute-start | bytes 3145736 | tf_op jit(solution)/shard_map/ppermute | solution.py:261
  136.0 28.8 %collective-permute-start.10 = (bf16[1,4,128,1024]{3,2,1,0:T(8,128)(2,1)}, bf16[1,4,128,1024]{3,2,1,0:T(8,128)(2,1)}, u32[]{:S(2)}, u32[]{:S(2)}) collective-permute-start(bf16[1,4,128,1024]{3,2,1,0:T(8,128)(2,1)} %delta.2.refs_0_), channel_id=1, source_target_pairs={{6,4},{7,5},{14,12},{15,13},{22,20},{23,21},{30,28},{31,29}} | collective-permute-start | bytes 3145736 | tf_op jit(solution)/shard_map/ppermute | solution.py:261
  137.7 27.2 %collective-permute-start.9 = (bf16[1,4,128,1024]{3,2,1,0:T(8,128)(2,1)}, bf16[1,4,128,1024]{3,2,1,0:T(8,128)(2,1)}, u32[]{:S(2)}, u32[]{:S(2)}) collective-permute-start(bf16[1,4,128,1024]{3,2,1,0:T(8,128)(2,1)} %delta.2.refs_0_), channel_id=1, source_target_pairs={{0,2},{1,3},{8,10},{9,11},{16,18},{17,19},{24,26},{25,27}} | collective-permute-start | bytes 3145736 | tf_op jit(solution)/shard_map/ppermute | solution.py:261
  143.3 21.5 %copy-start.8 = (bf16[4,128,1024]{2,1,0:T(8,128)(2,1)}, bf16[4,128,1024]{2,1,0:T(8,128)(2,1)S(1)}, u32[]{:S(2)}) copy-start(bf16[4,128,1024]{2,1,0:T(8,128)(2,1)S(1)} %collective-permute-done.11.refs_0_.refs_1_) | copy-start | bytes 3145732
  143.3 47.5 %collective-permute-start.15 = (bf16[4,128,1024]{2,1,0:T(8,128)(2,1)S(1)}, bf16[4,128,1024]{2,1,0:T(8,128)(2,1)}, u32[]{:S(2)}, u32[]{:S(2)}) collective-permute-start(bf16[4,128,1024]{2,1,0:T(8,128)(2,1)S(1)} %collective-permute-done.11.refs_0_.refs_1_), channel_id=1, source_target_pairs={{4,6},{5,7},{12,14},{13,15},{20,22},{21,23},{28,30},{29,31}} | collective-permute-start | bytes 3145736 | tf_op jit(solution)/shard_map/ppermute | solution.py:261
  151.4 39.4 %collective-permute-start.16 = (bf16[4,128,1024]{2,1,0:T(8,128)(2,1)}, bf16[4,128,1024]{2,1,0:T(8,128)(2,1)}, u32[]{:S(2)}, u32[]{:S(2)}) collective-permute-start(bf16[4,128,1024]{2,1,0:T(8,128)(2,1)} %collective-permute-done.12.refs_1_.refs_4_), channel_id=1, source_target_pairs={{2,0},{3,1},{10,8},{11,9},{18,16},{19,17},{26,24},{27,25}} | collective-permute-start | bytes 3145736 | tf_op jit(solution)/shard_map/ppermute | solution.py:261
  169.5 23.5 %collective-permute-start.13 = (bf16[1,4,128,1024]{3,2,1,0:T(8,128)(2,1)}, bf16[1,4,128,1024]{3,2,1,0:T(8,128)(2,1)S(1)}, u32[]{:S(2)}, u32[]{:S(2)}) collective-permute-start(bf16[1,4,128,1024]{3,2,1,0:T(8,128)(2,1)} %get-tuple-element.33), channel_id=1, source_target_pairs={{0,2},{2,4},{1,3},{3,5},{8,10},{10,12},{9,11},{11,13},{16,18},{18,... | collective-permute-start | bytes 3145736 | tf_op jit(solution)/shard_map/ppermute | solution.py:261
  175.1 18.0 %collective-permute-start.14 = (bf16[1,4,128,1024]{3,2,1,0:T(8,128)(2,1)}, bf16[1,4,128,1024]{3,2,1,0:T(8,128)(2,1)}, u32[]{:S(2)}, u32[]{:S(2)}) collective-permute-start(bf16[1,4,128,1024]{3,2,1,0:T(8,128)(2,1)} %get-tuple-element.34), channel_id=1, source_target_pairs={{4,2},{6,4},{5,3},{7,5},{12,10},{14,12},{13,11},{15,13},{20,18},{2... | collective-permute-start | bytes 3145736 | tf_op jit(solution)/shard_map/ppermute | solution.py:261
  196.5 38.9 %collective-permute-start.17 = (bf16[1,4,128,1024]{3,2,1,0:T(8,128)(2,1)S(1)}, bf16[1,4,128,1024]{3,2,1,0:T(8,128)(2,1)S(1)}, u32[]{:S(2)}, u32[]{:S(2)}) collective-permute-start(bf16[1,4,128,1024]{3,2,1,0:T(8,128)(2,1)S(1)} %get-tuple-element.35.refs_6_.after), channel_id=1, source_target_pairs={{0,2},{2,4},{4,6},{1,3},{3,5},{5,7},{8,10},{10,12},{12,14},{9,11},... | collective-permute-start | bytes 3145736 | tf_op jit(solution)/shard_map/ppermute | solution.py:261
  202.9 32.6 %collective-permute-start.18 = (bf16[1,4,128,1024]{3,2,1,0:T(8,128)(2,1)S(1)}, bf16[1,4,128,1024]{3,2,1,0:T(8,128)(2,1)S(1)}, u32[]{:S(2)}, u32[]{:S(2)}) collective-permute-start(bf16[1,4,128,1024]{3,2,1,0:T(8,128)(2,1)S(1)} %get-tuple-element.36), channel_id=1, source_target_pairs={{2,0},{4,2},{6,4},{3,1},{5,3},{7,5},{10,8},{12,10},{14,12},{11,9},... | collective-permute-start | bytes 3145736 | tf_op jit(solution)/shard_map/ppermute | solution.py:261
  215.6 23.7 %collective-permute-start.19 = (bf16[512,1024]{1,0:T(8,128)(2,1)S(1)}, bf16[512,1024]{1,0:T(8,128)(2,1)S(1)}, u32[]{:S(2)}, u32[]{:S(2)}) collective-permute-start(bf16[512,1024]{1,0:T(8,128)(2,1)S(1)} %weight.4.after), channel_id=1, source_target_pairs={{0,24},{8,16},{16,8},{24,0},{1,25},{9,17},{17,9},{25,1},{2,26},{10... | collective-permute-start | bytes 3145736 | tf_op jit(solution)/shard_map/ppermute | solution.py:257
  239.3 7.9 %collective-permute-start.22 = (bf16[128,1024]{1,0:T(8,128)(2,1)S(1)}, bf16[128,1024]{1,0:T(8,128)(2,1)S(1)}, u32[]{:S(2)}, u32[]{:S(2)}) collective-permute-start(bf16[128,1024]{1,0:T(8,128)(2,1)S(1)} %hold.7), channel_id=1, source_target_pairs={{0,24},{8,16},{16,8},{24,0},{1,25},{9,17},{17,9},{25,1},{2,26},{10... | collective-permute-start | bytes 786440 | tf_op jit(solution)/shard_map/ppermute | solution.py:257
  242.7 10.0 %collective-permute-start.21 = (bf16[128,1024]{1,0:T(8,128)(2,1)S(1)}, bf16[128,1024]{1,0:T(8,128)(2,1)S(1)}, u32[]{:S(2)}, u32[]{:S(2)}) collective-permute-start(bf16[128,1024]{1,0:T(8,128)(2,1)S(1)} %hold.6), channel_id=1, source_target_pairs={{0,16},{8,24},{16,0},{24,8},{1,17},{9,25},{17,1},{25,9},{2,18},{10... | collective-permute-start | bytes 786440 | tf_op jit(solution)/shard_map/ppermute | solution.py:257
  244.9 9.2 %collective-permute-start.20 = (bf16[128,1024]{1,0:T(8,128)(2,1)S(1)}, bf16[128,1024]{1,0:T(8,128)(2,1)S(1)}, u32[]{:S(2)}, u32[]{:S(2)}) collective-permute-start(bf16[128,1024]{1,0:T(8,128)(2,1)S(1)} %hold.5), channel_id=1, source_target_pairs={{0,8},{8,0},{16,24},{24,16},{1,9},{9,1},{17,25},{25,17},{2,10},{10... | collective-permute-start | bytes 786440 | tf_op jit(solution)/shard_map/ppermute | solution.py:257
  254.1 26.9 %collective-permute-start.27 = (bf16[512,1024]{1,0:T(8,128)(2,1)S(1)}, bf16[512,1024]{1,0:T(8,128)(2,1)S(1)}, u32[]{:S(2)}, u32[]{:S(2)}) collective-permute-start(bf16[512,1024]{1,0:T(8,128)(2,1)S(1)} %hold.9), channel_id=1, source_target_pairs={{0,16},{8,24},{16,0},{24,8},{1,17},{9,25},{17,1},{25,9},{2,18},{10... | collective-permute-start | bytes 3145736 | tf_op jit(solution)/shard_map/ppermute | solution.py:257
  255.1 25.9 %collective-permute-start.26 = (bf16[512,1024]{1,0:T(8,128)(2,1)S(1)}, bf16[512,1024]{1,0:T(8,128)(2,1)S(1)}, u32[]{:S(2)}, u32[]{:S(2)}) collective-permute-start(bf16[512,1024]{1,0:T(8,128)(2,1)S(1)} %hold.8), channel_id=1, source_target_pairs={{0,8},{8,0},{16,24},{24,16},{1,9},{9,1},{17,25},{25,17},{2,10},{10... | collective-permute-start | bytes 3145736 | tf_op jit(solution)/shard_map/ppermute | solution.py:257
  262.5 8.7 %collective-permute-start.23 = (bf16[16,4096]{1,0:T(8,128)(2,1)S(1)}, bf16[16,4096]{1,0:T(8,128)(2,1)S(1)}, u32[]{:S(2)}, u32[]{:S(2)}) collective-permute-start(bf16[16,4096]{1,0:T(8,128)(2,1)S(1)} %get-tuple-element.44), channel_id=1, source_target_pairs={{2,0},{4,2},{6,4},{3,1},{5,3},{7,5},{10,8},{12,10},{14,12},{11,9},... | collective-permute-start | bytes 393224 | tf_op jit(solution)/shard_map/ppermute | solution.py:261
  263.8 9.3 %collective-permute-start.24 = (bf16[16,4096]{1,0:T(8,128)(2,1)S(1)}, bf16[16,4096]{1,0:T(8,128)(2,1)S(1)}, u32[]{:S(2)}, u32[]{:S(2)}) collective-permute-start(bf16[16,4096]{1,0:T(8,128)(2,1)S(1)} %get-tuple-element.44), channel_id=1, source_target_pairs={{4,0},{6,2},{5,1},{7,3},{12,8},{14,10},{13,9},{15,11},{20,16},{22,... | collective-permute-start | bytes 393224 | tf_op jit(solution)/shard_map/ppermute | solution.py:261
  265.1 10.9 %collective-permute-start.25 = (bf16[16,4096]{1,0:T(8,128)(2,1)S(1)}, bf16[16,4096]{1,0:T(8,128)(2,1)S(1)}, u32[]{:S(2)}, u32[]{:S(2)}) collective-permute-start(bf16[16,4096]{1,0:T(8,128)(2,1)S(1)} %get-tuple-element.44), channel_id=1, source_target_pairs={{6,0},{7,1},{14,8},{15,9},{22,16},{23,17},{30,24},{31,25}} | collective-permute-start | bytes 393224 | tf_op jit(solution)/shard_map/ppermute | solution.py:261
  (22 other events, 176.6 us)
Sparse Core Ops, SparseCore 0:
  62.7 64.1 all-gather.2
